TPU v7x, 32 devices: a whole 2x2x4 slice. The times are simulated.
32 devices in a mesh: section: 2 (over y), dp: 4 (over x, core), mp: 4 (over z).
Axes of the slice: x: 2, y: 2, z: 4, core: 2. Of those that a mesh axis runs over, the one named last changes fastest.
Arguments:
- inputs: bfloat16 [2, 16, 2080, 512], P('section', 'dp', 'mp'), may hold values from -6 to 6
- text_lengths: int32 [16], P('dp'), may hold values from 5 to 77, as said below
- attn_norm_gain: float32 [2, 512], P('section'), may hold values from 0.5 to 1.5
- attn_norm_bias: float32 [2, 512], P('section'), may hold values from -1 to 1
- qkv_weight: bfloat16 [2, 512, 8, 192], P('section', None, 'mp'), may hold values from -0.25 to 0.25
- out_weight: bfloat16 [2, 8, 64, 512], P('section', 'mp'), may hold values from -4 to 4
- out_bias: float32 [2, 512], P('section'), may hold values from -1 to 1
- mlp_norm_gain: float32 [2, 512], P('section'), may hold values from 0.5 to 1.5
- mlp_norm_bias: float32 [2, 512], P('section'), may hold values from -1 to 1
- up_weight: bfloat16 [2, 512, 2048], P('section', None, 'mp'), may hold values from -0.25 to 0.25
- up_bias: float32 [2, 2048], P('section', 'mp'), may hold values from -1 to 1
- down_weight: bfloat16 [2, 2048, 512], P('section', 'mp'), may hold values from -0.125 to 0.125
- down_bias: float32 [2, 512], P('section'), may hold values from -1 to 1
Outputs:
- ends: float32 [2, 16, 2080, 512], P('section', 'dp', 'mp')
- grad_attn_gain: float32 [2, 512], P('section')
- grad_attn_bias: float32 [2, 512], P('section')
- grad_qkv_weight: float32 [2, 512, 8, 192], P('section', None, 'mp')
- grad_out_weight: float32 [2, 8, 64, 512], P('section', 'mp')
- grad_out_bias: float32 [2, 512], P('section')
- grad_mlp_gain: float32 [2, 512], P('section')
- grad_mlp_bias: float32 [2, 512], P('section')
- grad_up_weight: float32 [2, 512, 2048], P('section', None, 'mp')
- grad_up_bias: float32 [2, 2048], P('section', 'mp')
- grad_down_weight: float32 [2, 2048, 512], P('section', 'mp')
- grad_down_bias: float32 [2, 512], P('section')
Inputs may be any that keep to these rules, and one draw needn't show every extreme that they name: An item uses its first text_lengths language slots; some item of the batch has 77 and some has 5.
All inputs are finite; a program needn't handle non-finite values.
Results may differ from a plain program's by a relative error of at most 0.017.
Values may be sent and summed in bfloat16 or wider, within the bound.
A program may use at most 128 MiB of HBM per device.

v0:
```python
import jax
import jax.numpy as jnp
from jax import lax
from jax.sharding import PartitionSpec as P

VIEWS = 5
PATCH = 400
TEXT = 80


def from_behind(block, axis, distance):
    devices = range(lax.axis_size(axis))
    route = [(i - distance, i) for i in devices if i - distance in devices]
    return lax.ppermute(block, axis, route)


def layer_norm(values, scale_vec, shift_vec):
    center = jnp.mean(values, -1, keepdims=True)
    offset = values - center
    spread = jnp.mean(offset * offset, -1, keepdims=True)
    return offset * lax.rsqrt(spread + 1e-05) * scale_vec + shift_vec


def probabilities(queries, keys_in, key_mask):
    scores = (
        jnp.einsum("bqhe,bkhe->bhqk", queries, keys_in, preferred_element_type=jnp.float32) * 0.125
    )
    scores = jnp.where(key_mask[:, None, None, :], scores, -1e30)
    expon = jnp.exp(scores - jnp.max(scores, -1, keepdims=True))
    return expon / jnp.sum(expon, -1, keepdims=True)


def attend_forward(queries, keys_in, values_in, key_mask):
    weights = probabilities(queries, keys_in, key_mask).astype(jnp.bfloat16)
    return jnp.einsum("bhqk,bkhe->bqhe", weights, values_in, preferred_element_type=jnp.float32)


def attend_backward(queries, keys_in, values_in, key_mask, grad_out):
    probs = probabilities(queries, keys_in, key_mask)
    grad_values = jnp.einsum(
        "bhqk,bqhe->bkhe", probs.astype(jnp.bfloat16), grad_out, preferred_element_type=jnp.float32
    )
    grad_probs = jnp.einsum(
        "bqhe,bkhe->bhqk", grad_out, values_in, preferred_element_type=jnp.float32
    )
    grad_scores = (probs * (grad_probs - jnp.sum(probs * grad_probs, -1, keepdims=True))).astype(
        jnp.bfloat16
    )
    grad_queries = (
        jnp.einsum("bhqk,bkhe->bqhe", grad_scores, keys_in, preferred_element_type=jnp.float32)
        * 0.125
    )
    grad_keys = (
        jnp.einsum("bhqk,bqhe->bkhe", grad_scores, queries, preferred_element_type=jnp.float32)
        * 0.125
    )
    return (grad_queries, grad_keys, grad_values)


def split_heads(projected):
    head_size = projected.shape[-1] // 3
    return (
        projected[..., :head_size],
        projected[..., head_size : 2 * head_size],
        projected[..., 2 * head_size :],
    )


def by_views(tensor):
    return tensor[: VIEWS * PATCH].reshape((VIEWS, PATCH) + tensor.shape[1:])


def within_forward(queries, keys_in, values_in, allowed):
    patch_rows = VIEWS * PATCH
    patch_out = attend_forward(
        by_views(queries),
        by_views(keys_in),
        by_views(values_in),
        jnp.ones((VIEWS, PATCH), jnp.bool_),
    )
    text_out = attend_forward(
        queries[patch_rows:][None],
        keys_in[patch_rows:][None],
        values_in[patch_rows:][None],
        allowed[None],
    )
    return jnp.concatenate([patch_out.reshape((patch_rows,) + queries.shape[1:]), text_out[0]], 0)


def full_mask_of(allowed):
    return jnp.concatenate([jnp.ones((VIEWS * PATCH,), jnp.bool_), allowed])[None]


def joint_forward(queries, keys_in, values_in, allowed):
    full_mask = full_mask_of(allowed)
    blocks = queries.reshape((4, queries.shape[0] // 4) + queries.shape[1:])

    def one_block(block):
        return attend_forward(block[None], keys_in[None], values_in[None], full_mask)[0]

    return lax.map(one_block, blocks).reshape(queries.shape)


def within_backward(queries, keys_in, values_in, allowed, grad_out):
    patch_rows = VIEWS * PATCH
    patch_grads = attend_backward(
        by_views(queries),
        by_views(keys_in),
        by_views(values_in),
        jnp.ones((VIEWS, PATCH), jnp.bool_),
        by_views(grad_out),
    )
    text_grads = attend_backward(
        queries[patch_rows:][None],
        keys_in[patch_rows:][None],
        values_in[patch_rows:][None],
        allowed[None],
        grad_out[patch_rows:][None],
    )
    joined = [
        jnp.concatenate([patch.reshape((patch_rows,) + queries.shape[1:]), text[0]], 0)
        for patch, text in zip(patch_grads, text_grads)
    ]
    return jnp.concatenate(joined, -1)


def joint_backward(queries, keys_in, values_in, allowed, grad_out):
    full_mask = full_mask_of(allowed)
    block_shape = (4, queries.shape[0] // 4) + queries.shape[1:]

    def one_block(totals, pair):
        block, grad_block = pair
        grad_queries, grad_keys, grad_values = attend_backward(
            block[None], keys_in[None], values_in[None], full_mask, grad_block[None]
        )
        return ((totals[0] + grad_keys[0], totals[1] + grad_values[0]), grad_queries[0])

    empty = jnp.zeros(keys_in.shape, jnp.float32)
    (grad_keys, grad_values), grad_queries = lax.scan(
        one_block, (empty, empty), (queries.reshape(block_shape), grad_out.reshape(block_shape))
    )
    return jnp.concatenate([grad_queries.reshape(queries.shape), grad_keys, grad_values], -1)


def attention(projected, length, within):
    queries, keys_in, values_in = split_heads(projected)
    allowed = jnp.arange(TEXT) < length
    return lax.cond(within, within_forward, joint_forward, queries, keys_in, values_in, allowed)


def attention_back(projected, grad_out, length, within):
    queries, keys_in, values_in = split_heads(projected)
    allowed = jnp.arange(TEXT) < length
    return lax.cond(
        within, within_backward, joint_backward, queries, keys_in, values_in, allowed, grad_out
    )


def rows_of(left, weight, form):
    return jnp.einsum(form, left, weight, preferred_element_type=jnp.float32)


def branch_total(left, weight, form):
    return lax.psum_scatter(
        rows_of(left, weight, form).astype(jnp.bfloat16), "mp", scatter_dimension=0, tiled=True
    ).astype(jnp.float32)


def grad_total(left, weight, form):
    return lax.psum_scatter(
        rows_of(left, weight, form).astype(jnp.bfloat16), "mp", scatter_dimension=0, tiled=True
    ).astype(jnp.float32)


def gather_normed(values):
    return lax.all_gather(values, "mp", axis=0, tiled=True)


def gather_grads(values):
    return lax.all_gather(values, "mp", axis=0, tiled=True)


def layer_forward(source, length, params, within):
    (
        gain_one,
        bias_one,
        weight_qkv,
        weight_out,
        bias_out,
        gain_two,
        bias_two,
        weight_up,
        bias_up,
        weight_down,
        bias_down,
    ) = params
    normed = gather_normed(layer_norm(source, gain_one, bias_one).astype(jnp.bfloat16))
    projected = jnp.einsum(
        "sd,dhe->she", normed, weight_qkv, preferred_element_type=jnp.float32
    ).astype(jnp.bfloat16)
    mixed = attention(projected, length, within).astype(jnp.bfloat16)
    middle = source + branch_total(mixed, weight_out, "shc,hcd->sd") + bias_out
    second = gather_normed(layer_norm(middle, gain_two, bias_two).astype(jnp.bfloat16))
    hidden_pre = jnp.dot(second, weight_up, preferred_element_type=jnp.float32) + bias_up
    hidden = jax.nn.gelu(hidden_pre).astype(jnp.bfloat16)
    result = middle + branch_total(hidden, weight_down, "sf,fd->sd") + bias_down
    return (result, (normed, projected, mixed, middle, second, hidden_pre, hidden))


def layer_backward(source, upstream, length, params, within):
    (
        gain_one,
        bias_one,
        weight_qkv,
        weight_out,
        bias_out,
        gain_two,
        bias_two,
        weight_up,
        bias_up,
        weight_down,
        bias_down,
    ) = params
    kept_values = layer_forward(source, length, params, within)[1]
    normed, projected, mixed, middle, second, hidden_pre, hidden = kept_values
    grad_branch = gather_grads(upstream.astype(jnp.bfloat16))
    grad_down = jnp.einsum("sf,sd->fd", hidden, grad_branch, preferred_element_type=jnp.float32)
    grad_hidden = jnp.einsum(
        "sd,fd->sf", grad_branch, weight_down, preferred_element_type=jnp.float32
    )
    gelu_pull = jax.vjp(jax.nn.gelu, hidden_pre)[1]
    grad_pre = gelu_pull(grad_hidden)[0].astype(jnp.bfloat16)
    grad_up_bias = jnp.sum(grad_pre.astype(jnp.float32), 0)
    grad_up = jnp.einsum("sd,sf->df", second, grad_pre, preferred_element_type=jnp.float32)
    grad_second = grad_total(grad_pre, weight_up, "sf,df->sd")
    norm_pull = jax.vjp(layer_norm, middle, gain_two, bias_two)[1]
    part_middle, grad_gain_two, grad_bias_two = norm_pull(grad_second)
    grad_middle = upstream + part_middle
    grad_attn = gather_grads(grad_middle.astype(jnp.bfloat16))
    grad_out = jnp.einsum("shc,sd->hcd", mixed, grad_attn, preferred_element_type=jnp.float32)
    grad_mixed = jnp.einsum(
        "sd,hcd->shc", grad_attn, weight_out, preferred_element_type=jnp.float32
    ).astype(jnp.bfloat16)
    grad_projected = attention_back(projected, grad_mixed, length, within).astype(jnp.bfloat16)
    grad_qkv = jnp.einsum("sd,she->dhe", normed, grad_projected, preferred_element_type=jnp.float32)
    grad_normed = grad_total(grad_projected, weight_qkv, "she,dhe->sd")
    first_pull = jax.vjp(layer_norm, source, gain_one, bias_one)[1]
    part_source, grad_gain_one, grad_bias_one = first_pull(grad_normed)
    grads = (
        grad_gain_one,
        grad_bias_one,
        grad_qkv,
        grad_out,
        jnp.sum(grad_middle, 0),
        grad_gain_two,
        grad_bias_two,
        grad_up,
        grad_up_bias,
        grad_down,
        jnp.sum(upstream, 0),
    )
    return (grad_middle + part_source, grads)


def per_device(
    inputs,
    text_lengths,
    attn_norm_gain,
    attn_norm_bias,
    qkv_weight,
    out_weight,
    out_bias,
    mlp_norm_gain,
    mlp_norm_bias,
    up_weight,
    up_bias,
    down_weight,
    down_bias,
):
    weights = (
        attn_norm_gain,
        attn_norm_bias,
        qkv_weight,
        out_weight,
        out_bias,
        mlp_norm_gain,
        mlp_norm_bias,
        up_weight,
        up_bias,
        down_weight,
        down_bias,
    )
    params = tuple((entry[0] for entry in weights))
    first_section = lax.axis_index("section") == 0
    local_items = inputs[0]
    micro_count = local_items.shape[0]
    row_count = local_items.shape[1]
    width = local_items.shape[2]

    def pick(step_index):
        return jnp.clip(step_index, 0, micro_count - 1)

    def forward_tick(carried, step_index):
        own_rows = local_items[pick(step_index)]
        source = jnp.where(first_section, own_rows, carried).astype(jnp.float32)
        length = text_lengths[jnp.where(first_section, pick(step_index), pick(step_index - 1))]
        result = layer_forward(source, length, params, first_section)[0]
        passed = from_behind(result.astype(jnp.bfloat16), "section", 1)
        return (passed, (result, carried))

    blank = jnp.zeros((row_count, width), jnp.bfloat16)
    _, (forward_rows, arrived) = lax.scan(forward_tick, blank, jnp.arange(micro_count + 1))
    arrived = arrived[1:]

    def backward_tick(carried, step_index):
        returned, totals = carried
        fresh = layer_forward(
            local_items[pick(step_index)].astype(jnp.float32),
            text_lengths[pick(step_index)],
            params,
            first_section,
        )[0]
        boundary = from_behind(fresh.astype(jnp.bfloat16), "section", 1)
        source = jnp.where(first_section, local_items[pick(step_index - 1)], boundary).astype(
            jnp.float32
        )
        upstream = jnp.where(first_section, returned, local_items[pick(step_index)]).astype(
            jnp.float32
        )
        length = text_lengths[jnp.where(first_section, pick(step_index - 1), pick(step_index))]
        live = jnp.where(first_section, step_index >= 1, step_index < micro_count).astype(
            jnp.float32
        )
        grad_source, grads = layer_backward(source, upstream, length, params, first_section)
        totals = jax.tree.map(lambda total, grad: total + live * grad, totals, grads)
        passed = from_behind(grad_source.astype(jnp.bfloat16), "section", -1)
        return ((passed, totals), grad_source)

    start_totals = tuple((jnp.zeros(entry.shape, jnp.float32) for entry in params))
    (_, totals), grad_rows = lax.scan(
        backward_tick, (blank, start_totals), jnp.arange(micro_count + 1)
    )
    ends = jnp.where(first_section, grad_rows[1:], forward_rows[1:])[None]
    split_parts = (totals[2], totals[3], totals[7], totals[8], totals[9])
    sharded = (
        lax.psum(split_parts[0].astype(jnp.bfloat16), "dp").astype(jnp.float32),
        lax.psum(split_parts[1].astype(jnp.bfloat16), "dp").astype(jnp.float32),
        lax.psum(split_parts[2].astype(jnp.bfloat16), "dp").astype(jnp.float32),
        lax.psum(split_parts[3].astype(jnp.bfloat16), "dp").astype(jnp.float32),
        lax.psum(split_parts[4].astype(jnp.bfloat16), "dp").astype(jnp.float32),
    )
    shared = lax.psum(
        (totals[0], totals[1], totals[4], totals[5], totals[6], totals[10]), ("dp", "mp")
    )
    return (
        ends,
        shared[0][None],
        shared[1][None],
        sharded[0][None],
        sharded[1][None],
        shared[2][None],
        shared[3][None],
        shared[4][None],
        sharded[2][None],
        sharded[3][None],
        sharded[4][None],
        shared[5][None],
    )


def solution(mesh):
    placed = (
        P("section", "dp", "mp", None),
        P("dp"),
        P("section", None),
        P("section", None),
        P("section", None, "mp", None),
        P("section", "mp", None, None),
        P("section", None),
        P("section", None),
        P("section", None),
        P("section", None, "mp"),
        P("section", "mp"),
        P("section", "mp", None),
        P("section", None),
    )
    return jax.shard_map(
        per_device,
        mesh=mesh,
        in_specs=placed,
        out_specs=(
            P("section", "dp", "mp", None),
            P("section", None),
            P("section", None),
            P("section", None, "mp", None),
            P("section", "mp", None, None),
            P("section", None),
            P("section", None),
            P("section", None),
            P("section", None, "mp"),
            P("section", "mp"),
            P("section", "mp", None),
            P("section", None),
        ),
        check_vma=False,
    )
```

profile of v0, /device:TPU:0, one launch (start us, length us, event | category | flops | bytes accessed | tf_op | source)
XLA Modules:
  0.0 5841.7 jit_solution(16812516461574545175)
XLA Ops:
  12.0 4289.8 %while.97 = (s32[]{:T(128)}, bf16[520,512]{1,0:T(8,128)(2,1)}, f32[512]{0:T(512)}, f32[512]{0:T(512)}, f32[512,2,192]{0,2,1:T(8,128)}, /*index=5*/f32[2,64,512]{...) while((s32[]{:T(128)}, bf16[520,512]{1,0:T(8,128)(2,1)}, ...), condition=%wide.region_58.59_spmd.clone, body=%wide.region_0.58_spmd.clone.sunk | while | flops 15492165632 | bytes 495005024 | solution.py:340
  102.3 81.9 %reduce-scatter.12.cloned.1.call-done = bf16[520,512]{1,0:T(8,128)(2,1)} async-done(((bf16[2080,512]{1,0:T(8,128)(2,1)}), bf16[520,512]{1,0:T(8,128)(2,1)}) %reduce-scatter.12.cloned.1.call-update) | async-done | bytes 532496 | tf_op jit(solution)/shard_map/while/body/eval_jaxpr/reduce_scatter | solution.py:164
  384.4 77.6 %reduce-scatter.16.cloned.1.call-done = bf16[520,512]{1,0:T(8,128)(2,1)} async-done(((bf16[2080,512]{1,0:T(8,128)(2,1)}), bf16[520,512]{1,0:T(8,128)(2,1)}) %reduce-scatter.16.cloned.1.call-update) | async-done | bytes 532496 | tf_op jit(solution)/shard_map/while/body/eval_jaxpr/reduce_scatter | solution.py:164
  670.3 60.3 %conditional.34 = (bf16[2080,2,192]{0,2,1:T(8,128)(2,1)}) conditional(s32[]{:T(128)} %convert_element_type.813, (bf16[2080,2,64]{0,2,1:T(8,128)(2,1)S(1)}, bf16[2080,2,64]{0,2,1:T(8,128)(2,1)}, pred[80]{0:T(512)(128)(4,1)S(1)}, bf16[2080,2,64]{0,2,1:T(8,128)(2,1)S(1)}, bf16[2080,2,64]{0,2,1:T(8,128)(2,1)}) %tuple.261, ...), branch_computations={%region_35.40_spmd, %region_41.47_spmd} | conditional | flops 1702209536 | bytes 109120712
  746.9 101.1 %reduce-scatter.20.cloned.1.call-done = bf16[520,512]{1,0:T(8,128)(2,1)} async-done(((bf16[2080,512]{1,0:T(8,128)(2,1)}), bf16[520,512]{1,0:T(8,128)(2,1)}) %reduce-scatter.20.cloned.1.call-update) | async-done | bytes 532496 | tf_op jit(solution)/shard_map/while/body/eval_jaxpr/reduce_scatter | solution.py:170
  955.8 81.9 %reduce-scatter.12.cloned.1.call-done = bf16[520,512]{1,0:T(8,128)(2,1)} async-done(((bf16[2080,512]{1,0:T(8,128)(2,1)}), bf16[520,512]{1,0:T(8,128)(2,1)}) %reduce-scatter.12.cloned.1.call-update) | async-done | bytes 532496 | tf_op jit(solution)/shard_map/while/body/eval_jaxpr/reduce_scatter | solution.py:164
  1238.1 77.8 %reduce-scatter.16.cloned.1.call-done = bf16[520,512]{1,0:T(8,128)(2,1)} async-done(((bf16[2080,512]{1,0:T(8,128)(2,1)}), bf16[520,512]{1,0:T(8,128)(2,1)}) %reduce-scatter.16.cloned.1.call-update) | async-done | bytes 532496 | tf_op jit(solution)/shard_map/while/body/eval_jaxpr/reduce_scatter | solution.py:164
  1600.6 101.1 %reduce-scatter.20.cloned.1.call-done = bf16[520,512]{1,0:T(8,128)(2,1)} async-done(((bf16[2080,512]{1,0:T(8,128)(2,1)}), bf16[520,512]{1,0:T(8,128)(2,1)}) %reduce-scatter.20.cloned.1.call-update) | async-done | bytes 532496 | tf_op jit(solution)/shard_map/while/body/eval_jaxpr/reduce_scatter | solution.py:170
  1809.6 81.9 %reduce-scatter.12.cloned.1.call-done = bf16[520,512]{1,0:T(8,128)(2,1)} async-done(((bf16[2080,512]{1,0:T(8,128)(2,1)}), bf16[520,512]{1,0:T(8,128)(2,1)}) %reduce-scatter.12.cloned.1.call-update) | async-done | bytes 532496 | tf_op jit(solution)/shard_map/while/body/eval_jaxpr/reduce_scatter | solution.py:164
  2091.8 77.7 %reduce-scatter.16.cloned.1.call-done = bf16[520,512]{1,0:T(8,128)(2,1)} async-done(((bf16[2080,512]{1,0:T(8,128)(2,1)}), bf16[520,512]{1,0:T(8,128)(2,1)}) %reduce-scatter.16.cloned.1.call-update) | async-done | bytes 532496 | tf_op jit(solution)/shard_map/while/body/eval_jaxpr/reduce_scatter | solution.py:164
  2454.1 101.2 %reduce-scatter.20.cloned.1.call-done = bf16[520,512]{1,0:T(8,128)(2,1)} async-done(((bf16[2080,512]{1,0:T(8,128)(2,1)}), bf16[520,512]{1,0:T(8,128)(2,1)}) %reduce-scatter.20.cloned.1.call-update) | async-done | bytes 532496 | tf_op jit(solution)/shard_map/while/body/eval_jaxpr/reduce_scatter | solution.py:170
  2663.0 81.7 %reduce-scatter.12.cloned.1.call-done = bf16[520,512]{1,0:T(8,128)(2,1)} async-done(((bf16[2080,512]{1,0:T(8,128)(2,1)}), bf16[520,512]{1,0:T(8,128)(2,1)}) %reduce-scatter.12.cloned.1.call-update) | async-done | bytes 532496 | tf_op jit(solution)/shard_map/while/body/eval_jaxpr/reduce_scatter | solution.py:164
  2945.1 77.6 %reduce-scatter.16.cloned.1.call-done = bf16[520,512]{1,0:T(8,128)(2,1)} async-done(((bf16[2080,512]{1,0:T(8,128)(2,1)}), bf16[520,512]{1,0:T(8,128)(2,1)}) %reduce-scatter.16.cloned.1.call-update) | async-done | bytes 532496 | tf_op jit(solution)/shard_map/while/body/eval_jaxpr/reduce_scatter | solution.py:164
  3307.5 101.2 %reduce-scatter.20.cloned.1.call-done = bf16[520,512]{1,0:T(8,128)(2,1)} async-done(((bf16[2080,512]{1,0:T(8,128)(2,1)}), bf16[520,512]{1,0:T(8,128)(2,1)}) %reduce-scatter.20.cloned.1.call-update) | async-done | bytes 532496 | tf_op jit(solution)/shard_map/while/body/eval_jaxpr/reduce_scatter | solution.py:170
  3516.3 81.7 %reduce-scatter.12.cloned.1.call-done = bf16[520,512]{1,0:T(8,128)(2,1)} async-done(((bf16[2080,512]{1,0:T(8,128)(2,1)}), bf16[520,512]{1,0:T(8,128)(2,1)}) %reduce-scatter.12.cloned.1.call-update) | async-done | bytes 532496 | tf_op jit(solution)/shard_map/while/body/eval_jaxpr/reduce_scatter | solution.py:164
  3798.2 78.0 %reduce-scatter.16.cloned.1.call-done = bf16[520,512]{1,0:T(8,128)(2,1)} async-done(((bf16[2080,512]{1,0:T(8,128)(2,1)}), bf16[520,512]{1,0:T(8,128)(2,1)}) %reduce-scatter.16.cloned.1.call-update) | async-done | bytes 532496 | tf_op jit(solution)/shard_map/while/body/eval_jaxpr/reduce_scatter | solution.py:164
  4160.8 101.2 %reduce-scatter.20.cloned.1.call-done = bf16[520,512]{1,0:T(8,128)(2,1)} async-done(((bf16[2080,512]{1,0:T(8,128)(2,1)}), bf16[520,512]{1,0:T(8,128)(2,1)}) %reduce-scatter.20.cloned.1.call-update) | async-done | bytes 532496 | tf_op jit(solution)/shard_map/while/body/eval_jaxpr/reduce_scatter | solution.py:170
  4312.4 1440.4 %while.96 = (s32[]{:T(128)}, bf16[520,512]{1,0:T(8,128)(2,1)}, f32[5,520,512]{2,1,0:T(8,128)}, pred[]{:T(512)}, s32[5]{0:T(128)}, /*index=5*/bf16[4,520,512]{2,1...) while((s32[]{:T(128)}, bf16[520,512]{1,0:T(8,128)(2,1)}, ...), condition=%wide.region_76.77_spmd, body=%wide.region_59.76_spmd.sunk | while | flops 4148324864 | bytes 98649840 | solution.py:312
  4403.2 78.4 %reduce-scatter.8.cloned.1.call-done = bf16[520,512]{1,0:T(8,128)(2,1)} async-done(((bf16[2080,512]{1,0:T(8,128)(2,1)}), bf16[520,512]{1,0:T(8,128)(2,1)}) %reduce-scatter.8.cloned.1.call-update) | async-done | bytes 532496 | tf_op jit(solution)/shard_map/while/body/eval_jaxpr/reduce_scatter | solution.py:164
  4691.8 78.4 %reduce-scatter.8.cloned.1.call-done = bf16[520,512]{1,0:T(8,128)(2,1)} async-done(((bf16[2080,512]{1,0:T(8,128)(2,1)}), bf16[520,512]{1,0:T(8,128)(2,1)}) %reduce-scatter.8.cloned.1.call-update) | async-done | bytes 532496 | tf_op jit(solution)/shard_map/while/body/eval_jaxpr/reduce_scatter | solution.py:164
  4980.5 78.4 %reduce-scatter.8.cloned.1.call-done = bf16[520,512]{1,0:T(8,128)(2,1)} async-done(((bf16[2080,512]{1,0:T(8,128)(2,1)}), bf16[520,512]{1,0:T(8,128)(2,1)}) %reduce-scatter.8.cloned.1.call-update) | async-done | bytes 532496 | tf_op jit(solution)/shard_map/while/body/eval_jaxpr/reduce_scatter | solution.py:164
  5269.2 78.4 %reduce-scatter.8.cloned.1.call-done = bf16[520,512]{1,0:T(8,128)(2,1)} async-done(((bf16[2080,512]{1,0:T(8,128)(2,1)}), bf16[520,512]{1,0:T(8,128)(2,1)}) %reduce-scatter.8.cloned.1.call-update) | async-done | bytes 532496 | tf_op jit(solution)/shard_map/while/body/eval_jaxpr/reduce_scatter | solution.py:164
  5557.8 78.4 %reduce-scatter.8.cloned.1.call-done = bf16[520,512]{1,0:T(8,128)(2,1)} async-done(((bf16[2080,512]{1,0:T(8,128)(2,1)}), bf16[520,512]{1,0:T(8,128)(2,1)}) %reduce-scatter.8.cloned.1.call-update) | async-done | bytes 532496 | tf_op jit(solution)/shard_map/while/body/eval_jaxpr/reduce_scatter | solution.py:164
  5760.3 60.7 %all-reduce.4 = (f32[1,512]{1,0:T(1,128)}, f32[1,512]{1,0:T(1,128)}, f32[1,512]{1,0:T(1,128)}, f32[1,512]{1,0:T(1,128)}, f32[1,512]{1,0:T(1,128)}, /*index=5*/f32[1,512]{1,0:T(1,128)}) all-reduce(f32[1,512]{1,0:T(1,128)} %bitcast.641, f32[1,512]{1,0:T(1,128)} %bitcast.640, ...), channel_id=1, replica_groups=mesh['section'=2,'dp'=4,'mp'=4] {'dp','mp'}, use_global_device_ids=true, to_apply=%region_77.78 | all-reduce | flops 3072 | bytes 24576 | tf_op jit(solution)/shard_map/psum | solution.py:352
  (1905 shorter events, 4685.2 us)
Async XLA Ops:
  15.1 169.1 %reduce-scatter.12.cloned.1.call-start = ((), (), s32[]{:S(2)}) async-start(), calls=%async_computation.13 | async-start | bytes 2662400 | tf_op jit(solution)/shard_map/while/body/eval_jaxpr/reduce_scatter | solution.py:164
  384.4 172.1 %all-gather.21.cloned.1.call-start = ((), (), s32[]{:S(2)}) async-start(), calls=%async_computation.19 | async-start | bytes 2662400 | tf_op jit(solution)/shard_map/while/body/eval_jaxpr/all_gather | solution.py:176
  621.0 227.1 %reduce-scatter.20.cloned.1.call-start = ((), (), s32[]{:S(2)}) async-start(), calls=%async_computation.22 | async-start | bytes 2662400 | tf_op jit(solution)/shard_map/while/body/eval_jaxpr/reduce_scatter | solution.py:170
  872.8 165.0 %reduce-scatter.12.cloned.1.call-start = ((), (), s32[]{:S(2)}) async-start(), calls=%async_computation.13 | async-start | bytes 2662400 | tf_op jit(solution)/shard_map/while/body/eval_jaxpr/reduce_scatter | solution.py:164
  1156.1 159.8 %reduce-scatter.16.cloned.1.call-start = ((), (), s32[]{:S(2)}) async-start(), calls=%async_computation.18 | async-start | bytes 2662400 | tf_op jit(solution)/shard_map/while/body/eval_jaxpr/reduce_scatter | solution.py:164
  1238.0 172.1 %all-gather.21.cloned.1.call-start = ((), (), s32[]{:S(2)}) async-start(), calls=%async_computation.19 | async-start | bytes 2662400 | tf_op jit(solution)/shard_map/while/body/eval_jaxpr/all_gather | solution.py:176
  1474.7 227.1 %reduce-scatter.20.cloned.1.call-start = ((), (), s32[]{:S(2)}) async-start(), calls=%async_computation.22 | async-start | bytes 2662400 | tf_op jit(solution)/shard_map/while/body/eval_jaxpr/reduce_scatter | solution.py:170
  1726.3 165.2 %reduce-scatter.12.cloned.1.call-start = ((), (), s32[]{:S(2)}) async-start(), calls=%async_computation.13 | async-start | bytes 2662400 | tf_op jit(solution)/shard_map/while/body/eval_jaxpr/reduce_scatter | solution.py:164
  2009.8 159.6 %reduce-scatter.16.cloned.1.call-start = ((), (), s32[]{:S(2)}) async-start(), calls=%async_computation.18 | async-start | bytes 2662400 | tf_op jit(solution)/shard_map/while/body/eval_jaxpr/reduce_scatter | solution.py:164
  2091.7 172.0 %all-gather.21.cloned.1.call-start = ((), (), s32[]{:S(2)}) async-start(), calls=%async_computation.19 | async-start | bytes 2662400 | tf_op jit(solution)/shard_map/while/body/eval_jaxpr/all_gather | solution.py:176
  2328.2 227.1 %reduce-scatter.20.cloned.1.call-start = ((), (), s32[]{:S(2)}) async-start(), calls=%async_computation.22 | async-start | bytes 2662400 | tf_op jit(solution)/shard_map/while/body/eval_jaxpr/reduce_scatter | solution.py:170
  2579.7 165.0 %reduce-scatter.12.cloned.1.call-start = ((), (), s32[]{:S(2)}) async-start(), calls=%async_computation.13 | async-start | bytes 2662400 | tf_op jit(solution)/shard_map/while/body/eval_jaxpr/reduce_scatter | solution.py:164
  2863.1 159.6 %reduce-scatter.16.cloned.1.call-start = ((), (), s32[]{:S(2)}) async-start(), calls=%async_computation.18 | async-start | bytes 2662400 | tf_op jit(solution)/shard_map/while/body/eval_jaxpr/reduce_scatter | solution.py:164
  2945.0 172.1 %all-gather.21.cloned.1.call-start = ((), (), s32[]{:S(2)}) async-start(), calls=%async_computation.19 | async-start | bytes 2662400 | tf_op jit(solution)/shard_map/while/body/eval_jaxpr/all_gather | solution.py:176
  3181.6 227.1 %reduce-scatter.20.cloned.1.call-start = ((), (), s32[]{:S(2)}) async-start(), calls=%async_computation.22 | async-start | bytes 2662400 | tf_op jit(solution)/shard_map/while/body/eval_jaxpr/reduce_scatter | solution.py:170
  3433.1 165.0 %reduce-scatter.12.cloned.1.call-start = ((), (), s32[]{:S(2)}) async-start(), calls=%async_computation.13 | async-start | bytes 2662400 | tf_op jit(solution)/shard_map/while/body/eval_jaxpr/reduce_scatter | solution.py:164
  3716.4 159.8 %reduce-scatter.16.cloned.1.call-start = ((), (), s32[]{:S(2)}) async-start(), calls=%async_computation.18 | async-start | bytes 2662400 | tf_op jit(solution)/shard_map/while/body/eval_jaxpr/reduce_scatter | solution.py:164
  3798.1 172.3 %all-gather.21.cloned.1.call-start = ((), (), s32[]{:S(2)}) async-start(), calls=%async_computation.19 | async-start | bytes 2662400 | tf_op jit(solution)/shard_map/while/body/eval_jaxpr/all_gather | solution.py:176
  4034.9 227.1 %reduce-scatter.20.cloned.1.call-start = ((), (), s32[]{:S(2)}) async-start(), calls=%async_computation.22 | async-start | bytes 2662400 | tf_op jit(solution)/shard_map/while/body/eval_jaxpr/reduce_scatter | solution.py:170
  4316.0 165.6 %reduce-scatter.8.cloned.1.call-start = ((), (), s32[]{:S(2)}) async-start(), calls=%async_computation.9 | async-start | bytes 2662400 | tf_op jit(solution)/shard_map/while/body/eval_jaxpr/reduce_scatter | solution.py:164
  4601.7 168.5 %reduce-scatter.8.cloned.1.call-start = ((), (), s32[]{:S(2)}) async-start(), calls=%async_computation.9 | async-start | bytes 2662400 | tf_op jit(solution)/shard_map/while/body/eval_jaxpr/reduce_scatter | solution.py:164
  4890.4 168.5 %reduce-scatter.8.cloned.1.call-start = ((), (), s32[]{:S(2)}) async-start(), calls=%async_computation.9 | async-start | bytes 2662400 | tf_op jit(solution)/shard_map/while/body/eval_jaxpr/reduce_scatter | solution.py:164
  5179.1 168.5 %reduce-scatter.8.cloned.1.call-start = ((), (), s32[]{:S(2)}) async-start(), calls=%async_computation.9 | async-start | bytes 2662400 | tf_op jit(solution)/shard_map/while/body/eval_jaxpr/reduce_scatter | solution.py:164
  5467.7 168.5 %reduce-scatter.8.cloned.1.call-start = ((), (), s32[]{:S(2)}) async-start(), calls=%async_computation.9 | async-start | bytes 2662400 | tf_op jit(solution)/shard_map/while/body/eval_jaxpr/reduce_scatter | solution.py:164
  (504 other events, 17559.9 us)
Sparse Core Ops, SparseCore 0:
  15.2 49.2 all-gather.12
  102.3 81.8 reduce-scatter.11
  383.7 78.2 reduce-scatter.15
  734.9 113.1 reduce-scatter.19
  955.9 81.8 reduce-scatter.11
  1237.6 78.2 reduce-scatter.15
  1588.6 113.1 reduce-scatter.19
  1809.7 81.7 reduce-scatter.11
  2091.1 78.2 reduce-scatter.15
  2442.1 113.1 reduce-scatter.19
  2663.1 81.6 reduce-scatter.11
  2944.4 78.2 reduce-scatter.15
  3295.4 113.1 reduce-scatter.19
  3516.4 81.6 reduce-scatter.11
  3797.6 78.4 reduce-scatter.15
  4148.8 113.1 reduce-scatter.19
  4403.2 78.2 reduce-scatter.7
  4601.8 48.2 all-gather.8
  4691.9 78.2 reduce-scatter.7
  4890.5 48.1 all-gather.8
  4980.6 78.2 reduce-scatter.7
  5269.2 78.3 reduce-scatter.7
  5467.8 48.2 all-gather.8
  5557.9 78.2 reduce-scatter.7
  (51 shorter events, 2299.2 us)
Sparse Core Ops, SparseCore 1:
  5755.8 44.0 all-reduce.7
where the time goes:
time: 5880 us; the launch traced here: 5840 us
  waiting for transfers between devices  4300 us (73%)
  matrix products  662 us (11%)
  local copies, waits for them, and re-layouts  384 us (7%)
  other arithmetic  268 us (5%)
  loops' own time  91.3 us (2%)
  blocking collectives  66.3 us (1%)
    reduce_scatter x25, waiting for transfers between devices, branch_total(): lax.psum_scatter(rows_of(left, weight, form).astype(jnp.bfloat16), 'mp',...  1620 us
    all_gather x30, waiting for transfers between devices, gather_normed(): return lax.all_gather(values, 'mp', axis=0, tiled=True)  1340 us
    reduce_scatter x10, waiting for transfers between devices, grad_total(): lax.psum_scatter(rows_of(left, weight, form).astype(jnp.bfloat16), 'mp',...  722 us
    all_gather x10, waiting for transfers between devices, gather_grads(): return lax.all_gather(values, 'mp', axis=0, tiled=True)  446 us
    reshape x65, local copies, waits for them, and re-layouts, by_views(): return tensor[:VIEWS * PATCH].reshape((VIEWS, PATCH) + tensor.shape[1:])  174 us
    ppermute x15, waiting for transfers between devices, from_behind(): return lax.ppermute(block, axis, route)  164 us
    sub x40, matrix products, probabilities(): expon = jnp.exp(scores - jnp.max(scores, -1, keepdims=True))  158 us
    dot_general x35, matrix products, rows_of(): return jnp.einsum(form, left, weight, preferred_element_type=jnp.float32)  135 us
  transfers between devices with their start and end apart: 91, of which 90 were waited for; matrix products, arithmetic and copies ran while one was open for 2% of the time, Pallas kernels for 0%

commit v1 on v0

v1 whole, which is shorter than its diff:
```python
import functools

import jax
import jax.numpy as jnp
from jax import lax
from jax.experimental import pallas as pl
from jax.experimental.pallas import tpu as pltpu
from jax.sharding import PartitionSpec as P

VIEWS = 5
PATCH = 400
TEXT = 80
PATCH_ROWS = VIEWS * PATCH
HEAD = 64
PAIR = 2 * HEAD
LOW = jnp.bfloat16
F32 = jnp.float32
MESH = pl.DeviceIdType.MESH
MASKED = -1e30
VMEM_BYTES = 56 * 1024 * 1024


class Place:
    def __init__(self, mesh, items):
        self.ranks = mesh.shape["mp"]
        self.chips = self.ranks // items
        self.members = 2 * self.chips
        self.items = items

    def here(self):
        section, dp, mp = (lax.axis_index(name) for name in ("section", "dp", "mp"))
        return section, dp // 2, dp % 2, mp

    def member(self):
        _, _, core, mp = self.here()
        return (mp % self.chips) * 2 + core

    def owner_of(self, item):
        _, pair, core, mp = self.here()
        return (core, 2 * pair + (mp // 2) % 2, item * self.chips + mp // 4)

    def holder_of(self, which, half):
        section, pair, _, _ = self.here()
        return (which, 2 * pair + section, 2 * self.member() + half)

    def peer(self, step):
        section, pair, _, mp = self.here()
        rank = lax.rem(self.member() + step, self.members)
        return rank, (section, 2 * pair + rank % 2, (mp // self.chips) * self.chips + rank // 2)

    def is_here(self, device):
        section, pair, core, mp = self.here()
        same = (device[0] == section) & (device[1] == 2 * pair + core) & (device[2] == mp)
        return same


def greet(sources, targets_count, is_here):
    barrier = pltpu.get_barrier_semaphore()
    for device in sources:

        @pl.when(jnp.logical_not(is_here(device)))
        def _():
            pl.semaphore_signal(barrier, inc=1, device_id=device, device_id_type=MESH)

    pl.semaphore_wait(barrier, targets_count)


def deliver_kernel(place, x_ref, o_ref, send_sems, recv_sems, local_sem):
    section, _, _, mp = place.here()
    targets = [place.owner_of(item) for item in range(place.items)]
    sources = [(w, h, place.holder_of(w, h)) for w in range(2) for h in range(2)]
    others = sum(jnp.where(place.is_here(t), 0, 1) for t in targets)
    greet([s[2] for s in sources], others, place.is_here)
    slot = section * 2 + mp % 2

    def copy_of(item):
        return pltpu.make_async_remote_copy(
            src_ref=x_ref.at[item],
            dst_ref=o_ref.at[slot],
            send_sem=send_sems.at[item],
            recv_sem=recv_sems.at[slot],
            device_id=targets[item],
            device_id_type=MESH,
        )

    for item in range(place.items):

        @pl.when(jnp.logical_not(place.is_here(targets[item])))
        def _():
            copy_of(item).start()

        @pl.when(place.is_here(targets[item]))
        def _():
            own = pltpu.make_async_copy(x_ref.at[item], o_ref.at[slot], local_sem)
            own.start()
            own.wait()

    for which, half, device in sources:

        @pl.when(jnp.logical_not(place.is_here(device)))
        def _():
            pltpu.make_async_remote_copy(
                src_ref=x_ref.at[0],
                dst_ref=o_ref.at[which * 2 + half],
                send_sem=send_sems.at[0],
                recv_sem=recv_sems.at[which * 2 + half],
                device_id=device,
                device_id_type=MESH,
            ).wait_recv()

    for item in range(place.items):

        @pl.when(jnp.logical_not(place.is_here(targets[item])))
        def _():
            copy_of(item).wait_send()


def collect_kernel(place, x_ref, o_ref, send_sems, recv_sems, local_sem):
    targets = [(w, h, place.holder_of(w, h)) for w in range(2) for h in range(2)]
    sources = [place.owner_of(item) for item in range(place.items)]
    others = sum(jnp.where(place.is_here(t[2]), 0, 1) for t in targets)
    greet(sources, others, place.is_here)
    _, _, _, mp = place.here()
    slot = mp // place.chips

    def copy_of(index):
        return pltpu.make_async_remote_copy(
            src_ref=x_ref.at[index],
            dst_ref=o_ref.at[slot],
            send_sem=send_sems.at[index],
            recv_sem=recv_sems.at[slot],
            device_id=targets[index][2],
            device_id_type=MESH,
        )

    for index in range(4):

        @pl.when(jnp.logical_not(place.is_here(targets[index][2])))
        def _():
            copy_of(index).start()

        @pl.when(place.is_here(targets[index][2]))
        def _():
            own = pltpu.make_async_copy(x_ref.at[index], o_ref.at[slot], local_sem)
            own.start()
            own.wait()

    for item in range(place.items):

        @pl.when(jnp.logical_not(place.is_here(sources[item])))
        def _():
            pltpu.make_async_remote_copy(
                src_ref=x_ref.at[0],
                dst_ref=o_ref.at[item],
                send_sem=send_sems.at[0],
                recv_sem=recv_sems.at[item],
                device_id=sources[item],
                device_id_type=MESH,
            ).wait_recv()

    for index in range(4):

        @pl.when(jnp.logical_not(place.is_here(targets[index][2])))
        def _():
            copy_of(index).wait_send()


def moved(place, kernel, blocks, slots, collective_id):
    return pl.pallas_call(
        functools.partial(kernel, place),
        out_shape=jax.ShapeDtypeStruct((slots,) + blocks.shape[1:], blocks.dtype),
        in_specs=[pl.BlockSpec(memory_space=pl.ANY)],
        out_specs=pl.BlockSpec(memory_space=pl.ANY),
        scratch_shapes=[
            pltpu.SemaphoreType.DMA((4,)),
            pltpu.SemaphoreType.DMA((4,)),
            pltpu.SemaphoreType.DMA,
        ],
        compiler_params=pltpu.CompilerParams(collective_id=collective_id, has_side_effects=True),
    )(blocks)


def to_heads_kernel(place, x_ref, o_ref, send_sems, recv_sems, local_sem):
    width = o_ref.shape[-1]
    me = place.member()
    peers = [place.peer(step) for step in range(1, place.members)]
    greet([p[1] for p in peers], place.members - 1, place.is_here)
    copies = []
    for index, (rank, device) in enumerate(peers):
        columns = pl.ds(pl.multiple_of(rank * width, 128), width)
        copies.append(
            pltpu.make_async_remote_copy(
                src_ref=x_ref.at[:, columns],
                dst_ref=o_ref.at[me],
                send_sem=send_sems.at[index],
                recv_sem=recv_sems.at[index],
                device_id=device,
                device_id_type=MESH,
            )
        )
        copies[-1].start()
    columns = pl.ds(pl.multiple_of(me * width, 128), width)
    own = pltpu.make_async_copy(x_ref.at[:, columns], o_ref.at[me], local_sem)
    own.start()
    own.wait()
    for copy in copies:
        copy.wait()


def to_rows_kernel(place, x_ref, o_ref, send_sems, recv_sems, local_sem):
    width = x_ref.shape[-1]
    me = place.member()
    peers = [place.peer(step) for step in range(1, place.members)]
    greet([p[1] for p in peers], place.members - 1, place.is_here)
    columns = pl.ds(pl.multiple_of(me * width, 128), width)
    copies = []
    for index, (rank, device) in enumerate(peers):
        copies.append(
            pltpu.make_async_remote_copy(
                src_ref=x_ref.at[rank],
                dst_ref=o_ref.at[:, columns],
                send_sem=send_sems.at[index],
                recv_sem=recv_sems.at[index],
                device_id=device,
                device_id_type=MESH,
            )
        )
        copies[-1].start()
    own = pltpu.make_async_copy(x_ref.at[me], o_ref.at[:, columns], local_sem)
    own.start()
    own.wait()
    for copy in copies:
        copy.wait()


def swapped(place, kernel, x, out_shape, collective_id):
    return pl.pallas_call(
        functools.partial(kernel, place),
        out_shape=jax.ShapeDtypeStruct(out_shape, x.dtype),
        in_specs=[pl.BlockSpec(memory_space=pl.ANY)],
        out_specs=pl.BlockSpec(memory_space=pl.ANY),
        scratch_shapes=[
            pltpu.SemaphoreType.DMA((place.members - 1,)),
            pltpu.SemaphoreType.DMA((place.members - 1,)),
            pltpu.SemaphoreType.DMA,
        ],
        compiler_params=pltpu.CompilerParams(collective_id=collective_id, has_side_effects=True),
    )(x)


def to_heads(place, x, collective_id):
    rows, width = x.shape[0], x.shape[1] // place.members
    out = swapped(place, to_heads_kernel, x, (place.members, rows, width), collective_id)
    return out.reshape(place.members * rows, width)


def to_rows(place, x, collective_id):
    rows, width = x.shape[0] // place.members, x.shape[1]
    x = x.reshape(place.members, rows, width)
    return swapped(place, to_rows_kernel, x, (rows, place.members * width), collective_id)


def dot_rows(left, right):
    return lax.dot_general(left, right, (((1,), (1,)), ((), ())), preferred_element_type=F32)


def dot(left, right):
    return lax.dot_general(left, right, (((1,), (0,)), ((), ())), preferred_element_type=F32)


def half_of(block, head):
    lanes = lax.broadcasted_iota(jnp.int32, (1, PAIR), 1)
    mine = (lanes < HEAD) if head == 0 else (lanes >= HEAD)
    return jnp.where(mine, block, jnp.zeros((), block.dtype))


def joined(first, second):
    lanes = lax.broadcasted_iota(jnp.int32, (1, PAIR), 1)
    return jnp.where(lanes < HEAD, first, second)


def forward_pair(q, k, v, bias):
    outs, logs = [], []
    q = q * jnp.asarray(0.125, LOW)
    for head in range(2):
        scores = dot_rows(half_of(q, head), k)
        if bias is not None:
            scores = scores + bias
        top = jnp.max(scores, -1, keepdims=True)
        expon = jnp.exp(scores - top)
        total = jnp.sum(expon, -1, keepdims=True)
        outs.append(dot(expon.astype(LOW), v) / total)
        logs.append(top + jnp.log(total))
    return joined(*outs), logs


def joint_forward_kernel(pairs, length_ref, q_ref, k_ref, o_ref, log_ref):
    keys = k_ref.shape[0]
    column = lax.broadcasted_iota(jnp.int32, (1, keys), 1)
    bias = jnp.where(column < PATCH_ROWS + length_ref[0], 0.0, MASKED).astype(F32)
    lanes = lax.broadcasted_iota(jnp.int32, (1, 128), 1)
    kept = jnp.zeros(log_ref.shape, F32)
    for pair in range(pairs):
        base = pair * 3 * PAIR
        out, logs = forward_pair(
            q_ref[:, base : base + PAIR],
            k_ref[:, base + PAIR : base + 2 * PAIR],
            k_ref[:, base + 2 * PAIR : base + 3 * PAIR],
            bias,
        )
        o_ref[:, pair * PAIR : (pair + 1) * PAIR] = out.astype(LOW)
        for head in range(2):
            kept = jnp.where(lanes == pair * 2 + head, logs[head], kept)
    log_ref[...] = kept


def joint_forward(qkv, length):
    rows, width = qkv.shape
    pairs = width // (3 * PAIR)
    block = 208
    return pl.pallas_call(
        functools.partial(joint_forward_kernel, pairs),
        grid=(rows // block,),
        out_shape=(
            jax.ShapeDtypeStruct((rows, pairs * PAIR), LOW),
            jax.ShapeDtypeStruct((rows, 128), F32),
        ),
        in_specs=[
            pl.BlockSpec(memory_space=pltpu.SMEM),
            pl.BlockSpec((block, width), lambda i: (i, 0)),
            pl.BlockSpec((rows, width), lambda i: (0, 0)),
        ],
        out_specs=(
            pl.BlockSpec((block, pairs * PAIR), lambda i: (i, 0)),
            pl.BlockSpec((block, 128), lambda i: (i, 0)),
        ),
        compiler_params=pltpu.CompilerParams(vmem_limit_bytes=VMEM_BYTES),
    )(length, qkv, qkv)


def backward_head(q, k, v, grad, head, log, delta, limit):
    scores = dot_rows(k, half_of(q, head))
    if limit is not None:
        row = lax.broadcasted_iota(jnp.int32, (scores.shape[0], 1), 0)
        scores = jnp.where(row < limit, scores, MASKED)
    if log is None:
        top = jnp.max(scores, 0, keepdims=True)
        expon = jnp.exp(scores - top)
        probs = expon / jnp.sum(expon, 0, keepdims=True)
    else:
        probs = jnp.exp(scores - log)
    grad_probs = dot_rows(v, half_of(grad, head))
    if delta is None:
        delta = jnp.sum(probs * grad_probs, 0, keepdims=True)
    grad_scores = (probs * (grad_probs - delta)).astype(LOW)
    grad_v = dot(probs.astype(LOW), grad)
    grad_k = dot(grad_scores, q)
    k_turned = k[:, head * HEAD : (head + 1) * HEAD].T
    grad_q = dot(k_turned, grad_scores)
    return grad_q, grad_k, grad_v


def joint_backward_kernel(
    length_ref, q_ref, k_ref, v_ref, grad_ref, log_ref, delta_ref, o_ref, total_ref
):
    step = pl.program_id(1)
    block = k_ref.shape[0]
    limit = PATCH_ROWS + length_ref[0] - step * block
    q = q_ref[...] * jnp.asarray(0.125, LOW)
    k, v, grad = k_ref[...], v_ref[...], grad_ref[...]

    @pl.when(step == 0)
    def _():
        total_ref[...] = jnp.zeros_like(total_ref)

    grads_k, grads_v = [], []
    for head in range(2):
        grad_q, grad_k, grad_v = backward_head(
            q, k, v, grad, head, log_ref[0, head : head + 1], delta_ref[0, head : head + 1], limit
        )
        total_ref[head * HEAD : (head + 1) * HEAD] += grad_q
        grads_k.append(grad_k)
        grads_v.append(grad_v)
    here = pl.ds(pl.multiple_of(step * block, 16), block)
    o_ref[here, PAIR : 2 * PAIR] = joined(*grads_k).astype(LOW)
    o_ref[here, 2 * PAIR : 3 * PAIR] = joined(*grads_v).astype(LOW)

    @pl.when(step == pl.num_programs(1) - 1)
    def _():
        o_ref[:, 0:PAIR] = (total_ref[...].T * 0.125).astype(LOW)


def joint_backward(qkv, length, grad, log, delta):
    rows, width = qkv.shape
    pairs = width // (3 * PAIR)
    block = 208
    stats = pl.BlockSpec((1, 2, rows), lambda p, i: (p, 0, 0))
    return pl.pallas_call(
        joint_backward_kernel,
        grid=(pairs, rows // block),
        out_shape=jax.ShapeDtypeStruct((rows, width), LOW),
        in_specs=[
            pl.BlockSpec(memory_space=pltpu.SMEM),
            pl.BlockSpec((rows, PAIR), lambda p, i: (0, 3 * p)),
            pl.BlockSpec((block, PAIR), lambda p, i: (i, 3 * p + 1)),
            pl.BlockSpec((block, PAIR), lambda p, i: (i, 3 * p + 2)),
            pl.BlockSpec((rows, PAIR), lambda p, i: (0, p)),
            stats,
            stats,
        ],
        out_specs=pl.BlockSpec((rows, 3 * PAIR), lambda p, i: (0, p)),
        scratch_shapes=[pltpu.VMEM((PAIR, rows), F32)],
        compiler_params=pltpu.CompilerParams(vmem_limit_bytes=VMEM_BYTES),
    )(length, qkv, qkv, qkv, grad, log, delta)


def within_forward_kernel(pairs, length_ref, x_ref, o_ref):
    def group(rows, bias):
        for pair in range(pairs):
            base = pair * 3 * PAIR
            q, k, v = (x_ref[rows, base + part * PAIR : base + (part + 1) * PAIR] for part in range(3))
            out, _ = forward_pair(q, k, v, bias)
            o_ref[rows, pair * PAIR : (pair + 1) * PAIR] = out.astype(LOW)

    @pl.loop(0, VIEWS)
    def _(view):
        group(pl.ds(pl.multiple_of(view * PATCH, 16), PATCH), None)

    column = lax.broadcasted_iota(jnp.int32, (1, TEXT), 1)
    bias = jnp.where(column < length_ref[0], 0.0, MASKED).astype(F32)
    group(pl.ds(PATCH_ROWS, TEXT), bias)


def within_forward(qkv, length):
    rows, width = qkv.shape
    pairs = width // (3 * PAIR)
    return pl.pallas_call(
        functools.partial(within_forward_kernel, pairs),
        out_shape=jax.ShapeDtypeStruct((rows, pairs * PAIR), LOW),
        in_specs=[
            pl.BlockSpec(memory_space=pltpu.SMEM),
            pl.BlockSpec(memory_space=pltpu.VMEM),
        ],
        out_specs=pl.BlockSpec(memory_space=pltpu.VMEM),
        compiler_params=pltpu.CompilerParams(vmem_limit_bytes=VMEM_BYTES),
    )(length, qkv)


def within_backward_kernel(pairs, length_ref, x_ref, grad_ref, o_ref):
    def group(rows, limit):
        for pair in range(pairs):
            base = pair * 3 * PAIR
            q, k, v = (x_ref[rows, base + part * PAIR : base + (part + 1) * PAIR] for part in range(3))
            q = q * jnp.asarray(0.125, LOW)
            grad = grad_ref[rows, pair * PAIR : (pair + 1) * PAIR]
            both = [backward_head(q, k, v, grad, head, None, None, limit) for head in range(2)]
            grad_q = jnp.concatenate([both[0][0], both[1][0]], 0).T * 0.125
            o_ref[rows, base : base + PAIR] = grad_q.astype(LOW)
            o_ref[rows, base + PAIR : base + 2 * PAIR] = joined(both[0][1], both[1][1]).astype(LOW)
            o_ref[rows, base + 2 * PAIR : base + 3 * PAIR] = joined(both[0][2], both[1][2]).astype(LOW)

    @pl.loop(0, VIEWS)
    def _(view):
        group(pl.ds(pl.multiple_of(view * PATCH, 16), PATCH), None)

    group(pl.ds(PATCH_ROWS, TEXT), length_ref[0])


def within_backward(qkv, length, grad):
    rows, width = qkv.shape
    pairs = width // (3 * PAIR)
    return pl.pallas_call(
        functools.partial(within_backward_kernel, pairs),
        out_shape=jax.ShapeDtypeStruct((rows, width), LOW),
        in_specs=[
            pl.BlockSpec(memory_space=pltpu.SMEM),
            pl.BlockSpec(memory_space=pltpu.VMEM),
            pl.BlockSpec(memory_space=pltpu.VMEM),
        ],
        out_specs=pl.BlockSpec(memory_space=pltpu.VMEM),
        compiler_params=pltpu.CompilerParams(vmem_limit_bytes=VMEM_BYTES),
    )(length, qkv, grad)


def layer_norm(values, scale_vec, shift_vec):
    center = jnp.mean(values, -1, keepdims=True)
    offset = values - center
    spread = jnp.mean(offset * offset, -1, keepdims=True)
    return offset * lax.rsqrt(spread + 1e-05) * scale_vec + shift_vec


def times_turned(left, weight):
    return lax.dot_general(left, weight, (((1,), (1,)), ((), ())), preferred_element_type=F32)


def times(left, weight):
    return lax.dot_general(left, weight, (((1,), (0,)), ((), ())), preferred_element_type=F32)


def over_rows(left, right):
    return lax.dot_general(left, right, (((0,), (0,)), ((), ())), preferred_element_type=F32)


def layer_forward(place, source, length, params, within):
    normed = layer_norm(source, params["gain_one"], params["bias_one"]).astype(LOW)
    projected = times_turned(normed, params["qkv"]).astype(LOW)
    qkv = to_heads(place, projected, 2)
    if within:
        mixed_heads, logs = within_forward(qkv, length), None
    else:
        mixed_heads, logs = joint_forward(qkv, length)
    mixed = to_rows(place, mixed_heads, 3)
    middle = source + times(mixed, params["out"]) + params["bias_out"]
    second = layer_norm(middle, params["gain_two"], params["bias_two"]).astype(LOW)
    hidden_pre = times_turned(second, params["up"]) + params["bias_up"]
    hidden = jax.nn.gelu(hidden_pre).astype(LOW)
    result = middle + times(hidden, params["down"]) + params["bias_down"]
    return result, (source, normed, qkv, mixed_heads, logs, mixed, middle, second, hidden_pre, hidden)


def layer_backward(place, upstream, length, params, kept, within):
    source, normed, qkv, mixed_heads, logs, mixed, middle, second, hidden_pre, hidden = kept
    up_low = upstream.astype(LOW)
    grad_down = over_rows(hidden, up_low)
    grad_hidden = times_turned(up_low, params["down"])
    grad_pre = jax.vjp(jax.nn.gelu, hidden_pre)[1](grad_hidden)[0].astype(LOW)
    grad_up_bias = jnp.sum(grad_pre.astype(F32), 0)
    grad_up = over_rows(grad_pre, second)
    grad_second = times(grad_pre, params["up"])
    norm_pull = jax.vjp(layer_norm, middle, params["gain_two"], params["bias_two"])[1]
    part_middle, grad_gain_two, grad_bias_two = norm_pull(grad_second)
    grad_middle = upstream + part_middle
    mid_low = grad_middle.astype(LOW)
    grad_out = over_rows(mixed, mid_low)
    grad_mixed = times_turned(mid_low, params["out"]).astype(LOW)
    grad_heads = to_heads(place, grad_mixed, 4)
    if within:
        grad_qkv_heads = within_backward(qkv, length, grad_heads)
    else:
        rows, width = grad_heads.shape
        pairs = width // PAIR
        product = grad_heads.astype(F32) * mixed_heads.astype(F32)
        delta = jnp.sum(product.reshape(rows, pairs, 2, HEAD), -1).transpose(1, 2, 0)
        log = logs[:, : 2 * pairs].T.reshape(pairs, 2, rows)
        grad_qkv_heads = joint_backward(qkv, length, grad_heads, log, delta)
    grad_projected = to_rows(place, grad_qkv_heads, 5)
    grad_qkv = over_rows(grad_projected, normed)
    grad_normed = times(grad_projected, params["qkv"])
    first_pull = jax.vjp(layer_norm, source, params["gain_one"], params["bias_one"])[1]
    part_source, grad_gain_one, grad_bias_one = first_pull(grad_normed)
    matrices = (grad_qkv, grad_out, grad_up, grad_down)
    vectors = jnp.concatenate(
        [
            grad_gain_one,
            grad_bias_one,
            jnp.sum(grad_middle, 0),
            grad_gain_two,
            grad_bias_two,
            jnp.sum(upstream, 0),
            grad_up_bias,
        ]
    )
    return grad_middle + part_source, matrices, vectors


def per_device(mesh, inputs, text_lengths, *weights):
    (gain_one, bias_one, weight_qkv, weight_out, bias_out) = weights[:5]
    (gain_two, bias_two, weight_up, bias_up, weight_down, bias_down) = weights[5:]
    items, block_rows, width = inputs.shape[1:]
    place = Place(mesh, items)
    ranks = place.ranks
    section, pair, core, mp = place.here()
    heads_here = weight_qkv.shape[2]
    all_heads = heads_here * ranks
    per_pair = 2 // heads_here

    lengths = lax.all_gather(text_lengths, "dp")
    length = lengths[2 * pair + section, mp // place.chips][None]

    arrived = moved(place, deliver_kernel, inputs[0], 4, 0)
    rows = 2 * block_rows
    arrived = arrived.reshape(2, rows, width)

    own = (
        weight_qkv[0].reshape(width, heads_here, 3, HEAD).transpose(2, 1, 3, 0).reshape(-1, width),
        weight_out[0].reshape(-1, width),
        weight_up[0].T,
        weight_down[0],
    )
    full = [lax.all_gather(w, ("section", "mp"), tiled=True) for w in own]
    full = [w.reshape((2, -1, width)) for w in full]
    qkv_full = full[0].reshape(2, all_heads // 2, per_pair, 3, heads_here, HEAD, width)
    full[0] = qkv_full.swapaxes(2, 3).reshape(2, 3 * all_heads * HEAD, width)
    vectors = lax.all_gather(
        jnp.concatenate(
            [w[0] for w in (gain_one, bias_one, bias_out, gain_two, bias_two, bias_down, bias_up)]
        ),
        ("section", "mp"),
    ).reshape(2, ranks, -1)

    def params_of(layer):
        names = ("gain_one", "bias_one", "bias_out", "gain_two", "bias_two", "bias_down")
        found = {
            name: vectors[layer, 0, i * width : (i + 1) * width] for i, name in enumerate(names)
        }
        found["bias_up"] = vectors[layer, :, len(names) * width :].reshape(-1)
        for name, w in zip(("qkv", "out", "up", "down"), full):
            found[name] = w[layer]
        return found

    params = [params_of(layer) for layer in range(2)]
    boundary, kept_zero = layer_forward(place, arrived[0].astype(F32), length, params[0], True)
    result, kept_one = layer_forward(
        place, boundary.astype(LOW).astype(F32), length, params[1], False
    )
    upstream = arrived[1].astype(F32)
    grad_boundary, matrices_one, vectors_one = layer_backward(
        place, upstream, length, params[1], kept_one, False
    )
    grad_source, matrices_zero, vectors_zero = layer_backward(
        place, grad_boundary.astype(LOW).astype(F32), length, params[0], kept_zero, True
    )
    ends = jnp.stack([grad_source, result]).astype(LOW).reshape(4, block_rows, width)
    ends = moved(place, collect_kernel, ends, items, 1).astype(F32)[None]

    reduced = []
    for index, (zero, one) in enumerate(zip(matrices_zero, matrices_one)):
        both = jnp.stack([zero, one]).astype(LOW)
        if index == 0:
            both = both.reshape(2, all_heads // 2, 3, per_pair, heads_here, HEAD, width)
            both = both.swapaxes(2, 3)
        both = both.reshape(2 * ranks, -1, width)
        part = lax.psum_scatter(both, ("section", "mp"), scatter_dimension=0)
        reduced.append(lax.psum(part, "dp").astype(F32))
    sums = lax.psum(jnp.stack([vectors_zero, vectors_one]), ("section", "dp", "mp"))[section]
    small = [sums[i * width : (i + 1) * width][None] for i in range(6)]
    hidden_here = bias_up.shape[1]
    grad_bias_up = lax.dynamic_slice_in_dim(sums, 6 * width + mp * hidden_here, hidden_here)[None]
    grad_qkv = reduced[0].reshape(3, heads_here, HEAD, width).transpose(3, 1, 0, 2)
    grad_qkv = grad_qkv.reshape(1, width, heads_here, 3 * HEAD)
    grad_out = reduced[1].reshape(1, heads_here, HEAD, width)
    return (
        ends,
        small[0],
        small[1],
        grad_qkv,
        grad_out,
        small[2],
        small[3],
        small[4],
        reduced[2].T[None],
        grad_bias_up,
        reduced[3][None],
        small[5],
    )


def solution(mesh):
    vector = P("section", None)
    ends = P("section", "dp", "mp", None)
    qkv = P("section", None, "mp", None)
    out = P("section", "mp", None, None)
    up = P("section", None, "mp")
    up_bias = P("section", "mp")
    down = P("section", "mp", None)
    params = (vector, vector, qkv, out, vector, vector, vector, up, up_bias, down, vector)
    return jax.shard_map(
        functools.partial(per_device, mesh),
        mesh=mesh,
        in_specs=(ends, P("dp")) + params,
        out_specs=(ends,) + params,
        check_vma=False,
    )
```

time: 5880 us -> 1140 us (0.19)
  waiting for transfers between devices: 4300 us -> 344 us
  matrix products: 662 us -> 113 us
  Pallas kernels: 0 us -> 506 us
  local copies, waits for them, and re-layouts: 384 us -> 24.9 us
  other arithmetic: 268 us -> 47.5 us
  loops' own time: 91.3 us -> 0 us
    reduce_scatter x35 -> x4, waiting for transfers between devices: 2340 us -> 253 us  [per_device(): part = lax.psum_scatter(both, ('section', 'mp'), scatter_dimension=0)]
    all_gather x40 -> x4, waiting for transfers between devices: 1790 us -> 89 us  [per_device(): full = [lax.all_gather(w, ('section', 'mp'), tiled=True) for w in own]]
    pallas_call x0 -> x14, Pallas kernels: none -> 506 us  [the longest x8 269 us: swapped(): pl.pallas_call(functools.partial(kernel, place), out_shape=jax.ShapeDtype...]
    dot_general x150 -> x24, matrix products: 458 us -> 113 us  [the longest x8 42.3 us: over_rows(): lax.dot_general(left, right, (((0,), (0,)), ((), ())), preferred_element_...]
    reshape x95 -> x3, local copies, waits for them, and re-layouts: 230 us -> 2.48 us  [the longest x1 1.77 us: per_device(): reduced[0].reshape(3, heads_here, HEAD, width).transpose(3, 1, 0, 2)]
    ppermute x15 -> x0, waiting for transfers between devices: 164 us -> none  [from_behind(): return lax.ppermute(block, axis, route)]
    sub x40 -> x0, matrix products: 158 us -> none  [probabilities(): expon = jnp.exp(scores - jnp.max(scores, -1, keepdims=True))]
    convert_element_type x71 -> x1, other arithmetic: 97.7 us -> 1.02 us  [per_device(): grad_boundary.astype(LOW).astype(F32)]
  transfers between devices with their start and end apart: 91 -> 9, of which waited for: 90 -> 6; matrix products, arithmetic and copies ran while one was open for 2% -> 9% of each run, Pallas kernels for 0% -> 16%
where the time goes in v1:
time: 1140 us
  Pallas kernels  506 us (44%)
  waiting for transfers between devices  344 us (30%)
  matrix products  113 us (10%)
  blocking collectives  86 us (8%)
  other arithmetic  47.5 us (4%)
  local copies, waits for them, and re-layouts  24.9 us (2%)
  between operations  15.8 us (1%)
    pallas_call x8, Pallas kernels, swapped(): pl.pallas_call(functools.partial(kernel, place), out_shape=jax.ShapeDtype...  269 us
    reduce_scatter x4, waiting for transfers between devices, per_device(): part = lax.psum_scatter(both, ('section', 'mp'), scatter_dimension=0)  253 us
    pallas_call x2, Pallas kernels, moved(): pl.pallas_call(functools.partial(kernel, place), out_shape=jax.ShapeDtype...  102 us
    all_gather x4, waiting for transfers between devices, per_device(): full = [lax.all_gather(w, ('section', 'mp'), tiled=True) for w in own]  89 us
    pallas_call x1, Pallas kernels, joint_backward(): pl.pallas_call(joint_backward_kernel, grid=(pairs, rows // block), out_sh...  64.1 us
    psum x1, blocking collectives, per_device(): lax.psum(jnp.stack([vectors_zero, vectors_one]), ('section', 'dp', 'mp'))  48.1 us
    dot_general x8, matrix products, over_rows(): lax.dot_general(left, right, (((0,), (0,)), ((), ())), preferred_element_...  42.3 us
    dot_general x8, matrix products, times_turned(): lax.dot_general(left, weight, (((1,), (1,)), ((), ())), preferred_element...  38.5 us
  transfers between devices with their start and end apart: 9, of which 6 were waited for; matrix products, arithmetic and copies ran while one was open for 9% of the time, Pallas kernels for 16%

profile of v1, /device:TPU:0, one launch (start us, length us, event | category | flops | bytes accessed | tf_op | source)
XLA Modules:
  0.0 1138.8 jit_solution(8507271265048582519)
XLA Ops:
  13.0 32.7 %all-gather.3 = f32[8,1,3584]{2,1,0:T(1,128)S(1)} all-gather(f32[1,1,3584]{2,1,0:T(1,128)S(1)} %reshape.314), channel_id=4, replica_groups=mesh['section'=2,'dp'=4,'mp'=4] {'section','mp'}, dimensions={0}, use_global_device_ids=true | all-gather | bytes 129024 | tf_op jit(solution)/shard_map/all_gather | solution.py:594
  46.1 58.0 %shard_map.220 = bf16[4,520,512]{2,1,0:T(8,128)(2,1)} custom-call(bf16[4,520,512]{2,1,0:T(8,128)(2,1)} %bitcast.150), custom_call_target="tpu_custom_call" | custom-call | tf_op jit(solution)/shard_map/pallas_call | solution.py:169
  124.2 49.5 %shard_map.221 = bf16[2,1040,768]{2,1,0:T(8,128)(2,1)} custom-call(bf16[1040,1536]{1,0:T(8,128)(2,1)} %convolution_convert_fusion.1.x_ref), custom_call_target="tpu_custom_call" | custom-call | tf_op jit(solution)/shard_map/pallas_call | solution.py:237
  173.8 10.9 shard_map.222
  184.7 17.8 %shard_map.223 = bf16[1040,512]{1,0:T(8,128)(2,1)} custom-call(bf16[2,1040,256]{2,1,0:T(8,128)(2,1)} %bitcast.144), custom_call_target="tpu_custom_call" | custom-call | tf_op jit(solution)/shard_map/pallas_call | solution.py:237
  205.9 22.7 %all-gather.13.cloned.1.call-done = bf16[4096,512]{0,1:T(8,128)(2,1)} async-done(((bf16[512,512]{0,1:T(8,128)(2,1)}), bf16[4096,512]{0,1:T(8,128)(2,1)}) %all-gather.13.cloned.1.call-update) | async-done | bytes 4194320 | tf_op jit(solution)/shard_map/all_gather | solution.py:590
  236.0 66.3 %all-gather.15.cloned.1.call-done = bf16[1,4096,512]{2,1,0:T(8,128)(2,1)} async-done(((bf16[1,512,512]{2,1,0:T(8,128)(2,1)}), bf16[1,4096,512]{2,1,0:T(8,128)(2,1)}) %all-gather.15.cloned.1.call-update) | async-done | bytes 4194320 | tf_op jit(solution)/shard_map/all_gather | solution.py:590
  313.7 49.5 %shard_map.224 = bf16[2,1040,768]{2,1,0:T(8,128)(2,1)} custom-call(bf16[1040,1536]{1,0:T(8,128)(2,1)} %convolution_convert_fusion.x_ref), custom_call_target="tpu_custom_call" | custom-call | tf_op jit(solution)/shard_map/pallas_call | solution.py:237
  363.2 37.4 %shard_map.225 = (bf16[2080,256]{1,0:T(8,128)(2,1)}, f32[2080,128]{1,0:T(8,128)}) custom-call(s32[1]{0:T(128)} %bitcast.5.length_ref, bf16[2080,768]{1,0:T(8,128)(2,1)} %bitcast.129, bf16[2080,768]{1,0:T(8,128)(2,1)} %bitcast.130), custom_call_target="tpu_custom_call" | custom-call | tf_op jit(solution)/shard_map/pallas_call | solution.py:321
  403.0 17.8 %shard_map.226 = bf16[1040,512]{1,0:T(8,128)(2,1)} custom-call(bf16[2,1040,256]{2,1,0:T(8,128)(2,1)} %bitcast.147), custom_call_target="tpu_custom_call" | custom-call | tf_op jit(solution)/shard_map/pallas_call | solution.py:237
  426.3 7.9 convert_reduce_fusion
  441.1 17.7 %shard_map.227 = bf16[2,1040,256]{2,1,0:T(8,128)(2,1)} custom-call(bf16[1040,512]{1,0:T(8,128)(2,1)} %convolution_convert_fusion.9.x_ref), custom_call_target="tpu_custom_call" | custom-call | tf_op jit(solution)/shard_map/pallas_call | solution.py:237
  467.2 64.1 %shard_map.228 = bf16[2080,768]{1,0:T(8,128)(2,1)} custom-call(s32[1]{0:T(128)} %bitcast.5.length_ref, bf16[2080,768]{1,0:T(8,128)(2,1)} %bitcast.131, bf16[2080,768]{1,0:T(8,128)(2,1)} %bitcast.132, bf16[2080,768]{1,0:T(8,128)(2,1)} %bitcast.133, bf16[2080,256]{1,0:T(8,128)(2,1)} %bitcast.141, f32[2,2,2080]{2,1,0:T(2,128)} %reshape.290.log_ref, ...), custom_call_target="tpu_custom_call" | custom-call | tf_op jit(solution)/shard_map/pallas_call | solution.py:398
  531.3 49.7 %shard_map.229 = bf16[1040,1536]{1,0:T(8,128)(2,1)} custom-call(bf16[2,1040,768]{2,1,0:T(8,128)(2,1)} %bitcast.138), custom_call_target="tpu_custom_call" | custom-call | tf_op jit(solution)/shard_map/pallas_call | solution.py:237
  592.0 7.9 convert_reduce_fusion.1
  607.0 17.6 %shard_map.230 = bf16[2,1040,256]{2,1,0:T(8,128)(2,1)} custom-call(bf16[1040,512]{1,0:T(8,128)(2,1)} %convolution_convert_fusion.8.x_ref), custom_call_target="tpu_custom_call" | custom-call | tf_op jit(solution)/shard_map/pallas_call | solution.py:237
  624.6 22.3 %shard_map.231 = bf16[2080,768]{1,0:T(8,128)(2,1)} custom-call(s32[1]{0:T(128)} %bitcast.5.length_ref, bf16[2080,768]{1,0:T(8,128)(2,1)} %bitcast.135, bf16[2080,256]{1,0:T(8,128)(2,1)} %bitcast.148), custom_call_target="tpu_custom_call" | custom-call | tf_op jit(solution)/shard_map/pallas_call | solution.py:472
  647.0 49.7 %shard_map.232 = bf16[1040,1536]{1,0:T(8,128)(2,1)} custom-call(bf16[2,1040,768]{2,1,0:T(8,128)(2,1)} %bitcast.139), custom_call_target="tpu_custom_call" | custom-call | tf_op jit(solution)/shard_map/pallas_call | solution.py:237
  731.9 7.5 fusion.30
  778.4 64.7 %reduce-scatter.7.cloned.1.call-done = bf16[1,128,512]{2,1,0:T(8,128)(2,1)} async-done(((bf16[8,128,512]{2,1,0:T(8,128)(2,1)}), bf16[1,128,512]{2,1,0:T(8,128)(2,1)}) %reduce-scatter.7.cloned.1.call-update) | async-done | bytes 131088 | tf_op jit(solution)/shard_map/reduce_scatter | solution.py:633
  843.0 91.2 %reduce-scatter.9.cloned.1.call-done = bf16[1,512,512]{1,2,0:T(8,128)(2,1)} async-done(((bf16[8,512,512]{1,2,0:T(8,128)(2,1)}), bf16[1,512,512]{1,2,0:T(8,128)(2,1)}) %reduce-scatter.9.cloned.1.call-update) | async-done | bytes 524304 | tf_op jit(solution)/shard_map/reduce_scatter | solution.py:633
  934.2 92.0 %reduce-scatter.11.cloned.1.call-done = bf16[1,512,512]{2,1,0:T(8,128)(2,1)} async-done(((bf16[8,512,512]{2,1,0:T(8,128)(2,1)}), bf16[1,512,512]{2,1,0:T(8,128)(2,1)}) %reduce-scatter.11.cloned.1.call-update) | async-done | bytes 524304 | tf_op jit(solution)/shard_map/reduce_scatter | solution.py:633
  1027.8 44.3 %shard_map.233 = bf16[4,520,512]{2,1,0:T(8,128)(2,1)} custom-call(bf16[4,520,512]{2,1,0:T(8,128)(2,1)} %bitcast.142), custom_call_target="tpu_custom_call" | custom-call | tf_op jit(solution)/shard_map/pallas_call | solution.py:169
  1072.1 48.1 %psum.35 = f32[2,5120]{1,0:T(2,128)S(1)} all-reduce(f32[2,5120]{1,0:T(2,128)S(1)} %pad_maximum_fusion.5), channel_id=1, replica_groups=mesh['section'=2,'dp'=4,'mp'=4] {'section','dp','mp'}, use_global_device_ids=true, to_apply=%region_31.32 | all-reduce | flops 10240 | bytes 81920 | tf_op jit(solution)/shard_map/psum | solution.py:635
  (236 shorter events, 175.7 us)
Async XLA Ops:
  7.3 111.3 %all-gather.9.cloned.1.call-start = ((), (), s32[]{:S(2)}) async-start(), calls=%async_computation.4 | async-start | bytes 3538944 | tf_op jit(solution)/shard_map/all_gather | solution.py:590
  9.1 193.4 %all-gather.11.cloned.1.call-start = ((), (), s32[]{:S(2)}) async-start(), calls=%async_computation.5 | async-start | bytes 1179648 | tf_op jit(solution)/shard_map/all_gather | solution.py:590
  9.9 218.8 %all-gather.13.cloned.1.call-start = ((), (), s32[]{:S(2)}) async-start(), calls=%async_computation.6 | async-start | bytes 4718592 | tf_op jit(solution)/shard_map/all_gather | solution.py:590
  10.6 291.6 %all-gather.15.cloned.1.call-start = ((), (), s32[]{:S(2)}) async-start(), calls=%async_computation.11 | async-start | bytes 4718592 | tf_op jit(solution)/shard_map/all_gather | solution.py:590
  11.2 765.4 %reduce-scatter.5.cloned.1.call-start = ((), (), s32[]{:S(2)}) async-start(), calls=%async_computation.7 | async-start | bytes 3538944 | tf_op jit(solution)/shard_map/reduce_scatter | solution.py:633
  104.1 10.9 copy-start
  105.8 11.2 copy-start.22
  108.7 8.3 copy-start.24
  205.4 96.8 %copy-start.2 = (f32[1040,512]{1,0:T(8,128)}, f32[1040,512]{1,0:T(8,128)S(1)}, u32[]{:S(2)}) copy-start(f32[1040,512]{1,0:T(8,128)S(1)} %get-tuple-element.68) | copy-start | bytes 6389764
  302.3 7.8 copy-start.40
  402.0 18.8 %copy-start.18 = (bf16[1024,512]{1,0:T(8,128)(2,1)S(1)}, bf16[1024,512]{1,0:T(8,128)(2,1)}, u32[]{:S(2)}) copy-start(bf16[1024,512]{1,0:T(8,128)(2,1)} %all-gather.11.cloned.1.call-done) | copy-start | bytes 3145732
  423.0 14.2 %copy-start.6 = (f32[1040,512]{1,0:T(8,128)}, f32[1040,512]{1,0:T(8,128)S(1)}, u32[]{:S(2)}) copy-start(f32[1040,512]{1,0:T(8,128)S(1)} %get-tuple-element.72) | copy-start | bytes 6389764
  426.0 8.1 copy-start.44
  581.0 9.8 slice-start
  581.0 9.8 slice-start.1
  592.0 11.9 %copy-start.13 = (bf16[1040,512]{1,0:T(8,128)(2,1)}, bf16[1040,512]{1,0:T(8,128)(2,1)S(1)}, u32[]{:S(2)}) copy-start(bf16[1040,512]{1,0:T(8,128)(2,1)S(1)} %add_convert_fusion.1) | copy-start | bytes 3194884
  592.0 7.9 copy-start.3
  592.0 7.9 copy-start.39
  703.8 139.3 %reduce-scatter.7.cloned.1.call-start = ((), (), s32[]{:S(2)}) async-start(), calls=%async_computation.8 | async-start | bytes 1179648 | tf_op jit(solution)/shard_map/reduce_scatter | solution.py:633
  709.5 224.8 %reduce-scatter.9.cloned.1.call-start = ((), (), s32[]{:S(2)}) async-start(), calls=%async_computation.9 | async-start | bytes 4718592 | tf_op jit(solution)/shard_map/reduce_scatter | solution.py:633
  730.7 8.7 copy-start.14
  730.7 295.5 %reduce-scatter.11.cloned.1.call-start = ((), (), s32[]{:S(2)}) async-start(), calls=%async_computation.10 | async-start | bytes 4718592 | tf_op jit(solution)/shard_map/reduce_scatter | solution.py:633
  749.3 375.9 %all-reduce.5.cloned.1.call-start = ((), (), s32[]{:S(2)}) async-start(), calls=%async_computation.12 | async-start | bytes 3145728 | tf_op jit(solution)/shard_map/psum | solution.py:634
  771.0 255.3 %copy-start.15 = (bf16[1,1040,512]{2,1,0:T(8,128)(2,1)S(1)}, bf16[1,1040,512]{2,1,0:T(8,128)(2,1)}, u32[]{:S(2)}) copy-start(bf16[1,1040,512]{2,1,0:T(8,128)(2,1)} %get-tuple-element.43) | copy-start | bytes 3194884
  (35 other events, 132.5 us)
Sparse Core Ops, SparseCore 0:
  10.8 95.9 all-gather.8
  108.9 43.8 all-gather.10
  154.8 73.7 all-gather.12
  230.6 71.5 all-gather.14
  703.9 72.6 reduce-scatter.4
  780.4 62.5 reduce-scatter.6
  847.1 87.0 reduce-scatter.8
  938.4 87.8 reduce-scatter.10
  1029.6 43.1 all-reduce.4

commit v2 on v1

v2 whole, which is shorter than its diff:
```python
import functools

import jax
import jax.numpy as jnp
from jax import lax
from jax.experimental import pallas as pl
from jax.experimental.pallas import tpu as pltpu
from jax.sharding import PartitionSpec as P

VIEWS = 5
PATCH = 400
TEXT = 80
PATCH_ROWS = VIEWS * PATCH
HEAD = 64
PAIR = 2 * HEAD
LOW = jnp.bfloat16
F32 = jnp.float32
MESH = pl.DeviceIdType.MESH
MASKED = -1e30
VMEM_BYTES = 56 * 1024 * 1024


def cost(microseconds):
    return pl.CostEstimate(flops=int(microseconds * 1e9), bytes_accessed=0, transcendentals=0)


class Place:
    def __init__(self, mesh, items):
        self.ranks = mesh.shape["mp"]
        self.chips = self.ranks // items
        self.members = 2 * self.chips
        self.items = items

    def here(self):
        section, dp, mp = (lax.axis_index(name) for name in ("section", "dp", "mp"))
        return section, dp // 2, dp % 2, mp

    def member(self):
        _, _, core, mp = self.here()
        return (mp % self.chips) * 2 + core

    def owner_of(self, item):
        _, pair, core, mp = self.here()
        return (core, 2 * pair + (mp // 2) % 2, item * self.chips + mp // 4)

    def holder_of(self, which, half):
        section, pair, _, _ = self.here()
        return (which, 2 * pair + section, 2 * self.member() + half)

    def peer(self, step):
        section, pair, _, mp = self.here()
        rank = lax.rem(self.member() + step, self.members)
        return rank, (section, 2 * pair + rank % 2, (mp // self.chips) * self.chips + rank // 2)

    def is_here(self, device):
        section, pair, core, mp = self.here()
        same = (device[0] == section) & (device[1] == 2 * pair + core) & (device[2] == mp)
        return same


def greet(sources, targets_count, is_here):
    barrier = pltpu.get_barrier_semaphore()
    for device in sources:

        @pl.when(jnp.logical_not(is_here(device)))
        def _():
            pl.semaphore_signal(barrier, inc=1, device_id=device, device_id_type=MESH)

    pl.semaphore_wait(barrier, targets_count)


class Ring:
    def __init__(self, mesh):
        self.ranks = mesh.shape["mp"]
        self.section, self.dp, self.mp = (lax.axis_index(n) for n in ("section", "dp", "mp"))
        self.core, self.side = self.dp % 2, (self.dp // 2) % 2
        self.base = (self.dp // 4) * 4

    def at(self, section=None, side=None, core=None, mp=None):
        section = self.section if section is None else section
        side = self.side if side is None else side
        core = self.core if core is None else core
        return (section, self.base + 2 * side + core, self.mp if mp is None else mp)

    def other_section(self):
        return self.at(section=1 - self.section)

    def other_side(self):
        return self.at(side=1 - self.side)

    def other_core(self):
        return self.at(core=1 - self.core)

    def column(self, flip_side=False, flip_section=False, flip_core=False):
        side = 1 - self.side if flip_side else self.side
        section = 1 - self.section if flip_section else self.section
        core = 1 - self.core if flip_core else self.core
        return side * 4 + section * 2 + core

    def slots(self):
        yield self.mp, True
        for step in range(1, self.ranks):
            yield self.mp - step, self.mp >= step
            yield self.mp + step, self.mp + step < self.ranks

    def greet_all(self):
        barrier = pltpu.get_barrier_semaphore()
        for section in range(2):
            for place in range(4):
                for mp in range(self.ranks):
                    device = (section, self.base + place, mp)
                    mine = (self.section == section) & (self.dp == device[1]) & (self.mp == mp)

                    @pl.when(jnp.logical_not(mine))
                    def _():
                        pl.semaphore_signal(barrier, inc=1, device_id=device, device_id_type=MESH)

        pl.semaphore_wait(barrier, 8 * self.ranks - 1)


def remote(source, target, send_sem, recv_sem, device):
    return pltpu.make_async_remote_copy(
        src_ref=source,
        dst_ref=target,
        send_sem=send_sem,
        recv_sem=recv_sem,
        device_id=device,
        device_id_type=MESH,
    )


def start_kernel(
    mesh,
    place,
    x_ref,
    w_ref,
    vec_ref,
    rows_ref,
    first_ref,
    second_ref,
    vecs_ref,
    stage_ref,
    local_sems,
    row_send,
    row_recv,
    stage_send,
    stage_recv,
    vec_send,
    vec_recv,
    split_send,
    split_recv,
    up_send,
    down_send,
    line_recv,
    side_send,
    side_recv,
    section_send,
    section_recv,
    core_send,
    core_recv,
):
    ring = Ring(mesh)
    ranks, items = ring.ranks, place.items
    section, core, mp = ring.section, ring.core, ring.mp
    hands_out = core == section
    half = mp % 2
    own_column = ring.column()
    ring.greet_all()

    vec_copies = []
    for other in range(2 * ranks):
        device = (other // ranks, ring.dp, other % ranks)
        slot = section * ranks + mp
        elsewhere = (section * ranks + mp) != other
        copy = remote(vec_ref, vecs_ref.at[slot], vec_send.at[other], vec_recv.at[slot], device)
        vec_copies.append((elsewhere, copy))
    vec_copies.append(
        (
            True,
            remote(
                vec_ref,
                vecs_ref.at[2 * ranks],
                vec_send.at[2 * ranks],
                vec_recv.at[2 * ranks],
                ring.other_core(),
            ),
        )
    )
    own_vec = pltpu.make_async_copy(vec_ref, vecs_ref.at[section * ranks + mp], local_sems.at[0])

    split_first = remote(
        w_ref.at[ring.column(flip_section=True)],
        first_ref.at[mp, ring.column(flip_section=True)],
        split_send.at[0],
        split_recv.at[0],
        ring.other_section(),
    )
    split_second = remote(
        w_ref.at[ring.column(flip_section=True)],
        second_ref,
        split_send.at[0],
        split_recv.at[1],
        ring.other_section(),
    )
    own_first = pltpu.make_async_copy(
        w_ref.at[own_column], first_ref.at[mp, own_column], local_sems.at[1]
    )
    own_second = pltpu.make_async_copy(w_ref.at[own_column], second_ref, local_sems.at[1])

    @pl.when(section == 0)
    def _():
        split_first.start()
        own_first.start()

    @pl.when(section == 1)
    def _():
        split_second.start()
        own_second.start()

    def owner(item):
        return (section, ring.base + 2 * ring.side + (mp // 2) % 2, item * place.chips + mp // 4)

    def hand_out(source_ref, item, go):
        device = owner(item)
        here = (device[1] == ring.dp) & (device[2] == mp)

        @pl.when(go & jnp.logical_not(here))
        def _():
            remote(
                source_ref.at[item],
                rows_ref.at[half],
                row_send.at[item],
                row_recv.at[half],
                device,
            ).start()

        @pl.when(go & here)
        def _():
            pltpu.make_async_copy(
                source_ref.at[item], rows_ref.at[half], local_sems.at[2]
            ).start()

    for item in range(items):
        hand_out(x_ref, item, hands_out & (section == 0))

        @pl.when((section == 0) & (core == 1))
        def _():
            remote(
                x_ref.at[item],
                stage_ref.at[item],
                stage_send.at[item],
                stage_recv.at[item],
                ring.other_section(),
            ).start()

    own_vec.start()
    for go, copy in vec_copies:
        if go is True:
            copy.start()
        else:
            pl.when(go)(copy.start)

    @pl.when(section == 0)
    def _():
        own_first.wait()

    @pl.when(section == 1)
    def _():
        remote(
            w_ref.at[0],
            first_ref.at[mp, own_column],
            split_send.at[0],
            split_recv.at[0],
            ring.other_section(),
        ).wait_recv()

    def line_copy(slot, up):
        device = ring.at(mp=mp + 1 if up else mp - 1)
        sems = up_send if up else down_send
        ref = first_ref.at[slot, own_column]
        return remote(ref, ref, sems.at[slot], line_recv.at[slot], device)

    def side_copy(slot, which):
        column = ring.column(flip_section=which == 1)
        ref = first_ref.at[slot, column]
        return remote(
            ref, ref, side_send.at[which, slot], side_recv.at[which, slot], ring.other_side()
        )

    def section_copy(slot):
        ref = first_ref.at[slot, own_column]
        return remote(
            ref, ref, section_send.at[slot], section_recv.at[slot], ring.other_section()
        )

    def spread(slot):
        section_copy(slot).start()
        side_copy(slot, 0).start()

    def forward_rows(item):
        pl.when((section == 1) & (core == 1))(
            lambda: remote(
                x_ref.at[item],
                stage_ref.at[item],
                stage_send.at[item],
                stage_recv.at[item],
                ring.other_section(),
            ).wait_recv()
        )
        hand_out(stage_ref, item, (section == 1) & (core == 1))

    forwarded = 0
    for step in range(ranks - 1):
        low, high = mp - step, mp + step
        pl.when((low >= 0) & (mp + 1 < ranks))(lambda: line_copy(low, True).start())
        pl.when((high < ranks) & (mp >= 1))(lambda: line_copy(high, False).start())
        if step == 0:
            spread(mp)
        else:
            pl.when(low >= 0)(lambda: spread(low))
            pl.when(high < ranks)(lambda: spread(high))
        pl.when(low - 1 >= 0)(lambda: line_copy(low - 1, True).wait_recv())
        pl.when(high + 1 < ranks)(lambda: line_copy(high + 1, False).wait_recv())
        if forwarded < items:
            forward_rows(forwarded)
            forwarded += 1
    last = ranks - 1
    pl.when(mp - last >= 0)(lambda: spread(mp - last))
    pl.when(mp + last < ranks)(lambda: spread(mp + last))
    while forwarded < items:
        forward_rows(forwarded)
        forwarded += 1

    def core_copy(index):
        column = ring.column(flip_side=index % 2 == 1, flip_section=index // 2 == 1)
        ref = first_ref.at[:, column]
        return remote(ref, ref, core_send.at[index], core_recv.at[index], ring.other_core())

    core_copy(0).start()

    def section_arrival(slot):
        section_copy(slot).wait_recv()
        side_copy(slot, 1).start()

    for slot, there in ring.slots():
        if there is True:
            section_arrival(slot)
        else:
            pl.when(there)(functools.partial(section_arrival, slot))
    core_copy(2).start()
    for slot in range(ranks):
        side_copy(slot, 0).wait_recv()
    core_copy(1).start()
    for slot in range(ranks):
        side_copy(slot, 1).wait_recv()
    core_copy(3).start()

    for part in range(2):
        source = (section, ring.base + 2 * ring.side + section, 2 * place.member() + part)
        here = (source[1] == ring.dp) & (source[2] == mp)

        @pl.when(jnp.logical_not(here))
        def _():
            remote(
                x_ref.at[0], rows_ref.at[part], row_send.at[0], row_recv.at[part], source
            ).wait_recv()

        @pl.when(here)
        def _():
            pltpu.make_async_copy(x_ref.at[0], rows_ref.at[part], local_sems.at[2]).wait()

    own_vec.wait()
    for other in range(2 * ranks):

        @pl.when((section * ranks + mp) != other)
        def _():
            remote(
                vec_ref,
                vecs_ref.at[other],
                vec_send.at[other],
                vec_recv.at[other],
                ring.other_core(),
            ).wait_recv()

    vec_copies[-1][1].wait_recv()

    @pl.when(section == 0)
    def _():
        remote(
            w_ref.at[0], second_ref, split_send.at[0], split_recv.at[1], ring.other_section()
        ).wait_recv()

    @pl.when(section == 1)
    def _():
        own_second.wait()

    for index in range(4):
        core_copy(index).wait_recv()

    split_first.wait_send()
    for go, copy in vec_copies:
        if go is True:
            copy.wait_send()
        else:
            pl.when(go)(copy.wait_send)
    for item in range(items):
        device = owner(item)
        here = (device[1] == ring.dp) & (device[2] == mp)

        @pl.when(hands_out & jnp.logical_not(here))
        def _():
            remote(
                x_ref.at[item], rows_ref.at[half], row_send.at[item], row_recv.at[half], device
            ).wait_send()

        @pl.when((section == 0) & (core == 1))
        def _():
            remote(
                x_ref.at[item],
                stage_ref.at[item],
                stage_send.at[item],
                stage_recv.at[item],
                ring.other_section(),
            ).wait_send()

    for slot in range(ranks):
        pl.when((mp + 1 < ranks) & (slot <= mp))(lambda: line_copy(slot, True).wait_send())
        pl.when((mp >= 1) & (slot >= mp))(lambda: line_copy(slot, False).wait_send())
        section_copy(slot).wait_send()
        side_copy(slot, 0).wait_send()
        side_copy(slot, 1).wait_send()
    for index in range(4):
        core_copy(index).wait_send()


def start(mesh, place, rows, weights, vec):
    ranks, items = place.ranks, place.items
    held = pl.BlockSpec(memory_space=pltpu.VMEM)
    dma = pltpu.SemaphoreType.DMA
    return pl.pallas_call(
        functools.partial(start_kernel, mesh, place),
        out_shape=(
            jax.ShapeDtypeStruct((2,) + rows.shape[1:], rows.dtype),
            jax.ShapeDtypeStruct((ranks,) + weights.shape, weights.dtype),
            jax.ShapeDtypeStruct(weights.shape[1:], weights.dtype),
            jax.ShapeDtypeStruct((2 * ranks + 1,) + vec.shape, vec.dtype),
        ),
        in_specs=[held] * 3,
        out_specs=(held,) * 4,
        scratch_shapes=[
            pltpu.VMEM(rows.shape, rows.dtype),
            dma((3,)),
            dma((items,)),
            dma((2,)),
            dma((items,)),
            dma((items,)),
            dma((2 * ranks + 1,)),
            dma((2 * ranks + 1,)),
            dma((1,)),
            dma((2,)),
            dma((ranks,)),
            dma((ranks,)),
            dma((ranks,)),
            dma((2, ranks)),
            dma((2, ranks)),
            dma((ranks,)),
            dma((ranks,)),
            dma((4,)),
            dma((4,)),
        ],
        cost_estimate=cost(50),
        compiler_params=pltpu.CompilerParams(
            collective_id=0, has_side_effects=True, vmem_limit_bytes=VMEM_BYTES
        ),
    )(rows, weights, vec)


def swap_kernel(place, x_ref, o_ref, send_sems, recv_sems, local_sem):
    me = place.member()
    peers = [place.peer(step) for step in range(1, place.members)]
    greet([p[1] for p in peers], place.members - 1, place.is_here)
    copies = []
    for index, (rank, device) in enumerate(peers):
        copies.append(
            pltpu.make_async_remote_copy(
                src_ref=x_ref.at[rank],
                dst_ref=o_ref.at[me],
                send_sem=send_sems.at[index],
                recv_sem=recv_sems.at[index],
                device_id=device,
                device_id_type=MESH,
            )
        )
        copies[-1].start()
    own = pltpu.make_async_copy(x_ref.at[me], o_ref.at[me], local_sem)
    own.start()
    own.wait()
    for copy in copies:
        copy.wait()


def swapped(place, x, collective_id):
    held = pl.BlockSpec(memory_space=pltpu.VMEM)
    return pl.pallas_call(
        functools.partial(swap_kernel, place),
        out_shape=jax.ShapeDtypeStruct(x.shape, x.dtype),
        in_specs=[held],
        out_specs=held,
        scratch_shapes=[
            pltpu.SemaphoreType.DMA((place.members - 1,)),
            pltpu.SemaphoreType.DMA((place.members - 1,)),
            pltpu.SemaphoreType.DMA,
        ],
        cost_estimate=cost(5),
        compiler_params=pltpu.CompilerParams(
            collective_id=collective_id, has_side_effects=True, vmem_limit_bytes=VMEM_BYTES
        ),
    )(x)


def to_heads(place, x, collective_id):
    return swapped(place, x, collective_id).reshape(-1, x.shape[2])


def to_rows(place, x, collective_id):
    return swapped(place, x.reshape(place.members, -1, x.shape[1]), collective_id)


def finish_kernel(
    mesh,
    place,
    rows_ref,
    grad_ref,
    vec_ref,
    late_ref,
    second_ref,
    gone_ref,
    grad_out_ref,
    late_out_ref,
    second_out_ref,
    vec_out_ref,
    core_got,
    side_sent,
    side_got,
    section_sent,
    section_got,
    line_sent,
    line_got,
    piece_ref,
    vec_sent,
    vec_got,
    vec_line,
    local_sem,
    row_send,
    row_recv,
    core_send,
    core_recv,
    side_send,
    side_recv,
    section_send,
    section_recv,
    line_send,
    line_recv,
    piece_send,
    piece_recv,
    vec_send,
    vec_recv,
    vec_line_send,
    vec_line_recv,
):
    ring = Ring(mesh)
    ranks, items = ring.ranks, place.items
    section, mp = ring.section, ring.mp
    ring.greet_all()

    flips = ((True, False), (True, True), (False, True), (False, False))

    def core_copy(index):
        side, other = flips[index]
        return remote(
            grad_ref.at[:, ring.column(side, other, True)],
            core_got.at[index],
            core_send.at[index],
            core_recv.at[index],
            ring.other_core(),
        )

    for index in range(4):
        core_copy(index).start()

    partners = (ring.other_core(), ring.other_side(), ring.other_section())

    def vec_copy(step):
        return remote(
            vec_sent.at[step],
            vec_got.at[step],
            vec_send.at[step],
            vec_recv.at[step],
            partners[step],
        )

    vec_sent[0] = vec_ref[...]
    vec_copy(0).start()

    targets = [
        (0, ring.base + 2 * ring.side + section, 2 * place.member() + part) for part in range(2)
    ]
    slot = mp // place.chips

    def row_copy(index):
        return remote(
            rows_ref.at[index], gone_ref.at[slot], row_send.at[index], row_recv.at[slot], targets[index]
        )

    def own_row(index):
        return pltpu.make_async_copy(rows_ref.at[index], gone_ref.at[slot], local_sem)

    for index in range(2):
        pl.when(jnp.logical_not(place.is_here(targets[index])))(
            lambda index=index: row_copy(index).start()
        )
        pl.when(place.is_here(targets[index]))(lambda index=index: own_row(index).start())

    def piece_copy(which, near):
        source, target, section_to = (
            (piece_ref, grad_out_ref, 0),
            (late_ref, late_out_ref, 0),
            (second_ref, second_out_ref, 1),
        )[which]
        device = (section_to, ring.base + near, mp)
        return remote(
            source,
            target.at[ring.column()],
            piece_send.at[which, near],
            piece_recv.at[which, ring.column()],
            device,
        )

    def to_keepers(which, method):
        for near in range(4):
            mine = (section == (1 if which == 2 else 0)) & (ring.dp == ring.base + near)
            pl.when(jnp.logical_not(mine))(lambda near=near: method(piece_copy(which, near)))

    to_keepers(1, lambda copy: copy.start())
    to_keepers(2, lambda copy: copy.start())

    @pl.when(section == 0)
    def _():
        late_out_ref[ring.column()] = late_ref[...]

    @pl.when(section == 1)
    def _():
        second_out_ref[ring.column()] = second_ref[...]

    def side_copy(index):
        return remote(
            side_sent.at[index],
            side_got.at[index],
            side_send.at[index],
            side_recv.at[index],
            ring.other_side(),
        )

    def wide(value):
        return value.astype(F32)

    for index in range(2):
        side, other = flips[index]
        core_copy(index).wait_recv()
        kept = grad_ref[:, ring.column(side, other)]
        side_sent[index] = (wide(kept) + wide(core_got[index])).astype(LOW)
        side_copy(index).start()

    vec_copy(0).wait_recv()
    vec_sent[1] = vec_sent[0] + vec_got[0]
    vec_copy(1).start()

    core_copy(2).wait_recv()
    side_copy(1).wait_recv()
    kept = grad_ref[:, ring.column(False, True)]
    section_sent[...] = (wide(kept) + wide(core_got[2]) + wide(side_got[1])).astype(LOW)
    section_copy = remote(
        section_sent, section_got, section_send, section_recv, ring.other_section()
    )
    section_copy.start()
    vec_copy(1).wait_recv()
    vec_sent[2] = vec_sent[1] + vec_got[1]
    vec_copy(2).start()
    core_copy(3).wait_recv()
    side_copy(0).wait_recv()
    section_copy.wait_recv()
    kept = grad_ref[:, ring.column()]
    whole = wide(kept) + wide(core_got[3]) + wide(side_got[0]) + wide(section_got[...])
    line_sent[...] = whole.astype(LOW)

    def along(other, method):
        pl.when(mp != other)(lambda: method(other))

    def line_copy(other, mine=None):
        return remote(
            line_sent.at[other],
            line_got.at[mp if mine is None else mine],
            line_send.at[other],
            line_recv.at[mp if mine is None else mine],
            ring.at(mp=other),
        )

    def vec_line_copy(other, mine=None):
        return remote(
            vec_line.at[ranks],
            vec_line.at[mp if mine is None else mine],
            vec_line_send.at[other],
            vec_line_recv.at[mp if mine is None else mine],
            ring.at(mp=other),
        )

    for other in range(ranks):
        along(other, lambda other: line_copy(other).start())
    vec_copy(2).wait_recv()
    vec_line[ranks] = vec_sent[2] + vec_got[2]
    for other in range(ranks):
        along(other, lambda other: vec_line_copy(other).start())

    @pl.when(mp >= 0)
    def _():
        line_got[mp] = line_sent[mp]
        vec_line[mp] = vec_line[ranks]

    for other in range(ranks):
        along(other, lambda other: line_copy(other, other).wait_recv())
    total = wide(line_got[0])
    for other in range(1, ranks):
        total = total + wide(line_got[other])
    piece_ref[...] = total.astype(LOW)
    to_keepers(0, lambda copy: copy.start())

    @pl.when(section == 0)
    def _():
        grad_out_ref[ring.column()] = piece_ref[...]

    for other in range(ranks):
        along(other, lambda other: vec_line_copy(other, other).wait_recv())
    total = vec_line[0]
    for other in range(1, ranks):
        total = total + vec_line[other]
    vec_out_ref[...] = total

    for item in range(items):
        source = place.owner_of(item)
        pl.when((section == 0) & jnp.logical_not(place.is_here(source)))(
            lambda item=item, source=source: remote(
                rows_ref.at[0], gone_ref.at[item], row_send.at[0], row_recv.at[item], source
            ).wait_recv()
        )
    for index in range(2):
        pl.when(place.is_here(targets[index]))(lambda index=index: own_row(index).wait())
        pl.when(jnp.logical_not(place.is_here(targets[index])))(
            lambda index=index: row_copy(index).wait_send()
        )

    def piece_arrival(which, column):
        source, target = (
            (piece_ref, grad_out_ref),
            (late_ref, late_out_ref),
            (second_ref, second_out_ref),
        )[which]
        return remote(
            source,
            target.at[column],
            piece_send.at[which, 0],
            piece_recv.at[which, column],
            ring.other_core(),
        )

    for which in range(3):
        for column in range(8):
            keeper = section == (1 if which == 2 else 0)
            pl.when(keeper & (ring.column() != column))(
                lambda which=which, column=column: piece_arrival(which, column).wait_recv()
            )
        to_keepers(which, lambda copy: copy.wait_send())
    for index in range(4):
        core_copy(index).wait_send()
    for index in range(2):
        side_copy(index).wait_send()
    section_copy.wait_send()
    for step in range(3):
        vec_copy(step).wait_send()
    for other in range(ranks):
        along(other, lambda other: line_copy(other).wait_send())
        along(other, lambda other: vec_line_copy(other).wait_send())


def finish(mesh, place, rows, grads, vecs, late, second):
    ranks, items = place.ranks, place.items
    held = pl.BlockSpec(memory_space=pltpu.VMEM)
    dma = pltpu.SemaphoreType.DMA
    column = (ranks,) + grads.shape[2:]

    def like(lead, x):
        return jax.ShapeDtypeStruct(lead + x.shape, x.dtype)

    return pl.pallas_call(
        functools.partial(finish_kernel, mesh, place),
        out_shape=(
            jax.ShapeDtypeStruct((items,) + rows.shape[1:], rows.dtype),
            jax.ShapeDtypeStruct((8,) + grads.shape[2:], LOW),
            like((8,), late),
            like((8,), second),
            jax.ShapeDtypeStruct(vecs.shape, F32),
        ),
        in_specs=[held] * 5,
        out_specs=(held,) * 5,
        scratch_shapes=[
            pltpu.VMEM((4,) + column, LOW),
            pltpu.VMEM((2,) + column, LOW),
            pltpu.VMEM((2,) + column, LOW),
            pltpu.VMEM(column, LOW),
            pltpu.VMEM(column, LOW),
            pltpu.VMEM(column, LOW),
            pltpu.VMEM(column, LOW),
            pltpu.VMEM(column[1:], LOW),
            pltpu.VMEM((3,) + vecs.shape, F32),
            pltpu.VMEM((3,) + vecs.shape, F32),
            pltpu.VMEM((ranks + 1,) + vecs.shape, F32),
            dma,
            dma((2,)),
            dma((items,)),
            dma((4,)),
            dma((4,)),
            dma((2,)),
            dma((2,)),
            dma,
            dma,
            dma((ranks,)),
            dma((ranks,)),
            dma((3, 4)),
            dma((3, 8)),
            dma((3,)),
            dma((3,)),
            dma((ranks,)),
            dma((ranks,)),
        ],
        cost_estimate=cost(40),
        compiler_params=pltpu.CompilerParams(
            collective_id=1, has_side_effects=True, vmem_limit_bytes=VMEM_BYTES
        ),
    )(rows, grads, vecs, late, second)


def dot_rows(left, right):
    return lax.dot_general(left, right, (((1,), (1,)), ((), ())), preferred_element_type=F32)


def dot(left, right):
    return lax.dot_general(left, right, (((1,), (0,)), ((), ())), preferred_element_type=F32)


def half_of(block, head):
    lanes = lax.broadcasted_iota(jnp.int32, (1, PAIR), 1)
    mine = (lanes < HEAD) if head == 0 else (lanes >= HEAD)
    return jnp.where(mine, block, jnp.zeros((), block.dtype))


def joined(first, second):
    lanes = lax.broadcasted_iota(jnp.int32, (1, PAIR), 1)
    return jnp.where(lanes < HEAD, first, second)


def forward_pair(q, k, v, bias):
    outs, logs = [], []
    q = q * jnp.asarray(0.125, LOW)
    for head in range(2):
        scores = dot_rows(half_of(q, head), k)
        if bias is not None:
            scores = scores + bias
        top = jnp.max(scores, -1, keepdims=True)
        expon = jnp.exp(scores - top)
        total = jnp.sum(expon, -1, keepdims=True)
        outs.append(dot(expon.astype(LOW), v) / total)
        logs.append(top + jnp.log(total))
    return joined(*outs), logs


def joint_forward_kernel(pairs, length_ref, q_ref, k_ref, o_ref, log_ref):
    keys = k_ref.shape[0]
    column = lax.broadcasted_iota(jnp.int32, (1, keys), 1)
    bias = jnp.where(column < PATCH_ROWS + length_ref[0], 0.0, MASKED).astype(F32)
    lanes = lax.broadcasted_iota(jnp.int32, (1, 128), 1)
    kept = jnp.zeros(log_ref.shape, F32)
    for pair in range(pairs):
        base = pair * 3 * PAIR
        out, logs = forward_pair(
            q_ref[:, base : base + PAIR],
            k_ref[:, base + PAIR : base + 2 * PAIR],
            k_ref[:, base + 2 * PAIR : base + 3 * PAIR],
            bias,
        )
        o_ref[:, pair * PAIR : (pair + 1) * PAIR] = out.astype(LOW)
        for head in range(2):
            kept = jnp.where(lanes == pair * 2 + head, logs[head], kept)
    log_ref[...] = kept


def joint_forward(qkv, length):
    rows, width = qkv.shape
    pairs = width // (3 * PAIR)
    block = 208
    return pl.pallas_call(
        functools.partial(joint_forward_kernel, pairs),
        grid=(rows // block,),
        out_shape=(
            jax.ShapeDtypeStruct((rows, pairs * PAIR), LOW),
            jax.ShapeDtypeStruct((rows, 128), F32),
        ),
        in_specs=[
            pl.BlockSpec(memory_space=pltpu.SMEM),
            pl.BlockSpec((block, width), lambda i: (i, 0)),
            pl.BlockSpec((rows, width), lambda i: (0, 0)),
        ],
        out_specs=(
            pl.BlockSpec((block, pairs * PAIR), lambda i: (i, 0)),
            pl.BlockSpec((block, 128), lambda i: (i, 0)),
        ),
        cost_estimate=cost(36),
        compiler_params=pltpu.CompilerParams(vmem_limit_bytes=VMEM_BYTES),
    )(length, qkv, qkv)


def backward_head(q, k, v, grad, head, log, delta, limit):
    scores = dot_rows(k, half_of(q, head))
    if limit is not None:
        row = lax.broadcasted_iota(jnp.int32, (scores.shape[0], 1), 0)
        scores = jnp.where(row < limit, scores, MASKED)
    if log is None:
        top = jnp.max(scores, 0, keepdims=True)
        expon = jnp.exp(scores - top)
        probs = expon / jnp.sum(expon, 0, keepdims=True)
    else:
        probs = jnp.exp(scores - log)
    grad_probs = dot_rows(v, half_of(grad, head))
    if delta is None:
        delta = jnp.sum(probs * grad_probs, 0, keepdims=True)
    grad_scores = (probs * (grad_probs - delta)).astype(LOW)
    grad_v = dot(probs.astype(LOW), grad)
    grad_k = dot(grad_scores, q)
    k_turned = k[:, head * HEAD : (head + 1) * HEAD].T
    grad_q = dot(k_turned, grad_scores)
    return grad_q, grad_k, grad_v


def joint_backward_kernel(
    length_ref, q_ref, k_ref, v_ref, grad_ref, out_ref, log_ref, o_ref, total_ref, stat_ref
):
    pair, step = pl.program_id(0), pl.program_id(1)
    block = k_ref.shape[0]
    limit = PATCH_ROWS + length_ref[0] - step * block
    q = q_ref[...] * jnp.asarray(0.125, LOW)
    k, v, grad = k_ref[...], v_ref[...], grad_ref[...]

    @pl.when(step == 0)
    def _():
        total_ref[...] = jnp.zeros_like(total_ref)
        rows = lax.broadcasted_iota(jnp.int32, (8, PAIR), 0)
        lanes = lax.broadcasted_iota(jnp.int32, (8, PAIR), 1)
        which = jnp.where(lanes == pair * 2 + rows, 1.0, 0.0).astype(F32)
        own = jnp.where((lanes // HEAD) == rows, 1.0, 0.0).astype(F32)
        product = grad_ref[...].astype(F32) * out_ref[...].astype(F32)
        exact = functools.partial(
            lax.dot_general,
            dimension_numbers=(((1,), (1,)), ((), ())),
            precision=lax.Precision.HIGHEST,
            preferred_element_type=F32,
        )
        stat_ref[0] = exact(which, log_ref[...])
        stat_ref[1] = exact(own, product)

    grads_k, grads_v = [], []
    for head in range(2):
        grad_q, grad_k, grad_v = backward_head(
            q, k, v, grad, head, stat_ref[0, head : head + 1], stat_ref[1, head : head + 1], limit
        )
        total_ref[head * HEAD : (head + 1) * HEAD] += grad_q
        grads_k.append(grad_k)
        grads_v.append(grad_v)
    here = pl.ds(pl.multiple_of(step * block, 16), block)
    o_ref[here, PAIR : 2 * PAIR] = joined(*grads_k).astype(LOW)
    o_ref[here, 2 * PAIR : 3 * PAIR] = joined(*grads_v).astype(LOW)

    @pl.when(step == pl.num_programs(1) - 1)
    def _():
        o_ref[:, 0:PAIR] = (total_ref[...].T * 0.125).astype(LOW)


def joint_backward(qkv, length, grad, out, log):
    rows, width = qkv.shape
    pairs = width // (3 * PAIR)
    block = 208
    return pl.pallas_call(
        joint_backward_kernel,
        grid=(pairs, rows // block),
        out_shape=jax.ShapeDtypeStruct((rows, width), LOW),
        in_specs=[
            pl.BlockSpec(memory_space=pltpu.SMEM),
            pl.BlockSpec((rows, PAIR), lambda p, i: (0, 3 * p)),
            pl.BlockSpec((block, PAIR), lambda p, i: (i, 3 * p + 1)),
            pl.BlockSpec((block, PAIR), lambda p, i: (i, 3 * p + 2)),
            pl.BlockSpec((rows, PAIR), lambda p, i: (0, p)),
            pl.BlockSpec((rows, PAIR), lambda p, i: (0, p)),
            pl.BlockSpec((rows, 128), lambda p, i: (0, 0)),
        ],
        out_specs=pl.BlockSpec((rows, 3 * PAIR), lambda p, i: (0, p)),
        scratch_shapes=[pltpu.VMEM((PAIR, rows), F32), pltpu.VMEM((2, 8, rows), F32)],
        cost_estimate=cost(62),
        compiler_params=pltpu.CompilerParams(vmem_limit_bytes=VMEM_BYTES),
    )(length, qkv, qkv, qkv, grad, out, log)


def within_forward_kernel(pairs, length_ref, x_ref, o_ref):
    def group(rows, bias):
        for pair in range(pairs):
            base = pair * 3 * PAIR
            q, k, v = (x_ref[rows, base + part * PAIR : base + (part + 1) * PAIR] for part in range(3))
            out, _ = forward_pair(q, k, v, bias)
            o_ref[rows, pair * PAIR : (pair + 1) * PAIR] = out.astype(LOW)

    @pl.loop(0, VIEWS)
    def _(view):
        group(pl.ds(pl.multiple_of(view * PATCH, 16), PATCH), None)

    column = lax.broadcasted_iota(jnp.int32, (1, TEXT), 1)
    bias = jnp.where(column < length_ref[0], 0.0, MASKED).astype(F32)
    group(pl.ds(PATCH_ROWS, TEXT), bias)


def within_forward(qkv, length):
    rows, width = qkv.shape
    pairs = width // (3 * PAIR)
    return pl.pallas_call(
        functools.partial(within_forward_kernel, pairs),
        out_shape=jax.ShapeDtypeStruct((rows, pairs * PAIR), LOW),
        in_specs=[
            pl.BlockSpec(memory_space=pltpu.SMEM),
            pl.BlockSpec(memory_space=pltpu.VMEM),
        ],
        out_specs=pl.BlockSpec(memory_space=pltpu.VMEM),
        cost_estimate=cost(10),
        compiler_params=pltpu.CompilerParams(vmem_limit_bytes=VMEM_BYTES),
    )(length, qkv)


def within_backward_kernel(pairs, length_ref, x_ref, grad_ref, o_ref):
    def group(rows, limit):
        for pair in range(pairs):
            base = pair * 3 * PAIR
            q, k, v = (x_ref[rows, base + part * PAIR : base + (part + 1) * PAIR] for part in range(3))
            q = q * jnp.asarray(0.125, LOW)
            grad = grad_ref[rows, pair * PAIR : (pair + 1) * PAIR]
            both = [backward_head(q, k, v, grad, head, None, None, limit) for head in range(2)]
            grad_q = jnp.concatenate([both[0][0], both[1][0]], 0).T * 0.125
            o_ref[rows, base : base + PAIR] = grad_q.astype(LOW)
            o_ref[rows, base + PAIR : base + 2 * PAIR] = joined(both[0][1], both[1][1]).astype(LOW)
            o_ref[rows, base + 2 * PAIR : base + 3 * PAIR] = joined(both[0][2], both[1][2]).astype(LOW)

    @pl.loop(0, VIEWS)
    def _(view):
        group(pl.ds(pl.multiple_of(view * PATCH, 16), PATCH), None)

    group(pl.ds(PATCH_ROWS, TEXT), length_ref[0])


def within_backward(qkv, length, grad):
    rows, width = qkv.shape
    pairs = width // (3 * PAIR)
    return pl.pallas_call(
        functools.partial(within_backward_kernel, pairs),
        out_shape=jax.ShapeDtypeStruct((rows, width), LOW),
        in_specs=[
            pl.BlockSpec(memory_space=pltpu.SMEM),
            pl.BlockSpec(memory_space=pltpu.VMEM),
            pl.BlockSpec(memory_space=pltpu.VMEM),
        ],
        out_specs=pl.BlockSpec(memory_space=pltpu.VMEM),
        cost_estimate=cost(22),
        compiler_params=pltpu.CompilerParams(vmem_limit_bytes=VMEM_BYTES),
    )(length, qkv, grad)


def layer_norm(values, scale_vec, shift_vec):
    center = jnp.mean(values, -1, keepdims=True)
    offset = values - center
    spread = jnp.mean(offset * offset, -1, keepdims=True)
    return offset * lax.rsqrt(spread + 1e-05) * scale_vec + shift_vec


def times_turned(left, weight):
    return lax.dot_general(left, weight, (((1,), (1,)), ((), ())), preferred_element_type=F32)


def times(left, weight):
    return lax.dot_general(left, weight, (((1,), (0,)), ((), ())), preferred_element_type=F32)


def over_rows(left, right):
    return lax.dot_general(left, right, (((0,), (0,)), ((), ())), preferred_element_type=F32)


def layer_forward(place, source, length, params, within):
    normed = layer_norm(source, params["gain_one"], params["bias_one"]).astype(LOW)
    projected = jnp.einsum("sd,red->rse", normed, params["qkv"], preferred_element_type=F32)
    qkv = to_heads(place, projected.astype(LOW), 2)
    if within:
        mixed_heads, logs = within_forward(qkv, length), None
    else:
        mixed_heads, logs = joint_forward(qkv, length)
    mixed = to_rows(place, mixed_heads, 3)
    branch = jnp.einsum("rse,red->sd", mixed, params["out"], preferred_element_type=F32)
    middle = source + branch + params["bias_out"]
    second = layer_norm(middle, params["gain_two"], params["bias_two"]).astype(LOW)
    hidden_pre = times_turned(second, params["up"]) + params["bias_up"]
    hidden = jax.nn.gelu(hidden_pre).astype(LOW)
    result = middle + times(hidden, params["down"]) + params["bias_down"]
    return result, (source, normed, qkv, mixed_heads, logs, mixed, middle, second, hidden_pre, hidden)


def layer_backward(place, upstream, length, params, kept, within):
    source, normed, qkv, mixed_heads, logs, mixed, middle, second, hidden_pre, hidden = kept
    up_low = upstream.astype(LOW)
    grad_down = over_rows(hidden, up_low)
    grad_hidden = times_turned(up_low, params["down"])
    grad_pre = jax.vjp(jax.nn.gelu, hidden_pre)[1](grad_hidden)[0].astype(LOW)
    grad_up_bias = jnp.sum(grad_pre.astype(F32), 0)
    grad_up = over_rows(grad_pre, second)
    grad_second = times(grad_pre, params["up"])
    norm_pull = jax.vjp(layer_norm, middle, params["gain_two"], params["bias_two"])[1]
    part_middle, grad_gain_two, grad_bias_two = norm_pull(grad_second)
    grad_middle = upstream + part_middle
    mid_low = grad_middle.astype(LOW)
    grad_out = jnp.einsum("rse,sd->red", mixed, mid_low, preferred_element_type=F32)
    grad_mixed = jnp.einsum("sd,red->rse", mid_low, params["out"], preferred_element_type=F32)
    grad_heads = to_heads(place, grad_mixed.astype(LOW), 4)
    if within:
        grad_qkv_heads = within_backward(qkv, length, grad_heads)
    else:
        grad_qkv_heads = joint_backward(qkv, length, grad_heads, mixed_heads, logs)
    grad_projected = to_rows(place, grad_qkv_heads, 5)
    grad_qkv = jnp.einsum("rse,sd->red", grad_projected, normed, preferred_element_type=F32)
    grad_normed = jnp.einsum("rse,red->sd", grad_projected, params["qkv"], preferred_element_type=F32)
    first_pull = jax.vjp(layer_norm, source, params["gain_one"], params["bias_one"])[1]
    part_source, grad_gain_one, grad_bias_one = first_pull(grad_normed)
    matrices = (grad_qkv, grad_out, grad_up, grad_down)
    vectors = (
        grad_gain_one,
        grad_bias_one,
        jnp.sum(grad_middle, 0),
        grad_gain_two,
        grad_bias_two,
        jnp.sum(upstream, 0),
        grad_up_bias,
    )
    return grad_middle + part_source, matrices, jnp.concatenate(vectors)


AXES = ("section", "dp", "mp")


def permuted(mesh, x, place_of):
    sections, dps, ranks = (mesh.shape[n] for n in AXES)
    route = []
    for section in range(sections):
        for dp in range(dps):
            for mp in range(ranks):
                to = place_of(section, dp, mp)
                if to is not None:
                    route.append(((section * dps + dp) * ranks + mp, (to[0] * dps + to[1]) * ranks + to[2]))
    return lax.ppermute(x, AXES, route)


def across_core(mesh, x):
    return permuted(mesh, x, lambda s, d, z: (s, d ^ 1, z))


def across_side(mesh, x):
    return permuted(mesh, x, lambda s, d, z: (s, d ^ 2, z))


def across_section(mesh, x):
    return permuted(mesh, x, lambda s, d, z: (1 - s, d, z))


def pick(x, index, axis):
    return lax.dynamic_index_in_dim(x, index, axis, keepdims=False)


def bring_cotangents(mesh, place, blocks):
    items, chips = place.items, place.chips
    mp = lax.axis_index("mp")
    got = []
    for turn in range(items):

        def to(s, d, z):
            if s == 0:
                return None
            item = (turn + 2 * (z % 2)) % items
            return (d % 2, (d // 2) * 2 + (z // 2) % 2, item * chips + z // 4)

        got.append(permuted(mesh, pick(blocks, (turn + 2 * (mp % 2)) % items, 0), to))
    item = mp // chips
    halves = []
    for half in range(2):
        found = got[(0 - 2 * half) % items]
        for other in range(1, items):
            found = jnp.where(item == other, got[(other - 2 * half) % items], found)
        halves.append(found)
    return jnp.concatenate(halves, 0)


def return_results(mesh, place, blocks):
    items, chips = place.items, place.chips
    mp = lax.axis_index("mp")
    mine = mp // chips
    got = []
    for turn in range(items):

        def to(s, d, z):
            shift = (z // chips - turn) % items
            if shift % 2:
                return None
            rank = (z % chips) * 2 + d % 2
            return (1, (d // 2) * 2 + s, 2 * rank + shift // 2)

        got.append(permuted(mesh, pick(blocks, ((mine - turn) % items) // 2, 0), to))
    return got


def ends_kernel(gone_ref, *refs):
    got_refs, o_ref = refs[:-1], refs[-1]
    section, odd = lax.axis_index("section"), lax.axis_index("mp") % 2
    items = len(got_refs)

    @pl.when(section == 0)
    def _():
        o_ref[...] = gone_ref[...].astype(F32)

    for shift in range(2):

        @pl.when((section == 1) & (odd == shift))
        def _():
            for item in range(items):
                o_ref[item] = got_refs[(item - 2 * shift) % items][...].astype(F32)


def ends_of(gone, got):
    held = pl.BlockSpec(memory_space=pltpu.VMEM)
    return pl.pallas_call(
        ends_kernel,
        out_shape=jax.ShapeDtypeStruct(gone.shape, F32),
        in_specs=[held] * (1 + len(got)),
        out_specs=held,
        cost_estimate=cost(3),
        compiler_params=pltpu.CompilerParams(vmem_limit_bytes=VMEM_BYTES),
    )(gone, *got)


def turned(mesh, x, turn):
    ranks = mesh.shape["mp"]
    return permuted(mesh, x, lambda s, d, z: (s, d, (z + turn) % ranks))


def gathered_line(mesh, piece):
    ranks, mp = mesh.shape["mp"], lax.axis_index("mp")
    got = [piece] + [turned(mesh, piece, turn) for turn in range(1, ranks)]
    return jnp.stack([sum_select(got, (mp - rank) % ranks) for rank in range(ranks)])


def sum_select(choices, index):
    found = choices[0]
    for other in range(1, len(choices)):
        found = jnp.where(index == other, choices[other], found)
    return found


def scattered_line(mesh, pieces):
    ranks, mp = mesh.shape["mp"], lax.axis_index("mp")
    total = pick(pieces, mp, 0).astype(F32)
    for turn in range(1, ranks):
        total = total + turned(mesh, pick(pieces, (mp + turn) % ranks, 0), turn).astype(F32)
    return total.astype(LOW)


def assemble_kernel(mesh, a_ref, b_ref, c_ref, d_ref, e_ref, o_ref, sems):
    ring = Ring(mesh)
    index = 0
    for source, flip_side, flip_section in (
        (a_ref, False, False),
        (b_ref, True, False),
        (c_ref, False, True),
        (d_ref, True, True),
    ):
        pltpu.make_async_copy(source, o_ref.at[:, ring.column(flip_side, flip_section)], sems.at[index]).start()
        pltpu.make_async_copy(
            e_ref.at[index], o_ref.at[:, ring.column(flip_side, flip_section, True)], sems.at[4 + index]
        ).start()
        index += 1
    for i in range(4):
        pltpu.make_async_copy(a_ref, o_ref.at[:, i], sems.at[i]).wait()
        pltpu.make_async_copy(e_ref.at[i], o_ref.at[:, i], sems.at[4 + i]).wait()


def gather_second(mesh, piece):
    own = gathered_line(mesh, piece)
    section = across_section(mesh, own)
    side = across_side(mesh, own)
    both = across_side(mesh, section)
    core = across_core(mesh, jnp.stack([own, side, section, both]))
    held = pl.BlockSpec(memory_space=pltpu.VMEM)
    return pl.pallas_call(
        functools.partial(assemble_kernel, mesh),
        out_shape=jax.ShapeDtypeStruct((own.shape[0], 8) + piece.shape, piece.dtype),
        in_specs=[held] * 5,
        out_specs=held,
        scratch_shapes=[pltpu.SemaphoreType.DMA((8,))],
        cost_estimate=cost(8),
        compiler_params=pltpu.CompilerParams(vmem_limit_bytes=VMEM_BYTES),
    )(own, side, section, both, core)


def reduce_all(mesh, grads):
    section, dp = lax.axis_index("section"), lax.axis_index("dp")
    core, side = dp % 2, (dp // 2) % 2

    def halved(x, bit, axis, across):
        kept, sent = pick(x, bit, axis), pick(x, 1 - bit, axis)
        return (kept.astype(F32) + across(mesh, sent).astype(F32)).astype(LOW)

    x = grads.reshape((grads.shape[0], 2, 2, 2) + grads.shape[2:])
    x = halved(x, core, 3, across_core)
    x = halved(x, side, 1, across_side)
    x = halved(x, section, 1, across_section)
    x = scattered_line(mesh, x)
    dps = mesh.shape["dp"]
    if dps > 4:
        x = lax.psum(x, "dp", axis_index_groups=far_groups(dps))
    return x


def far_groups(dps):
    return [[low + 4 * high for high in range(dps // 4)] for low in range(4)]


def per_device(mesh, inputs, text_lengths, *weights):
    (gain_one, bias_one, weight_qkv, weight_out, bias_out) = weights[:5]
    (gain_two, bias_two, weight_up, bias_up, weight_down, bias_down) = weights[5:]
    items, block_rows, width = inputs.shape[1:]
    place = Place(mesh, items)
    ranks = place.ranks
    section, pair, core, mp = place.here()
    heads_here = weight_qkv.shape[2]
    all_heads = heads_here * ranks
    per_pair = 2 // heads_here
    hidden_here = bias_up.shape[1]

    own = (
        weight_qkv[0].reshape(width, heads_here, 3, HEAD).transpose(2, 1, 3, 0),
        weight_out[0],
        weight_up[0].T,
        weight_down[0],
    )
    own = [w.reshape(8, -1, width) for w in own]
    cuts = [w.shape[1] for w in own]
    packed = jnp.concatenate(own, 1)
    vec = [w[0] for w in (gain_one, bias_one, bias_out, gain_two, bias_two, bias_down, bias_up)]
    vec.append(text_lengths.astype(F32))
    vec = jnp.stack([jnp.pad(v, (0, width - v.shape[0])) for v in vec])

    arrived, first, second, vecs = start(mesh, place, inputs[0], packed, vec)
    mine = vecs[section * ranks + mp, 7]
    lengths = jnp.where(core == section, mine, vecs[2 * ranks, 7])
    length = pick(lengths, mp // place.chips, 0).astype(jnp.int32)[None]
    cotangent = bring_cotangents(mesh, place, inputs[0])
    second = gather_second(mesh, second)

    def params_of(layer, full):
        names = ("gain_one", "bias_one", "bias_out", "gain_two", "bias_two", "bias_down")
        rows = vecs[layer * ranks : (layer + 1) * ranks]
        found = {name: rows[0, i] for i, name in enumerate(names)}
        found["bias_up"] = rows[:, 6, :hidden_here].reshape(-1)
        at = 0
        for name, cut in zip(("qkv", "out", "up", "down"), cuts):
            found[name] = full[:, :, at : at + cut].reshape(-1, width)
            at += cut
        qkv = found["qkv"].reshape(all_heads // 2, per_pair, 3, heads_here, HEAD, width)
        found["qkv"] = qkv.swapaxes(1, 2).reshape(place.members, -1, width)
        found["out"] = found["out"].reshape(place.members, -1, width)
        return found

    def packed_grads(matrices):
        grad_qkv = matrices[0].astype(LOW)
        grad_qkv = grad_qkv.reshape(all_heads // 2, 3, per_pair, heads_here, HEAD, width)
        found = [grad_qkv.swapaxes(1, 2)] + [m.astype(LOW) for m in matrices[1:]]
        return [m.reshape(ranks, 8, -1, width) for m in found]

    params = (params_of(0, first), params_of(1, second))
    source = arrived.reshape(-1, width).astype(F32)
    boundary, kept_zero = layer_forward(place, source, length, params[0], True)
    result, kept_one = layer_forward(
        place, boundary.astype(LOW).astype(F32), length, params[1], False
    )
    results = return_results(mesh, place, result.astype(LOW).reshape(2, block_rows, width))
    upstream = cotangent.reshape(-1, width).astype(F32)
    grad_boundary, matrices, vectors_one = layer_backward(
        place, upstream, length, params[1], kept_one, False
    )
    reduced_one = reduce_all(mesh, jnp.concatenate(packed_grads(matrices), 2))
    grad_source, matrices, vectors_zero = layer_backward(
        place, grad_boundary.astype(LOW).astype(F32), length, params[0], kept_zero, True
    )
    grads_zero = packed_grads(matrices)
    late = reduce_all(mesh, jnp.concatenate(grads_zero[1:], 2))
    rows = grad_source.astype(LOW).reshape(2, block_rows, width)
    vectors = jnp.stack([vectors_zero, vectors_one]).reshape(2, -1, width)
    gone, first, late, second, sums = finish(
        mesh, place, rows, grads_zero[0], vectors, late, reduced_one
    )
    if mesh.shape["dp"] > 4:
        far = far_groups(mesh.shape["dp"])
        sums = lax.psum(sums, "dp", axis_index_groups=far)
        first = lax.psum(first, "dp", axis_index_groups=far)

    ends = ends_of(gone, results)[None]
    total = jnp.where(section == 0, jnp.concatenate([first, late], 1), second)
    parts, at = [], 0
    for cut in cuts:
        parts.append(total[:, at : at + cut].reshape(-1, width).astype(F32))
        at += cut
    sums = pick(sums, section, 0).reshape(-1)
    small = [sums[i * width : (i + 1) * width][None] for i in range(6)]
    grad_bias_up = lax.dynamic_slice_in_dim(sums, 6 * width + mp * hidden_here, hidden_here)[None]
    grad_qkv = parts[0].reshape(3, heads_here, HEAD, width).transpose(3, 1, 0, 2)
    grad_qkv = grad_qkv.reshape(1, width, heads_here, 3 * HEAD)
    return (
        ends,
        small[0],
        small[1],
        grad_qkv,
        parts[1].reshape(1, heads_here, HEAD, width),
        small[2],
        small[3],
        small[4],
        parts[2].T[None],
        grad_bias_up,
        parts[3][None],
        small[5],
    )


def solution(mesh):
    vector = P("section", None)
    ends = P("section", "dp", "mp", None)
    qkv = P("section", None, "mp", None)
    out = P("section", "mp", None, None)
    up = P("section", None, "mp")
    up_bias = P("section", "mp")
    down = P("section", "mp", None)
    params = (vector, vector, qkv, out, vector, vector, vector, up, up_bias, down, vector)
    return jax.shard_map(
        functools.partial(per_device, mesh),
        mesh=mesh,
        in_specs=(ends, P("dp")) + params,
        out_specs=(ends,) + params,
        check_vma=False,
    )
```

time: 1140 us -> 662 us (0.58)
  waiting for transfers between devices: 344 us -> 84 us
  Pallas kernels: 506 us -> 352 us
  blocking collectives: 86 us -> 0 us
  starting transfers between devices: 0.94 us -> 52.4 us
  matrix products: 113 us -> 87 us
  local copies, waits for them, and re-layouts: 24.9 us -> 37.8 us
  between operations: 15.8 us -> 3.57 us
    reduce_scatter x4 -> x0, waiting for transfers between devices: 253 us -> none  [per_device(): part = lax.psum_scatter(both, ('section', 'mp'), scatter_dimension=0)]
    pallas_call x10 -> x12, Pallas kernels: 371 us -> 215 us  [the longest x1 74.7 us: start(): pl.pallas_call(functools.partial(start_kernel, mesh, place), out_shape=(j...]
    all_gather x4 -> x0, waiting for transfers between devices: 89 us -> none  [per_device(): full = [lax.all_gather(w, ('section', 'mp'), tiled=True) for w in own]]
    ppermute x0 -> x27, waiting for transfers between devices: none -> 84 us  [permuted(): return lax.ppermute(x, AXES, route)]
    ppermute x0 -> x27, starting transfers between devices: none -> 52.4 us  [permuted(): return lax.ppermute(x, AXES, route)]
    psum x1 -> x0, blocking collectives: 48.1 us -> none  [per_device(): lax.psum(jnp.stack([vectors_zero, vectors_one]), ('section', 'dp', 'mp'))]
    all_gather x1 -> x0, blocking collectives: 32.7 us -> none  [per_device(): lax.all_gather(jnp.concatenate([w[0] for w in (gain_one, bias_one, bias_o...]
    dot_general x0 -> x12, matrix products: none -> 31.2 us  [the longest x2 7.92 us: layer_backward(): jnp.einsum('rse,sd->red', grad_projected, normed, preferred_element_type=...]
  transfers between devices with their start and end apart: 9 -> 27, of which waited for: 6 -> 9; matrix products, arithmetic and copies ran while one was open for 9% -> 11% of each run, Pallas kernels for 16% -> 20%
where the time goes in v2:
time: 662 us; the launch traced here: 653 us
  Pallas kernels  352 us (53%)
  matrix products  87 us (13%)
  waiting for transfers between devices  84 us (13%)
  starting transfers between devices  52.4 us (8%)
  local copies, waits for them, and re-layouts  37.8 us (6%)
  other arithmetic  37 us (6%)
    ppermute x27, waiting for transfers between devices, permuted(): return lax.ppermute(x, AXES, route)  84 us
    pallas_call x1, Pallas kernels, start(): pl.pallas_call(functools.partial(start_kernel, mesh, place), out_shape=(j...  74.7 us
    pallas_call x1, Pallas kernels, finish(): pl.pallas_call(functools.partial(finish_kernel, mesh, place), out_shape=(...  70.1 us
    pallas_call x1, Pallas kernels, joint_backward(): pl.pallas_call(joint_backward_kernel, grid=(pairs, rows // block), out_sh...  67.7 us
    pallas_call x8, Pallas kernels, swapped(): pl.pallas_call(functools.partial(swap_kernel, place), out_shape=jax.Shape...  59.7 us
    ppermute x27, starting transfers between devices, permuted(): return lax.ppermute(x, AXES, route)  52.4 us
    pallas_call x1, Pallas kernels, joint_forward(): pl.pallas_call(functools.partial(joint_forward_kernel, pairs), grid=(rows...  36.8 us
    dot_general x4, matrix products, times_turned(): lax.dot_general(left, weight, (((1,), (1,)), ((), ())), preferred_element...  22 us
  transfers between devices with their start and end apart: 27, of which 9 were waited for; matrix products, arithmetic and copies ran while one was open for 11% of the time, Pallas kernels for 20%

profile of v2, /device:TPU:0, one launch (start us, length us, event | category | flops | bytes accessed | tf_op | source)
XLA Modules:
  0.0 653.4 jit_solution(4406386341874029698)
XLA Ops:
  6.7 74.7 %shard_map.220 = (bf16[2,520,512]{2,1,0:T(8,128)(2,1)}, bf16[4,8,192,512]{3,2,1,0:T(8,128)(2,1)}, bf16[192,512]{1,0:T(8,128)(2,1)}, f32[9,8,512]{2,1,0:T(8,128)}) custom-call(bf16[4,520,512]{2,1,0:T(8,128)(2,1)} %bitcast.253, bf16[8,192,512]{2,1,0:T(8,128)(2,1)} %pad_maximum_fusion.3.w_ref, f32[8,512]{1,0:T(8,128)} %stack.53.vec_ref), custom_call_target="tpu_custom_call" | custom-call | flops 49999998976 | tf_op jit(solution)/shard_map/pallas_call | solution.py:440
  99.6 7.1 %shard_map.222 = bf16[2,1040,768]{2,1,0:T(8,128)(2,1)} custom-call(bf16[2,1040,768]{2,1,0:T(8,128)(2,1)} %fusion.16.x_ref), custom_call_target="tpu_custom_call" | custom-call | flops 5000000000 | tf_op jit(solution)/shard_map/pallas_call | solution.py:504
  106.7 10.3 %shard_map.223 = bf16[2080,256]{1,0:T(8,128)(2,1)} custom-call(s32[1]{0:T(128)} %bitcast.24.length_ref, bf16[2080,768]{1,0:T(8,128)(2,1)} %bitcast.326), custom_call_target="tpu_custom_call" | custom-call | flops 10000000000 | tf_op jit(solution)/shard_map/pallas_call | solution.py:1039
  120.7 8.5 %collective-permute-start.8 = (bf16[4,192,512]{2,1,0:T(8,128)(2,1)}, bf16[4,192,512]{2,1,0:T(8,128)(2,1)S(1)}, u32[]{:S(2)}, u32[]{:S(2)}) collective-permute-start(bf16[4,192,512]{2,1,0:T(8,128)(2,1)} %get-tuple-element.81.a_ref), channel_id=1, source_target_pairs={{0,16},{1,17},{2,18},{3,19},{4,20},{5,21},{6,22},{7,23},{8,24},{9,... | collective-permute-start | bytes 2359304 | tf_op jit(solution)/shard_map/ppermute | solution.py:1176
  140.0 7.5 %collective-permute-done.8.c_ref = bf16[4,192,512]{2,1,0:T(8,128)(2,1)S(1)} collective-permute-done((bf16[4,192,512]{2,1,0:T(8,128)(2,1)}, bf16[4,192,512]{2,1,0:T(8,128)(2,1)S(1)}, u32[]{:S(2)}, u32[]{:S(2)}) %collective-permute-start.8) | collective-permute-done | bytes 786464 | tf_op jit(solution)/shard_map/ppermute | solution.py:1176
  152.4 6.7 %collective-permute-done.7.b_ref = bf16[4,192,512]{2,1,0:T(8,128)(2,1)S(1)} collective-permute-done((bf16[4,192,512]{2,1,0:T(8,128)(2,1)}, bf16[4,192,512]{2,1,0:T(8,128)(2,1)S(1)}, u32[]{:S(2)}, u32[]{:S(2)}) %collective-permute-start.7) | collective-permute-done | bytes 786464 | tf_op jit(solution)/shard_map/ppermute | solution.py:1176
  160.6 14.7 %collective-permute-done.9.d_ref = bf16[4,192,512]{2,1,0:T(8,128)(2,1)S(1)} collective-permute-done((bf16[4,192,512]{2,1,0:T(8,128)(2,1)S(1)}, bf16[4,192,512]{2,1,0:T(8,128)(2,1)S(1)}, u32[]{:S(2)}, u32[]{:S(2)}) %collective-permute-start.9) | collective-permute-done | bytes 786464 | tf_op jit(solution)/shard_map/ppermute | solution.py:1176
  185.9 6.0 shard_map.221
  201.3 7.2 %shard_map.225 = bf16[2,1040,768]{2,1,0:T(8,128)(2,1)} custom-call(bf16[2,1040,768]{2,1,0:T(8,128)(2,1)} %fusion.17.x_ref), custom_call_target="tpu_custom_call" | custom-call | flops 5000000000 | tf_op jit(solution)/shard_map/pallas_call | solution.py:504
  208.6 36.8 %shard_map.226 = (bf16[2080,256]{1,0:T(8,128)(2,1)}, f32[2080,128]{1,0:T(8,128)}) custom-call(s32[1]{0:T(128)} %bitcast.24.length_ref, bf16[2080,768]{1,0:T(8,128)(2,1)} %bitcast.328, bf16[2080,768]{1,0:T(8,128)(2,1)} %bitcast.329), custom_call_target="tpu_custom_call" | custom-call | flops 35999997952 | tf_op jit(solution)/shard_map/pallas_call | solution.py:909
  245.3 15.9 %shard_map.227 = bf16[2,1040,256]{2,1,0:T(8,128)(2,1)} custom-call(bf16[2,1040,256]{2,1,0:T(8,128)(2,1)} %bitcast.337), custom_call_target="tpu_custom_call" | custom-call | flops 5000000000 | tf_op jit(solution)/shard_map/pallas_call | solution.py:504
  266.3 9.1 %convert_reduce_fusion = (f32[2048]{0:T(1024)}, bf16[1040,2048]{1,0:T(8,128)(2,1)S(1)}) fusion(f32[1040,2048]{1,0:T(8,128)S(1)} %convolution_add_fusion, bf16[2048,512]{1,0:T(8,128)(2,1)S(1)} %bitcast.256, bf16[520,512]{1,0:T(8,128)(2,1)S(1)} %get-tuple-element.66, bf16[520,512]{1,0:T(8,128)(2,1)S(1)} %get-tuple-element.65), kind=kOutput, calls=%fused_computation.21 | convolution fusion | flops 2230024192 | bytes 15949824 | tf_op jit(solution)/shard_map/dot_general | solution.py:1097
  296.8 67.7 %shard_map.229 = bf16[2080,768]{1,0:T(8,128)(2,1)} custom-call(s32[1]{0:T(128)} %bitcast.24.length_ref, bf16[2080,768]{1,0:T(8,128)(2,1)} %bitcast.330, bf16[2080,768]{1,0:T(8,128)(2,1)} %bitcast.331, bf16[2080,768]{1,0:T(8,128)(2,1)} %bitcast.332, bf16[2080,256]{1,0:T(8,128)(2,1)} %bitcast.338, bf16[2080,256]{1,0:T(8,128)(2,1)} %get-tuple-element.27.out_ref, ...), custom_call_target="tpu_custom_call" | custom-call | flops 62000001024 | tf_op jit(solution)/shard_map/pallas_call | solution.py:999
  364.5 7.1 %shard_map.230 = bf16[2,1040,768]{2,1,0:T(8,128)(2,1)} custom-call(bf16[2,1040,768]{2,1,0:T(8,128)(2,1)} %bitcast.333), custom_call_target="tpu_custom_call" | custom-call | flops 5000000000 | tf_op jit(solution)/shard_map/pallas_call | solution.py:504
  381.6 7.9 %convert_reduce_fusion.1 = (f32[2048]{0:T(1024)S(1)}, bf16[1040,2048]{1,0:T(8,128)(2,1)S(1)}) fusion(f32[1040,2048]{1,0:T(8,128)S(1)} %bitcast.341, bf16[1040,512]{1,0:T(8,128)(2,1)S(1)} %get-tuple-element.64, bf16[2048,512]{1,0:T(8,128)(2,1)S(1)} %bitcast.261), kind=kOutput, calls=%fused_computation.22 | convolution fusion | flops 2227894272 | bytes 15949824 | tf_op jit(solution)/shard_map/dot_general | solution.py:1097
  415.3 6.3 shard_map.231
  421.7 21.7 %shard_map.232 = bf16[2080,768]{1,0:T(8,128)(2,1)} custom-call(s32[1]{0:T(128)} %bitcast.24.length_ref, bf16[2080,768]{1,0:T(8,128)(2,1)} %bitcast.327, bf16[2080,256]{1,0:T(8,128)(2,1)} %bitcast.339), custom_call_target="tpu_custom_call" | custom-call | flops 22000001024 | tf_op jit(solution)/shard_map/pallas_call | solution.py:1075
  443.4 7.3 %shard_map.233 = bf16[2,1040,768]{2,1,0:T(8,128)(2,1)} custom-call(bf16[2,1040,768]{2,1,0:T(8,128)(2,1)} %bitcast.334), custom_call_target="tpu_custom_call" | custom-call | flops 5000000000 | tf_op jit(solution)/shard_map/pallas_call | solution.py:504
  469.4 6.4 fusion.29
  482.5 9.5 %collective-permute-done.12 = bf16[4,2,144,512]{3,2,0,1:T(8,128)(2,1)S(1)} collective-permute-done((bf16[4,2,144,512]{3,2,0,1:T(8,128)(2,1)S(1)}, bf16[4,2,144,512]{3,2,0,1:T(8,128)(2,1)S(1)}, u32[]{:S(2)}, u32[]{:S(2)}) %collective-permute-start.12) | collective-permute-done | bytes 1179680 | tf_op jit(solution)/shard_map/ppermute | solution.py:1176
  492.9 32.1 %collective-permute-done.18 = bf16[4,2,192,512]{3,2,0,1:T(8,128)(2,1)S(1)} collective-permute-done((bf16[4,2,192,512]{3,2,0,1:T(8,128)(2,1)S(1)}, bf16[4,2,192,512]{3,2,0,1:T(8,128)(2,1)S(1)}, u32[]{:S(2)}, u32[]{:S(2)}) %collective-permute-start.18) | collective-permute-done | bytes 1572896 | tf_op jit(solution)/shard_map/ppermute | solution.py:1176
  537.5 6.9 %collective-permute-done.19 = bf16[4,192,512]{2,1,0:T(8,128)(2,1)S(1)} collective-permute-done((bf16[4,192,512]{2,1,0:T(8,128)(2,1)S(1)}, bf16[4,192,512]{2,1,0:T(8,128)(2,1)S(1)}, u32[]{:S(2)}, u32[]{:S(2)}) %collective-permute-start.19) | collective-permute-done | bytes 786464 | tf_op jit(solution)/shard_map/ppermute | solution.py:1176
  544.3 7.3 %collective-permute-start.16 = (bf16[144,512]{1,0:T(8,128)(2,1)S(1)}, bf16[144,512]{1,0:T(8,128)(2,1)S(1)}, u32[]{:S(2)}, u32[]{:S(2)}) collective-permute-start(bf16[144,512]{1,0:T(8,128)(2,1)S(1)} %get-tuple-element.87), channel_id=1, source_target_pairs={{0,3},{1,0},{2,1},{3,2},{4,7},{5,4},{6,5},{7,6},{8,11},{9,8},{10,9... | collective-permute-start | bytes 442376 | tf_op jit(solution)/shard_map/ppermute | solution.py:1176
  569.8 70.1 %shard_map.234 = (bf16[4,520,512]{2,1,0:T(8,128)(2,1)}, bf16[8,48,512]{2,1,0:T(8,128)(2,1)}, bf16[8,144,512]{2,1,0:T(8,128)(2,1)}, bf16[8,192,512]{2,1,0:T(8,128)(2,1)}, f32[2,10,512]{2,1,0:T(8,128)}) custom-call(bf16[2,520,512]{2,1,0:T(8,128)(2,1)} %bitcast.276, bf16[4,8,48,512]{3,2,1,0:T(8,128)(2,1)} %bitcast.335, ...), custom_call_target="tpu_custom_call" | custom-call | flops 40000000000 | tf_op jit(solution)/shard_map/pallas_call | solution.py:803
  (350 shorter events, 194.9 us)
Async XLA Ops:
  81.4 35.6 %collective-permute-start.4 = (bf16[192,512]{1,0:T(8,128)(2,1)}, bf16[192,512]{1,0:T(8,128)(2,1)S(1)}, u32[]{:S(2)}, u32[]{:S(2)}) collective-permute-start(bf16[192,512]{1,0:T(8,128)(2,1)} %get-tuple-element.23), channel_id=1, source_target_pairs={{0,3},{1,0},{2,1},{3,2},{4,7},{5,4},{6,5},{7,6},{8,11},{9,8},{10,9... | collective-permute-start | bytes 589832 | tf_op jit(solution)/shard_map/ppermute | solution.py:1176
  81.9 36.6 %collective-permute-start.5 = (bf16[192,512]{1,0:T(8,128)(2,1)}, bf16[192,512]{1,0:T(8,128)(2,1)}, u32[]{:S(2)}, u32[]{:S(2)}) collective-permute-start(bf16[192,512]{1,0:T(8,128)(2,1)} %get-tuple-element.23), channel_id=1, source_target_pairs={{0,2},{1,3},{2,0},{3,1},{4,6},{5,7},{6,4},{7,5},{8,10},{9,11},{10,... | collective-permute-start | bytes 589832 | tf_op jit(solution)/shard_map/ppermute | solution.py:1176
  81.9 36.6 %collective-permute-start.6 = (bf16[192,512]{1,0:T(8,128)(2,1)}, bf16[192,512]{1,0:T(8,128)(2,1)}, u32[]{:S(2)}, u32[]{:S(2)}) collective-permute-start(bf16[192,512]{1,0:T(8,128)(2,1)} %get-tuple-element.23), channel_id=1, source_target_pairs={{0,1},{1,2},{2,3},{3,0},{4,5},{5,6},{6,7},{7,4},{8,9},{9,10},{10,1... | collective-permute-start | bytes 589832 | tf_op jit(solution)/shard_map/ppermute | solution.py:1176
  84.9 99.4 %collective-permute-start = (bf16[520,512]{1,0:T(8,128)(2,1)}, bf16[520,512]{1,0:T(8,128)(2,1)}, u32[]{:S(2)}, u32[]{:S(2)}) collective-permute-start(bf16[520,512]{1,0:T(8,128)(2,1)} %get-tuple-element.69), channel_id=1, source_target_pairs={{16,3},{17,1},{18,7},{19,5},{20,19},{21,17},{22,23},{23,21},{24,11... | collective-permute-start | bytes 1597448 | tf_op jit(solution)/shard_map/ppermute | solution.py:1176
  86.4 98.0 %collective-permute-start.1 = (bf16[520,512]{1,0:T(8,128)(2,1)}, bf16[520,512]{1,0:T(8,128)(2,1)}, u32[]{:S(2)}, u32[]{:S(2)}) collective-permute-start(bf16[520,512]{1,0:T(8,128)(2,1)} %get-tuple-element.67), channel_id=1, source_target_pairs={{16,2},{17,0},{18,6},{19,4},{20,18},{21,16},{22,22},{23,20},{24,10... | collective-permute-start | bytes 1597448 | tf_op jit(solution)/shard_map/ppermute | solution.py:1176
  117.1 67.3 %collective-permute-start.2 = (bf16[520,512]{1,0:T(8,128)(2,1)}, bf16[520,512]{1,0:T(8,128)(2,1)}, u32[]{:S(2)}, u32[]{:S(2)}) collective-permute-start(bf16[520,512]{1,0:T(8,128)(2,1)} %get-tuple-element.68), channel_id=1, source_target_pairs={{16,1},{17,3},{18,5},{19,7},{20,17},{21,19},{22,21},{23,23},{24,9}... | collective-permute-start | bytes 1597448 | tf_op jit(solution)/shard_map/ppermute | solution.py:1176
  120.7 26.8 %collective-permute-start.8 = (bf16[4,192,512]{2,1,0:T(8,128)(2,1)}, bf16[4,192,512]{2,1,0:T(8,128)(2,1)S(1)}, u32[]{:S(2)}, u32[]{:S(2)}) collective-permute-start(bf16[4,192,512]{2,1,0:T(8,128)(2,1)} %get-tuple-element.81.a_ref), channel_id=1, source_target_pairs={{0,16},{1,17},{2,18},{3,19},{4,20},{5,21},{6,22},{7,23},{8,24},{9,... | collective-permute-start | bytes 2359304 | tf_op jit(solution)/shard_map/ppermute | solution.py:1176
  138.4 20.6 %collective-permute-start.7 = (bf16[4,192,512]{2,1,0:T(8,128)(2,1)}, bf16[4,192,512]{2,1,0:T(8,128)(2,1)S(1)}, u32[]{:S(2)}, u32[]{:S(2)}) collective-permute-start(bf16[4,192,512]{2,1,0:T(8,128)(2,1)} %get-tuple-element.81.a_ref), channel_id=1, source_target_pairs={{0,8},{1,9},{2,10},{3,11},{4,12},{5,13},{6,14},{7,15},{8,0},{9,1},... | collective-permute-start | bytes 2359304 | tf_op jit(solution)/shard_map/ppermute | solution.py:1176
  147.4 27.9 %collective-permute-start.9 = (bf16[4,192,512]{2,1,0:T(8,128)(2,1)S(1)}, bf16[4,192,512]{2,1,0:T(8,128)(2,1)S(1)}, u32[]{:S(2)}, u32[]{:S(2)}) collective-permute-start(bf16[4,192,512]{2,1,0:T(8,128)(2,1)S(1)} %collective-permute-done.8.c_ref), channel_id=1, source_target_pairs={{0,8},{1,9},{2,10},{3,11},{4,12},{5,13},{6,14},{7,15},{8,0},{9,1},... | collective-permute-start | bytes 2359304 | tf_op jit(solution)/shard_map/ppermute | solution.py:1176
  159.1 25.3 %collective-permute-start.3 = (bf16[520,512]{1,0:T(8,128)(2,1)S(1)}, bf16[520,512]{1,0:T(8,128)(2,1)S(1)}, u32[]{:S(2)}, u32[]{:S(2)}) collective-permute-start(bf16[520,512]{1,0:T(8,128)(2,1)S(1)} %copy-done.28), channel_id=1, source_target_pairs={{16,0},{17,2},{18,4},{19,6},{20,16},{21,18},{22,20},{23,22},{24,8}... | collective-permute-start | bytes 1597448 | tf_op jit(solution)/shard_map/ppermute | solution.py:1176
  410.8 53.9 %collective-permute-start.17 = (bf16[4,2,2,192,512]{4,3,0,2,1:T(8,128)(2,1)}, bf16[4,2,2,192,512]{4,3,0,2,1:T(8,128)(2,1)}, u32[]{:S(2)}, u32[]{:S(2)}) collective-permute-start(bf16[4,2,2,192,512]{4,3,0,2,1:T(8,128)(2,1)} %bitcast.247), channel_id=1, source_target_pairs={{0,4},{1,5},{2,6},{3,7},{4,0},{5,1},{6,2},{7,3},{8,12},{9,13},{10,... | collective-permute-start | bytes 9437192 | tf_op jit(solution)/shard_map/ppermute | solution.py:1176
  415.0 44.8 %collective-permute-start.11 = (bf16[4,2,2,144,512]{4,3,0,2,1:T(8,128)(2,1)}, bf16[4,2,2,144,512]{4,3,0,2,1:T(8,128)(2,1)}, u32[]{:S(2)}, u32[]{:S(2)}) collective-permute-start(bf16[4,2,2,144,512]{4,3,0,2,1:T(8,128)(2,1)} %bitcast.248), channel_id=1, source_target_pairs={{0,4},{1,5},{2,6},{3,7},{4,0},{5,1},{6,2},{7,3},{8,12},{9,13},{10,... | collective-permute-start | bytes 7077896 | tf_op jit(solution)/shard_map/ppermute | solution.py:1176
  463.2 28.9 %collective-permute-start.12 = (bf16[4,2,144,512]{3,2,0,1:T(8,128)(2,1)S(1)}, bf16[4,2,144,512]{3,2,0,1:T(8,128)(2,1)S(1)}, u32[]{:S(2)}, u32[]{:S(2)}) collective-permute-start(bf16[4,2,144,512]{3,2,0,1:T(8,128)(2,1)S(1)} %dynamic-slice_bitcast_fusion.1), channel_id=1, source_target_pairs={{0,8},{1,9},{2,10},{3,11},{4,12},{5,13},{6,14},{7,15},{8,0},{9,1},... | collective-permute-start | bytes 3538952 | tf_op jit(solution)/shard_map/ppermute | solution.py:1176
  467.9 57.0 %collective-permute-start.18 = (bf16[4,2,192,512]{3,2,0,1:T(8,128)(2,1)S(1)}, bf16[4,2,192,512]{3,2,0,1:T(8,128)(2,1)S(1)}, u32[]{:S(2)}, u32[]{:S(2)}) collective-permute-start(bf16[4,2,192,512]{3,2,0,1:T(8,128)(2,1)S(1)} %dynamic-slice_bitcast_fusion), channel_id=1, source_target_pairs={{0,8},{1,9},{2,10},{3,11},{4,12},{5,13},{6,14},{7,15},{8,0},{9,1},... | collective-permute-start | bytes 4718600 | tf_op jit(solution)/shard_map/ppermute | solution.py:1176
  477.2 171.3 %collective-permute-start.23 = (bf16[520,512]{1,0:T(8,128)(2,1)}, bf16[520,512]{1,0:T(8,128)(2,1)}, u32[]{:S(2)}, u32[]{:S(2)}) collective-permute-start(bf16[520,512]{1,0:T(8,128)(2,1)} %get-tuple-element.76), channel_id=1, source_target_pairs={{0,16},{2,17},{4,18},{6,19},{8,24},{10,25},{12,26},{14,27},{16,20}... | collective-permute-start | bytes 1597448 | tf_op jit(solution)/shard_map/ppermute | solution.py:1176
  480.2 168.3 %collective-permute-start.24 = (bf16[520,512]{1,0:T(8,128)(2,1)}, bf16[520,512]{1,0:T(8,128)(2,1)}, u32[]{:S(2)}, u32[]{:S(2)}) collective-permute-start(bf16[520,512]{1,0:T(8,128)(2,1)} %get-tuple-element.75), channel_id=1, source_target_pairs={{1,16},{3,17},{5,18},{7,19},{9,24},{11,25},{13,26},{15,27},{17,20}... | collective-permute-start | bytes 1597448 | tf_op jit(solution)/shard_map/ppermute | solution.py:1176
  492.5 36.9 %collective-permute-start.13 = (bf16[4,144,512]{2,1,0:T(8,128)(2,1)S(1)}, bf16[4,144,512]{2,1,0:T(8,128)(2,1)S(1)}, u32[]{:S(2)}, u32[]{:S(2)}) collective-permute-start(bf16[4,144,512]{2,1,0:T(8,128)(2,1)S(1)} %dynamic-slice_bitcast_fusion.3), channel_id=1, source_target_pairs={{0,16},{1,17},{2,18},{3,19},{4,20},{5,21},{6,22},{7,23},{8,24},{9,... | collective-permute-start | bytes 1769480 | tf_op jit(solution)/shard_map/ppermute | solution.py:1176
  525.5 18.8 %collective-permute-start.19 = (bf16[4,192,512]{2,1,0:T(8,128)(2,1)S(1)}, bf16[4,192,512]{2,1,0:T(8,128)(2,1)S(1)}, u32[]{:S(2)}, u32[]{:S(2)}) collective-permute-start(bf16[4,192,512]{2,1,0:T(8,128)(2,1)S(1)} %dynamic-slice_bitcast_fusion.2), channel_id=1, source_target_pairs={{0,16},{1,17},{2,18},{3,19},{4,20},{5,21},{6,22},{7,23},{8,24},{9,... | collective-permute-start | bytes 2359304 | tf_op jit(solution)/shard_map/ppermute | solution.py:1176
  529.6 22.3 %collective-permute-start.14 = (bf16[144,512]{1,0:T(8,128)(2,1)S(1)}, bf16[144,512]{1,0:T(8,128)(2,1)S(1)}, u32[]{:S(2)}, u32[]{:S(2)}) collective-permute-start(bf16[144,512]{1,0:T(8,128)(2,1)S(1)} %get-tuple-element.86), channel_id=1, source_target_pairs={{0,1},{1,2},{2,3},{3,0},{4,5},{5,6},{6,7},{7,4},{8,9},{9,10},{10,1... | collective-permute-start | bytes 442376 | tf_op jit(solution)/shard_map/ppermute | solution.py:1176
  533.3 18.6 %collective-permute-start.15 = (bf16[144,512]{1,0:T(8,128)(2,1)S(1)}, bf16[144,512]{1,0:T(8,128)(2,1)S(1)}, u32[]{:S(2)}, u32[]{:S(2)}) collective-permute-start(bf16[144,512]{1,0:T(8,128)(2,1)S(1)} %get-tuple-element.88), channel_id=1, source_target_pairs={{0,2},{1,3},{2,0},{3,1},{4,6},{5,7},{6,4},{7,5},{8,10},{9,11},{10,... | collective-permute-start | bytes 442376 | tf_op jit(solution)/shard_map/ppermute | solution.py:1176
  551.9 15.6 %collective-permute-start.21 = (bf16[192,512]{1,0:T(8,128)(2,1)S(1)}, bf16[192,512]{1,0:T(8,128)(2,1)S(1)}, u32[]{:S(2)}, u32[]{:S(2)}) collective-permute-start(bf16[192,512]{1,0:T(8,128)(2,1)S(1)} %get-tuple-element.79), channel_id=1, source_target_pairs={{0,2},{1,3},{2,0},{3,1},{4,6},{5,7},{6,4},{7,5},{8,10},{9,11},{10,... | collective-permute-start | bytes 589832 | tf_op jit(solution)/shard_map/ppermute | solution.py:1176
  555.9 13.1 %collective-permute-start.22 = (bf16[192,512]{1,0:T(8,128)(2,1)S(1)}, bf16[192,512]{1,0:T(8,128)(2,1)S(1)}, u32[]{:S(2)}, u32[]{:S(2)}) collective-permute-start(bf16[192,512]{1,0:T(8,128)(2,1)S(1)} %get-tuple-element.78), channel_id=1, source_target_pairs={{0,3},{1,0},{2,1},{3,2},{4,7},{5,4},{6,5},{7,6},{8,11},{9,8},{10,9... | collective-permute-start | bytes 589832 | tf_op jit(solution)/shard_map/ppermute | solution.py:1176
  561.6 86.8 %collective-permute-start.25 = (bf16[520,512]{1,0:T(8,128)(2,1)}, bf16[520,512]{1,0:T(8,128)(2,1)}, u32[]{:S(2)}, u32[]{:S(2)}) collective-permute-start(bf16[520,512]{1,0:T(8,128)(2,1)} %get-tuple-element.74), channel_id=1, source_target_pairs={{0,17},{2,16},{4,19},{6,18},{8,25},{10,24},{12,27},{14,26},{16,21}... | collective-permute-start | bytes 1597448 | tf_op jit(solution)/shard_map/ppermute | solution.py:1176
  567.5 80.9 %collective-permute-start.26 = (bf16[520,512]{1,0:T(8,128)(2,1)}, bf16[520,512]{1,0:T(8,128)(2,1)}, u32[]{:S(2)}, u32[]{:S(2)}) collective-permute-start(bf16[520,512]{1,0:T(8,128)(2,1)} %get-tuple-element.73), channel_id=1, source_target_pairs={{1,17},{3,16},{5,19},{7,18},{9,25},{11,24},{13,27},{15,26},{17,21}... | collective-permute-start | bytes 1597448 | tf_op jit(solution)/shard_map/ppermute | solution.py:1176
  (89 other events, 1290.1 us)

commit v3 on v2

--- a/solution.py
+++ b/solution.py
@@ -102,6 +102,18 @@
         for step in range(1, self.ranks):
             yield self.mp - step, self.mp >= step
             yield self.mp + step, self.mp + step < self.ranks
+
+    def greet_lines(self):
+        barrier = pltpu.get_barrier_semaphore()
+        for device in (self.other_core(), self.other_side(), self.other_section()):
+            pl.semaphore_signal(barrier, inc=1, device_id=device, device_id_type=MESH)
+        for mp in range(self.ranks):
+
+            @pl.when(self.mp != mp)
+            def _():
+                pl.semaphore_signal(barrier, inc=1, device_id=self.at(mp=mp), device_id_type=MESH)
+
+        pl.semaphore_wait(barrier, 3 + self.ranks - 1)
 
     def greet_all(self):
         barrier = pltpu.get_barrier_semaphore()
@@ -526,68 +538,175 @@
     return swapped(place, x.reshape(place.members, -1, x.shape[1]), collective_id)
 
 
-def finish_kernel(
-    mesh,
-    place,
-    rows_ref,
-    grad_ref,
-    vec_ref,
-    late_ref,
-    second_ref,
-    gone_ref,
-    grad_out_ref,
-    late_out_ref,
-    second_out_ref,
-    vec_out_ref,
-    core_got,
-    side_sent,
-    side_got,
-    section_sent,
-    section_got,
-    line_sent,
-    line_got,
-    piece_ref,
-    vec_sent,
-    vec_got,
-    vec_line,
-    local_sem,
-    row_send,
-    row_recv,
-    core_send,
-    core_recv,
-    side_send,
-    side_recv,
-    section_send,
-    section_recv,
-    line_send,
-    line_recv,
-    piece_send,
-    piece_recv,
-    vec_send,
-    vec_recv,
-    vec_line_send,
-    vec_line_recv,
-):
+def wide(value):
+    return value.astype(F32)
+
+
+class Reduction:
+    FLIPS = ((True, True), (True, False), (False, True), (False, False))
+
+    @staticmethod
+    def scratch(ranks, rows, width):
+        slots = ranks // 2
+        dma = pltpu.SemaphoreType.DMA
+        shapes = (
+            (4, ranks, rows, width),
+            (2, 2, slots, rows, width),
+            (2, 2, slots, rows, width),
+            (2, slots, rows, width),
+            (2, slots, rows, width),
+            (ranks, rows, width),
+            (ranks, rows, width),
+        )
+        sems = (dma((4,)), dma((4,)), dma((2,)), dma((2,)), dma((2,)), dma((2,)), dma((ranks,)), dma((ranks,)))
+        return [pltpu.VMEM(shape, LOW) for shape in shapes] + list(sems)
+
+    COUNT = 15
+
+    def __init__(self, ring, grad_ref, piece_ref, scratch):
+        self.ring, self.grad_ref, self.piece_ref = ring, grad_ref, piece_ref
+        (
+            self.core_got,
+            self.one_sent,
+            self.one_got,
+            self.two_sent,
+            self.two_got,
+            self.line_sent,
+            self.line_got,
+            self.core_send,
+            self.core_recv,
+            self.one_send,
+            self.one_recv,
+            self.two_send,
+            self.two_recv,
+            self.line_send,
+            self.line_recv,
+        ) = scratch
+        self.slots = ring.ranks // 2
+        self.halves = (pl.ds(0, self.slots), pl.ds(self.slots, self.slots))
+
+    def core_copy(self, index):
+        side, section = self.FLIPS[index]
+        return remote(
+            self.grad_ref.at[:, self.ring.column(side, section, True)],
+            self.core_got.at[index],
+            self.core_send.at[index],
+            self.core_recv.at[index],
+            self.ring.other_core(),
+        )
+
+    def one_copy(self, way):
+        device = self.ring.other_side() if way == 0 else self.ring.other_section()
+        return remote(
+            self.one_sent.at[way], self.one_got.at[way], self.one_send.at[way], self.one_recv.at[way], device
+        )
+
+    def two_copy(self, way):
+        device = self.ring.other_section() if way == 0 else self.ring.other_side()
+        return remote(
+            self.two_sent.at[way], self.two_got.at[way], self.two_send.at[way], self.two_recv.at[way], device
+        )
+
+    def line_copy(self, other, mine=None):
+        mine = self.ring.mp if mine is None else mine
+        return remote(
+            self.line_sent.at[other],
+            self.line_got.at[mine],
+            self.line_send.at[other],
+            self.line_recv.at[mine],
+            self.ring.at(mp=other),
+        )
+
+    def along(self, method):
+        for other in range(self.ring.ranks):
+            pl.when(self.ring.mp != other)(functools.partial(method, other))
+
+    def own(self, index, half):
+        side, section = self.FLIPS[index]
+        slots = self.halves[half]
+        return wide(self.grad_ref[slots, self.ring.column(side, section)]) + wide(
+            self.core_got[index, slots]
+        )
+
+    def phase(self, number):
+        if number == 0:
+            for index in range(4):
+                self.core_copy(index).start()
+        elif number == 1:
+            for index in range(4):
+                self.core_copy(index).wait_recv()
+            for way, index in ((0, 1), (1, 2)):
+                self.one_sent[way, 0] = self.own(index, way).astype(LOW)
+                self.one_sent[way, 1] = self.own(0, way).astype(LOW)
+                self.one_copy(way).start()
+        elif number == 2:
+            for way, index in ((0, 2), (1, 1)):
+                self.one_copy(way).wait_recv()
+                self.two_sent[way] = (self.own(index, way) + wide(self.one_got[way, 1])).astype(LOW)
+                self.two_copy(way).start()
+        elif number == 3:
+            for way in range(2):
+                self.two_copy(way).wait_recv()
+                whole = self.own(3, way) + wide(self.one_got[way, 0]) + wide(self.two_got[way])
+                self.line_sent[self.halves[way]] = whole.astype(LOW)
+            self.along(lambda other: self.line_copy(other).start())
+            self.line_got[self.ring.mp] = self.line_sent[self.ring.mp]
+        elif number == 4:
+            self.along(lambda other: self.line_copy(other, other).wait_recv())
+            total = wide(self.line_got[0])
+            for other in range(1, self.ring.ranks):
+                total = total + wide(self.line_got[other])
+            self.piece_ref[...] = total.astype(LOW)
+        else:
+            for index in range(4):
+                self.core_copy(index).wait_send()
+            for way in range(2):
+                self.one_copy(way).wait_send()
+                self.two_copy(way).wait_send()
+            self.along(lambda other: self.line_copy(other).wait_send())
+
+
+def reductions_of(ring, grad_refs, piece_refs, scratch):
+    count = Reduction.COUNT
+    return [
+        Reduction(ring, grad_ref, piece_ref, scratch[i * count : (i + 1) * count])
+        for i, (grad_ref, piece_ref) in enumerate(zip(grad_refs, piece_refs))
+    ]
+
+
+def reduction_scratch(grads):
+    found = []
+    for grad in grads:
+        found += Reduction.scratch(grad.shape[0], *grad.shape[2:])
+    return found
+
+
+def piece_shapes(grads):
+    return tuple(jax.ShapeDtypeStruct(grad.shape[2:], LOW) for grad in grads)
+
+
+def finish_kernel(mesh, place, count, *refs):
+    rows_ref, vec_ref = refs[:2]
+    grad_refs, second_refs = refs[2 : 2 + count], refs[2 + count : 2 + 2 * count]
+    at = 2 + 2 * count
+    gone_ref, vec_out_ref = refs[at : at + 2]
+    out_refs = refs[at + 2 : at + 2 + count]
+    at += 2 + count
+    (vec_sent, vec_got, vec_line, local_sem, row_send, row_recv) = refs[at : at + 6]
+    (piece_send, piece_recv, vec_send, vec_recv, vec_line_send, vec_line_recv) = refs[at + 6 : at + 12]
+    at += 12
+    piece_refs, scratch = refs[at : at + count], refs[at + count :]
     ring = Ring(mesh)
     ranks, items = ring.ranks, place.items
     section, mp = ring.section, ring.mp
+    reductions = reductions_of(ring, grad_refs, piece_refs, scratch)
     ring.greet_all()
 
-    flips = ((True, False), (True, True), (False, True), (False, False))
-
-    def core_copy(index):
-        side, other = flips[index]
-        return remote(
-            grad_ref.at[:, ring.column(side, other, True)],
-            core_got.at[index],
-            core_send.at[index],
-            core_recv.at[index],
-            ring.other_core(),
-        )
-
-    for index in range(4):
-        core_copy(index).start()
-
+    def every(number):
+        for reduction in reductions:
+            reduction.phase(number)
+
+    every(0)
     partners = (ring.other_core(), ring.other_side(), ring.other_section())
 
     def vec_copy(step):
@@ -615,95 +734,46 @@
     def own_row(index):
         return pltpu.make_async_copy(rows_ref.at[index], gone_ref.at[slot], local_sem)
 
+    def piece_copy(layer, which, near):
+        device = (layer, ring.base + near, mp)
+        return remote(
+            (piece_refs, second_refs)[layer][which],
+            out_refs[which].at[ring.column()],
+            piece_send.at[layer, which, near],
+            piece_recv.at[which, ring.column()],
+            device,
+        )
+
+    def to_keepers(layer, which, method):
+        for near in range(4):
+            mine = (section == layer) & (ring.dp == ring.base + near)
+            pl.when(jnp.logical_not(mine))(
+                lambda near=near: method(piece_copy(layer, which, near))
+            )
+
+    def keep(layer, which):
+        def store():
+            out_refs[which][ring.column()] = (piece_refs, second_refs)[layer][which][...]
+
+        pl.when(section == layer)(store)
+
+    every(1)
     for index in range(2):
         pl.when(jnp.logical_not(place.is_here(targets[index])))(
             lambda index=index: row_copy(index).start()
         )
         pl.when(place.is_here(targets[index]))(lambda index=index: own_row(index).start())
-
-    def piece_copy(which, near):
-        source, target, section_to = (
-            (piece_ref, grad_out_ref, 0),
-            (late_ref, late_out_ref, 0),
-            (second_ref, second_out_ref, 1),
-        )[which]
-        device = (section_to, ring.base + near, mp)
-        return remote(
-            source,
-            target.at[ring.column()],
-            piece_send.at[which, near],
-            piece_recv.at[which, ring.column()],
-            device,
-        )
-
-    def to_keepers(which, method):
-        for near in range(4):
-            mine = (section == (1 if which == 2 else 0)) & (ring.dp == ring.base + near)
-            pl.when(jnp.logical_not(mine))(lambda near=near: method(piece_copy(which, near)))
-
-    to_keepers(1, lambda copy: copy.start())
-    to_keepers(2, lambda copy: copy.start())
-
-    @pl.when(section == 0)
-    def _():
-        late_out_ref[ring.column()] = late_ref[...]
-
-    @pl.when(section == 1)
-    def _():
-        second_out_ref[ring.column()] = second_ref[...]
-
-    def side_copy(index):
-        return remote(
-            side_sent.at[index],
-            side_got.at[index],
-            side_send.at[index],
-            side_recv.at[index],
-            ring.other_side(),
-        )
-
-    def wide(value):
-        return value.astype(F32)
-
-    for index in range(2):
-        side, other = flips[index]
-        core_copy(index).wait_recv()
-        kept = grad_ref[:, ring.column(side, other)]
-        side_sent[index] = (wide(kept) + wide(core_got[index])).astype(LOW)
-        side_copy(index).start()
-
+    for which in range(count):
+        to_keepers(1, which, lambda copy: copy.start())
+        keep(1, which)
     vec_copy(0).wait_recv()
     vec_sent[1] = vec_sent[0] + vec_got[0]
     vec_copy(1).start()
-
-    core_copy(2).wait_recv()
-    side_copy(1).wait_recv()
-    kept = grad_ref[:, ring.column(False, True)]
-    section_sent[...] = (wide(kept) + wide(core_got[2]) + wide(side_got[1])).astype(LOW)
-    section_copy = remote(
-        section_sent, section_got, section_send, section_recv, ring.other_section()
-    )
-    section_copy.start()
+    every(2)
     vec_copy(1).wait_recv()
     vec_sent[2] = vec_sent[1] + vec_got[1]
     vec_copy(2).start()
-    core_copy(3).wait_recv()
-    side_copy(0).wait_recv()
-    section_copy.wait_recv()
-    kept = grad_ref[:, ring.column()]
-    whole = wide(kept) + wide(core_got[3]) + wide(side_got[0]) + wide(section_got[...])
-    line_sent[...] = whole.astype(LOW)
-
-    def along(other, method):
-        pl.when(mp != other)(lambda: method(other))
-
-    def line_copy(other, mine=None):
-        return remote(
-            line_sent.at[other],
-            line_got.at[mp if mine is None else mine],
-            line_send.at[other],
-            line_recv.at[mp if mine is None else mine],
-            ring.at(mp=other),
-        )
+    every(3)
 
     def vec_line_copy(other, mine=None):
         return remote(
@@ -714,32 +784,19 @@
             ring.at(mp=other),
         )
 
-    for other in range(ranks):
-        along(other, lambda other: line_copy(other).start())
+    def along(method):
+        for other in range(ranks):
+            pl.when(mp != other)(functools.partial(method, other))
+
     vec_copy(2).wait_recv()
     vec_line[ranks] = vec_sent[2] + vec_got[2]
-    for other in range(ranks):
-        along(other, lambda other: vec_line_copy(other).start())
-
-    @pl.when(mp >= 0)
-    def _():
-        line_got[mp] = line_sent[mp]
-        vec_line[mp] = vec_line[ranks]
-
-    for other in range(ranks):
-        along(other, lambda other: line_copy(other, other).wait_recv())
-    total = wide(line_got[0])
-    for other in range(1, ranks):
-        total = total + wide(line_got[other])
-    piece_ref[...] = total.astype(LOW)
-    to_keepers(0, lambda copy: copy.start())
-
-    @pl.when(section == 0)
-    def _():
-        grad_out_ref[ring.column()] = piece_ref[...]
-
-    for other in range(ranks):
-        along(other, lambda other: vec_line_copy(other, other).wait_recv())
+    along(lambda other: vec_line_copy(other).start())
+    vec_line[mp] = vec_line[ranks]
+    for which, reduction in enumerate(reductions):
+        reduction.phase(4)
+        to_keepers(0, which, lambda copy: copy.start())
+        keep(0, which)
+    along(lambda other: vec_line_copy(other, other).wait_recv())
     total = vec_line[0]
     for other in range(1, ranks):
         total = total + vec_line[other]
@@ -759,93 +816,59 @@
         )
 
     def piece_arrival(which, column):
-        source, target = (
-            (piece_ref, grad_out_ref),
-            (late_ref, late_out_ref),
-            (second_ref, second_out_ref),
-        )[which]
-        return remote(
-            source,
-            target.at[column],
-            piece_send.at[which, 0],
+        remote(
+            piece_refs[which],
+            out_refs[which].at[column],
+            piece_send.at[0, which, 0],
             piece_recv.at[which, column],
             ring.other_core(),
-        )
-
-    for which in range(3):
+        ).wait_recv()
+
+    for which in range(count):
         for column in range(8):
-            keeper = section == (1 if which == 2 else 0)
-            pl.when(keeper & (ring.column() != column))(
-                lambda which=which, column=column: piece_arrival(which, column).wait_recv()
-            )
-        to_keepers(which, lambda copy: copy.wait_send())
-    for index in range(4):
-        core_copy(index).wait_send()
-    for index in range(2):
-        side_copy(index).wait_send()
-    section_copy.wait_send()
+            pl.when(ring.column() != column)(functools.partial(piece_arrival, which, column))
+        for layer in range(2):
+            to_keepers(layer, which, lambda copy: copy.wait_send())
+    every(5)
     for step in range(3):
         vec_copy(step).wait_send()
-    for other in range(ranks):
-        along(other, lambda other: line_copy(other).wait_send())
-        along(other, lambda other: vec_line_copy(other).wait_send())
-
-
-def finish(mesh, place, rows, grads, vecs, late, second):
-    ranks, items = place.ranks, place.items
+    along(lambda other: vec_line_copy(other).wait_send())
+
+
+def finish(mesh, place, rows, vecs, grads, seconds):
+    ranks, items, count = place.ranks, place.items, len(grads)
     held = pl.BlockSpec(memory_space=pltpu.VMEM)
     dma = pltpu.SemaphoreType.DMA
-    column = (ranks,) + grads.shape[2:]
-
-    def like(lead, x):
-        return jax.ShapeDtypeStruct(lead + x.shape, x.dtype)
-
     return pl.pallas_call(
-        functools.partial(finish_kernel, mesh, place),
+        functools.partial(finish_kernel, mesh, place, count),
         out_shape=(
             jax.ShapeDtypeStruct((items,) + rows.shape[1:], rows.dtype),
-            jax.ShapeDtypeStruct((8,) + grads.shape[2:], LOW),
-            like((8,), late),
-            like((8,), second),
             jax.ShapeDtypeStruct(vecs.shape, F32),
-        ),
-        in_specs=[held] * 5,
-        out_specs=(held,) * 5,
+        )
+        + tuple(jax.ShapeDtypeStruct(grad.shape[1:], LOW) for grad in grads),
+        in_specs=[held] * (2 + 2 * count),
+        out_specs=(held,) * (2 + count),
         scratch_shapes=[
-            pltpu.VMEM((4,) + column, LOW),
-            pltpu.VMEM((2,) + column, LOW),
-            pltpu.VMEM((2,) + column, LOW),
-            pltpu.VMEM(column, LOW),
-            pltpu.VMEM(column, LOW),
-            pltpu.VMEM(column, LOW),
-            pltpu.VMEM(column, LOW),
-            pltpu.VMEM(column[1:], LOW),
             pltpu.VMEM((3,) + vecs.shape, F32),
             pltpu.VMEM((3,) + vecs.shape, F32),
             pltpu.VMEM((ranks + 1,) + vecs.shape, F32),
             dma,
             dma((2,)),
             dma((items,)),
-            dma((4,)),
-            dma((4,)),
-            dma((2,)),
-            dma((2,)),
-            dma,
-            dma,
-            dma((ranks,)),
-            dma((ranks,)),
-            dma((3, 4)),
-            dma((3, 8)),
+            dma((2, count, 4)),
+            dma((count, 8)),
             dma((3,)),
             dma((3,)),
             dma((ranks,)),
             dma((ranks,)),
-        ],
+        ]
+        + [pltpu.VMEM(grad.shape[2:], LOW) for grad in grads]
+        + reduction_scratch(grads),
         cost_estimate=cost(40),
         compiler_params=pltpu.CompilerParams(
             collective_id=1, has_side_effects=True, vmem_limit_bytes=VMEM_BYTES
         ),
-    )(rows, grads, vecs, late, second)
+    )(rows, vecs, *grads, *seconds)
 
 
 def dot_rows(left, right):
@@ -950,9 +973,24 @@
 
 
 def joint_backward_kernel(
-    length_ref, q_ref, k_ref, v_ref, grad_ref, out_ref, log_ref, o_ref, total_ref, stat_ref
+    mesh, count, length_ref, q_ref, k_ref, v_ref, grad_ref, out_ref, log_ref, *refs
 ):
+    matrix_refs, o_ref = refs[:count], refs[count]
+    piece_refs = refs[count + 1 : 2 * count + 1]
+    total_ref, stat_ref = refs[2 * count + 1 : 2 * count + 3]
     pair, step = pl.program_id(0), pl.program_id(1)
+    steps = pl.num_programs(1)
+    ring = Ring(mesh)
+    reductions = reductions_of(ring, matrix_refs, piece_refs, refs[2 * count + 3 :])
+    whole_step = pair * steps + step
+    pl.when(whole_step == 0)(ring.greet_lines)
+    for number, when in enumerate(REDUCTION_STEPS):
+
+        @pl.when(whole_step == when)
+        def _():
+            for reduction in reductions:
+                reduction.phase(number)
+
     block = k_ref.shape[0]
     limit = PATCH_ROWS + length_ref[0] - step * block
     q = q_ref[...] * jnp.asarray(0.125, LOW)
@@ -992,14 +1030,17 @@
         o_ref[:, 0:PAIR] = (total_ref[...].T * 0.125).astype(LOW)
 
 
-def joint_backward(qkv, length, grad, out, log):
+REDUCTION_STEPS = (0, 3, 8, 11, 16, 19)
+
+
+def joint_backward(mesh, qkv, length, grad, out, log, matrices):
     rows, width = qkv.shape
     pairs = width // (3 * PAIR)
     block = 208
     return pl.pallas_call(
-        joint_backward_kernel,
+        functools.partial(joint_backward_kernel, mesh, len(matrices)),
         grid=(pairs, rows // block),
-        out_shape=jax.ShapeDtypeStruct((rows, width), LOW),
+        out_shape=(jax.ShapeDtypeStruct((rows, width), LOW),) + piece_shapes(matrices),
         in_specs=[
             pl.BlockSpec(memory_space=pltpu.SMEM),
             pl.BlockSpec((rows, PAIR), lambda p, i: (0, 3 * p)),
@@ -1008,12 +1049,21 @@
             pl.BlockSpec((rows, PAIR), lambda p, i: (0, p)),
             pl.BlockSpec((rows, PAIR), lambda p, i: (0, p)),
             pl.BlockSpec((rows, 128), lambda p, i: (0, 0)),
-        ],
-        out_specs=pl.BlockSpec((rows, 3 * PAIR), lambda p, i: (0, p)),
-        scratch_shapes=[pltpu.VMEM((PAIR, rows), F32), pltpu.VMEM((2, 8, rows), F32)],
+        ]
+        + [whole_block(m.shape) for m in matrices],
+        out_specs=(pl.BlockSpec((rows, 3 * PAIR), lambda p, i: (0, p)),)
+        + tuple(whole_block(m.shape[2:]) for m in matrices),
+        scratch_shapes=[pltpu.VMEM((PAIR, rows), F32), pltpu.VMEM((2, 8, rows), F32)]
+        + reduction_scratch(matrices),
         cost_estimate=cost(62),
-        compiler_params=pltpu.CompilerParams(vmem_limit_bytes=VMEM_BYTES),
-    )(length, qkv, qkv, qkv, grad, out, log)
+        compiler_params=pltpu.CompilerParams(
+            collective_id=6, has_side_effects=True, vmem_limit_bytes=VMEM_BYTES
+        ),
+    )(length, qkv, qkv, qkv, grad, out, log, *matrices)
+
+
+def whole_block(shape):
+    return pl.BlockSpec(shape, lambda *_: (0,) * len(shape))
 
 
 def within_forward_kernel(pairs, length_ref, x_ref, o_ref):
@@ -1049,7 +1099,15 @@
     )(length, qkv)
 
 
-def within_backward_kernel(pairs, length_ref, x_ref, grad_ref, o_ref):
+def within_backward_kernel(mesh, pairs, count, length_ref, x_ref, grad_ref, *refs):
+    matrix_refs, o_ref = refs[:count], refs[count]
+    ring = Ring(mesh)
+    reductions = reductions_of(ring, matrix_refs, refs[count + 1 : 2 * count + 1], refs[2 * count + 1 :])
+
+    def every(number):
+        for reduction in reductions:
+            reduction.phase(number)
+
     def group(rows, limit):
         for pair in range(pairs):
             base = pair * 3 * PAIR
@@ -1062,28 +1120,34 @@
             o_ref[rows, base + PAIR : base + 2 * PAIR] = joined(both[0][1], both[1][1]).astype(LOW)
             o_ref[rows, base + 2 * PAIR : base + 3 * PAIR] = joined(both[0][2], both[1][2]).astype(LOW)
 
+    ring.greet_lines()
+    every(0)
+
     @pl.loop(0, VIEWS)
     def _(view):
         group(pl.ds(pl.multiple_of(view * PATCH, 16), PATCH), None)
+        for number in range(1, 5):
+            pl.when(view == number)(functools.partial(every, number))
 
     group(pl.ds(PATCH_ROWS, TEXT), length_ref[0])
-
-
-def within_backward(qkv, length, grad):
+    every(5)
+
+
+def within_backward(mesh, qkv, length, grad, matrices):
     rows, width = qkv.shape
     pairs = width // (3 * PAIR)
+    held = pl.BlockSpec(memory_space=pltpu.VMEM)
     return pl.pallas_call(
-        functools.partial(within_backward_kernel, pairs),
-        out_shape=jax.ShapeDtypeStruct((rows, width), LOW),
-        in_specs=[
-            pl.BlockSpec(memory_space=pltpu.SMEM),
-            pl.BlockSpec(memory_space=pltpu.VMEM),
-            pl.BlockSpec(memory_space=pltpu.VMEM),
-        ],
-        out_specs=pl.BlockSpec(memory_space=pltpu.VMEM),
+        functools.partial(within_backward_kernel, mesh, pairs, len(matrices)),
+        out_shape=(jax.ShapeDtypeStruct((rows, width), LOW),) + piece_shapes(matrices),
+        in_specs=[pl.BlockSpec(memory_space=pltpu.SMEM)] + [held] * (2 + len(matrices)),
+        out_specs=(held,) * (1 + len(matrices)),
+        scratch_shapes=reduction_scratch(matrices),
         cost_estimate=cost(22),
-        compiler_params=pltpu.CompilerParams(vmem_limit_bytes=VMEM_BYTES),
-    )(length, qkv, grad)
+        compiler_params=pltpu.CompilerParams(
+            collective_id=7, has_side_effects=True, vmem_limit_bytes=VMEM_BYTES
+        ),
+    )(length, qkv, grad, *matrices)
 
 
 def layer_norm(values, scale_vec, shift_vec):
@@ -1123,7 +1187,7 @@
     return result, (source, normed, qkv, mixed_heads, logs, mixed, middle, second, hidden_pre, hidden)
 
 
-def layer_backward(place, upstream, length, params, kept, within):
+def layer_backward(mesh, place, upstream, length, params, kept, pack, waiting):
     source, normed, qkv, mixed_heads, logs, mixed, middle, second, hidden_pre, hidden = kept
     up_low = upstream.astype(LOW)
     grad_down = over_rows(hidden, up_low)
@@ -1139,16 +1203,18 @@
     grad_out = jnp.einsum("rse,sd->red", mixed, mid_low, preferred_element_type=F32)
     grad_mixed = jnp.einsum("sd,red->rse", mid_low, params["out"], preferred_element_type=F32)
     grad_heads = to_heads(place, grad_mixed.astype(LOW), 4)
-    if within:
-        grad_qkv_heads = within_backward(qkv, length, grad_heads)
+    later = [pack(m) for m in (grad_out, grad_up, grad_down)]
+    if waiting is None:
+        grad_qkv_heads, *done = joint_backward(
+            mesh, qkv, length, grad_heads, mixed_heads, logs, later
+        )
     else:
-        grad_qkv_heads = joint_backward(qkv, length, grad_heads, mixed_heads, logs)
+        grad_qkv_heads, *done = within_backward(mesh, qkv, length, grad_heads, waiting)
     grad_projected = to_rows(place, grad_qkv_heads, 5)
     grad_qkv = jnp.einsum("rse,sd->red", grad_projected, normed, preferred_element_type=F32)
     grad_normed = jnp.einsum("rse,red->sd", grad_projected, params["qkv"], preferred_element_type=F32)
     first_pull = jax.vjp(layer_norm, source, params["gain_one"], params["bias_one"])[1]
     part_source, grad_gain_one, grad_bias_one = first_pull(grad_normed)
-    matrices = (grad_qkv, grad_out, grad_up, grad_down)
     vectors = (
         grad_gain_one,
         grad_bias_one,
@@ -1158,7 +1224,7 @@
         jnp.sum(upstream, 0),
         grad_up_bias,
     )
-    return grad_middle + part_source, matrices, jnp.concatenate(vectors)
+    return grad_middle + part_source, grad_qkv, later, done, jnp.concatenate(vectors)
 
 
 AXES = ("section", "dp", "mp")
@@ -1278,14 +1344,6 @@
     for other in range(1, len(choices)):
         found = jnp.where(index == other, choices[other], found)
     return found
-
-
-def scattered_line(mesh, pieces):
-    ranks, mp = mesh.shape["mp"], lax.axis_index("mp")
-    total = pick(pieces, mp, 0).astype(F32)
-    for turn in range(1, ranks):
-        total = total + turned(mesh, pick(pieces, (mp + turn) % ranks, 0), turn).astype(F32)
-    return total.astype(LOW)
 
 
 def assemble_kernel(mesh, a_ref, b_ref, c_ref, d_ref, e_ref, o_ref, sems):
@@ -1325,25 +1383,6 @@
     )(own, side, section, both, core)
 
 
-def reduce_all(mesh, grads):
-    section, dp = lax.axis_index("section"), lax.axis_index("dp")
-    core, side = dp % 2, (dp // 2) % 2
-
-    def halved(x, bit, axis, across):
-        kept, sent = pick(x, bit, axis), pick(x, 1 - bit, axis)
-        return (kept.astype(F32) + across(mesh, sent).astype(F32)).astype(LOW)
-
-    x = grads.reshape((grads.shape[0], 2, 2, 2) + grads.shape[2:])
-    x = halved(x, core, 3, across_core)
-    x = halved(x, side, 1, across_side)
-    x = halved(x, section, 1, across_section)
-    x = scattered_line(mesh, x)
-    dps = mesh.shape["dp"]
-    if dps > 4:
-        x = lax.psum(x, "dp", axis_index_groups=far_groups(dps))
-    return x
-
-
 def far_groups(dps):
     return [[low + 4 * high for high in range(dps // 4)] for low in range(4)]
 
@@ -1394,11 +1433,12 @@
         found["out"] = found["out"].reshape(place.members, -1, width)
         return found
 
-    def packed_grads(matrices):
-        grad_qkv = matrices[0].astype(LOW)
-        grad_qkv = grad_qkv.reshape(all_heads // 2, 3, per_pair, heads_here, HEAD, width)
-        found = [grad_qkv.swapaxes(1, 2)] + [m.astype(LOW) for m in matrices[1:]]
-        return [m.reshape(ranks, 8, -1, width) for m in found]
+    def pack(grad):
+        return grad.astype(LOW).reshape(ranks, 8, -1, width)
+
+    def pack_qkv(grad):
+        grad = grad.astype(LOW).reshape(all_heads // 2, 3, per_pair, heads_here, HEAD, width)
+        return pack(grad.swapaxes(1, 2))
 
     params = (params_of(0, first), params_of(1, second))
     source = arrived.reshape(-1, width).astype(F32)
@@ -1408,31 +1448,25 @@
     )
     results = return_results(mesh, place, result.astype(LOW).reshape(2, block_rows, width))
     upstream = cotangent.reshape(-1, width).astype(F32)
-    grad_boundary, matrices, vectors_one = layer_backward(
-        place, upstream, length, params[1], kept_one, False
+    grad_boundary, grad_qkv_one, _, done, vectors_one = layer_backward(
+        mesh, place, upstream, length, params[1], kept_one, pack, None
     )
-    reduced_one = reduce_all(mesh, jnp.concatenate(packed_grads(matrices), 2))
-    grad_source, matrices, vectors_zero = layer_backward(
-        place, grad_boundary.astype(LOW).astype(F32), length, params[0], kept_zero, True
+    upstream = grad_boundary.astype(LOW).astype(F32)
+    grad_source, grad_qkv_zero, later, done_qkv, vectors_zero = layer_backward(
+        mesh, place, upstream, length, params[0], kept_zero, pack, [pack_qkv(grad_qkv_one)]
     )
-    grads_zero = packed_grads(matrices)
-    late = reduce_all(mesh, jnp.concatenate(grads_zero[1:], 2))
     rows = grad_source.astype(LOW).reshape(2, block_rows, width)
     vectors = jnp.stack([vectors_zero, vectors_one]).reshape(2, -1, width)
-    gone, first, late, second, sums = finish(
-        mesh, place, rows, grads_zero[0], vectors, late, reduced_one
-    )
-    if mesh.shape["dp"] > 4:
-        far = far_groups(mesh.shape["dp"])
-        sums = lax.psum(sums, "dp", axis_index_groups=far)
-        first = lax.psum(first, "dp", axis_index_groups=far)
+    grads = [pack_qkv(grad_qkv_zero)] + later
+    gone, sums, *matrices = finish(mesh, place, rows, vectors, grads, done_qkv + done)
+    dps = mesh.shape["dp"]
+    if dps > 4:
+        sums, *matrices = (
+            lax.psum(m, "dp", axis_index_groups=far_groups(dps)) for m in (sums, *matrices)
+        )
 
     ends = ends_of(gone, results)[None]
-    total = jnp.where(section == 0, jnp.concatenate([first, late], 1), second)
-    parts, at = [], 0
-    for cut in cuts:
-        parts.append(total[:, at : at + cut].reshape(-1, width).astype(F32))
-        at += cut
+    parts = [m.reshape(-1, width).astype(F32) for m in matrices]
     sums = pick(sums, section, 0).reshape(-1)
     small = [sums[i * width : (i + 1) * width][None] for i in range(6)]
     grad_bias_up = lax.dynamic_slice_in_dim(sums, 6 * width + mp * hidden_here, hidden_here)[None]

time: 662 us -> 590 us (0.89)
  waiting for transfers between devices: 84 us -> 29 us
  starting transfers between devices: 52.4 us -> 30.3 us
  Pallas kernels: 352 us -> 373 us
  local copies, waits for them, and re-layouts: 37.8 us -> 24 us
  other arithmetic: 37 us -> 27.4 us
  matrix products: 87 us -> 94.2 us
    ppermute x27 -> x15, waiting for transfers between devices: 84 us -> 29 us  [permuted(): return lax.ppermute(x, AXES, route)]
    pallas_call x3, Pallas kernels: 160 us -> 195 us  [the longest x1 84.7 us: finish(): pl.pallas_call(functools.partial(finish_kernel, mesh, place, count), out_...]
    ppermute x27 -> x15, starting transfers between devices: 52.4 us -> 30.3 us  [permuted(): return lax.ppermute(x, AXES, route)]
    pallas_call x8, Pallas kernels: 59.7 us -> 45.8 us  [swapped(): pl.pallas_call(functools.partial(swap_kernel, place), out_shape=jax.Shape...]
    convert_element_type x10 -> x2, other arithmetic: 10.8 us -> 2.87 us  [per_device(): parts = [m.reshape(-1, width).astype(F32) for m in matrices]]
    unnamed x184 -> x182, local copies, waits for them, and re-layouts: 8.12 us -> 1.23 us
  transfers between devices with their start and end apart: 27 -> 15, of which waited for: 9 -> 3; matrix products, arithmetic and copies ran while one was open for 11% -> 7% of each run, Pallas kernels for 20% -> 18%
where the time goes in v3:
time: 590 us; the launch traced here: 581 us
  Pallas kernels  373 us (63%)
  matrix products  94.2 us (16%)
  starting transfers between devices  30.3 us (5%)
  waiting for transfers between devices  29 us (5%)
  other arithmetic  27.4 us (5%)
  local copies, waits for them, and re-layouts  24 us (4%)
    pallas_call x1, Pallas kernels, finish(): pl.pallas_call(functools.partial(finish_kernel, mesh, place, count), out_...  84.7 us
    pallas_call x1, Pallas kernels, joint_backward(): pl.pallas_call(functools.partial(joint_backward_kernel, mesh, len(matrice...  80.6 us
    pallas_call x1, Pallas kernels, start(): pl.pallas_call(functools.partial(start_kernel, mesh, place), out_shape=(j...  74.8 us
    pallas_call x8, Pallas kernels, swapped(): pl.pallas_call(functools.partial(swap_kernel, place), out_shape=jax.Shape...  45.8 us
    pallas_call x1, Pallas kernels, joint_forward(): pl.pallas_call(functools.partial(joint_forward_kernel, pairs), grid=(rows...  36.8 us
    ppermute x15, starting transfers between devices, permuted(): return lax.ppermute(x, AXES, route)  30.3 us
    pallas_call x1, Pallas kernels, within_backward(): pl.pallas_call(functools.partial(within_backward_kernel, mesh, pairs, len...  29.5 us
    ppermute x15, waiting for transfers between devices, permuted(): return lax.ppermute(x, AXES, route)  29 us
  transfers between devices with their start and end apart: 15, of which 3 were waited for; matrix products, arithmetic and copies ran while one was open for 7% of the time, Pallas kernels for 18%

profile of v3, /device:TPU:0, one launch (start us, length us, event | category | flops | bytes accessed | tf_op | source)
XLA Modules:
  0.0 581.4 jit_solution(16185480916910255422)
XLA Ops:
  6.7 74.8 %shard_map.220 = (bf16[2,520,512]{2,1,0:T(8,128)(2,1)}, bf16[4,8,192,512]{3,2,1,0:T(8,128)(2,1)}, bf16[192,512]{1,0:T(8,128)(2,1)}, f32[9,8,512]{2,1,0:T(8,128)}) custom-call(bf16[4,520,512]{2,1,0:T(8,128)(2,1)} %bitcast.198, bf16[8,192,512]{2,1,0:T(8,128)(2,1)} %pad_maximum_fusion.1.w_ref, f32[8,512]{1,0:T(8,128)} %stack.53.vec_ref), custom_call_target="tpu_custom_call" | custom-call | flops 49999998976 | tf_op jit(solution)/shard_map/pallas_call | solution.py:452
  99.2 7.0 %shard_map.222 = bf16[2,1040,768]{2,1,0:T(8,128)(2,1)} custom-call(bf16[2,1040,768]{2,1,0:T(8,128)(2,1)} %fusion.14.x_ref), custom_call_target="tpu_custom_call" | custom-call | flops 5000000000 | tf_op jit(solution)/shard_map/pallas_call | solution.py:516
  106.2 10.3 %shard_map.223 = bf16[2080,256]{1,0:T(8,128)(2,1)} custom-call(s32[1]{0:T(128)} %bitcast.24.length_ref, bf16[2080,768]{1,0:T(8,128)(2,1)} %bitcast.265), custom_call_target="tpu_custom_call" | custom-call | flops 10000000000 | tf_op jit(solution)/shard_map/pallas_call | solution.py:1089
  119.2 8.5 %collective-permute-start.8 = (bf16[4,192,512]{2,1,0:T(8,128)(2,1)}, bf16[4,192,512]{2,1,0:T(8,128)(2,1)S(1)}, u32[]{:S(2)}, u32[]{:S(2)}) collective-permute-start(bf16[4,192,512]{2,1,0:T(8,128)(2,1)} %get-tuple-element.86.a_ref), channel_id=1, source_target_pairs={{0,16},{1,17},{2,18},{3,19},{4,20},{5,21},{6,22},{7,23},{8,24},{9,... | collective-permute-start | bytes 2359304 | tf_op jit(solution)/shard_map/ppermute | solution.py:1242
  138.4 7.5 %collective-permute-done.8.c_ref = bf16[4,192,512]{2,1,0:T(8,128)(2,1)S(1)} collective-permute-done((bf16[4,192,512]{2,1,0:T(8,128)(2,1)}, bf16[4,192,512]{2,1,0:T(8,128)(2,1)S(1)}, u32[]{:S(2)}, u32[]{:S(2)}) %collective-permute-start.8) | collective-permute-done | bytes 786464 | tf_op jit(solution)/shard_map/ppermute | solution.py:1242
  150.9 6.6 %collective-permute-done.7.b_ref = bf16[4,192,512]{2,1,0:T(8,128)(2,1)S(1)} collective-permute-done((bf16[4,192,512]{2,1,0:T(8,128)(2,1)}, bf16[4,192,512]{2,1,0:T(8,128)(2,1)S(1)}, u32[]{:S(2)}, u32[]{:S(2)}) %collective-permute-start.7) | collective-permute-done | bytes 786464 | tf_op jit(solution)/shard_map/ppermute | solution.py:1242
  159.0 14.8 %collective-permute-done.9.d_ref = bf16[4,192,512]{2,1,0:T(8,128)(2,1)S(1)} collective-permute-done((bf16[4,192,512]{2,1,0:T(8,128)(2,1)S(1)}, bf16[4,192,512]{2,1,0:T(8,128)(2,1)S(1)}, u32[]{:S(2)}, u32[]{:S(2)}) %collective-permute-start.9) | collective-permute-done | bytes 786464 | tf_op jit(solution)/shard_map/ppermute | solution.py:1242
  184.3 6.1 %shard_map.221 = bf16[4,8,192,512]{3,2,1,0:T(8,128)(2,1)} custom-call(bf16[4,192,512]{2,1,0:T(8,128)(2,1)} %get-tuple-element.86.a_ref, bf16[4,192,512]{2,1,0:T(8,128)(2,1)} %copy-done.19, bf16[4,192,512]{2,1,0:T(8,128)(2,1)} %copy-done.18, bf16[4,192,512]{2,1,0:T(8,128)(2,1)} %copy-done.20, bf16[4,4,192,512]{3,2,1,0:T(8,128)(2,1)} %collective-permute-done.10.e_ref), custom_call_target="tpu_custom_call" | custom-call | flops 8000000000 | tf_op jit(solution)/shard_map/pallas_call | solution.py:1375
  199.8 7.2 %shard_map.225 = bf16[2,1040,768]{2,1,0:T(8,128)(2,1)} custom-call(bf16[2,1040,768]{2,1,0:T(8,128)(2,1)} %fusion.15.x_ref), custom_call_target="tpu_custom_call" | custom-call | flops 5000000000 | tf_op jit(solution)/shard_map/pallas_call | solution.py:516
  207.0 36.8 %shard_map.226 = (bf16[2080,256]{1,0:T(8,128)(2,1)}, f32[2080,128]{1,0:T(8,128)}) custom-call(s32[1]{0:T(128)} %bitcast.24.length_ref, bf16[2080,768]{1,0:T(8,128)(2,1)} %bitcast.267, bf16[2080,768]{1,0:T(8,128)(2,1)} %bitcast.268), custom_call_target="tpu_custom_call" | custom-call | flops 35999997952 | tf_op jit(solution)/shard_map/pallas_call | solution.py:932
  253.0 9.1 %convert_reduce_fusion = (f32[2048]{0:T(1024)}, bf16[1040,2048]{1,0:T(8,128)(2,1)S(1)}) fusion(f32[1040,2048]{1,0:T(8,128)S(1)} %convolution_add_fusion, bf16[2048,512]{1,0:T(8,128)(2,1)S(1)} %bitcast.200, bf16[520,512]{1,0:T(8,128)(2,1)S(1)} %get-tuple-element.76, bf16[520,512]{1,0:T(8,128)(2,1)S(1)} %get-tuple-element.75), kind=kOutput, calls=%fused_computation.20 | convolution fusion | flops 2230024192 | bytes 15949824 | tf_op jit(solution)/shard_map/dot_general | solution.py:1161
  270.3 4.9 convolution_convert_fusion.5
  275.2 5.3 convolution_convert_fusion.4
  284.7 80.6 %shard_map.229 = (bf16[2080,768]{1,0:T(8,128)(2,1)}, bf16[16,512]{1,0:T(8,128)(2,1)}, bf16[64,512]{1,0:T(8,128)(2,1)}, bf16[64,512]{1,0:T(8,128)(2,1)}) custom-call(s32[1]{0:T(128)} %bitcast.24.length_ref, bf16[2080,768]{1,0:T(8,128)(2,1)} %bitcast.269, bf16[2080,768]{1,0:T(8,128)(2,1)} %bitcast.270, bf16[2080,768]{1,0:T(8,128)(2,1)} %bitcast.271, ...), custom_call_target="tpu_custom_call" | custom-call | flops 62000001024 | tf_op jit(solution)/shard_map/pallas_call | solution.py:1040
  365.4 7.2 %shard_map.230 = bf16[2,1040,768]{2,1,0:T(8,128)(2,1)} custom-call(bf16[2,1040,768]{2,1,0:T(8,128)(2,1)} %bitcast.272), custom_call_target="tpu_custom_call" | custom-call | flops 5000000000 | tf_op jit(solution)/shard_map/pallas_call | solution.py:516
  383.6 7.9 %convert_reduce_fusion.1 = (f32[2048]{0:T(1024)S(1)}, bf16[1040,2048]{1,0:T(8,128)(2,1)S(1)}) fusion(f32[1040,2048]{1,0:T(8,128)S(1)} %bitcast.287, bf16[1040,512]{1,0:T(8,128)(2,1)S(1)} %get-tuple-element.74, bf16[2048,512]{1,0:T(8,128)(2,1)S(1)} %bitcast.205), kind=kOutput, calls=%fused_computation.21 | convolution fusion | flops 2227894272 | bytes 15949824 | tf_op jit(solution)/shard_map/dot_general | solution.py:1161
  401.5 29.5 %shard_map.232 = (bf16[2080,768]{1,0:T(8,128)(2,1)}, bf16[48,512]{1,0:T(8,128)(2,1)}) custom-call(s32[1]{0:T(128)} %bitcast.24.length_ref, bf16[2080,768]{1,0:T(8,128)(2,1)} %bitcast.266, bf16[2080,256]{1,0:T(8,128)(2,1)} %bitcast.283, bf16[4,8,48,512]{3,2,1,0:T(8,128)(2,1)} %bitcast.279), custom_call_target="tpu_custom_call" | custom-call | flops 22000001024 | tf_op jit(solution)/shard_map/pallas_call | solution.py:1140
  431.1 7.2 %shard_map.233 = bf16[2,1040,768]{2,1,0:T(8,128)(2,1)} custom-call(bf16[2,1040,768]{2,1,0:T(8,128)(2,1)} %bitcast.273), custom_call_target="tpu_custom_call" | custom-call | flops 5000000000 | tf_op jit(solution)/shard_map/pallas_call | solution.py:516
  438.3 5.0 fusion.67
  448.8 5.0 convolution_convert_fusion.3
  453.8 5.2 convolution_convert_fusion.2
  463.7 7.6 %fusion.26 = bf16[1040,512]{1,0:T(8,128)(2,1)S(1)} fusion(f32[1040,512]{1,0:T(8,128)} %copy-done.4, bf16[2048,512]{1,0:T(8,128)(2,1)} %bitcast.201, f32[512]{0:T(512)S(1)} %bitcast.254, f32[1040,2048]{1,0:T(8,128)} %copy-done.72), kind=kOutput, calls=%fused_computation.55 | convolution fusion | flops 2201804800 | bytes 13813760 | tf_op jit(solution)/shard_map/dot_general | solution.py:1165
  476.1 4.8 collective-permute-start.13
  483.0 84.7 %shard_map.234 = (bf16[4,520,512]{2,1,0:T(8,128)(2,1)}, f32[2,10,512]{2,1,0:T(8,128)}, bf16[8,48,512]{2,1,0:T(8,128)(2,1)}, bf16[8,16,512]{2,1,0:T(8,128)(2,1)},...) custom-call(bf16[2,520,512]{2,1,0:T(8,128)(2,1)} %bitcast.214, f32[2,10,512]{2,1,0:T(8,128)} %pad_maximum_fusion.4.refs_1_, ...), custom_call_target="tpu_custom_call" | custom-call | flops 40000000000 | tf_op jit(solution)/shard_map/pallas_call | solution.py:842
  (303 shorter events, 134.3 us)
Async XLA Ops:
  6.7 76.9 %copy-start.8 = (bf16[1,4,520,512]{3,2,1,0:T(8,128)(2,1)S(1)}, bf16[1,4,520,512]{3,2,1,0:T(8,128)(2,1)}, u32[]{:S(2)}) copy-start(bf16[1,4,520,512]{3,2,1,0:T(8,128)(2,1)} %param.13) | copy-start | bytes 6389764
  81.5 35.1 %collective-permute-start.4 = (bf16[192,512]{1,0:T(8,128)(2,1)}, bf16[192,512]{1,0:T(8,128)(2,1)S(1)}, u32[]{:S(2)}, u32[]{:S(2)}) collective-permute-start(bf16[192,512]{1,0:T(8,128)(2,1)} %get-tuple-element.30), channel_id=1, source_target_pairs={{0,3},{1,0},{2,1},{3,2},{4,7},{5,4},{6,5},{7,6},{8,11},{9,8},{10,9... | collective-permute-start | bytes 589832 | tf_op jit(solution)/shard_map/ppermute | solution.py:1242
  82.0 36.1 %collective-permute-start.5 = (bf16[192,512]{1,0:T(8,128)(2,1)}, bf16[192,512]{1,0:T(8,128)(2,1)S(1)}, u32[]{:S(2)}, u32[]{:S(2)}) collective-permute-start(bf16[192,512]{1,0:T(8,128)(2,1)} %get-tuple-element.30), channel_id=1, source_target_pairs={{0,2},{1,3},{2,0},{3,1},{4,6},{5,7},{6,4},{7,5},{8,10},{9,11},{10,... | collective-permute-start | bytes 589832 | tf_op jit(solution)/shard_map/ppermute | solution.py:1242
  82.0 36.1 %collective-permute-start.6 = (bf16[192,512]{1,0:T(8,128)(2,1)}, bf16[192,512]{1,0:T(8,128)(2,1)S(1)}, u32[]{:S(2)}, u32[]{:S(2)}) collective-permute-start(bf16[192,512]{1,0:T(8,128)(2,1)} %get-tuple-element.30), channel_id=1, source_target_pairs={{0,1},{1,2},{2,3},{3,0},{4,5},{5,6},{6,7},{7,4},{8,9},{9,10},{10,1... | collective-permute-start | bytes 589832 | tf_op jit(solution)/shard_map/ppermute | solution.py:1242
  85.0 97.8 %collective-permute-start = (bf16[520,512]{1,0:T(8,128)(2,1)}, bf16[520,512]{1,0:T(8,128)(2,1)}, u32[]{:S(2)}, u32[]{:S(2)}) collective-permute-start(bf16[520,512]{1,0:T(8,128)(2,1)} %get-tuple-element.79), channel_id=1, source_target_pairs={{16,3},{17,1},{18,7},{19,5},{20,19},{21,17},{22,23},{23,21},{24,11... | collective-permute-start | bytes 1597448 | tf_op jit(solution)/shard_map/ppermute | solution.py:1242
  86.6 96.2 %collective-permute-start.1 = (bf16[520,512]{1,0:T(8,128)(2,1)}, bf16[520,512]{1,0:T(8,128)(2,1)}, u32[]{:S(2)}, u32[]{:S(2)}) collective-permute-start(bf16[520,512]{1,0:T(8,128)(2,1)} %get-tuple-element.77), channel_id=1, source_target_pairs={{16,2},{17,0},{18,6},{19,4},{20,18},{21,16},{22,22},{23,20},{24,10... | collective-permute-start | bytes 1597448 | tf_op jit(solution)/shard_map/ppermute | solution.py:1242
  89.6 85.1 %copy-start.51 = (f32[1,1,512]{2,1,0:T(1,128)}, f32[1,1,512]{2,1,0:T(1,128)S(1)}, u32[]{:S(2)}) copy-start(f32[1,1,512]{2,1,0:T(1,128)S(1)} %get-tuple-element.99) | copy-start | bytes 6148
  89.6 85.1 %copy-start.66 = (f32[1,1,512]{2,1,0:T(1,128)}, f32[1,1,512]{2,1,0:T(1,128)S(1)}, u32[]{:S(2)}) copy-start(f32[1,1,512]{2,1,0:T(1,128)S(1)} %get-tuple-element.98) | copy-start | bytes 6148
  89.6 106.4 %copy-start.49 = (f32[1,1,512]{2,1,0:T(1,128)}, f32[1,1,512]{2,1,0:T(1,128)S(1)}, u32[]{:S(2)}) copy-start(f32[1,1,512]{2,1,0:T(1,128)S(1)} %get-tuple-element.96) | copy-start | bytes 6148
  89.6 106.4 %copy-start.68 = (f32[1,1,512]{2,1,0:T(1,128)}, f32[1,1,512]{2,1,0:T(1,128)S(1)}, u32[]{:S(2)}) copy-start(f32[1,1,512]{2,1,0:T(1,128)S(1)} %get-tuple-element.95) | copy-start | bytes 6148
  116.6 66.2 %collective-permute-start.2 = (bf16[520,512]{1,0:T(8,128)(2,1)}, bf16[520,512]{1,0:T(8,128)(2,1)}, u32[]{:S(2)}, u32[]{:S(2)}) collective-permute-start(bf16[520,512]{1,0:T(8,128)(2,1)} %get-tuple-element.78), channel_id=1, source_target_pairs={{16,1},{17,3},{18,5},{19,7},{20,17},{21,19},{22,21},{23,23},{24,9}... | collective-permute-start | bytes 1597448 | tf_op jit(solution)/shard_map/ppermute | solution.py:1242
  119.2 26.7 %collective-permute-start.8 = (bf16[4,192,512]{2,1,0:T(8,128)(2,1)}, bf16[4,192,512]{2,1,0:T(8,128)(2,1)S(1)}, u32[]{:S(2)}, u32[]{:S(2)}) collective-permute-start(bf16[4,192,512]{2,1,0:T(8,128)(2,1)} %get-tuple-element.86.a_ref), channel_id=1, source_target_pairs={{0,16},{1,17},{2,18},{3,19},{4,20},{5,21},{6,22},{7,23},{8,24},{9,... | collective-permute-start | bytes 2359304 | tf_op jit(solution)/shard_map/ppermute | solution.py:1242
  133.5 47.6 %copy-start.33 = (f32[1040]{0:T(1024)}, f32[1040]{0:T(1024)S(1)}, u32[]{:S(2)}) copy-start(f32[1040]{0:T(1024)S(1)} %div.131) | copy-start | bytes 12484
  136.9 20.7 %collective-permute-start.7 = (bf16[4,192,512]{2,1,0:T(8,128)(2,1)}, bf16[4,192,512]{2,1,0:T(8,128)(2,1)S(1)}, u32[]{:S(2)}, u32[]{:S(2)}) collective-permute-start(bf16[4,192,512]{2,1,0:T(8,128)(2,1)} %get-tuple-element.86.a_ref), channel_id=1, source_target_pairs={{0,8},{1,9},{2,10},{3,11},{4,12},{5,13},{6,14},{7,15},{8,0},{9,1},... | collective-permute-start | bytes 2359304 | tf_op jit(solution)/shard_map/ppermute | solution.py:1242
  145.9 27.9 %collective-permute-start.9 = (bf16[4,192,512]{2,1,0:T(8,128)(2,1)S(1)}, bf16[4,192,512]{2,1,0:T(8,128)(2,1)S(1)}, u32[]{:S(2)}, u32[]{:S(2)}) collective-permute-start(bf16[4,192,512]{2,1,0:T(8,128)(2,1)S(1)} %collective-permute-done.8.c_ref), channel_id=1, source_target_pairs={{0,8},{1,9},{2,10},{3,11},{4,12},{5,13},{6,14},{7,15},{8,0},{9,1},... | collective-permute-start | bytes 2359304 | tf_op jit(solution)/shard_map/ppermute | solution.py:1242
  157.5 25.2 %collective-permute-start.3 = (bf16[520,512]{1,0:T(8,128)(2,1)S(1)}, bf16[520,512]{1,0:T(8,128)(2,1)S(1)}, u32[]{:S(2)}, u32[]{:S(2)}) collective-permute-start(bf16[520,512]{1,0:T(8,128)(2,1)S(1)} %copy-done.21), channel_id=1, source_target_pairs={{16,0},{17,2},{18,4},{19,6},{20,16},{21,18},{22,20},{23,22},{24,8}... | collective-permute-start | bytes 1597448 | tf_op jit(solution)/shard_map/ppermute | solution.py:1242
  174.7 9.6 %collective-permute-start.10 = (bf16[4,4,192,512]{3,2,1,0:T(8,128)(2,1)S(1)}, bf16[4,4,192,512]{3,2,1,0:T(8,128)(2,1)}, u32[]{:S(2)}, u32[]{:S(2)}) collective-permute-start(bf16[4,4,192,512]{3,2,1,0:T(8,128)(2,1)S(1)} %pad_maximum_fusion), channel_id=1, source_target_pairs={{0,4},{1,5},{2,6},{3,7},{4,0},{5,1},{6,2},{7,3},{8,12},{9,13},{10,... | collective-permute-start | bytes 9437192 | tf_op jit(solution)/shard_map/ppermute | solution.py:1242
  196.0 57.0 %copy-start.9 = (bf16[4,8,64,512]{3,2,1,0:T(8,128)(2,1)}, bf16[4,8,64,512]{3,2,1,0:T(8,128)(2,1)S(1)}, u32[]{:S(2)}) copy-start(bf16[4,8,64,512]{3,2,1,0:T(8,128)(2,1)S(1)} %get-tuple-element.69) | copy-start | bytes 6291460
  383.5 70.2 %copy-start.6 = (bf16[1040,512]{1,0:T(8,128)(2,1)}, bf16[1040,512]{1,0:T(8,128)(2,1)S(1)}, u32[]{:S(2)}) copy-start(bf16[1040,512]{1,0:T(8,128)(2,1)S(1)} %get-tuple-element.74) | copy-start | bytes 3194884
  395.5 51.4 %copy-start.5 = (f32[1040,512]{1,0:T(8,128)}, f32[1040,512]{1,0:T(8,128)S(1)}, u32[]{:S(2)}) copy-start(f32[1040,512]{1,0:T(8,128)S(1)} %get-tuple-element.66) | copy-start | bytes 6389764
  471.4 105.0 %collective-permute-start.11 = (bf16[520,512]{1,0:T(8,128)(2,1)S(1)}, bf16[520,512]{1,0:T(8,128)(2,1)}, u32[]{:S(2)}, u32[]{:S(2)}) collective-permute-start(bf16[520,512]{1,0:T(8,128)(2,1)S(1)} %get-tuple-element.84), channel_id=1, source_target_pairs={{0,16},{2,17},{4,18},{6,19},{8,24},{10,25},{12,26},{14,27},{16,20}... | collective-permute-start | bytes 1597448 | tf_op jit(solution)/shard_map/ppermute | solution.py:1242
  474.6 101.9 %collective-permute-start.12 = (bf16[520,512]{1,0:T(8,128)(2,1)S(1)}, bf16[520,512]{1,0:T(8,128)(2,1)}, u32[]{:S(2)}, u32[]{:S(2)}) collective-permute-start(bf16[520,512]{1,0:T(8,128)(2,1)S(1)} %get-tuple-element.83), channel_id=1, source_target_pairs={{1,16},{3,17},{5,18},{7,19},{9,24},{11,25},{13,26},{15,27},{17,20}... | collective-permute-start | bytes 1597448 | tf_op jit(solution)/shard_map/ppermute | solution.py:1242
  476.1 100.4 %collective-permute-start.13 = (bf16[520,512]{1,0:T(8,128)(2,1)S(1)}, bf16[520,512]{1,0:T(8,128)(2,1)}, u32[]{:S(2)}, u32[]{:S(2)}) collective-permute-start(bf16[520,512]{1,0:T(8,128)(2,1)S(1)} %get-tuple-element.82), channel_id=1, source_target_pairs={{0,17},{2,16},{4,19},{6,18},{8,25},{10,24},{12,27},{14,26},{16,21}... | collective-permute-start | bytes 1597448 | tf_op jit(solution)/shard_map/ppermute | solution.py:1242
  480.9 95.6 %collective-permute-start.14 = (bf16[520,512]{1,0:T(8,128)(2,1)S(1)}, bf16[520,512]{1,0:T(8,128)(2,1)}, u32[]{:S(2)}, u32[]{:S(2)}) collective-permute-start(bf16[520,512]{1,0:T(8,128)(2,1)S(1)} %get-tuple-element.81), channel_id=1, source_target_pairs={{1,17},{3,16},{5,19},{7,18},{9,25},{11,24},{13,27},{15,26},{17,21}... | collective-permute-start | bytes 1597448 | tf_op jit(solution)/shard_map/ppermute | solution.py:1242
  (76 other events, 607.3 us)

commit v4 on v1

v4 whole, which is shorter than its diff:
```python
import functools

import jax
import jax.numpy as jnp
from jax import lax
from jax.experimental import pallas as pl
from jax.experimental.pallas import tpu as pltpu
from jax.sharding import PartitionSpec as P

VIEWS = 5
PATCH = 400
TEXT = 80
PATCH_ROWS = VIEWS * PATCH
HEAD = 64
PAIR = 2 * HEAD
LOW = jnp.bfloat16
F32 = jnp.float32
MESH = pl.DeviceIdType.MESH
MASKED = -1e30
VMEM_BYTES = 56 * 1024 * 1024


def cost(microseconds):
    return pl.CostEstimate(flops=int(microseconds * 1e9), bytes_accessed=0, transcendentals=0)


class Place:
    def __init__(self, mesh, items):
        self.ranks = mesh.shape["mp"]
        self.chips = self.ranks // items
        self.members = 2 * self.chips
        self.items = items

    def here(self):
        section, dp, mp = (lax.axis_index(name) for name in ("section", "dp", "mp"))
        return section, dp // 2, dp % 2, mp

    def member(self):
        _, _, core, mp = self.here()
        return (mp % self.chips) * 2 + core

    def owner_of(self, item):
        _, pair, core, mp = self.here()
        return (core, 2 * pair + (mp // 2) % 2, item * self.chips + mp // 4)

    def holder_of(self, which, half):
        section, pair, _, _ = self.here()
        return (which, 2 * pair + section, 2 * self.member() + half)

    def peer(self, step):
        section, pair, _, mp = self.here()
        rank = lax.rem(self.member() + step, self.members)
        return rank, (section, 2 * pair + rank % 2, (mp // self.chips) * self.chips + rank // 2)

    def is_here(self, device):
        section, pair, core, mp = self.here()
        same = (device[0] == section) & (device[1] == 2 * pair + core) & (device[2] == mp)
        return same


def greet(sources, targets_count, is_here):
    barrier = pltpu.get_barrier_semaphore()
    for device in sources:

        @pl.when(jnp.logical_not(is_here(device)))
        def _():
            pl.semaphore_signal(barrier, inc=1, device_id=device, device_id_type=MESH)

    pl.semaphore_wait(barrier, targets_count)


class Ring:
    def __init__(self, mesh):
        self.ranks = mesh.shape["mp"]
        self.section, self.dp, self.mp = (lax.axis_index(n) for n in ("section", "dp", "mp"))
        self.core, self.side = self.dp % 2, (self.dp // 2) % 2
        self.base = (self.dp // 4) * 4

    def at(self, section=None, side=None, core=None, mp=None):
        section = self.section if section is None else section
        side = self.side if side is None else side
        core = self.core if core is None else core
        return (section, self.base + 2 * side + core, self.mp if mp is None else mp)

    def other_section(self):
        return self.at(section=1 - self.section)

    def other_side(self):
        return self.at(side=1 - self.side)

    def other_core(self):
        return self.at(core=1 - self.core)

    def column(self, flip_side=False, flip_section=False, flip_core=False):
        side = 1 - self.side if flip_side else self.side
        section = 1 - self.section if flip_section else self.section
        core = 1 - self.core if flip_core else self.core
        return side * 4 + section * 2 + core

    def slots(self):
        yield self.mp, True
        for step in range(1, self.ranks):
            yield self.mp - step, self.mp >= step
            yield self.mp + step, self.mp + step < self.ranks

    def greet_lines(self):
        barrier = pltpu.get_barrier_semaphore()
        for device in (self.other_core(), self.other_side(), self.other_section()):
            pl.semaphore_signal(barrier, inc=1, device_id=device, device_id_type=MESH)
        for mp in range(self.ranks):

            @pl.when(self.mp != mp)
            def _():
                pl.semaphore_signal(barrier, inc=1, device_id=self.at(mp=mp), device_id_type=MESH)

        pl.semaphore_wait(barrier, 3 + self.ranks - 1)

    def greet_all(self):
        barrier = pltpu.get_barrier_semaphore()
        for section in range(2):
            for place in range(4):
                for mp in range(self.ranks):
                    device = (section, self.base + place, mp)
                    mine = (self.section == section) & (self.dp == device[1]) & (self.mp == mp)

                    @pl.when(jnp.logical_not(mine))
                    def _():
                        pl.semaphore_signal(barrier, inc=1, device_id=device, device_id_type=MESH)

        pl.semaphore_wait(barrier, 8 * self.ranks - 1)


def remote(source, target, send_sem, recv_sem, device):
    return pltpu.make_async_remote_copy(
        src_ref=source,
        dst_ref=target,
        send_sem=send_sem,
        recv_sem=recv_sem,
        device_id=device,
        device_id_type=MESH,
    )


class Rows:
    @staticmethod
    def scratch(items):
        dma = pltpu.SemaphoreType.DMA
        return [dma((items,)), dma((2,)), dma((items,)), dma((items,)), dma]

    def __init__(self, ring, place, which, x_ref, rows_ref, stage_ref, sems):
        self.ring, self.place, self.which = ring, place, which
        self.x_ref, self.rows_ref, self.stage_ref = x_ref, rows_ref, stage_ref
        self.send, self.recv, self.stage_send, self.stage_recv, self.local = sems
        self.hands_out = ring.core == ring.section
        self.holds = ring.section == which
        self.half = ring.mp % 2

    def owner(self, item):
        ring, chips = self.ring, self.place.chips
        return (
            ring.section,
            ring.base + 2 * ring.side + (ring.mp // 2) % 2,
            item * chips + ring.mp // 4,
        )

    def is_here(self, device):
        return (device[1] == self.ring.dp) & (device[2] == self.ring.mp)

    def copy(self, source_ref, item):
        return remote(
            source_ref.at[item],
            self.rows_ref.at[self.half],
            self.send.at[item],
            self.recv.at[self.half],
            self.owner(item),
        )

    def stage_copy(self, item):
        return remote(
            self.x_ref.at[item],
            self.stage_ref.at[item],
            self.stage_send.at[item],
            self.stage_recv.at[item],
            self.ring.other_section(),
        )

    def hand_out(self, source_ref, item, go):
        here = self.is_here(self.owner(item))
        pl.when(go & jnp.logical_not(here))(lambda: self.copy(source_ref, item).start())

        @pl.when(go & here)
        def _():
            pltpu.make_async_copy(
                source_ref.at[item], self.rows_ref.at[self.half], self.local
            ).start()

    def begin(self, item):
        self.hand_out(self.x_ref, item, self.hands_out & self.holds)
        pl.when(jnp.logical_not(self.hands_out))(lambda: self.stage_copy(item).start())

    def forward(self, item):
        go = self.hands_out & jnp.logical_not(self.holds)
        pl.when(go)(lambda: self.stage_copy(item).wait_recv())
        self.hand_out(self.stage_ref, item, go)

    def give(self, item):
        self.hand_out(self.x_ref, item, self.hands_out & self.holds)
        self.hand_out(self.stage_ref, item, self.hands_out & jnp.logical_not(self.holds))

    def arrive(self):
        ring = self.ring
        for part in range(2):
            source = (
                ring.section,
                ring.base + 2 * ring.side + ring.section,
                2 * self.place.member() + part,
            )
            here = self.is_here(source)

            @pl.when(jnp.logical_not(here))
            def _():
                remote(
                    self.x_ref.at[0],
                    self.rows_ref.at[part],
                    self.send.at[0],
                    self.recv.at[part],
                    source,
                ).wait_recv()

            @pl.when(here)
            def _():
                pltpu.make_async_copy(self.x_ref.at[0], self.rows_ref.at[part], self.local).wait()

    def end_given(self):
        for item in range(self.place.items):
            here = self.is_here(self.owner(item))
            pl.when(self.hands_out & jnp.logical_not(here))(
                lambda item=item: self.copy(self.x_ref, item).wait_send()
            )

    def end(self):
        self.end_given()
        for item in range(self.place.items):
            pl.when(jnp.logical_not(self.hands_out))(
                lambda item=item: self.stage_copy(item).wait_send()
            )
            pl.when(self.hands_out & self.holds)(
                lambda item=item: self.stage_copy(item).wait_recv()
            )


class Gather:
    COUNT = 10

    @staticmethod
    def scratch(ranks):
        dma = pltpu.SemaphoreType.DMA
        line, near, pair, four = dma((ranks,)), dma((2, ranks)), dma((2,)), dma((4,))
        return [line, line, near, near, near, near, four, four, dma, pair]

    def __init__(self, ring, full_ref, sems, piece_ref=None, owner=None, w_ref=None):
        self.ring, self.full_ref, self.piece_ref, self.w_ref = ring, full_ref, piece_ref, w_ref
        self.owns = None if owner is None else ring.section == owner
        (
            self.line_send,
            self.line_recv,
            self.near_send,
            self.near_recv,
            self.both_send,
            self.both_recv,
            self.core_send,
            self.core_recv,
            self.local,
            self.split_sems,
        ) = sems

    def at(self, slot, flip_side=False, flip_section=False):
        ring = self.ring
        side = 1 - ring.side if flip_side else ring.side
        section = 1 - ring.section if flip_section else ring.section
        return self.full_ref.at[slot, side, section, ring.core]

    def own_copy(self):
        ring = self.ring
        source = self.piece_ref
        if source is None:
            source = self.w_ref.at[ring.side, ring.section, ring.core]
        return pltpu.make_async_copy(source, self.at(ring.mp), self.local)

    def split_copy(self):
        ring = self.ring
        return remote(
            self.w_ref.at[ring.side, 1 - ring.section, ring.core],
            self.at(ring.mp, flip_section=True),
            self.split_sems.at[0],
            self.split_sems.at[1],
            ring.other_section(),
        )

    def line_copy(self, other, slot):
        ref = self.at(slot)
        return remote(ref, ref, self.line_send.at[other], self.line_recv.at[slot], self.ring.at(mp=other))

    def others(self, method):
        for other in range(self.ring.ranks):
            pl.when(self.ring.mp != other)(functools.partial(method, other))

    def near_copy(self, way, slot):
        ring = self.ring
        ref = self.at(slot)
        device = ring.other_side() if way == 0 else ring.other_section()
        return remote(ref, ref, self.near_send.at[way, slot], self.near_recv.at[way, slot], device)

    def both_copy(self, way, slot):
        ring = self.ring
        ref = self.at(slot, flip_side=way == 1, flip_section=way == 0)
        device = ring.other_side() if way == 0 else ring.other_section()
        return remote(ref, ref, self.both_send.at[way, slot], self.both_recv.at[way, slot], device)

    def ways(self, method):
        for slot in range(self.ring.ranks):
            method(2 * slot // self.ring.ranks, slot)

    def core_copy(self, index):
        ref = self.at(slice(None), index % 2 == 1, index // 2 == 1)
        return remote(ref, ref, self.core_send.at[index], self.core_recv.at[index], self.ring.other_core())

    def near(self, slot):
        self.near_copy(0, slot).start()
        self.near_copy(1, slot).start()

    def split(self):
        @pl.when(self.owns)
        def _():
            self.split_copy().start()
            self.own_copy().start()

    def open(self):
        if self.owns is None:
            self.own_copy().start()
            self.own_copy().wait()
        else:
            pl.when(self.owns)(lambda: self.own_copy().wait())
            pl.when(jnp.logical_not(self.owns))(lambda: self.split_copy().wait_recv())
        self.others(lambda other: self.line_copy(other, self.ring.mp).start())
        self.near(self.ring.mp)

    def along(self):
        def got(other):
            self.line_copy(other, other).wait_recv()
            self.near(other)

        self.others(got)

    def turn(self):
        self.core_copy(0).start()

        def relay(way, slot):
            self.near_copy(1 - way, slot).wait_recv()
            self.both_copy(way, slot).start()

        self.ways(relay)
        self.ways(lambda way, slot: self.near_copy(way, slot).wait_recv())
        self.core_copy(1).start()
        self.core_copy(2).start()

    def last(self):
        self.ways(lambda way, slot: self.both_copy(way, slot).wait_recv())
        self.core_copy(3).start()

    def arrive(self):
        for index in range(4):
            self.core_copy(index).wait_recv()

    def end(self):
        if self.owns is not None:
            pl.when(self.owns)(lambda: self.split_copy().wait_send())
        self.others(lambda other: self.line_copy(other, self.ring.mp).wait_send())
        for slot in range(self.ring.ranks):
            self.near_copy(0, slot).wait_send()
            self.near_copy(1, slot).wait_send()
        self.ways(lambda way, slot: self.both_copy(way, slot).wait_send())
        for index in range(4):
            self.core_copy(index).wait_send()

    def phase(self, number):
        (self.open, self.along, self.turn, self.last, self.arrive, self.end)[number]()


def full_shapes(ranks, pieces):
    return tuple(jax.ShapeDtypeStruct((ranks, 2, 2, 2) + p.shape, p.dtype) for p in pieces)


class Swap:
    COUNT = 2

    @staticmethod
    def scratch(members):
        dma = pltpu.SemaphoreType.DMA
        return [dma((members - 1,)), dma((members - 1,))]

    def __init__(self, place, sent, got, sems):
        self.place, self.sent, self.got = place, sent, got
        self.send, self.recv = sems

    def copy(self, step):
        rank, device = self.place.peer(step)
        me = self.place.member()
        return remote(
            self.sent(rank), self.got(me), self.send.at[step - 1], self.recv.at[step - 1], device
        )

    def begin(self):
        for step in range(1, self.place.members):
            self.copy(step).start()

    def arrive(self):
        for step in range(1, self.place.members):
            self.copy(step).wait_recv()

    def end(self):
        for step in range(1, self.place.members):
            self.copy(step).wait_send()


def start_kernel(mesh, place, count, fused, x_ref, vec_ref, *refs):
    def take(count):
        nonlocal refs
        taken, refs = refs[:count], refs[count:]
        return taken

    w_refs = take(count)
    rows_ref, vecs_ref, stage_ref = take(3)
    full_refs = take(count + 1)
    second_refs = take(count - 1)
    qkv_ref, mixed_ref = take(2) if fused else (None, None)
    local_vec, vec_send, vec_recv, piece_send, piece_recv = take(5)
    ring = Ring(mesh)
    ranks, items = ring.ranks, place.items
    section, mp = ring.section, ring.mp
    rows = Rows(ring, place, 0, x_ref, rows_ref, stage_ref, take(5))
    lead, *rest = [
        Gather(ring, full_ref, take(Gather.COUNT), owner=which // count, w_ref=w_refs[which % count])
        for which, full_ref in enumerate(full_refs)
    ]
    work = None
    if fused:
        work = FirstAttention(place, rows_ref, full_refs[0], vecs_ref, qkv_ref, mixed_ref, refs)
    ring.greet_all()

    def piece_copy(which):
        return remote(
            w_refs[which + 1].at[ring.side, 0, ring.core],
            second_refs[which],
            piece_send.at[which],
            piece_recv.at[which],
            ring.other_section(),
        )

    def own_piece(which):
        return pltpu.make_async_copy(
            w_refs[which + 1].at[ring.side, 1, ring.core], second_refs[which], piece_recv.at[which]
        )

    def all_vecs(method):
        for other in range(2 * ranks):
            device = (other // ranks, ring.dp, other % ranks)
            slot = section * ranks + mp
            copy = remote(
                vec_ref, vecs_ref.at[slot], vec_send.at[other], vec_recv.at[slot], device
            )
            pl.when(slot != other)(functools.partial(method, copy))
        method(
            remote(
                vec_ref,
                vecs_ref.at[2 * ranks],
                vec_send.at[2 * ranks],
                vec_recv.at[2 * ranks],
                ring.other_core(),
            )
        )

    own_vec = pltpu.make_async_copy(vec_ref, vecs_ref.at[section * ranks + mp], local_vec)

    own_vec.start()
    all_vecs(lambda copy: copy.start())
    lead.split()
    for gather in rest:
        gather.split()
    lead.open()
    for item in range(items):
        rows.begin(item)

    @pl.when(section == 1)
    def _():
        for which in range(count - 1):
            piece_copy(which).start()
            own_piece(which).start()

    for gather in rest:
        gather.open()
    lead.along()
    rows.forward(0)
    lead.turn()
    for item in range(1, items // 2):
        rows.forward(item)
    for gather in rest:
        gather.along()
    lead.last()
    for item in range(items // 2, items):
        rows.forward(item)
    own_vec.wait()
    for other in range(2 * ranks + 1):
        copy = remote(
            vec_ref,
            vecs_ref.at[other],
            vec_send.at[other],
            vec_recv.at[other],
            ring.other_core(),
        )
        pl.when((section * ranks + mp) != other)(lambda copy=copy: copy.wait_recv())
    rows.arrive()
    lead.arrive()
    if fused:
        for step in range(place.members):
            work.project(step)
    for gather in rest:
        gather.turn()
    if fused:

        def between(view):
            @pl.when(view == 2)
            def _():
                for gather in rest:
                    gather.last()

        work.attend(between)
    else:
        for gather in rest:
            gather.last()
    for which in range(count - 1):

        @pl.when(section == 0)
        def _():
            piece_copy(which).wait_recv()

        @pl.when(section == 1)
        def _():
            own_piece(which).wait()
            piece_copy(which).wait_send()

    for gather in rest:
        gather.arrive()
    if fused:
        work.end()
    lead.end()
    for gather in rest:
        gather.end()
    all_vecs(lambda copy: copy.wait_send())
    rows.end()


class FirstAttention:
    BLOCK = 208

    @staticmethod
    def scratch(place, rows, width, heads_width):
        dma = pltpu.SemaphoreType.DMA
        return [
            pltpu.VMEM((rows, width), F32),
            pltpu.VMEM((rows, width), LOW),
            pltpu.VMEM((place.members - 1, rows, 3 * heads_width), LOW),
            pltpu.VMEM((place.members * rows, heads_width), LOW),
            *Swap.scratch(place.members),
            *Swap.scratch(place.members),
            dma,
        ]

    def __init__(self, place, rows_ref, weight_ref, vecs_ref, qkv_ref, mixed_ref, scratch):
        self.place, self.rows_ref, self.weight_ref, self.vecs_ref = place, rows_ref, weight_ref, vecs_ref
        self.qkv_ref, self.mixed_ref = qkv_ref, mixed_ref
        self.wide_ref, self.normed_ref, self.sent_ref, self.heads_ref, *sems = scratch
        self.rows = self.wide_ref.shape[0]
        me, members = place.member(), place.members
        self.to_heads = Swap(
            place,
            lambda rank: self.sent_ref.at[lax.rem(rank - me + members - 1, members)],
            lambda rank: qkv_ref.at[self.span(rank)],
            sems[:2],
        )
        self.to_rows = Swap(
            place,
            lambda rank: self.heads_ref.at[self.span(rank)],
            lambda rank: mixed_ref.at[rank],
            sems[2:4],
        )
        self.local = sems[4]

    def span(self, rank):
        return pl.ds(pl.multiple_of(rank * self.rows, 16), self.rows)

    def norm(self):
        half = self.rows // 2
        for part in range(2):
            self.wide_ref[part * half : (part + 1) * half] = wide(self.rows_ref[part])
        gain, bias = self.vecs_ref[0, 0:1], self.vecs_ref[0, 1:2]

        @pl.loop(0, self.rows // self.BLOCK)
        def _(block):
            span = pl.ds(pl.multiple_of(block * self.BLOCK, 16), self.BLOCK)
            normed = layer_norm(self.wide_ref[span], gain, bias)
            self.normed_ref[span] = normed.astype(LOW)

    def project(self, step):
        if step == 0:
            self.norm()
        members = self.place.members
        turn = (step + 1) % members
        rank = lax.rem(self.place.member() + turn, members)
        shards = self.weight_ref.shape[0] // members
        cut = 8 * self.weight_ref.shape[4]
        weights = [
            self.weight_ref[rank * shards + shard].reshape(cut, -1) for shard in range(shards)
        ]

        @pl.loop(0, self.rows // self.BLOCK)
        def _(block):
            start = pl.multiple_of(block * self.BLOCK, 16)
            normed = self.normed_ref[pl.ds(start, self.BLOCK)]
            for shard in range(shards):
                part = dot_rows(normed, weights[shard]).astype(LOW)
                columns = slice(shard * cut, (shard + 1) * cut)
                if turn > 0:
                    self.sent_ref[turn - 1, pl.ds(start, self.BLOCK), columns] = part
                else:
                    at = pl.multiple_of(rank * self.rows + start, 16)
                    self.qkv_ref[pl.ds(at, self.BLOCK), columns] = part

        if turn > 0:
            self.to_heads.copy(turn).start()

    def attend(self, between):
        self.to_heads.arrive()
        place, width = self.place, self.heads_ref.shape[1]
        me = place.member()
        section, _, core, mp = place.here()

        def group(rows, bias):
            for pair in range(width // PAIR):
                base = pair * 3 * PAIR
                q, k, v = (
                    self.qkv_ref[rows, base + part * PAIR : base + (part + 1) * PAIR] for part in range(3)
                )
                out, _ = forward_pair(q, k, v, bias)
                self.heads_ref[rows, pair * PAIR : (pair + 1) * PAIR] = out.astype(LOW)

        @pl.loop(0, VIEWS)
        def _(view):
            group(pl.ds(pl.multiple_of(view * PATCH, 16), PATCH), None)
            between(view)

        ranks = self.place.ranks
        own, other = self.vecs_ref[section * ranks + mp], self.vecs_ref[2 * ranks]
        lengths = jnp.where(core == section, own[7:8], other[7:8])
        lane = lax.broadcasted_iota(jnp.int32, lengths.shape, 1)
        used = jnp.sum(jnp.where(lane == mp // place.chips, lengths, 0.0), -1, keepdims=True)
        column = wide(lax.broadcasted_iota(jnp.int32, (1, TEXT), 1))
        bias = jnp.where(column < used, 0.0, MASKED)
        group(pl.ds(PATCH_ROWS, TEXT), bias)
        self.to_rows.begin()
        own = pltpu.make_async_copy(self.heads_ref.at[self.span(me)], self.mixed_ref.at[me], self.local)
        own.start()
        own.wait()

    def end(self):
        self.to_rows.arrive()
        self.to_heads.end()
        self.to_rows.end()


def start(mesh, place, rows, vec, weights, fused):
    ranks, items, count = place.ranks, place.items, len(weights)
    held, away = pl.BlockSpec(memory_space=pltpu.VMEM), pl.BlockSpec(memory_space=pl.ANY)
    dma = pltpu.SemaphoreType.DMA
    fulls = tuple(jax.ShapeDtypeStruct((ranks,) + w.shape, w.dtype) for w in weights)
    pieces = tuple(jax.ShapeDtypeStruct(w.shape[3:], w.dtype) for w in weights[1:])
    fused_out, fused_scratch = (), []
    if fused:
        here, width = 2 * rows.shape[1], rows.shape[2]
        heads_width = 8 * ranks * weights[0].shape[3] // (3 * place.members)
        fused_out = (
            jax.ShapeDtypeStruct((place.members * here, 3 * heads_width), LOW),
            jax.ShapeDtypeStruct((place.members, here, heads_width), LOW),
        )
        fused_scratch = FirstAttention.scratch(place, here, width, heads_width)
    out = pl.pallas_call(
        functools.partial(start_kernel, mesh, place, count, fused),
        out_shape=(
            jax.ShapeDtypeStruct((2,) + rows.shape[1:], rows.dtype),
            jax.ShapeDtypeStruct((2 * ranks + 1,) + vec.shape, vec.dtype),
            jax.ShapeDtypeStruct(rows.shape, rows.dtype),
        )
        + fulls
        + fulls[:1]
        + pieces
        + fused_out,
        in_specs=[held] * (2 + count),
        out_specs=(held, held, away, held) + (away,) * (2 * count - 1) + (held,) * len(fused_out),
        scratch_shapes=[
            dma,
            dma((2 * ranks + 1,)),
            dma((2 * ranks + 1,)),
            dma((count - 1,)),
            dma((count - 1,)),
        ]
        + Rows.scratch(items)
        + Gather.scratch(ranks) * (count + 1)
        + fused_scratch,
        cost_estimate=cost(60),
        compiler_params=pltpu.CompilerParams(
            collective_id=0, has_side_effects=True, vmem_limit_bytes=VMEM_BYTES
        ),
    )(rows, vec, *weights)
    at = 3 + 2 * count
    return out[:3], out[3 : 3 + count], out[3 + count : 4 + count], out[4 + count : at], out[at:]


def swap_kernel(place, x_ref, o_ref, send_sems, recv_sems, local_sem):
    me = place.member()
    peers = [place.peer(step) for step in range(1, place.members)]
    greet([p[1] for p in peers], place.members - 1, place.is_here)
    copies = []
    for index, (rank, device) in enumerate(peers):
        copies.append(
            pltpu.make_async_remote_copy(
                src_ref=x_ref.at[rank],
                dst_ref=o_ref.at[me],
                send_sem=send_sems.at[index],
                recv_sem=recv_sems.at[index],
                device_id=device,
                device_id_type=MESH,
            )
        )
        copies[-1].start()
    own = pltpu.make_async_copy(x_ref.at[me], o_ref.at[me], local_sem)
    own.start()
    own.wait()
    for copy in copies:
        copy.wait()


def swapped(place, x, collective_id):
    held = pl.BlockSpec(memory_space=pltpu.VMEM)
    return pl.pallas_call(
        functools.partial(swap_kernel, place),
        out_shape=jax.ShapeDtypeStruct(x.shape, x.dtype),
        in_specs=[held],
        out_specs=held,
        scratch_shapes=[
            pltpu.SemaphoreType.DMA((place.members - 1,)),
            pltpu.SemaphoreType.DMA((place.members - 1,)),
            pltpu.SemaphoreType.DMA,
        ],
        cost_estimate=cost(5),
        compiler_params=pltpu.CompilerParams(
            collective_id=collective_id, has_side_effects=True, vmem_limit_bytes=VMEM_BYTES
        ),
    )(x)


def to_heads(place, x, collective_id):
    return swapped(place, x, collective_id).reshape(-1, x.shape[2])


def to_rows(place, x, collective_id):
    return swapped(place, x.reshape(place.members, -1, x.shape[1]), collective_id)


def wide(value):
    return value.astype(F32)


class Hops:
    FLIPS = ((True, True), (True, False), (False, True), (False, False))
    COUNT = 11

    @staticmethod
    def scratch(ranks, rows, width):
        slots = ranks // 2
        dma = pltpu.SemaphoreType.DMA
        shapes = (
            (4, ranks, rows, width),
            (2, 2, slots, rows, width),
            (2, 2, slots, rows, width),
            (2, slots, rows, width),
            (2, slots, rows, width),
        )
        sems = [dma((4,)), dma((4,)), dma((2,)), dma((2,)), dma((2,)), dma((2,))]
        return [pltpu.VMEM(shape, LOW) for shape in shapes] + sems

    def __init__(self, ring, grad_ref, line_ref, scratch):
        self.ring, self.grad_ref, self.line_ref = ring, grad_ref, line_ref
        (
            self.core_got,
            self.one_sent,
            self.one_got,
            self.two_sent,
            self.two_got,
            self.core_send,
            self.core_recv,
            self.one_send,
            self.one_recv,
            self.two_send,
            self.two_recv,
        ) = scratch
        self.slots = ring.ranks // 2
        self.halves = (pl.ds(0, self.slots), pl.ds(self.slots, self.slots))

    def core_copy(self, index):
        side, section = self.FLIPS[index]
        return remote(
            self.grad_ref.at[:, self.ring.column(side, section, True)],
            self.core_got.at[index],
            self.core_send.at[index],
            self.core_recv.at[index],
            self.ring.other_core(),
        )

    def one_copy(self, way):
        device = self.ring.other_side() if way == 0 else self.ring.other_section()
        return remote(
            self.one_sent.at[way], self.one_got.at[way], self.one_send.at[way], self.one_recv.at[way], device
        )

    def two_copy(self, way):
        device = self.ring.other_section() if way == 0 else self.ring.other_side()
        return remote(
            self.two_sent.at[way], self.two_got.at[way], self.two_send.at[way], self.two_recv.at[way], device
        )

    def own(self, index, half):
        side, section = self.FLIPS[index]
        slots = self.halves[half]
        return wide(self.grad_ref[slots, self.ring.column(side, section)]) + wide(
            self.core_got[index, slots]
        )

    def begin(self):
        for index in range(4):
            self.core_copy(index).start()

    def one(self):
        for index in range(4):
            self.core_copy(index).wait_recv()
        for way, index in ((0, 1), (1, 2)):
            self.one_sent[way, 0] = self.own(index, way).astype(LOW)
            self.one_sent[way, 1] = self.own(0, way).astype(LOW)
            self.one_copy(way).start()

    def two(self):
        for way, index in ((0, 2), (1, 1)):
            self.one_copy(way).wait_recv()
            self.two_sent[way] = (self.own(index, way) + wide(self.one_got[way, 1])).astype(LOW)
            self.two_copy(way).start()

    def line(self):
        for way in range(2):
            self.two_copy(way).wait_recv()
            whole = self.own(3, way) + wide(self.one_got[way, 0]) + wide(self.two_got[way])
            self.line_ref[self.halves[way]] = whole.astype(LOW)

    def end(self):
        for index in range(4):
            self.core_copy(index).wait_send()
        for way in range(2):
            self.one_copy(way).wait_send()
            self.two_copy(way).wait_send()

    def phase(self, number):
        (self.begin, self.one, self.two, self.line)[number]()


class Line:
    COUNT = 3

    @staticmethod
    def scratch(ranks, rows, width):
        dma = pltpu.SemaphoreType.DMA
        return [pltpu.VMEM((ranks, rows, width), LOW), dma((ranks,)), dma((ranks,))]

    def __init__(self, ring, line_ref, piece_ref, scratch):
        self.ring, self.line_ref, self.piece_ref = ring, line_ref, piece_ref
        self.got, self.send, self.recv = scratch

    def copy(self, other, mine=None):
        mine = self.ring.mp if mine is None else mine
        return remote(
            self.line_ref.at[other],
            self.got.at[mine],
            self.send.at[other],
            self.recv.at[mine],
            self.ring.at(mp=other),
        )

    def along(self, method):
        for other in range(self.ring.ranks):
            pl.when(self.ring.mp != other)(functools.partial(method, other))

    def begin(self):
        self.along(lambda other: self.copy(other).start())
        self.got[self.ring.mp] = self.line_ref[self.ring.mp]

    def total(self):
        self.along(lambda other: self.copy(other, other).wait_recv())
        total = wide(self.got[0])
        for other in range(1, self.ring.ranks):
            total = total + wide(self.got[other])
        self.piece_ref[...] = total.astype(LOW)

    def end(self):
        self.along(lambda other: self.copy(other).wait_send())


def each_of(kind, ring, from_refs, to_refs, scratch):
    count = kind.COUNT
    return [
        kind(ring, from_ref, to_ref, scratch[i * count : (i + 1) * count])
        for i, (from_ref, to_ref) in enumerate(zip(from_refs, to_refs))
    ]


def scratch_of(kind, grads):
    found = []
    for grad in grads:
        found += kind.scratch(grad.shape[0], *grad.shape[-2:])
    return found


def line_shapes(grads):
    return tuple(jax.ShapeDtypeStruct((g.shape[0],) + g.shape[2:], LOW) for g in grads)


def piece_shapes(grads):
    return tuple(jax.ShapeDtypeStruct(g.shape[-2:], LOW) for g in grads)


class Fan:
    COUNT = 6

    @staticmethod
    def scratch():
        return [pltpu.SemaphoreType.DMA] * 6

    def __init__(self, ring, out_ref, sems):
        self.ring, self.out_ref = ring, out_ref
        (
            self.section_send,
            self.section_recv,
            self.side_send,
            self.side_recv,
            self.core_send,
            self.core_recv,
        ) = sems

    def section_copy(self, piece_ref):
        ring = self.ring
        return remote(
            piece_ref,
            self.out_ref.at[ring.side, ring.section, ring.core],
            self.section_send,
            self.section_recv,
            ring.other_section(),
        )

    def side_copy(self):
        ref = self.out_ref.at[self.ring.side, :, self.ring.core]
        return remote(ref, ref, self.side_send, self.side_recv, self.ring.other_side())

    def core_copy(self):
        ref = self.out_ref.at[:, :, self.ring.core]
        return remote(ref, ref, self.core_send, self.core_recv, self.ring.other_core())

    def leave(self, layer, piece_ref):
        ring = self.ring
        self.piece_ref = piece_ref
        pl.when(ring.section != layer)(lambda: self.section_copy(piece_ref).start())

        @pl.when(ring.section == layer)
        def _():
            self.out_ref[ring.side, ring.section, ring.core] = piece_ref[...]

    def to_side(self):
        self.section_copy(self.piece_ref).wait_recv()
        self.side_copy().start()

    def to_core(self):
        self.side_copy().wait_recv()
        self.core_copy().start()

    def end(self):
        self.core_copy().wait_recv()
        self.section_copy(self.piece_ref).wait_send()
        self.side_copy().wait_send()
        self.core_copy().wait_send()


class Home:
    @staticmethod
    def scratch(items):
        dma = pltpu.SemaphoreType.DMA
        return [dma, dma((2,)), dma((items,))]

    def __init__(self, ring, place, keeper, rows_ref, gone_ref, sems):
        self.place, self.rows_ref, self.gone_ref = place, rows_ref, gone_ref
        self.local, self.send, self.recv = sems
        self.keeps = ring.section == keeper
        self.slot = ring.mp // place.chips
        group = ring.base + 2 * ring.side + ring.section
        self.targets = [(keeper, group, 2 * place.member() + part) for part in range(2)]

    def copy(self, index):
        return remote(
            self.rows_ref.at[index],
            self.gone_ref.at[self.slot],
            self.send.at[index],
            self.recv.at[self.slot],
            self.targets[index],
        )

    def own(self, index):
        return pltpu.make_async_copy(
            self.rows_ref.at[index], self.gone_ref.at[self.slot], self.local
        )

    def begin(self):
        for index in range(2):
            here = self.place.is_here(self.targets[index])
            pl.when(jnp.logical_not(here))(lambda index=index: self.copy(index).start())
            pl.when(here)(lambda index=index: self.own(index).start())

    def end(self):
        for item in range(self.place.items):
            source = self.place.owner_of(item)
            pl.when(self.keeps & jnp.logical_not(self.place.is_here(source)))(
                lambda item=item, source=source: remote(
                    self.rows_ref.at[0],
                    self.gone_ref.at[item],
                    self.send.at[0],
                    self.recv.at[item],
                    source,
                ).wait_recv()
            )
        for index in range(2):
            here = self.place.is_here(self.targets[index])
            pl.when(here)(lambda index=index: self.own(index).wait())
            pl.when(jnp.logical_not(here))(lambda index=index: self.copy(index).wait_send())


def finish_kernel(mesh, place, layers, hops, lines, *refs):
    def take(count):
        nonlocal refs
        taken, refs = refs[:count], refs[count:]
        return taken

    pieces = len(layers) // 2 * 2
    rows_ref, vec_ref = take(2)
    hop_refs, line_in_refs = take(hops), take(lines)
    whole_refs = take(pieces - hops - lines)
    gone_ref, vec_out_ref = take(2)
    out_refs = take(pieces // 2)
    vec_sent, vec_got, vec_line = take(3)
    home_sems = take(3)
    (vec_send, vec_recv, vec_line_send, vec_line_recv) = take(4)
    piece_refs = take(hops + lines)
    line_refs = take(hops)
    ring = Ring(mesh)
    ranks = ring.ranks
    section, mp = ring.section, ring.mp
    sums = each_of(Hops, ring, hop_refs, line_refs, take(Hops.COUNT * hops))
    alongs = each_of(Line, ring, line_refs + line_in_refs, piece_refs, take(Line.COUNT * (hops + lines)))
    home = Home(ring, place, 0, rows_ref, gone_ref, home_sems)
    piece_refs = piece_refs + whole_refs
    ring.greet_all()

    for along in alongs[hops:]:
        along.begin()
    for one in sums:
        one.begin()
    partners = (ring.other_core(), ring.other_side(), ring.other_section())

    def vec_copy(step):
        return remote(
            vec_sent.at[step],
            vec_got.at[step],
            vec_send.at[step],
            vec_recv.at[step],
            partners[step],
        )

    vec_sent[0] = vec_ref[...]
    vec_copy(0).start()

    fans = [Fan(ring, out_ref, take(Fan.COUNT)) for out_ref in out_refs]

    def leave(which):
        layer, matrix = layers[which]
        fans[matrix].leave(layer, piece_refs[which])

    for one in sums:
        one.one()
    home.begin()
    for which in range(hops + lines, pieces):
        leave(which)
    vec_copy(0).wait_recv()
    vec_sent[1] = vec_sent[0] + vec_got[0]
    vec_copy(1).start()
    for one in sums:
        one.two()
    vec_copy(1).wait_recv()
    vec_sent[2] = vec_sent[1] + vec_got[1]
    vec_copy(2).start()
    for one, along in zip(sums, alongs):
        one.line()
        along.begin()

    def vec_line_copy(other, mine=None):
        return remote(
            vec_line.at[ranks],
            vec_line.at[mp if mine is None else mine],
            vec_line_send.at[other],
            vec_line_recv.at[mp if mine is None else mine],
            ring.at(mp=other),
        )

    def others(method):
        for other in range(ranks):
            pl.when(mp != other)(functools.partial(method, other))

    vec_copy(2).wait_recv()
    vec_line[ranks] = vec_sent[2] + vec_got[2]
    others(lambda other: vec_line_copy(other).start())
    vec_line[mp] = vec_line[ranks]
    for which in (*range(hops, hops + lines), *range(hops)):
        alongs[which].total()
        leave(which)
    others(lambda other: vec_line_copy(other, other).wait_recv())
    total = vec_line[0]
    for other in range(1, ranks):
        total = total + vec_line[other]
    vec_out_ref[...] = total
    for fan in fans:
        fan.to_side()
    for fan in fans:
        fan.to_core()
    home.end()
    for fan in fans:
        fan.end()
    for one in sums:
        one.end()
    for along in alongs:
        along.end()
    for step in range(3):
        vec_copy(step).wait_send()
    others(lambda other: vec_line_copy(other).wait_send())


def finish(mesh, place, rows, vecs, grads, lines, wholes, layers):
    ranks, items = place.ranks, place.items
    held = pl.BlockSpec(memory_space=pltpu.VMEM)
    dma = pltpu.SemaphoreType.DMA
    pieces = len(layers)
    sources = list(grads) + list(lines) + list(wholes)
    sizes = [None] * (pieces // 2)
    for (_, matrix), source in zip(layers, sources):
        sizes[matrix] = (2, 2, 2) + source.shape[-2:]
    return pl.pallas_call(
        functools.partial(finish_kernel, mesh, place, layers, len(grads), len(lines)),
        out_shape=(
            jax.ShapeDtypeStruct((items,) + rows.shape[1:], rows.dtype),
            jax.ShapeDtypeStruct(vecs.shape, F32),
        )
        + tuple(jax.ShapeDtypeStruct(size, LOW) for size in sizes),
        in_specs=[held] * (2 + pieces),
        out_specs=(held,) * (2 + pieces // 2),
        scratch_shapes=[
            pltpu.VMEM((3,) + vecs.shape, F32),
            pltpu.VMEM((3,) + vecs.shape, F32),
            pltpu.VMEM((ranks + 1,) + vecs.shape, F32),
            *Home.scratch(items),
            dma((3,)),
            dma((3,)),
            dma((ranks,)),
            dma((ranks,)),
        ]
        + [pltpu.VMEM(x.shape[-2:], LOW) for x in sources[: len(grads) + len(lines)]]
        + [pltpu.VMEM((ranks,) + x.shape[-2:], LOW) for x in grads]
        + scratch_of(Hops, grads)
        + scratch_of(Line, sources[: len(grads) + len(lines)])
        + Fan.scratch() * (pieces // 2),
        cost_estimate=cost(40),
        compiler_params=pltpu.CompilerParams(
            collective_id=1, has_side_effects=True, vmem_limit_bytes=VMEM_BYTES
        ),
    )(rows, vecs, *sources)


def dot_rows(left, right):
    return lax.dot_general(left, right, (((1,), (1,)), ((), ())), preferred_element_type=F32)


def dot(left, right):
    return lax.dot_general(left, right, (((1,), (0,)), ((), ())), preferred_element_type=F32)


def half_of(block, head):
    lanes = lax.broadcasted_iota(jnp.int32, (1, PAIR), 1)
    mine = (lanes < HEAD) if head == 0 else (lanes >= HEAD)
    return jnp.where(mine, block, jnp.zeros((), block.dtype))


def joined(first, second):
    lanes = lax.broadcasted_iota(jnp.int32, (1, PAIR), 1)
    return jnp.where(lanes < HEAD, first, second)


def forward_pair(q, k, v, bias):
    outs, logs = [], []
    q = q * jnp.asarray(0.125, LOW)
    for head in range(2):
        scores = dot_rows(half_of(q, head), k)
        if bias is not None:
            scores = scores + bias
        top = jnp.max(scores, -1, keepdims=True)
        expon = jnp.exp(scores - top)
        total = jnp.sum(expon, -1, keepdims=True)
        outs.append(dot(expon.astype(LOW), v) / total)
        logs.append(top + jnp.log(total))
    return joined(*outs), logs


def joint_forward_kernel(mesh, place, pairs, block, count, fused, length_ref, x_ref, near_ref, far_ref, *refs):
    def take(count):
        nonlocal refs
        taken, refs = refs[:count], refs[count:]
        return taken

    piece_refs = take(count)
    o_ref, log_ref, rows_ref = take(3)
    full_refs = take(count)
    qkv_ref, mixed_ref = take(2) if fused else (x_ref, None)
    gather_sems = [take(Gather.COUNT) for _ in range(count)]
    steps = o_ref.shape[0] // block
    ring = Ring(mesh)
    gathers = [
        Gather(ring, full_ref, sems, piece_ref=piece_ref)
        for piece_ref, full_ref, sems in zip(piece_refs, full_refs, gather_sems)
    ]
    rows = Rows(ring, place, 1, near_ref, rows_ref, far_ref, take(5))
    ring.greet_all()
    first = each = 0
    if fused:
        me, members = place.member(), place.members
        here = o_ref.shape[0] // members
        span = functools.partial(row_span, here)
        to_heads = Swap(place, lambda rank: x_ref.at[rank], lambda rank: qkv_ref.at[span(rank)], take(2))
        to_rows = Swap(place, lambda rank: o_ref.at[span(rank)], lambda rank: mixed_ref.at[rank], take(2))
        (local,) = take(1)
        each = here // block
        first = each * (me + 1)
        to_heads.begin()
        keep(x_ref.at[me], qkv_ref.at[span(me)], local)

    keys = qkv_ref.shape[0]
    column = lax.broadcasted_iota(jnp.int32, (1, keys), 1)
    bias = jnp.where(column < PATCH_ROWS + length_ref[0], 0.0, MASKED).astype(F32)
    lanes = lax.broadcasted_iota(jnp.int32, (1, 128), 1)

    def phases(step):
        for number, when in enumerate(GATHER_STEPS):

            @pl.when(step == when)
            def _():
                for gather in gathers:
                    gather.phase(number)

        for item, when in enumerate(GIVE_STEPS):
            pl.when(step == when)(functools.partial(rows.give, item))
        if fused:
            pl.when(step == 0)(to_heads.arrive)
            for member in range(1, members):
                pl.when(step == member * each)(lambda member=member: to_rows.copy(member).start())

    @pl.loop(0, steps)
    def _(step):
        phases(step)
        turn = lax.rem(step + first, steps)
        here_rows = pl.ds(pl.multiple_of(turn * block, 16), block)
        kept = jnp.zeros((block, 128), F32)
        for pair in range(pairs):
            base = pair * 3 * PAIR
            out, logs = forward_pair(
                qkv_ref[here_rows, base : base + PAIR],
                qkv_ref[:, base + PAIR : base + 2 * PAIR],
                qkv_ref[:, base + 2 * PAIR : base + 3 * PAIR],
                bias,
            )
            o_ref[here_rows, pair * PAIR : (pair + 1) * PAIR] = out.astype(LOW)
            for head in range(2):
                kept = jnp.where(lanes == pair * 2 + head, logs[head], kept)
        log_ref[here_rows] = kept

    rows.arrive()
    rows.end_given()
    if fused:
        keep(o_ref.at[span(me)], mixed_ref.at[me], local)
        to_heads.end()
        to_rows.arrive()
        to_rows.end()


def row_span(rows, rank):
    return pl.ds(pl.multiple_of(rank * rows, 16), rows)


def keep(source, target, sem):
    copy = pltpu.make_async_copy(source, target, sem)
    copy.start()
    copy.wait()


GATHER_STEPS = (0, 2, 6, 8, 9, 9)
GIVE_STEPS = (4, 4, 5, 5)


def joint_forward(mesh, place, x, length, pieces, near, far, fused):
    width = x.shape[-1]
    rows = x.shape[-2] * (place.members if fused else 1)
    pairs = width // (3 * PAIR)
    block = 208
    ranks = mesh.shape["mp"]
    fulls = full_shapes(ranks, pieces)
    held, away = pl.BlockSpec(memory_space=pltpu.VMEM), pl.BlockSpec(memory_space=pl.ANY)
    more, sems = (), []
    if fused:
        more = (
            jax.ShapeDtypeStruct((rows, width), LOW),
            jax.ShapeDtypeStruct((place.members, rows // place.members, pairs * PAIR), LOW),
        )
        sems = [*Swap.scratch(place.members), *Swap.scratch(place.members), pltpu.SemaphoreType.DMA]
    out = pl.pallas_call(
        functools.partial(joint_forward_kernel, mesh, place, pairs, block, len(pieces), fused),
        out_shape=(
            jax.ShapeDtypeStruct((rows, pairs * PAIR), LOW),
            jax.ShapeDtypeStruct((rows, 128), F32),
            jax.ShapeDtypeStruct((2,) + near.shape[1:], near.dtype),
        )
        + fulls
        + more,
        in_specs=[pl.BlockSpec(memory_space=pltpu.SMEM), held, away, away]
        + [held] * len(pieces),
        out_specs=(held,) * 3 + (away,) * len(fulls) + (held,) * len(more),
        scratch_shapes=Gather.scratch(ranks) * len(pieces) + Rows.scratch(place.items) + sems,
        cost_estimate=cost(40),
        compiler_params=pltpu.CompilerParams(
            collective_id=8, has_side_effects=True, vmem_limit_bytes=VMEM_BYTES
        ),
    )(length, x, near, far, *pieces)
    heads, logs, given = out[:3]
    fulls = out[3 : 3 + len(fulls)]
    qkv, mixed = out[-2:] if fused else (x, to_rows(place, heads, 3))
    return qkv, heads, logs, mixed, given, fulls


def backward_head(q, k, v, grad, head, log, delta, limit):
    scores = dot_rows(k, half_of(q, head))
    if limit is not None:
        row = lax.broadcasted_iota(jnp.int32, (scores.shape[0], 1), 0)
        scores = jnp.where(row < limit, scores, MASKED)
    if log is None:
        top = jnp.max(scores, 0, keepdims=True)
        expon = jnp.exp(scores - top)
        probs = expon / jnp.sum(expon, 0, keepdims=True)
    else:
        probs = jnp.exp(scores - log)
    grad_probs = dot_rows(v, half_of(grad, head))
    if delta is None:
        delta = jnp.sum(probs * grad_probs, 0, keepdims=True)
    grad_scores = (probs * (grad_probs - delta)).astype(LOW)
    grad_v = dot(probs.astype(LOW), grad)
    grad_k = dot(grad_scores, q)
    k_turned = k[:, head * HEAD : (head + 1) * HEAD].T
    grad_q = dot(k_turned, grad_scores)
    return grad_q, grad_k, grad_v


def joint_backward_kernel(
    mesh, place, pairs, block, count, fused, length_ref, qkv_ref, heads_ref, out_ref, log_ref, rows_ref, *refs
):
    def take(count):
        nonlocal refs
        taken, refs = refs[:count], refs[count:]
        return taken

    matrix_refs, (swapped_ref,) = take(count), take(1)
    piece_refs, (gone_ref,) = take(count), take(1)
    total_ref, stat_ref = take(2)
    steps = qkv_ref.shape[0] // block
    ring = Ring(mesh)
    ring.greet_all()
    backs, sent_ref = [], swapped_ref
    if fused:
        sent_ref, got_ref, local = take(3)
        me, members = place.member(), place.members
        span = functools.partial(row_span, got_ref.shape[0] // members)
        own_ref, heads_ref = heads_ref, got_ref
        to_heads = Swap(place, lambda rank: own_ref.at[rank], lambda rank: got_ref.at[span(rank)], take(2))
        backs = [
            Swap(
                place,
                lambda rank, pair=pair: sent_ref.at[pair, span(rank)],
                lambda rank, pair=pair: swapped_ref.at[rank, pair],
                take(2),
            )
            for pair in range(pairs)
        ]
        to_heads.begin()
        keep(own_ref.at[me], got_ref.at[span(me)], local)
    home = Home(ring, place, 1, rows_ref, gone_ref, take(3))
    line_refs = take(count)
    sums = each_of(Hops, ring, matrix_refs, line_refs, take(Hops.COUNT * count))
    alongs = each_of(Line, ring, line_refs, piece_refs, take(Line.COUNT * count))
    home.begin()

    def phases(whole_step):
        for number, when in enumerate(REDUCTION_STEPS[:4]):

            @pl.when(whole_step == when)
            def _():
                for one in sums:
                    one.phase(number)
                if number == 3:
                    for along in alongs:
                        along.begin()

        @pl.when(whole_step == REDUCTION_STEPS[4])
        def _():
            for one in sums:
                one.end()
            for along in alongs:
                along.total()
                along.end()
            home.end()

        if fused:
            pl.when(whole_step == 0)(to_heads.arrive)

    @pl.loop(0, pairs * steps)
    def _(whole_step):
        phases(whole_step)
        pair, step = whole_step // steps, lax.rem(whole_step, steps)
        here = pl.ds(pl.multiple_of(step * block, 16), block)

        def lanes_of(part):
            return pl.ds(pl.multiple_of(pair * 3 * PAIR + part * PAIR, PAIR), PAIR)

        limit = PATCH_ROWS + length_ref[0] - step * block
        q = qkv_ref[:, lanes_of(0)] * jnp.asarray(0.125, LOW)
        k, v = qkv_ref[here, lanes_of(1)], qkv_ref[here, lanes_of(2)]
        own_lanes = pl.ds(pl.multiple_of(pair * PAIR, PAIR), PAIR)
        grad = heads_ref[:, own_lanes]

        @pl.when(step == 0)
        def _():
            total_ref[...] = jnp.zeros_like(total_ref)
            rows = lax.broadcasted_iota(jnp.int32, (8, PAIR), 0)
            lanes = lax.broadcasted_iota(jnp.int32, (8, PAIR), 1)
            which = jnp.where(lanes == pair * 2 + rows, 1.0, 0.0).astype(F32)
            own = jnp.where((lanes // HEAD) == rows, 1.0, 0.0).astype(F32)
            product = wide(heads_ref[:, own_lanes]) * wide(out_ref[:, own_lanes])
            exact = functools.partial(
                lax.dot_general,
                dimension_numbers=(((1,), (1,)), ((), ())),
                precision=lax.Precision.HIGHEST,
                preferred_element_type=F32,
            )
            stat_ref[0] = exact(which, log_ref[...])
            stat_ref[1] = exact(own, product)

        grads_k, grads_v = [], []
        for head in range(2):
            grad_q, grad_k, grad_v = backward_head(
                q, k, v, grad, head, stat_ref[0, head : head + 1], stat_ref[1, head : head + 1], limit
            )
            total_ref[head * HEAD : (head + 1) * HEAD] += grad_q
            grads_k.append(grad_k)
            grads_v.append(grad_v)
        sent_ref[pair, here, PAIR : 2 * PAIR] = joined(*grads_k).astype(LOW)
        sent_ref[pair, here, 2 * PAIR : 3 * PAIR] = joined(*grads_v).astype(LOW)

        @pl.when(step == steps - 1)
        def _():
            sent_ref[pair, :, 0:PAIR] = (total_ref[...].T * 0.125).astype(LOW)

        for index, back in enumerate(backs):

            @pl.when(whole_step == (index + 1) * steps - 1)
            def _():
                back.begin()
                keep(sent_ref.at[index, span(me)], swapped_ref.at[me, index], local)

    if fused:
        to_heads.end()
    for back in backs:
        back.arrive()
        back.end()


REDUCTION_STEPS = (0, 2, 11, 14, 19)


def joint_backward(mesh, place, qkv, length, grad, out, log, blocks, matrices, fused):
    rows, width = qkv.shape
    pairs, members = width // (3 * PAIR), place.members
    block = 208
    gone = jax.ShapeDtypeStruct((place.items,) + blocks.shape[1:], blocks.dtype)
    held = pl.BlockSpec(memory_space=pltpu.VMEM)
    swap_scratch, shape = [], (pairs, rows, 3 * PAIR)
    if fused:
        shape = (members, pairs, rows // members, 3 * PAIR)
        swap_scratch = [
            pltpu.VMEM((pairs, rows, 3 * PAIR), LOW),
            pltpu.VMEM((rows, pairs * PAIR), LOW),
            pltpu.SemaphoreType.DMA,
        ] + Swap.scratch(members) * (1 + pairs)
    grads, *more = pl.pallas_call(
        functools.partial(joint_backward_kernel, mesh, place, pairs, block, len(matrices), fused),
        out_shape=(jax.ShapeDtypeStruct(shape, LOW),) + piece_shapes(matrices) + (gone,),
        in_specs=[
            pl.BlockSpec(memory_space=pltpu.SMEM),
            *[held] * (5 + len(matrices)),
        ],
        out_specs=(held,) * (2 + len(matrices)),
        scratch_shapes=[pltpu.VMEM((PAIR, rows), F32), pltpu.VMEM((2, 8, rows), F32)]
        + swap_scratch
        + Home.scratch(place.items)
        + [pltpu.VMEM(line.shape, LOW) for line in line_shapes(matrices)]
        + scratch_of(Hops, matrices)
        + scratch_of(Line, matrices),
        cost_estimate=cost(66),
        compiler_params=pltpu.CompilerParams(
            collective_id=6, has_side_effects=True, vmem_limit_bytes=VMEM_BYTES
        ),
    )(length, qkv, grad, out, log, blocks, *matrices)
    if not fused:
        grads = to_rows(place, grads.swapaxes(0, 1).reshape(rows, width), 5)
        grads = grads.reshape(members, -1, pairs, 3 * PAIR).swapaxes(1, 2)
    return grads, more


def within_forward_kernel(pairs, length_ref, x_ref, o_ref):
    def group(rows, bias):
        for pair in range(pairs):
            base = pair * 3 * PAIR
            q, k, v = (x_ref[rows, base + part * PAIR : base + (part + 1) * PAIR] for part in range(3))
            out, _ = forward_pair(q, k, v, bias)
            o_ref[rows, pair * PAIR : (pair + 1) * PAIR] = out.astype(LOW)

    @pl.loop(0, VIEWS)
    def _(view):
        group(pl.ds(pl.multiple_of(view * PATCH, 16), PATCH), None)

    column = lax.broadcasted_iota(jnp.int32, (1, TEXT), 1)
    bias = jnp.where(column < length_ref[0], 0.0, MASKED).astype(F32)
    group(pl.ds(PATCH_ROWS, TEXT), bias)


def within_forward(qkv, length):
    rows, width = qkv.shape
    pairs = width // (3 * PAIR)
    held = pl.BlockSpec(memory_space=pltpu.VMEM)
    return pl.pallas_call(
        functools.partial(within_forward_kernel, pairs),
        out_shape=jax.ShapeDtypeStruct((rows, pairs * PAIR), LOW),
        in_specs=[pl.BlockSpec(memory_space=pltpu.SMEM), held],
        out_specs=held,
        cost_estimate=cost(10),
        compiler_params=pltpu.CompilerParams(vmem_limit_bytes=VMEM_BYTES),
    )(length, qkv)


def within_backward_kernel(mesh, place, pairs, count, fused, length_ref, x_ref, grad_ref, *refs):
    matrix_refs, swapped_ref, refs = refs[:count], refs[count], refs[count + 1 :]
    line_refs, refs = refs[:count], refs[count:]
    ring = Ring(mesh)
    ring.greet_lines()
    o_ref = swapped_ref
    if fused:
        (sent_ref, got_ref, local), refs = refs[:3], refs[3:]
        me = place.member()
        span = functools.partial(row_span, got_ref.shape[0] // place.members)
        own_ref, o_ref = grad_ref, sent_ref
        to_heads = Swap(
            place, lambda rank: own_ref.at[rank], lambda rank: got_ref.at[span(rank)], refs[:2]
        )
        back = Swap(
            place, lambda rank: sent_ref.at[span(rank)], lambda rank: swapped_ref.at[rank], refs[2:4]
        )
        refs = refs[4:]
        to_heads.begin()
        keep(own_ref.at[me], got_ref.at[span(me)], local)
        grad_ref = got_ref
    sums = each_of(Hops, ring, matrix_refs, line_refs, refs)

    def every(number):
        for one in sums:
            one.phase(number)

    def group(rows, limit):
        for pair in range(pairs):
            base = pair * 3 * PAIR
            q, k, v = (x_ref[rows, base + part * PAIR : base + (part + 1) * PAIR] for part in range(3))
            q = q * jnp.asarray(0.125, LOW)
            grad = grad_ref[rows, pair * PAIR : (pair + 1) * PAIR]
            both = [backward_head(q, k, v, grad, head, None, None, limit) for head in range(2)]
            grad_q = jnp.concatenate([both[0][0], both[1][0]], 0).T * 0.125
            o_ref[rows, base : base + PAIR] = grad_q.astype(LOW)
            o_ref[rows, base + PAIR : base + 2 * PAIR] = joined(both[0][1], both[1][1]).astype(LOW)
            o_ref[rows, base + 2 * PAIR : base + 3 * PAIR] = joined(both[0][2], both[1][2]).astype(LOW)

    every(0)
    if fused:
        to_heads.arrive()

    @pl.loop(0, VIEWS)
    def _(view):
        group(pl.ds(pl.multiple_of(view * PATCH, 16), PATCH), None)
        for number, when in ((1, 0), (2, 3)):
            pl.when(view == when)(functools.partial(every, number))

    group(pl.ds(PATCH_ROWS, TEXT), length_ref[0])
    if fused:
        back.begin()
        keep(sent_ref.at[span(me)], swapped_ref.at[me], local)
    every(3)
    for one in sums:
        one.end()
    if fused:
        to_heads.end()
        back.arrive()
        back.end()


def within_backward(mesh, place, qkv, length, grad, matrices, fused):
    rows, width = qkv.shape
    pairs, members = width // (3 * PAIR), place.members
    held = pl.BlockSpec(memory_space=pltpu.VMEM)
    swap_scratch, shape = [], (rows, width)
    if fused:
        shape = (members, rows // members, width)
        swap_scratch = [
            pltpu.VMEM((rows, width), LOW),
            pltpu.VMEM((rows, pairs * PAIR), LOW),
            pltpu.SemaphoreType.DMA,
        ] + Swap.scratch(members) * 2
    grads, *lines = pl.pallas_call(
        functools.partial(within_backward_kernel, mesh, place, pairs, len(matrices), fused),
        out_shape=(jax.ShapeDtypeStruct(shape, LOW),) + line_shapes(matrices),
        in_specs=[pl.BlockSpec(memory_space=pltpu.SMEM)] + [held] * (2 + len(matrices)),
        out_specs=(held,) * (1 + len(matrices)),
        scratch_shapes=swap_scratch + scratch_of(Hops, matrices),
        cost_estimate=cost(30),
        compiler_params=pltpu.CompilerParams(
            collective_id=7, has_side_effects=True, vmem_limit_bytes=VMEM_BYTES
        ),
    )(length, qkv, grad, *matrices)
    if not fused:
        grads = to_rows(place, grads, 5)
    return grads.reshape(members, -1, 1, width).swapaxes(1, 2), lines


def layer_norm(values, scale_vec, shift_vec):
    center = jnp.mean(values, -1, keepdims=True)
    offset = values - center
    spread = jnp.mean(offset * offset, -1, keepdims=True)
    return offset * lax.rsqrt(spread + 1e-05) * scale_vec + shift_vec


def times_turned(left, weight):
    return lax.dot_general(left, weight, (((1,), (1,)), ((), ())), preferred_element_type=F32)


def times(left, weight):
    return lax.dot_general(left, weight, (((1,), (0,)), ((), ())), preferred_element_type=F32)


def over_rows(left, right):
    return lax.dot_general(left, right, (((0,), (0,)), ((), ())), preferred_element_type=F32)


def projection(normed, params):
    return jnp.einsum("sd,red->rse", normed, params["qkv"], preferred_element_type=F32).astype(LOW)


def layer_end(source, mixed, params):
    branch = jnp.einsum("rse,red->sd", mixed, params["out"], preferred_element_type=F32)
    middle = source + branch + params["bias_out"]
    second = layer_norm(middle, params["gain_two"], params["bias_two"]).astype(LOW)
    hidden_pre = times_turned(second, params["up"]) + params["bias_up"]
    hidden = jax.nn.gelu(hidden_pre).astype(LOW)
    result = middle + times(hidden, params["down"]) + params["bias_down"]
    return result, (middle, second, hidden_pre, hidden)


def first_norm(source, params):
    return layer_norm(source, params["gain_one"], params["bias_one"]).astype(LOW)


def first_forward(place, source, length, params, ready):
    normed = first_norm(source, params)
    if ready:
        qkv, mixed = ready
    else:
        qkv = to_heads(place, projection(normed, params), 2)
        mixed = to_rows(place, within_forward(qkv, length), 3)
    result, kept = layer_end(source, mixed, params)
    return result, (source, normed, qkv, None, None, mixed) + kept


def second_forward(mesh, place, source, length, params, pieces, near, far, fused):
    normed = first_norm(source, params)
    x = projection(normed, params)
    if not fused:
        x = to_heads(place, x, 2)
    qkv, heads, logs, mixed, given, fulls = joint_forward(
        mesh, place, x, length, pieces, near, far, fused
    )
    params.update(matrices_of(place, ("out", "up", "down"), fulls))
    result, kept = layer_end(source, mixed, params)
    return result, given, (source, normed, qkv, heads, logs, mixed) + kept


def matrices_of(place, names, fulls):
    found = {}
    for name, full in zip(names, fulls):
        width = full.shape[-1]
        if name == "qkv":
            heads = 8 * full.shape[-2] // (3 * HEAD)
            full = full.reshape(-1, 2 // heads, 3, heads, HEAD, width).swapaxes(1, 2)
        if name in ("qkv", "out"):
            found[name] = full.reshape(place.members, -1, width)
        else:
            found[name] = full.reshape(-1, width)
    return found


def layer_backward(mesh, place, upstream, length, params, kept, pack, fused, blocks=None):
    source, normed, qkv, mixed_heads, logs, mixed, middle, second, hidden_pre, hidden = kept
    up_low = upstream.astype(LOW)
    grad_down = over_rows(hidden, up_low)
    grad_hidden = times_turned(up_low, params["down"])
    grad_pre = jax.vjp(jax.nn.gelu, hidden_pre)[1](grad_hidden)[0].astype(LOW)
    grad_up_bias = jnp.sum(grad_pre.astype(F32), 0)
    grad_up = over_rows(grad_pre, second)
    grad_second = times(grad_pre, params["up"])
    norm_pull = jax.vjp(layer_norm, middle, params["gain_two"], params["bias_two"])[1]
    part_middle, grad_gain_two, grad_bias_two = norm_pull(grad_second)
    grad_middle = upstream + part_middle
    mid_low = grad_middle.astype(LOW)
    grad_out = jnp.einsum("rse,sd->red", mixed, mid_low, preferred_element_type=F32)
    grad_mixed = jnp.einsum("sd,red->rse", mid_low, params["out"], preferred_element_type=F32)
    grad_heads = grad_mixed.astype(LOW)
    if not fused:
        grad_heads = to_heads(place, grad_heads, 4)
    later = [pack(m) for m in (grad_out, grad_up, grad_down)]
    if blocks is not None:
        grad_projected, done = joint_backward(
            mesh, place, qkv, length, grad_heads, mixed_heads, logs, blocks, later, fused
        )
    else:
        grad_projected, done = within_backward(mesh, place, qkv, length, grad_heads, later, fused)
    members, pairs = grad_projected.shape[:2]
    weight = params["qkv"].reshape(members, pairs, -1, params["qkv"].shape[-1])
    grad_qkv = jnp.einsum("rpse,sd->rped", grad_projected, normed, preferred_element_type=F32)
    grad_normed = jnp.einsum("rpse,rped->sd", grad_projected, weight, preferred_element_type=F32)
    first_pull = jax.vjp(layer_norm, source, params["gain_one"], params["bias_one"])[1]
    part_source, grad_gain_one, grad_bias_one = first_pull(grad_normed)
    vectors = (
        grad_gain_one,
        grad_bias_one,
        jnp.sum(grad_middle, 0),
        grad_gain_two,
        grad_bias_two,
        jnp.sum(upstream, 0),
        grad_up_bias,
    )
    return grad_middle + part_source, grad_qkv, done, jnp.concatenate(vectors)


def pick(x, index, axis):
    return lax.dynamic_index_in_dim(x, index, axis, keepdims=False)


def ends_kernel(zero_ref, one_ref, o_ref):
    section = lax.axis_index("section")
    for index, ref in enumerate((zero_ref, one_ref)):

        @pl.when(section == index)
        def _():
            o_ref[...] = ref[...].astype(F32)


def ends_of(zero, one):
    block = (1,) + zero.shape[1:]
    spec = pl.BlockSpec(block, lambda i: (i, 0, 0))
    return pl.pallas_call(
        ends_kernel,
        grid=(zero.shape[0],),
        out_shape=jax.ShapeDtypeStruct(zero.shape, F32),
        in_specs=[spec] * 2,
        out_specs=spec,
        cost_estimate=cost(3),
        compiler_params=pltpu.CompilerParams(vmem_limit_bytes=VMEM_BYTES),
    )(zero, one)


def far_groups(dps):
    return [[low + 4 * high for high in range(dps // 4)] for low in range(4)]


def per_device(mesh, inputs, text_lengths, *weights):
    (gain_one, bias_one, weight_qkv, weight_out, bias_out) = weights[:5]
    (gain_two, bias_two, weight_up, bias_up, weight_down, bias_down) = weights[5:]
    items, block_rows, width = inputs.shape[1:]
    place = Place(mesh, items)
    ranks = place.ranks
    section, pair, core, mp = place.here()
    heads_here = weight_qkv.shape[2]
    all_heads = heads_here * ranks
    per_pair = 2 // heads_here
    hidden_here = bias_up.shape[1]

    own = (
        weight_qkv[0].reshape(width, heads_here, 3, HEAD).transpose(2, 1, 3, 0),
        weight_out[0],
        weight_up[0].T,
        weight_down[0],
    )
    own = [w.reshape(2, 2, 2, -1, width) for w in own]
    vec = [w[0] for w in (gain_one, bias_one, bias_out, gain_two, bias_two, bias_down, bias_up)]
    vec.append(text_lengths.astype(F32))
    vec = jnp.stack([jnp.pad(v, (0, width - v.shape[0])) for v in vec])

    fused = heads_here == 2 and own[0].shape[3] % 16 == 0 and (2 * block_rows) % FirstAttention.BLOCK == 0
    (arrived, vecs, staged), first, first_of_second, second, ready = start(
        mesh, place, inputs[0], vec, own, fused
    )
    mine = vecs[section * ranks + mp, 7]
    lengths = jnp.where(core == section, mine, vecs[2 * ranks, 7])
    length = pick(lengths, mp // place.chips, 0).astype(jnp.int32)[None]

    def params_of(layer):
        names = ("gain_one", "bias_one", "bias_out", "gain_two", "bias_two", "bias_down")
        rows = vecs[layer * ranks : (layer + 1) * ranks]
        found = {name: rows[0, i] for i, name in enumerate(names)}
        found["bias_up"] = rows[:, 6, :hidden_here].reshape(-1)
        return found

    def pack(grad):
        return grad.astype(LOW).reshape(ranks, 8, -1, width)

    def pack_qkv(grad):
        grad = grad.astype(LOW).reshape(all_heads // 2, 3, per_pair, heads_here, HEAD, width)
        return pack(grad.swapaxes(1, 2))

    params = (params_of(0), params_of(1))
    params[0].update(matrices_of(place, ("qkv", "out", "up", "down"), first))
    source = arrived.reshape(-1, width).astype(F32)
    params[1].update(matrices_of(place, ("qkv",), first_of_second))
    boundary, kept_zero = first_forward(place, source, length, params[0], ready)
    source = boundary.astype(LOW).astype(F32)
    result, cotangent, kept_one = second_forward(
        mesh, place, source, length, params[1], second, inputs[0], staged, fused
    )
    results = result.astype(LOW).reshape(2, block_rows, width)
    upstream = cotangent.reshape(-1, width).astype(F32)
    grad_boundary, grad_qkv_one, done, vectors_one = layer_backward(
        mesh, place, upstream, length, params[1], kept_one, pack, fused, results
    )
    *done, results = done
    upstream = grad_boundary.astype(LOW).astype(F32)
    grad_source, grad_qkv_zero, lines, vectors_zero = layer_backward(
        mesh, place, upstream, length, params[0], kept_zero, pack, fused
    )
    rows = grad_source.astype(LOW).reshape(2, block_rows, width)
    vectors = jnp.stack([vectors_zero, vectors_one]).reshape(2, -1, width)
    grads = [pack_qkv(grad_qkv_zero), pack_qkv(grad_qkv_one)]
    layers = ((0, 0), (1, 0), (0, 1), (0, 2), (0, 3), (1, 1), (1, 2), (1, 3))
    gone, sums, *matrices = finish(mesh, place, rows, vectors, grads, lines, done, layers)
    dps = mesh.shape["dp"]
    if dps > 4:
        sums, *matrices = (
            lax.psum(m, "dp", axis_index_groups=far_groups(dps)) for m in (sums, *matrices)
        )

    ends = ends_of(gone, results)[None]
    parts = [m.reshape(-1, width).astype(F32) for m in matrices]
    sums = pick(sums, section, 0).reshape(-1)
    small = [sums[i * width : (i + 1) * width][None] for i in range(6)]
    grad_bias_up = lax.dynamic_slice_in_dim(sums, 6 * width + mp * hidden_here, hidden_here)[None]
    grad_qkv = parts[0].reshape(3, heads_here, HEAD, width).transpose(3, 1, 0, 2)
    grad_qkv = grad_qkv.reshape(1, width, heads_here, 3 * HEAD)
    return (
        ends,
        small[0],
        small[1],
        grad_qkv,
        parts[1].reshape(1, heads_here, HEAD, width),
        small[2],
        small[3],
        small[4],
        parts[2].T[None],
        grad_bias_up,
        parts[3][None],
        small[5],
    )


def solution(mesh):
    vector = P("section", None)
    ends = P("section", "dp", "mp", None)
    qkv = P("section", None, "mp", None)
    out = P("section", "mp", None, None)
    up = P("section", None, "mp")
    up_bias = P("section", "mp")
    down = P("section", "mp", None)
    params = (vector, vector, qkv, out, vector, vector, vector, up, up_bias, down, vector)
    return jax.shard_map(
        functools.partial(per_device, mesh),
        mesh=mesh,
        in_specs=(ends, P("dp")) + params,
        out_specs=(ends,) + params,
        check_vma=False,
    )
```

time: 1140 us -> 483 us (0.42)
  waiting for transfers between devices: 344 us -> 0 us
  Pallas kernels: 506 us -> 347 us
  blocking collectives: 86 us -> 0 us
  other arithmetic: 47.5 us -> 21.6 us
  matrix products: 113 us -> 91.1 us
  between operations: 15.8 us -> 2.61 us
    reduce_scatter x4 -> x0, waiting for transfers between devices: 253 us -> none  [per_device(): part = lax.psum_scatter(both, ('section', 'mp'), scatter_dimension=0)]
    pallas_call x14 -> x6, Pallas kernels: 506 us -> 347 us  [the longest x1 87.3 us: joint_backward(): pl.pallas_call(functools.partial(joint_backward_kernel, mesh, place, pair...]
    all_gather x4 -> x0, waiting for transfers between devices: 89 us -> none  [per_device(): full = [lax.all_gather(w, ('section', 'mp'), tiled=True) for w in own]]
    psum x1 -> x0, blocking collectives: 48.1 us -> none  [per_device(): lax.psum(jnp.stack([vectors_zero, vectors_one]), ('section', 'dp', 'mp'))]
    dot_general x0 -> x11, matrix products: none -> 34.7 us  [the longest x2 8.97 us: layer_backward(): jnp.einsum('rpse,sd->rped', grad_projected, normed, preferred_element_typ...]
    all_gather x1 -> x0, blocking collectives: 32.7 us -> none  [per_device(): lax.all_gather(jnp.concatenate([w[0] for w in (gain_one, bias_one, bias_o...]
    dot_general x8 -> x4, matrix products: 42.3 us -> 19.6 us  [over_rows(): lax.dot_general(left, right, (((0,), (0,)), ((), ())), preferred_element_...]
    dot_general x8 -> x4, matrix products: 32.2 us -> 13.5 us  [times(): lax.dot_general(left, weight, (((1,), (0,)), ((), ())), preferred_element...]
  transfers between devices with their start and end apart: 9 -> 0, of which waited for: 6 -> 0; matrix products, arithmetic and copies ran while one was open for 9% -> 0% of each run, Pallas kernels for 16% -> 0%
where the time goes in v4:
time: 483 us; the launch traced here: 479 us
  Pallas kernels  347 us (72%)
  matrix products  91.1 us (19%)
  other arithmetic  21.6 us (4%)
  local copies, waits for them, and re-layouts  16.3 us (3%)
    pallas_call x1, Pallas kernels, joint_backward(): pl.pallas_call(functools.partial(joint_backward_kernel, mesh, place, pair...  87.3 us
    pallas_call x1, Pallas kernels, start(): pl.pallas_call(functools.partial(start_kernel, mesh, place, count, fused)...  83.9 us
    pallas_call x1, Pallas kernels, finish(): pl.pallas_call(functools.partial(finish_kernel, mesh, place, layers, len(...  67.9 us
    pallas_call x1, Pallas kernels, joint_forward(): pl.pallas_call(functools.partial(joint_forward_kernel, mesh, place, pairs...  67.4 us
    pallas_call x1, Pallas kernels, within_backward(): pl.pallas_call(functools.partial(within_backward_kernel, mesh, place, pai...  35.7 us
    dot_general x4, matrix products, times_turned(): lax.dot_general(left, weight, (((1,), (1,)), ((), ())), preferred_element...  23.3 us
    dot_general x4, matrix products, over_rows(): lax.dot_general(left, right, (((0,), (0,)), ((), ())), preferred_element_...  19.6 us
    dot_general x4, matrix products, times(): lax.dot_general(left, weight, (((1,), (0,)), ((), ())), preferred_element...  13.5 us

profile of v4, /device:TPU:0, one launch (start us, length us, event | category | flops | bytes accessed | tf_op | source)
XLA Modules:
  0.0 478.6 jit_solution(12294698818442408972)
XLA Ops:
  6.5 83.9 %shard_map.220 = (bf16[2,520,512]{2,1,0:T(8,128)(2,1)}, f32[9,8,512]{2,1,0:T(8,128)}, bf16[4,520,512]{2,1,0:T(8,128)(2,1)}, bf16[4,2,2,2,48,512]{5,4,3,2,1,0:T(8...) custom-call(bf16[4,520,512]{2,1,0:T(8,128)(2,1)} %bitcast.208, ...), custom_call_target="tpu_custom_call" | custom-call | flops 60000002048 | tf_op jit(solution)/shard_map/pallas_call | solution.py:696
  95.2 2.6 fusion.64
  103.2 3.1 convert_reduce_fusion.2
  107.8 3.7 fusion.14.x_ref
  111.4 67.4 %shard_map.221 = (bf16[2080,256]{1,0:T(8,128)(2,1)}, f32[2080,128]{1,0:T(8,128)}, bf16[2,520,512]{2,1,0:T(8,128)(2,1)}, bf16[4,2,2,2,16,512]{5,4,3,2,1,0:T(8,128...) custom-call(s32[1]{0:T(128)} %bitcast.10.length_ref, ...), custom_call_target="tpu_custom_call" | custom-call | flops 40000000000 | tf_op jit(solution)/shard_map/pallas_call | solution.py:1350
  185.2 8.4 %convert_reduce_fusion = (f32[2048]{0:T(1024)}, bf16[1040,2048]{1,0:T(8,128)(2,1)S(1)}) fusion(f32[1040,2048]{1,0:T(8,128)S(1)} %convolution_add_fusion, bf16[1040,512]{1,0:T(8,128)(2,1)S(1)} %bitcast.162, bf16[2048,512]{1,0:T(8,128)(2,1)S(1)} %bitcast.217), kind=kOutput, calls=%fused_computation.20 | convolution fusion | flops 2227894272 | bytes 15949824 | tf_op jit(solution)/shard_map/dot_general | solution.py:1689
  193.6 3.4 multiply_reduce_fusion
  200.8 4.0 fusion.26
  206.5 4.9 %convolution_convert_fusion.4 = bf16[2048,512]{1,0:T(8,128)(2,1)} fusion(bf16[1040,2048]{1,0:T(8,128)(2,1)S(1)} %get-tuple-element.140, f32[1040,512]{1,0:T(8,128)S(1)} %get-tuple-element.134, f32[512]{0:T(512)S(1)} %bitcast.203, f32[512]{0:T(512)S(1)} %bitcast.193, f32[1040]{0:T(1024)S(1)} %fusion.50, f32[1040]{0:T(1024)S(1)} %broadcast_multiply_fusion), kind=kOutput, calls=%fused_computation.52 | convolution fusion | flops 2184749056 | bytes 8499328 | tf_op jit(solution)/shard_map/dot_general | solution.py:1697
  211.4 4.9 %convolution_convert_fusion.3 = bf16[2048,512]{1,0:T(8,128)(2,1)} fusion(bf16[1040,512]{1,0:T(8,128)(2,1)S(1)} %bitcast.163, f32[1040,2048]{1,0:T(8,128)S(1)} %convolution_add_fusion), kind=kOutput, calls=%fused_computation.51 | convolution fusion | flops 2201255936 | bytes 11681792 | tf_op jit(solution)/shard_map/dot_general | solution.py:1697
  216.2 87.3 %shard_map.222 = (bf16[2,2,1040,384]{3,2,1,0:T(8,128)(2,1)}, bf16[16,512]{1,0:T(8,128)(2,1)}, bf16[64,512]{1,0:T(8,128)(2,1)}, bf16[64,512]{1,0:T(8,128)(2,1)}, bf16[4,520,512]{2,1,0:T(8,128)(2,1)}) custom-call(s32[1]{0:T(128)} %bitcast.10.length_ref, bf16[2080,768]{1,0:T(8,128)(2,1)} %get-tuple-element.64.qkv_ref, bf16[2,1040,256]{2,1,0:T(8,128)(2,1)} %fusion.28.heads_ref, ...), custom_call_target="tpu_custom_call" | custom-call | flops 65999998976 | tf_op jit(solution)/shard_map/pallas_call | solution.py:1535
  303.6 4.0 fusion.57
  310.4 9.9 %convert_reduce_fusion.1 = (f32[2048]{0:T(1024)S(1)}, bf16[1040,2048]{1,0:T(8,128)(2,1)S(1)}) fusion(f32[1040,2048]{1,0:T(8,128)} %copy-done.53, bf16[1040,512]{1,0:T(8,128)(2,1)S(1)} %add_convert_fusion.2, bf16[2048,512]{1,0:T(8,128)(2,1)S(1)} %bitcast.216), kind=kOutput, calls=%fused_computation.21 | convolution fusion | flops 2227894272 | bytes 15949824 | tf_op jit(solution)/shard_map/dot_general | solution.py:1689
  320.3 3.0 multiply_reduce_fusion.1
  328.0 4.0 fusion.29.grad_ref
  333.9 5.0 %convolution_convert_fusion.2 = bf16[2048,512]{1,0:T(8,128)(2,1)} fusion(bf16[1040,2048]{1,0:T(8,128)(2,1)S(1)} %copy-done.55, f32[1040,512]{1,0:T(8,128)S(1)} %copy-done.4, f32[512]{0:T(512)S(1)} %bitcast.201, f32[512]{0:T(512)S(1)} %bitcast.189, f32[1040]{0:T(1024)S(1)} %copy-done.26, f32[1040]{0:T(1024)S(1)} %copy-done.20), kind=kOutput, calls=%fused_computation.50 | convolution fusion | flops 2184749056 | bytes 8499328 | tf_op jit(solution)/shard_map/dot_general | solution.py:1697
  338.8 4.9 %convolution_convert_fusion.1 = bf16[2048,512]{1,0:T(8,128)(2,1)} fusion(bf16[1040,512]{1,0:T(8,128)(2,1)S(1)} %copy-done.8, f32[1040,2048]{1,0:T(8,128)S(1)} %bitcast.236), kind=kOutput, calls=%fused_computation.49 | convolution fusion | flops 2201255936 | bytes 11681792 | tf_op jit(solution)/shard_map/dot_general | solution.py:1697
  343.7 35.7 %shard_map.223 = (bf16[2,1040,768]{2,1,0:T(8,128)(2,1)}, bf16[4,16,512]{2,1,0:T(8,128)(2,1)}, bf16[4,64,512]{2,1,0:T(8,128)(2,1)}, bf16[4,64,512]{2,1,0:T(8,128)(2,1)}) custom-call(s32[1]{0:T(128)} %bitcast.10.length_ref, bf16[2080,768]{1,0:T(8,128)(2,1)} %get-tuple-element.68.x_ref, bf16[2,1040,256]{2,1,0:T(8,128)(2,1)} %fusion.29.grad_ref, ...), custom_call_target="tpu_custom_call" | custom-call | flops 30000001024 | tf_op jit(solution)/shard_map/pallas_call | solution.py:1665
  379.5 4.1 fusion.56
  384.5 3.5 convert_reduce_fusion.3
  390.8 5.4 %convolution_convert_fusion.8 = bf16[2,768,512]{2,1,0:T(8,128)(2,1)} fusion(bf16[2,1040,768]{2,1,0:T(8,128)(2,1)} %get-tuple-element.69, bf16[1040,512,1]{1,0,2:T(8,128)(2,1)S(1)} %bitcast.164), kind=kOutput, calls=%fused_computation.87 | convolution fusion | flops 1636564992 | bytes 5832704 | tf_op jit(solution)/shard_map/rpse,sd->rped/dot_general | solution.py:1783
  396.3 3.5 convolution_convert_fusion.7
  399.8 67.9 %shard_map.224 = (bf16[4,520,512]{2,1,0:T(8,128)(2,1)}, f32[2,10,512]{2,1,0:T(8,128)}, bf16[2,2,2,48,512]{4,3,2,1,0:T(8,128)(2,1)}, bf16[2,2,2,16,512]{4,3,2,1,0...) custom-call(bf16[2,520,512]{2,1,0:T(8,128)(2,1)} %bitcast.165, ...), custom_call_target="tpu_custom_call" | custom-call | flops 40000000000 | tf_op jit(solution)/shard_map/pallas_call | solution.py:1176
  467.7 4.8 shard_map.225
  (199 shorter events, 46.8 us)
Async XLA Ops:
  92.0 7.5 %copy-start.33 = (f32[1,1,512]{2,1,0:T(1,128)}, f32[1,1,512]{2,1,0:T(1,128)S(1)}, u32[]{:S(2)}) copy-start(f32[1,1,512]{2,1,0:T(1,128)S(1)} %get-tuple-element.116) | copy-start | bytes 6148
  92.0 7.5 %copy-start.40 = (f32[1,1,512]{2,1,0:T(1,128)}, f32[1,1,512]{2,1,0:T(1,128)S(1)}, u32[]{:S(2)}) copy-start(f32[1,1,512]{2,1,0:T(1,128)S(1)} %get-tuple-element.115) | copy-start | bytes 6148
  92.0 15.7 %copy-start.29 = (f32[1,1,512]{2,1,0:T(1,128)}, f32[1,1,512]{2,1,0:T(1,128)S(1)}, u32[]{:S(2)}) copy-start(f32[1,1,512]{2,1,0:T(1,128)S(1)} %get-tuple-element.113) | copy-start | bytes 6148
  92.0 15.7 %copy-start.38 = (f32[1,1,512]{2,1,0:T(1,128)}, f32[1,1,512]{2,1,0:T(1,128)S(1)}, u32[]{:S(2)}) copy-start(f32[1,1,512]{2,1,0:T(1,128)S(1)} %get-tuple-element.112) | copy-start | bytes 6148
  106.6 202.1 %copy-start.1 = (bf16[1040,512]{1,0:T(8,128)(2,1)}, bf16[1040,512]{1,0:T(8,128)(2,1)S(1)}, u32[]{:S(2)}) copy-start(bf16[1040,512]{1,0:T(8,128)(2,1)S(1)} %get-tuple-element.132) | copy-start | bytes 3194884
  216.2 87.3 %copy-start.15 = (f32[1040]{0:T(1024)S(1)}, f32[1040]{0:T(1024)}, u32[]{:S(2)}) copy-start(f32[1040]{0:T(1024)} %copy-done.14) | copy-start | bytes 12484
  216.2 87.3 %copy-start.30 = (f32[1,1,512]{2,1,0:T(1,128)S(1)}, f32[1,1,512]{2,1,0:T(1,128)}, u32[]{:S(2)}) copy-start(f32[1,1,512]{2,1,0:T(1,128)} %copy-done.29) | copy-start | bytes 6148
  216.2 87.4 %copy-start.50 = (bf16[4,2,2,2,48,512]{5,4,3,2,1,0:T(8,128)(2,1)S(1)}, bf16[4,2,2,2,48,512]{5,4,3,2,1,0:T(8,128)(2,1)}, u32[]{:S(2)}) copy-start(bf16[4,2,2,2,48,512]{5,4,3,2,1,0:T(8,128)(2,1)} %get-tuple-element.49) | copy-start | bytes 4718596
  310.3 9.9 %copy-start.7 = (bf16[1040,512]{1,0:T(8,128)(2,1)}, bf16[1040,512]{1,0:T(8,128)(2,1)S(1)}, u32[]{:S(2)}) copy-start(bf16[1040,512]{1,0:T(8,128)(2,1)S(1)} %add_convert_fusion.2) | copy-start | bytes 3194884
  310.3 10.0 %copy-start.4 = (f32[1040,512]{1,0:T(8,128)S(1)}, f32[1040,512]{1,0:T(8,128)}, u32[]{:S(2)}) copy-start(f32[1040,512]{1,0:T(8,128)} %copy-done.3) | copy-start | bytes 6389764
  310.3 10.0 %copy-start.20 = (f32[1040]{0:T(1024)S(1)}, f32[1040]{0:T(1024)}, u32[]{:S(2)}) copy-start(f32[1040]{0:T(1024)} %copy-done.19) | copy-start | bytes 12484
  310.3 10.0 %copy-start.26 = (f32[1040]{0:T(1024)S(1)}, f32[1040]{0:T(1024)}, u32[]{:S(2)}) copy-start(f32[1040]{0:T(1024)} %copy-done.25) | copy-start | bytes 12484
  310.3 10.0 %copy-start.34 = (f32[1,1,512]{2,1,0:T(1,128)S(1)}, f32[1,1,512]{2,1,0:T(1,128)}, u32[]{:S(2)}) copy-start(f32[1,1,512]{2,1,0:T(1,128)} %copy-done.33) | copy-start | bytes 6148
  310.3 10.0 %copy-start.43 = (bf16[4,2,2,2,64,512]{5,4,3,2,1,0:T(8,128)(2,1)S(1)}, bf16[4,2,2,2,64,512]{5,4,3,2,1,0:T(8,128)(2,1)}, u32[]{:S(2)}) copy-start(bf16[4,2,2,2,64,512]{5,4,3,2,1,0:T(8,128)(2,1)} %get-tuple-element.53) | copy-start | bytes 6291460
  328.0 5.9 %copy-start.55 = (bf16[1040,2048]{1,0:T(8,128)(2,1)S(1)}, bf16[1040,2048]{1,0:T(8,128)(2,1)}, u32[]{:S(2)}) copy-start(bf16[1040,2048]{1,0:T(8,128)(2,1)} %copy-done.54) | copy-start | bytes 12779524
  332.0 6.8 %slice-start = ((s8[8519680]{0:T(1024)(128)(4,1)}), s8[4194304]{0:T(1024)(128)(4,1)S(1)}, s32[]{:S(2)}) async-start(s8[8519680]{0:T(1024)(128)(4,1)} %bitcast.235), calls=%async_computation | async-start | bytes 8388608
  343.7 35.7 %copy-start.9 = (f32[1040,512]{1,0:T(8,128)S(1)}, f32[1040,512]{1,0:T(8,128)}, u32[]{:S(2)}) copy-start(f32[1040,512]{1,0:T(8,128)} %bitcast_subtract_fusion) | copy-start | bytes 6389764
  343.7 35.7 %copy-start.28 = (f32[1,1,512]{2,1,0:T(1,128)S(1)}, f32[1,1,512]{2,1,0:T(1,128)}, u32[]{:S(2)}) copy-start(f32[1,1,512]{2,1,0:T(1,128)} %get-tuple-element.107) | copy-start | bytes 6148
  343.7 35.7 %copy-start.48 = (bf16[4,2,2,2,48,512]{5,4,3,2,1,0:T(8,128)(2,1)S(1)}, bf16[4,2,2,2,48,512]{5,4,3,2,1,0:T(8,128)(2,1)}, u32[]{:S(2)}) copy-start(bf16[4,2,2,2,48,512]{5,4,3,2,1,0:T(8,128)(2,1)} %get-tuple-element.70) | copy-start | bytes 4718596
  384.5 5.9 %copy-start.32 = (f32[1,1,512]{2,1,0:T(1,128)S(1)}, f32[1,1,512]{2,1,0:T(1,128)}, u32[]{:S(2)}) copy-start(f32[1,1,512]{2,1,0:T(1,128)} %get-tuple-element.106) | copy-start | bytes 6148
  390.8 5.5 %copy-start.2 = (bf16[1040,512]{1,0:T(8,128)(2,1)S(1)}, bf16[1040,512]{1,0:T(8,128)(2,1)}, u32[]{:S(2)}) copy-start(bf16[1040,512]{1,0:T(8,128)(2,1)} %copy-done.1) | copy-start | bytes 3194884
  390.8 5.5 %copy-start.39 = (f32[1,1,512]{2,1,0:T(1,128)S(1)}, f32[1,1,512]{2,1,0:T(1,128)}, u32[]{:S(2)}) copy-start(f32[1,1,512]{2,1,0:T(1,128)} %copy-done.38) | copy-start | bytes 6148
  390.8 5.5 %copy-start.56 = (bf16[2,2,1040,384]{3,2,1,0:T(8,128)(2,1)S(1)}, bf16[2,2,1040,384]{3,2,1,0:T(8,128)(2,1)}, u32[]{:S(2)}) copy-start(bf16[2,2,1040,384]{3,2,1,0:T(8,128)(2,1)} %get-tuple-element.67) | copy-start | bytes 9584644
  467.7 5.4 %copy-start.13 = (bf16[2,2,2,48,512]{4,3,2,1,0:T(8,128)(2,1)S(1)}, bf16[2,2,2,48,512]{4,3,2,1,0:T(8,128)(2,1)}, u32[]{:S(2)}) copy-start(bf16[2,2,2,48,512]{4,3,2,1,0:T(8,128)(2,1)} %get-tuple-element.80) | copy-start | bytes 1179652
  (36 other events, 110.4 us)

commit v5 on v4

--- a/solution.py
+++ b/solution.py
@@ -91,17 +91,11 @@
     def other_core(self):
         return self.at(core=1 - self.core)
 
-    def column(self, flip_side=False, flip_section=False, flip_core=False):
+    def cell(self, flip_side=False, flip_section=False, flip_core=False):
         side = 1 - self.side if flip_side else self.side
         section = 1 - self.section if flip_section else self.section
         core = 1 - self.core if flip_core else self.core
-        return side * 4 + section * 2 + core
-
-    def slots(self):
-        yield self.mp, True
-        for step in range(1, self.ranks):
-            yield self.mp - step, self.mp >= step
-            yield self.mp + step, self.mp + step < self.ranks
+        return (side, section, core)
 
     def greet_lines(self):
         barrier = pltpu.get_barrier_semaphore()
@@ -560,50 +554,34 @@
     rows.end()
 
 
-class FirstAttention:
+class Projection:
     BLOCK = 208
 
     @staticmethod
     def scratch(place, rows, width, heads_width):
-        dma = pltpu.SemaphoreType.DMA
         return [
             pltpu.VMEM((rows, width), F32),
             pltpu.VMEM((rows, width), LOW),
             pltpu.VMEM((place.members - 1, rows, 3 * heads_width), LOW),
-            pltpu.VMEM((place.members * rows, heads_width), LOW),
             *Swap.scratch(place.members),
-            *Swap.scratch(place.members),
-            dma,
         ]
 
-    def __init__(self, place, rows_ref, weight_ref, vecs_ref, qkv_ref, mixed_ref, scratch):
-        self.place, self.rows_ref, self.weight_ref, self.vecs_ref = place, rows_ref, weight_ref, vecs_ref
-        self.qkv_ref, self.mixed_ref = qkv_ref, mixed_ref
-        self.wide_ref, self.normed_ref, self.sent_ref, self.heads_ref, *sems = scratch
+    COUNT = 5
+
+    def __init__(self, place, weight_ref, vecs_ref, slot, qkv_ref, scratch):
+        self.place, self.weight_ref, self.vecs_ref, self.slot, self.qkv_ref = place, weight_ref, vecs_ref, slot, qkv_ref
+        self.wide_ref, self.normed_ref, self.sent_ref, *sems = scratch
         self.rows = self.wide_ref.shape[0]
         me, members = place.member(), place.members
         self.to_heads = Swap(
             place,
             lambda rank: self.sent_ref.at[lax.rem(rank - me + members - 1, members)],
-            lambda rank: qkv_ref.at[self.span(rank)],
-            sems[:2],
-        )
-        self.to_rows = Swap(
-            place,
-            lambda rank: self.heads_ref.at[self.span(rank)],
-            lambda rank: mixed_ref.at[rank],
-            sems[2:4],
-        )
-        self.local = sems[4]
-
-    def span(self, rank):
-        return pl.ds(pl.multiple_of(rank * self.rows, 16), self.rows)
+            lambda rank: qkv_ref.at[row_span(self.rows, rank)],
+            sems,
+        )
 
     def norm(self):
-        half = self.rows // 2
-        for part in range(2):
-            self.wide_ref[part * half : (part + 1) * half] = wide(self.rows_ref[part])
-        gain, bias = self.vecs_ref[0, 0:1], self.vecs_ref[0, 1:2]
+        gain, bias = self.vecs_ref[self.slot, 0:1], self.vecs_ref[self.slot, 1:2]
 
         @pl.loop(0, self.rows // self.BLOCK)
         def _(block):
@@ -612,8 +590,6 @@
             self.normed_ref[span] = normed.astype(LOW)
 
     def project(self, step):
-        if step == 0:
-            self.norm()
         members = self.place.members
         turn = (step + 1) % members
         rank = lax.rem(self.place.member() + turn, members)
@@ -639,11 +615,46 @@
         if turn > 0:
             self.to_heads.copy(turn).start()
 
+
+class FirstAttention:
+    @staticmethod
+    def scratch(place, rows, width, heads_width):
+        return [
+            *Projection.scratch(place, rows, width, heads_width),
+            pltpu.VMEM((place.members * rows, heads_width), LOW),
+            *Swap.scratch(place.members),
+            pltpu.SemaphoreType.DMA,
+        ]
+
+    def __init__(self, place, rows_ref, weight_ref, vecs_ref, qkv_ref, mixed_ref, scratch):
+        self.place, self.rows_ref, self.vecs_ref = place, rows_ref, vecs_ref
+        self.qkv_ref, self.mixed_ref = qkv_ref, mixed_ref
+        count = Projection.COUNT
+        self.projection = Projection(place, weight_ref, vecs_ref, 0, qkv_ref, scratch[:count])
+        self.to_heads = self.projection.to_heads
+        self.heads_ref, *sems = scratch[count:]
+        self.rows = self.projection.rows
+        self.to_rows = Swap(
+            place,
+            lambda rank: self.heads_ref.at[self.span(rank)],
+            lambda rank: mixed_ref.at[rank],
+            sems[:2],
+        )
+        self.local = sems[2]
+
+    def span(self, rank):
+        return row_span(self.rows, rank)
+
+    def project(self, step):
+        if step == 0:
+            halves_into(self.projection.wide_ref, self.rows_ref)
+            self.projection.norm()
+        self.projection.project(step)
+
     def attend(self, between):
         self.to_heads.arrive()
         place, width = self.place, self.heads_ref.shape[1]
         me = place.member()
-        section, _, core, mp = place.here()
 
         def group(rows, bias):
             for pair in range(width // PAIR):
@@ -659,11 +670,7 @@
             group(pl.ds(pl.multiple_of(view * PATCH, 16), PATCH), None)
             between(view)
 
-        ranks = self.place.ranks
-        own, other = self.vecs_ref[section * ranks + mp], self.vecs_ref[2 * ranks]
-        lengths = jnp.where(core == section, own[7:8], other[7:8])
-        lane = lax.broadcasted_iota(jnp.int32, lengths.shape, 1)
-        used = jnp.sum(jnp.where(lane == mp // place.chips, lengths, 0.0), -1, keepdims=True)
+        used = used_slots(place, self.vecs_ref)
         column = wide(lax.broadcasted_iota(jnp.int32, (1, TEXT), 1))
         bias = jnp.where(column < used, 0.0, MASKED)
         group(pl.ds(PATCH_ROWS, TEXT), bias)
@@ -819,7 +826,7 @@
     def core_copy(self, index):
         side, section = self.FLIPS[index]
         return remote(
-            self.grad_ref.at[:, self.ring.column(side, section, True)],
+            self.grad_ref.at[(slice(None),) + self.ring.cell(side, section, True)],
             self.core_got.at[index],
             self.core_send.at[index],
             self.core_recv.at[index],
@@ -841,7 +848,7 @@
     def own(self, index, half):
         side, section = self.FLIPS[index]
         slots = self.halves[half]
-        return wide(self.grad_ref[slots, self.ring.column(side, section)]) + wide(
+        return wide(self.grad_ref[(slots,) + self.ring.cell(side, section)]) + wide(
             self.core_got[index, slots]
         )
 
@@ -937,7 +944,7 @@
 
 
 def line_shapes(grads):
-    return tuple(jax.ShapeDtypeStruct((g.shape[0],) + g.shape[2:], LOW) for g in grads)
+    return tuple(jax.ShapeDtypeStruct((g.shape[0],) + g.shape[-2:], LOW) for g in grads)
 
 
 def piece_shapes(grads):
@@ -1082,10 +1089,11 @@
     piece_refs = piece_refs + whole_refs
     ring.greet_all()
 
+    for one in sums:
+        one.begin()
+    home.begin()
     for along in alongs[hops:]:
         along.begin()
-    for one in sums:
-        one.begin()
     partners = (ring.other_core(), ring.other_side(), ring.other_section())
 
     def vec_copy(step):
@@ -1108,7 +1116,6 @@
 
     for one in sums:
         one.one()
-    home.begin()
     for which in range(hops + lines, pieces):
         leave(which)
     vec_copy(0).wait_recv()
@@ -1181,7 +1188,7 @@
         )
         + tuple(jax.ShapeDtypeStruct(size, LOW) for size in sizes),
         in_specs=[held] * (2 + pieces),
-        out_specs=(held,) * (2 + pieces // 2),
+        out_specs=(pl.BlockSpec(memory_space=pl.ANY),) + (held,) * (1 + pieces // 2),
         scratch_shapes=[
             pltpu.VMEM((3,) + vecs.shape, F32),
             pltpu.VMEM((3,) + vecs.shape, F32),
@@ -1238,17 +1245,35 @@
     return joined(*outs), logs
 
 
-def joint_forward_kernel(mesh, place, pairs, block, count, fused, length_ref, x_ref, near_ref, far_ref, *refs):
+def used_slots(place, vecs_ref):
+    section, _, core, mp = place.here()
+    ranks = place.ranks
+    own, other = vecs_ref[section * ranks + mp], vecs_ref[2 * ranks]
+    lengths = jnp.where(core == section, own[7:8], other[7:8])
+    lane = lax.broadcasted_iota(jnp.int32, lengths.shape, 1)
+    return jnp.sum(jnp.where(lane == mp // place.chips, lengths, 0.0), -1, keepdims=True)
+
+
+def gelu_of(x):
+    return x * (0.5 + 0.5 * jnp.tanh(x * (GELU_A + GELU_A * GELU_B * (x * x))))
+
+
+def joint_forward_kernel(mesh, place, pairs, block, count, fused, length_ref, near_ref, far_ref, *refs):
     def take(count):
         nonlocal refs
         taken, refs = refs[:count], refs[count:]
         return taken
 
+    if fused:
+        rows_in_ref, before_ref, vecs_ref, weight_ref, out_ref, up_ref, down_ref = take(7)
+    else:
+        (x_ref,) = take(1)
     piece_refs = take(count)
     o_ref, log_ref, rows_ref = take(3)
     full_refs = take(count)
-    qkv_ref, mixed_ref = take(2) if fused else (x_ref, None)
+    qkv_ref, mixed_ref, boundary_ref = take(3) if fused else (x_ref, None, None)
     gather_sems = [take(Gather.COUNT) for _ in range(count)]
+    score_ref, value_ref, bias_ref = take(3)
     steps = o_ref.shape[0] // block
     ring = Ring(mesh)
     gathers = [
@@ -1257,58 +1282,126 @@
     ]
     rows = Rows(ring, place, 1, near_ref, rows_ref, far_ref, take(5))
     ring.greet_all()
+
+    def gather_phase(number):
+        for gather in gathers:
+            gather.phase(number)
+
+    gather_phase(0)
     first = each = 0
     if fused:
         me, members = place.member(), place.members
         here = o_ref.shape[0] // members
         span = functools.partial(row_span, here)
-        to_heads = Swap(place, lambda rank: x_ref.at[rank], lambda rank: qkv_ref.at[span(rank)], take(2))
+        projection = Projection(place, weight_ref, vecs_ref, ring.ranks, qkv_ref, take(Projection.COUNT))
+        to_heads = projection.to_heads
         to_rows = Swap(place, lambda rank: o_ref.at[span(rank)], lambda rank: mixed_ref.at[rank], take(2))
-        (local,) = take(1)
+        local, result_ref, second_ref, hidden_ref = take(4)
         each = here // block
         first = each * (me + 1)
-        to_heads.begin()
-        keep(x_ref.at[me], qkv_ref.at[span(me)], local)
+
+        wide_ref, width = projection.wide_ref, result_ref.shape[1]
+        _, _, bias_out, gain_two, bias_two, bias_down = [vecs_ref[0, i : i + 1] for i in range(6)]
+        shards = ring.ranks // members
+        halves_into(wide_ref, rows_in_ref)
+        for at in range(0, here, Projection.BLOCK):
+            some = slice(at, at + Projection.BLOCK)
+            middle = wide_ref[some] + bias_out
+            for rank in range(members):
+                weight = out_ref[rank * shards : (rank + 1) * shards].reshape(-1, width)
+                middle = middle + dot(before_ref[rank, some], weight)
+            second_ref[some] = layer_norm(middle, gain_two, bias_two).astype(LOW)
+            result_ref[some] = middle + bias_down
+        for rank in range(ring.ranks):
+            up, down = up_ref[rank].reshape(-1, width), down_ref[rank].reshape(-1, width)
+            pre = dot_rows(second_ref[...], up) + vecs_ref[rank, 6:7]
+            hidden_ref[...] = gelu_of(pre).astype(LOW)
+            result_ref[...] += dot(hidden_ref[...], down)
+            if rank == 0:
+                gather_phase(1)
+            for item in range(place.items):
+                if item * 2 // place.items == rank:
+                    rows.give(item)
+        for part in range(2):
+            low = result_ref[part * here // 2 : (part + 1) * here // 2].astype(LOW)
+            boundary_ref[part] = low
+            wide_ref[part * here // 2 : (part + 1) * here // 2] = wide(low)
+        projection.norm()
+        for member in range(members):
+            projection.project(member)
+        gather_phase(2)
+        mask_keys(bias_ref, used_slots(place, vecs_ref))
+    else:
+        gather_phase(1)
+        for item in range(place.items):
+            rows.give(item)
+        mask_keys(bias_ref, wide(length_ref[0]))
 
     keys = qkv_ref.shape[0]
-    column = lax.broadcasted_iota(jnp.int32, (1, keys), 1)
-    bias = jnp.where(column < PATCH_ROWS + length_ref[0], 0.0, MASKED).astype(F32)
+    heads = 2 * pairs
     lanes = lax.broadcasted_iota(jnp.int32, (1, 128), 1)
 
+    def rows_at(step):
+        turn = lax.rem(step + first, steps)
+        return pl.ds(pl.multiple_of(turn * block, 16), block)
+
+    def score(step, head, slot, start, size, top):
+        base = (head // 2) * 3 * PAIR
+        q = half_of(qkv_ref[rows_at(step), base : base + PAIR] * jnp.asarray(0.125, LOW), head % 2)
+        scores = dot_rows(q, qkv_ref[start : start + size, base + PAIR : base + 2 * PAIR])
+        if start + size > PATCH_ROWS:
+            scores = scores + bias_ref[0:1, start : start + size]
+        score_ref[slot, :, start : start + size] = scores
+        here = jnp.max(scores, -1, keepdims=True)
+        return here if top is None else jnp.maximum(top, here)
+
     def phases(step):
-        for number, when in enumerate(GATHER_STEPS):
-
-            @pl.when(step == when)
-            def _():
-                for gather in gathers:
-                    gather.phase(number)
-
-        for item, when in enumerate(GIVE_STEPS):
-            pl.when(step == when)(functools.partial(rows.give, item))
+        if not fused:
+            pl.when(step == 3)(functools.partial(gather_phase, 2))
+        pl.when(step == 4)(functools.partial(gather_phase, 3))
         if fused:
-            pl.when(step == 0)(to_heads.arrive)
             for member in range(1, members):
                 pl.when(step == member * each)(lambda member=member: to_rows.copy(member).start())
 
-    @pl.loop(0, steps)
-    def _(step):
+    if fused:
+        to_heads.arrive()
+    for pair in range(pairs):
+        base = pair * 3 * PAIR
+        value_ref[pair, :, 0:PAIR] = qkv_ref[:, base + 2 * PAIR : base + 3 * PAIR]
+        value_ref[pair, :, PAIR:] = jnp.ones((keys, PAIR), LOW)
+    top = None
+    tiles = tiles_of(keys, 2)
+    for start, size in tiles:
+        top = score(0, 0, 0, start, size, top)
+
+    def body(step, top):
         phases(step)
-        turn = lax.rem(step + first, steps)
-        here_rows = pl.ds(pl.multiple_of(turn * block, 16), block)
+        here_rows = rows_at(step)
         kept = jnp.zeros((block, 128), F32)
-        for pair in range(pairs):
-            base = pair * 3 * PAIR
-            out, logs = forward_pair(
-                qkv_ref[here_rows, base : base + PAIR],
-                qkv_ref[:, base + PAIR : base + 2 * PAIR],
-                qkv_ref[:, base + 2 * PAIR : base + 3 * PAIR],
-                bias,
-            )
-            o_ref[here_rows, pair * PAIR : (pair + 1) * PAIR] = out.astype(LOW)
-            for head in range(2):
-                kept = jnp.where(lanes == pair * 2 + head, logs[head], kept)
+        outs = []
+        for head in range(heads):
+            now, later = head % 2, (head + 1) % 2
+            next_head = (head + 1) % heads
+            next_step = step if next_head > 0 else step + 1
+            next_top = out = None
+            for start, size in tiles:
+                next_top = score(next_step, next_head, later, start, size, next_top)
+                expon = jnp.exp(score_ref[now, :, start : start + size] - top).astype(LOW)
+                part = dot(expon, value_ref[head // 2, start : start + size])
+                out = part if out is None else out + part
+            total = out[:, PAIR : PAIR + 1]
+            outs.append(out[:, :PAIR] / total)
+            kept = jnp.where(lanes == head, top + jnp.log(total), kept)
+            if head % 2 == 1:
+                at = (head // 2) * PAIR
+                o_ref[here_rows, at : at + PAIR] = joined(*outs[-2:]).astype(LOW)
+            top = next_top
         log_ref[here_rows] = kept
-
+        return top
+
+    lax.fori_loop(0, steps, body, top)
+    gather_phase(4)
+    gather_phase(5)
     rows.arrive()
     rows.end_given()
     if fused:
@@ -1318,6 +1411,16 @@
         to_rows.end()
 
 
+def mask_keys(bias_ref, length):
+    column = wide(lax.broadcasted_iota(jnp.int32, bias_ref.shape, 1))
+    bias_ref[...] = jnp.where(column < PATCH_ROWS + length, 0.0, MASKED).astype(F32)
+
+
+def tiles_of(keys, count):
+    each = keys // count // 128 * 128
+    return [(i * each, each if i < count - 1 else keys - i * each) for i in range(count)]
+
+
 def row_span(rows, rank):
     return pl.ds(pl.multiple_of(rank * rows, 16), rows)
 
@@ -1328,25 +1431,30 @@
     copy.wait()
 
 
-GATHER_STEPS = (0, 2, 6, 8, 9, 9)
-GIVE_STEPS = (4, 4, 5, 5)
-
-
-def joint_forward(mesh, place, x, length, pieces, near, far, fused):
-    width = x.shape[-1]
-    rows = x.shape[-2] * (place.members if fused else 1)
-    pairs = width // (3 * PAIR)
+def joint_forward(mesh, place, inputs, length, pieces, near, far, fused):
+    ranks = mesh.shape["mp"]
+    held, away = pl.BlockSpec(memory_space=pltpu.VMEM), pl.BlockSpec(memory_space=pl.ANY)
+    fulls = full_shapes(ranks, pieces)
     block = 208
-    ranks = mesh.shape["mp"]
-    fulls = full_shapes(ranks, pieces)
-    held, away = pl.BlockSpec(memory_space=pltpu.VMEM), pl.BlockSpec(memory_space=pl.ANY)
     more, sems = (), []
     if fused:
+        here, width = 2 * near.shape[1], near.shape[2]
+        rows, pairs = here * place.members, inputs[1].shape[2] // PAIR
         more = (
-            jax.ShapeDtypeStruct((rows, width), LOW),
-            jax.ShapeDtypeStruct((place.members, rows // place.members, pairs * PAIR), LOW),
-        )
-        sems = [*Swap.scratch(place.members), *Swap.scratch(place.members), pltpu.SemaphoreType.DMA]
+            jax.ShapeDtypeStruct((rows, 3 * pairs * PAIR), LOW),
+            jax.ShapeDtypeStruct((place.members, here, pairs * PAIR), LOW),
+            jax.ShapeDtypeStruct((2,) + near.shape[1:], LOW),
+        )
+        sems = [
+            *Projection.scratch(place, here, width, pairs * PAIR),
+            *Swap.scratch(place.members),
+            pltpu.SemaphoreType.DMA,
+            pltpu.VMEM((here, width), F32),
+            pltpu.VMEM((here, width), LOW),
+            pltpu.VMEM((here, width), LOW),
+        ]
+    else:
+        rows, pairs = inputs[0].shape[0], inputs[0].shape[1] // (3 * PAIR)
     out = pl.pallas_call(
         functools.partial(joint_forward_kernel, mesh, place, pairs, block, len(pieces), fused),
         out_shape=(
@@ -1356,35 +1464,39 @@
         )
         + fulls
         + more,
-        in_specs=[pl.BlockSpec(memory_space=pltpu.SMEM), held, away, away]
-        + [held] * len(pieces),
+        in_specs=[pl.BlockSpec(memory_space=pltpu.SMEM), away, away]
+        + [held] * (len(inputs) + len(pieces)),
         out_specs=(held,) * 3 + (away,) * len(fulls) + (held,) * len(more),
-        scratch_shapes=Gather.scratch(ranks) * len(pieces) + Rows.scratch(place.items) + sems,
-        cost_estimate=cost(40),
+        scratch_shapes=Gather.scratch(ranks) * len(pieces)
+        + [
+            pltpu.VMEM((2, block, rows), F32),
+            pltpu.VMEM((pairs, rows, 2 * PAIR), LOW),
+            pltpu.VMEM((8, rows), F32),
+        ]
+        + Rows.scratch(place.items)
+        + sems,
+        cost_estimate=cost(45),
         compiler_params=pltpu.CompilerParams(
             collective_id=8, has_side_effects=True, vmem_limit_bytes=VMEM_BYTES
         ),
-    )(length, x, near, far, *pieces)
+    )(length, near, far, *inputs, *pieces)
     heads, logs, given = out[:3]
     fulls = out[3 : 3 + len(fulls)]
-    qkv, mixed = out[-2:] if fused else (x, to_rows(place, heads, 3))
-    return qkv, heads, logs, mixed, given, fulls
-
-
-def backward_head(q, k, v, grad, head, log, delta, limit):
+    if fused:
+        qkv, mixed, boundary = out[-3:]
+        return (qkv, heads, logs, mixed), given, fulls, boundary
+    return (inputs[0], heads, logs, to_rows(place, heads, 3)), given, fulls, None
+
+
+def backward_head(q, k, v, grad, head, limit):
     scores = dot_rows(k, half_of(q, head))
     if limit is not None:
         row = lax.broadcasted_iota(jnp.int32, (scores.shape[0], 1), 0)
         scores = jnp.where(row < limit, scores, MASKED)
-    if log is None:
-        top = jnp.max(scores, 0, keepdims=True)
-        expon = jnp.exp(scores - top)
-        probs = expon / jnp.sum(expon, 0, keepdims=True)
-    else:
-        probs = jnp.exp(scores - log)
+    expon = jnp.exp(scores - jnp.max(scores, 0, keepdims=True))
+    probs = expon / jnp.sum(expon, 0, keepdims=True)
     grad_probs = dot_rows(v, half_of(grad, head))
-    if delta is None:
-        delta = jnp.sum(probs * grad_probs, 0, keepdims=True)
+    delta = jnp.sum(probs * grad_probs, 0, keepdims=True)
     grad_scores = (probs * (grad_probs - delta)).astype(LOW)
     grad_v = dot(probs.astype(LOW), grad)
     grad_k = dot(grad_scores, q)
@@ -1403,8 +1515,9 @@
 
     matrix_refs, (swapped_ref,) = take(count), take(1)
     piece_refs, (gone_ref,) = take(count), take(1)
-    total_ref, stat_ref = take(2)
-    steps = qkv_ref.shape[0] // block
+    score_ref, slope_ref, weight_ref, grad_score_ref, grad_k_ref, grad_v_ref, bias_ref, pair_ref = take(8)
+    keys = qkv_ref.shape[0]
+    steps = keys // block
     ring = Ring(mesh)
     ring.greet_all()
     backs, sent_ref = [], swapped_ref
@@ -1425,11 +1538,13 @@
         ]
         to_heads.begin()
         keep(own_ref.at[me], got_ref.at[span(me)], local)
-    home = Home(ring, place, 1, rows_ref, gone_ref, take(3))
+    home_sems = take(3)
     line_refs = take(count)
     sums = each_of(Hops, ring, matrix_refs, line_refs, take(Hops.COUNT * count))
     alongs = each_of(Line, ring, line_refs, piece_refs, take(Line.COUNT * count))
+    home = Home(ring, place, 1, rows_ref, gone_ref, home_sems)
     home.begin()
+    mask_keys(bias_ref, wide(length_ref[0]))
 
     def phases(whole_step):
         for number, when in enumerate(REDUCTION_STEPS[:4]):
@@ -1463,43 +1578,49 @@
         def lanes_of(part):
             return pl.ds(pl.multiple_of(pair * 3 * PAIR + part * PAIR, PAIR), PAIR)
 
-        limit = PATCH_ROWS + length_ref[0] - step * block
-        q = qkv_ref[:, lanes_of(0)] * jnp.asarray(0.125, LOW)
-        k, v = qkv_ref[here, lanes_of(1)], qkv_ref[here, lanes_of(2)]
         own_lanes = pl.ds(pl.multiple_of(pair * PAIR, PAIR), PAIR)
-        grad = heads_ref[:, own_lanes]
+        q = qkv_ref[here, lanes_of(0)] * jnp.asarray(0.125, LOW)
+        grad = heads_ref[here, own_lanes]
+        product = wide(grad) * wide(out_ref[here, own_lanes])
+        logs = log_ref[here]
+        lane = lax.broadcasted_iota(jnp.int32, (1, 128), 1)
+        q_turned, grad_turned = q.T, grad.T
 
         @pl.when(step == 0)
         def _():
-            total_ref[...] = jnp.zeros_like(total_ref)
-            rows = lax.broadcasted_iota(jnp.int32, (8, PAIR), 0)
-            lanes = lax.broadcasted_iota(jnp.int32, (8, PAIR), 1)
-            which = jnp.where(lanes == pair * 2 + rows, 1.0, 0.0).astype(F32)
-            own = jnp.where((lanes // HEAD) == rows, 1.0, 0.0).astype(F32)
-            product = wide(heads_ref[:, own_lanes]) * wide(out_ref[:, own_lanes])
-            exact = functools.partial(
-                lax.dot_general,
-                dimension_numbers=(((1,), (1,)), ((), ())),
-                precision=lax.Precision.HIGHEST,
-                preferred_element_type=F32,
-            )
-            stat_ref[0] = exact(which, log_ref[...])
-            stat_ref[1] = exact(own, product)
-
-        grads_k, grads_v = [], []
+            grad_k_ref[...] = jnp.zeros_like(grad_k_ref)
+            grad_v_ref[...] = jnp.zeros_like(grad_v_ref)
+            for part in range(2):
+                pair_ref[part] = qkv_ref[:, lanes_of(1 + part)]
+
+        grads_q = []
         for head in range(2):
-            grad_q, grad_k, grad_v = backward_head(
-                q, k, v, grad, head, stat_ref[0, head : head + 1], stat_ref[1, head : head + 1], limit
-            )
-            total_ref[head * HEAD : (head + 1) * HEAD] += grad_q
-            grads_k.append(grad_k)
-            grads_v.append(grad_v)
-        sent_ref[pair, here, PAIR : 2 * PAIR] = joined(*grads_k).astype(LOW)
-        sent_ref[pair, here, 2 * PAIR : 3 * PAIR] = joined(*grads_v).astype(LOW)
+            log = jnp.sum(jnp.where(lane == pair * 2 + head, logs, 0.0), -1, keepdims=True)
+            delta = jnp.sum(half_of(product, head), -1, keepdims=True)
+            own_q, own_grad = half_of(q, head), half_of(grad, head)
+            for start, size in tiles_of(keys, 4):
+                span_keys = slice(start, start + size)
+                scores = dot_rows(own_q, pair_ref[0, span_keys])
+                if start + size > PATCH_ROWS:
+                    scores = scores + bias_ref[0:1, span_keys]
+                score_ref[:, span_keys] = scores
+                slope_ref[:, span_keys] = dot_rows(own_grad, pair_ref[1, span_keys])
+            for start, size in tiles_of(keys, 4):
+                span_keys = slice(start, start + size)
+                probs = jnp.exp(score_ref[:, span_keys] - log)
+                grad_scores = probs * (slope_ref[:, span_keys] - delta)
+                weight_ref[:, span_keys] = probs.astype(LOW)
+                grad_score_ref[:, span_keys] = grad_scores.astype(LOW)
+            half = slice(head * HEAD, (head + 1) * HEAD)
+            grad_v_ref[half] += dot(grad_turned[half], weight_ref[...])
+            grad_k_ref[half] += dot(q_turned[half], grad_score_ref[...])
+            grads_q.append(dot(grad_score_ref[...], pair_ref[0]))
+        sent_ref[pair, here, 0:PAIR] = (joined(*grads_q) * 0.125).astype(LOW)
 
         @pl.when(step == steps - 1)
         def _():
-            sent_ref[pair, :, 0:PAIR] = (total_ref[...].T * 0.125).astype(LOW)
+            sent_ref[pair, :, PAIR : 2 * PAIR] = grad_k_ref[...].T.astype(LOW)
+            sent_ref[pair, :, 2 * PAIR : 3 * PAIR] = grad_v_ref[...].T.astype(LOW)
 
         for index, back in enumerate(backs):
 
@@ -1515,13 +1636,13 @@
         back.end()
 
 
-REDUCTION_STEPS = (0, 2, 11, 14, 19)
+REDUCTION_STEPS = (0, 1, 4, 6, 9)
 
 
 def joint_backward(mesh, place, qkv, length, grad, out, log, blocks, matrices, fused):
     rows, width = qkv.shape
     pairs, members = width // (3 * PAIR), place.members
-    block = 208
+    block = 416
     gone = jax.ShapeDtypeStruct((place.items,) + blocks.shape[1:], blocks.dtype)
     held = pl.BlockSpec(memory_space=pltpu.VMEM)
     swap_scratch, shape = [], (pairs, rows, 3 * PAIR)
@@ -1539,8 +1660,17 @@
             pl.BlockSpec(memory_space=pltpu.SMEM),
             *[held] * (5 + len(matrices)),
         ],
-        out_specs=(held,) * (2 + len(matrices)),
-        scratch_shapes=[pltpu.VMEM((PAIR, rows), F32), pltpu.VMEM((2, 8, rows), F32)]
+        out_specs=(held,) * (1 + len(matrices)) + (pl.BlockSpec(memory_space=pl.ANY),),
+        scratch_shapes=[
+            pltpu.VMEM((block, rows), F32),
+            pltpu.VMEM((block, rows), F32),
+            pltpu.VMEM((block, rows), LOW),
+            pltpu.VMEM((block, rows), LOW),
+            pltpu.VMEM((PAIR, rows), F32),
+            pltpu.VMEM((PAIR, rows), F32),
+            pltpu.VMEM((8, rows), F32),
+            pltpu.VMEM((2, rows, PAIR), LOW),
+        ]
         + swap_scratch
         + Home.scratch(place.items)
         + [pltpu.VMEM(line.shape, LOW) for line in line_shapes(matrices)]
@@ -1588,9 +1718,11 @@
     )(length, qkv)
 
 
-def within_backward_kernel(mesh, place, pairs, count, fused, length_ref, x_ref, grad_ref, *refs):
-    matrix_refs, swapped_ref, refs = refs[:count], refs[count], refs[count + 1 :]
+def within_backward_kernel(mesh, place, pairs, count, ready, fused, length_ref, x_ref, grad_ref, *refs):
+    matrix_refs, refs = refs[:count], refs[count:]
+    ready_refs, swapped_ref, refs = refs[:ready], refs[ready], refs[ready + 1 :]
     line_refs, refs = refs[:count], refs[count:]
+    piece_refs, refs = refs[:ready], refs[ready:]
     ring = Ring(mesh)
     ring.greet_lines()
     o_ref = swapped_ref
@@ -1610,6 +1742,9 @@
         keep(own_ref.at[me], got_ref.at[span(me)], local)
         grad_ref = got_ref
     sums = each_of(Hops, ring, matrix_refs, line_refs, refs)
+    alongs = each_of(Line, ring, ready_refs, piece_refs, refs[Hops.COUNT * count :])
+    for along in alongs:
+        along.begin()
 
     def every(number):
         for one in sums:
@@ -1621,7 +1756,7 @@
             q, k, v = (x_ref[rows, base + part * PAIR : base + (part + 1) * PAIR] for part in range(3))
             q = q * jnp.asarray(0.125, LOW)
             grad = grad_ref[rows, pair * PAIR : (pair + 1) * PAIR]
-            both = [backward_head(q, k, v, grad, head, None, None, limit) for head in range(2)]
+            both = [backward_head(q, k, v, grad, head, limit) for head in range(2)]
             grad_q = jnp.concatenate([both[0][0], both[1][0]], 0).T * 0.125
             o_ref[rows, base : base + PAIR] = grad_q.astype(LOW)
             o_ref[rows, base + PAIR : base + 2 * PAIR] = joined(both[0][1], both[1][1]).astype(LOW)
@@ -1644,13 +1779,16 @@
     every(3)
     for one in sums:
         one.end()
+    for along in alongs:
+        along.total()
+        along.end()
     if fused:
         to_heads.end()
         back.arrive()
         back.end()
 
 
-def within_backward(mesh, place, qkv, length, grad, matrices, fused):
+def within_backward(mesh, place, qkv, length, grad, matrices, ready, fused):
     rows, width = qkv.shape
     pairs, members = width // (3 * PAIR), place.members
     held = pl.BlockSpec(memory_space=pltpu.VMEM)
@@ -1663,19 +1801,181 @@
             pltpu.SemaphoreType.DMA,
         ] + Swap.scratch(members) * 2
     grads, *lines = pl.pallas_call(
-        functools.partial(within_backward_kernel, mesh, place, pairs, len(matrices), fused),
-        out_shape=(jax.ShapeDtypeStruct(shape, LOW),) + line_shapes(matrices),
-        in_specs=[pl.BlockSpec(memory_space=pltpu.SMEM)] + [held] * (2 + len(matrices)),
-        out_specs=(held,) * (1 + len(matrices)),
-        scratch_shapes=swap_scratch + scratch_of(Hops, matrices),
+        functools.partial(within_backward_kernel, mesh, place, pairs, len(matrices), len(ready), fused),
+        out_shape=(jax.ShapeDtypeStruct(shape, LOW),) + line_shapes(matrices) + piece_shapes(ready),
+        in_specs=[pl.BlockSpec(memory_space=pltpu.SMEM)] + [held] * (2 + len(matrices) + len(ready)),
+        out_specs=(held,) * (1 + len(matrices) + len(ready)),
+        scratch_shapes=swap_scratch + scratch_of(Hops, matrices) + scratch_of(Line, ready),
         cost_estimate=cost(30),
         compiler_params=pltpu.CompilerParams(
             collective_id=7, has_side_effects=True, vmem_limit_bytes=VMEM_BYTES
         ),
-    )(length, qkv, grad, *matrices)
+    )(length, qkv, grad, *matrices, *ready)
     if not fused:
         grads = to_rows(place, grads, 5)
     return grads.reshape(members, -1, 1, width).swapaxes(1, 2), lines
+
+
+def gelu_both(x):
+    square = x * x
+    turn = jnp.tanh(x * (GELU_A + GELU_A * GELU_B * square))
+    half = 0.5 + 0.5 * turn
+    slope = half + 0.5 * x * (1.0 - turn * turn) * (GELU_A + 3.0 * GELU_A * GELU_B * square)
+    return x * half, slope
+
+
+GELU_A = 0.7978845608028654
+GELU_B = 0.044715
+
+
+def dot_columns(left, right):
+    return lax.dot_general(left, right, (((0,), (0,)), ((), ())), preferred_element_type=F32)
+
+
+def halves_into(wide_ref, halves_ref):
+    rows = halves_ref.shape[1]
+    for part in range(2):
+        wide_ref[part * rows : (part + 1) * rows] = wide(halves_ref[part])
+
+
+def mlp_backward_kernel(mesh, place, layer, count, *refs):
+    def take(count):
+        nonlocal refs
+        taken, refs = refs[:count], refs[count:]
+        return taken
+
+    source_ref, mixed_ref, upstream_ref, vecs_ref, out_ref, up_ref, down_ref = take(7)
+    matrix_refs = take(count)
+    middle_out_ref, heads_ref, grad_out_ref, grad_up_ref, grad_down_ref, sums_ref = take(6)
+    (blocks_ref,) = take(1) if layer == 1 else (None,)
+    line_refs = take(count)
+    middle_ref, wide_ref, slope_ref, low_ref, second_ref, hidden_ref, grad_pre_ref = take(7)
+    ring = Ring(mesh)
+    ranks, members = ring.ranks, place.members
+    rows, width = middle_ref.shape
+    if layer == 1:
+        (result_ref,) = take(1)
+    sums = each_of(Hops, ring, matrix_refs, line_refs, take(Hops.COUNT * count))
+    if sums:
+        ring.greet_lines()
+    for one in sums:
+        one.begin()
+    slot = layer * ranks
+    vector = [vecs_ref[slot, i : i + 1] for i in range(6)]
+    _, _, bias_out, gain_two, bias_two, bias_down = vector
+    block = Projection.BLOCK
+    blocks = [slice(i * block, (i + 1) * block) for i in range(rows // block)]
+    shards = ranks // members
+
+    def of_member(ref, rank):
+        return ref[rank * shards : (rank + 1) * shards].reshape(-1, width)
+
+    halves_into(wide_ref, upstream_ref)
+    low_ref[...] = wide_ref[...].astype(LOW)
+    halves_into(wide_ref, source_ref)
+    outs = [of_member(out_ref, rank) for rank in range(members)]
+    for span in blocks:
+        branch = dot(mixed_ref[0, span], outs[0])
+        for rank in range(1, members):
+            branch = branch + dot(mixed_ref[rank, span], outs[rank])
+        middle = wide_ref[span] + branch + bias_out
+        middle_ref[span] = middle
+        second_ref[span] = layer_norm(middle, gain_two, bias_two).astype(LOW)
+        if layer == 1:
+            result_ref[span] = middle + bias_down
+    for one in sums:
+        one.one()
+    for rank in range(ranks):
+        up, down = up_ref[rank].reshape(-1, width), down_ref[rank].reshape(-1, width)
+        value, slope = gelu_both(dot_rows(second_ref[...], up) + vecs_ref[slot + rank, 6:7])
+        hidden_ref[...] = value.astype(LOW)
+        if layer == 1:
+            result_ref[...] += dot(hidden_ref[...], down)
+        grad_pre = (dot_rows(low_ref[...], down) * slope).astype(LOW)
+        grad_pre_ref[...] = grad_pre
+        sums_ref[4 + rank : 5 + rank] = jnp.sum(wide(grad_pre), 0, keepdims=True)
+        part = dot(grad_pre_ref[...], up)
+        if rank == 0:
+            slope_ref[...] = part
+        else:
+            slope_ref[...] += part
+        grad_up_ref[rank] = dot_columns(grad_pre_ref[...], second_ref[...]).astype(LOW).reshape(grad_up_ref.shape[1:])
+        grad_down_ref[rank] = dot_columns(hidden_ref[...], low_ref[...]).astype(LOW).reshape(grad_down_ref.shape[1:])
+        if rank == ranks // 2:
+            for one in sums:
+                one.two()
+    if layer == 1:
+        for part in range(2):
+            blocks_ref[part] = result_ref[part * rows // 2 : (part + 1) * rows // 2].astype(LOW)
+    totals = [jnp.zeros((1, width), F32)] * 4
+    for span in blocks:
+        middle, grad = middle_ref[span], slope_ref[span]
+        offset = middle - jnp.mean(middle, -1, keepdims=True)
+        scale = lax.rsqrt(jnp.mean(offset * offset, -1, keepdims=True) + 1e-05)
+        unit = offset * scale
+        inner = grad * gain_two
+        back = inner - jnp.mean(inner, -1, keepdims=True) - unit * jnp.mean(inner * unit, -1, keepdims=True)
+        upstream = wide(low_ref[span])
+        grad_middle = upstream + back * scale
+        for index, term in enumerate((grad * unit, grad, grad_middle, upstream)):
+            totals[index] = totals[index] + jnp.sum(term, 0, keepdims=True)
+        middle_out_ref[span] = grad_middle
+        low = grad_middle.astype(LOW)
+        hidden_ref[span] = low
+        for rank in range(members):
+            heads_ref[rank, span] = dot_rows(low, outs[rank]).astype(LOW)
+    for index, total in enumerate(totals):
+        sums_ref[index : index + 1] = total
+    for rank in range(members):
+        grad_out = dot_columns(mixed_ref[rank], hidden_ref[...]).astype(LOW)
+        shape = (shards,) + grad_out_ref.shape[1:]
+        grad_out_ref[rank * shards : (rank + 1) * shards] = grad_out.reshape(shape)
+    for one in sums:
+        one.line()
+    for one in sums:
+        one.end()
+
+
+def mlp_backward(mesh, place, layer, source, mixed, upstream, vecs, weights, matrices):
+    ranks = place.ranks
+    _, half, width = source.shape
+    rows = 2 * half
+    held = pl.BlockSpec(memory_space=pltpu.VMEM)
+    shape = jax.ShapeDtypeStruct
+    blocks, more = (), []
+    if layer == 1:
+        blocks, more = (shape((2, half, width), LOW),), [pltpu.VMEM((rows, width), F32)]
+    lines = line_shapes(matrices)
+    return pl.pallas_call(
+        functools.partial(mlp_backward_kernel, mesh, place, layer, len(matrices)),
+        out_shape=(
+            shape((rows, width), F32),
+            shape(mixed.shape, LOW),
+            *(shape(w.shape, LOW) for w in weights),
+            shape((4 + ranks, width), F32),
+        )
+        + blocks
+        + lines,
+        in_specs=[held] * (7 + len(matrices)),
+        out_specs=(held,) * (6 + len(blocks) + len(lines)),
+        scratch_shapes=[
+            pltpu.VMEM((rows, width), F32),
+            pltpu.VMEM((rows, width), F32),
+            pltpu.VMEM((rows, width), F32),
+            pltpu.VMEM((rows, width), LOW),
+            pltpu.VMEM((rows, width), LOW),
+            pltpu.VMEM((rows, width), LOW),
+            pltpu.VMEM((rows, width), LOW),
+        ]
+        + more
+        + scratch_of(Hops, matrices),
+        cost_estimate=cost(25),
+        compiler_params=pltpu.CompilerParams(
+            collective_id=10 if matrices else None,
+            has_side_effects=bool(matrices),
+            vmem_limit_bytes=VMEM_BYTES,
+        ),
+    )(source, mixed, upstream, vecs, *weights, *matrices)
 
 
 def layer_norm(values, scale_vec, shift_vec):
@@ -1697,7 +1997,7 @@
     return lax.dot_general(left, right, (((0,), (0,)), ((), ())), preferred_element_type=F32)
 
 
-def projection(normed, params):
+def projection_of(normed, params):
     return jnp.einsum("sd,red->rse", normed, params["qkv"], preferred_element_type=F32).astype(LOW)
 
 
@@ -1715,28 +2015,21 @@
     return layer_norm(source, params["gain_one"], params["bias_one"]).astype(LOW)
 
 
-def first_forward(place, source, length, params, ready):
+def first_forward(place, source, length, params):
     normed = first_norm(source, params)
-    if ready:
-        qkv, mixed = ready
-    else:
-        qkv = to_heads(place, projection(normed, params), 2)
-        mixed = to_rows(place, within_forward(qkv, length), 3)
+    qkv = to_heads(place, projection_of(normed, params), 2)
+    mixed = to_rows(place, within_forward(qkv, length), 3)
     result, kept = layer_end(source, mixed, params)
     return result, (source, normed, qkv, None, None, mixed) + kept
 
 
-def second_forward(mesh, place, source, length, params, pieces, near, far, fused):
+def second_forward(mesh, place, source, length, params, pieces, near, far):
     normed = first_norm(source, params)
-    x = projection(normed, params)
-    if not fused:
-        x = to_heads(place, x, 2)
-    qkv, heads, logs, mixed, given, fulls = joint_forward(
-        mesh, place, x, length, pieces, near, far, fused
-    )
+    x = to_heads(place, projection_of(normed, params), 2)
+    attended, given, fulls, _ = joint_forward(mesh, place, (x,), length, pieces, near, far, False)
     params.update(matrices_of(place, ("out", "up", "down"), fulls))
-    result, kept = layer_end(source, mixed, params)
-    return result, given, (source, normed, qkv, heads, logs, mixed) + kept
+    result, kept = layer_end(source, attended[-1], params)
+    return result, given, (source, normed) + attended + kept
 
 
 def matrices_of(place, names, fulls):
@@ -1769,31 +2062,40 @@
     grad_out = jnp.einsum("rse,sd->red", mixed, mid_low, preferred_element_type=F32)
     grad_mixed = jnp.einsum("sd,red->rse", mid_low, params["out"], preferred_element_type=F32)
     grad_heads = grad_mixed.astype(LOW)
+    later = [pack(m) for m in (grad_out, grad_up, grad_down)]
+    vectors = (
+        jnp.sum(grad_middle, 0),
+        grad_gain_two,
+        grad_bias_two,
+        jnp.sum(upstream, 0),
+        grad_up_bias,
+    )
+    grad_projected, done = attention_backward(
+        mesh, place, qkv, length, grad_heads, mixed_heads, logs, later, fused, blocks
+    )
+    found = layer_start_backward(source, normed, grad_middle, grad_projected, params, vectors)
+    return found[0], found[1], done, found[2]
+
+
+def attention_backward(mesh, place, qkv, length, grad_heads, mixed_heads, logs, later, fused, blocks, ready=()):
     if not fused:
         grad_heads = to_heads(place, grad_heads, 4)
-    later = [pack(m) for m in (grad_out, grad_up, grad_down)]
     if blocks is not None:
-        grad_projected, done = joint_backward(
+        return joint_backward(
             mesh, place, qkv, length, grad_heads, mixed_heads, logs, blocks, later, fused
         )
-    else:
-        grad_projected, done = within_backward(mesh, place, qkv, length, grad_heads, later, fused)
+    return within_backward(mesh, place, qkv, length, grad_heads, later, ready, fused)
+
+
+def layer_start_backward(source, normed, grad_middle, grad_projected, params, vectors):
     members, pairs = grad_projected.shape[:2]
     weight = params["qkv"].reshape(members, pairs, -1, params["qkv"].shape[-1])
     grad_qkv = jnp.einsum("rpse,sd->rped", grad_projected, normed, preferred_element_type=F32)
     grad_normed = jnp.einsum("rpse,rped->sd", grad_projected, weight, preferred_element_type=F32)
     first_pull = jax.vjp(layer_norm, source, params["gain_one"], params["bias_one"])[1]
     part_source, grad_gain_one, grad_bias_one = first_pull(grad_normed)
-    vectors = (
-        grad_gain_one,
-        grad_bias_one,
-        jnp.sum(grad_middle, 0),
-        grad_gain_two,
-        grad_bias_two,
-        jnp.sum(upstream, 0),
-        grad_up_bias,
-    )
-    return grad_middle + part_source, grad_qkv, done, jnp.concatenate(vectors)
+    vectors = jnp.concatenate((grad_gain_one, grad_bias_one) + vectors)
+    return grad_middle + part_source, grad_qkv, vectors
 
 
 def pick(x, index, axis):
@@ -1850,7 +2152,7 @@
     vec.append(text_lengths.astype(F32))
     vec = jnp.stack([jnp.pad(v, (0, width - v.shape[0])) for v in vec])
 
-    fused = heads_here == 2 and own[0].shape[3] % 16 == 0 and (2 * block_rows) % FirstAttention.BLOCK == 0
+    fused = heads_here == 2 and own[0].shape[3] % 16 == 0 and (2 * block_rows) % Projection.BLOCK == 0
     (arrived, vecs, staged), first, first_of_second, second, ready = start(
         mesh, place, inputs[0], vec, own, fused
     )
@@ -1866,7 +2168,7 @@
         return found
 
     def pack(grad):
-        return grad.astype(LOW).reshape(ranks, 8, -1, width)
+        return grad.astype(LOW).reshape(ranks, 2, 2, 2, -1, width)
 
     def pack_qkv(grad):
         grad = grad.astype(LOW).reshape(all_heads // 2, 3, per_pair, heads_here, HEAD, width)
@@ -1876,25 +2178,55 @@
     params[0].update(matrices_of(place, ("qkv", "out", "up", "down"), first))
     source = arrived.reshape(-1, width).astype(F32)
     params[1].update(matrices_of(place, ("qkv",), first_of_second))
-    boundary, kept_zero = first_forward(place, source, length, params[0], ready)
-    source = boundary.astype(LOW).astype(F32)
-    result, cotangent, kept_one = second_forward(
-        mesh, place, source, length, params[1], second, inputs[0], staged, fused
-    )
-    results = result.astype(LOW).reshape(2, block_rows, width)
-    upstream = cotangent.reshape(-1, width).astype(F32)
-    grad_boundary, grad_qkv_one, done, vectors_one = layer_backward(
-        mesh, place, upstream, length, params[1], kept_one, pack, fused, results
-    )
-    *done, results = done
-    upstream = grad_boundary.astype(LOW).astype(F32)
-    grad_source, grad_qkv_zero, lines, vectors_zero = layer_backward(
-        mesh, place, upstream, length, params[0], kept_zero, pack, fused
-    )
+    if fused:
+        qkv_zero, mixed_zero = ready
+        inputs_two = (arrived, mixed_zero, vecs, first_of_second[0], *first[1:])
+        (qkv, heads, logs, mixed), cotangent, fulls, boundary = joint_forward(
+            mesh, place, inputs_two, length, second, inputs[0], staged, True
+        )
+        source_one = boundary.reshape(-1, width).astype(F32)
+        grad_middle, grad_heads, *later, found, results = mlp_backward(
+            mesh, place, 1, boundary, mixed, cotangent, vecs, fulls, ()
+        )
+        vectors = (found[2], found[0], found[1], found[3], found[4:].reshape(-1))
+        grad_projected, (*done, results) = attention_backward(
+            mesh, place, qkv, length, grad_heads, heads, logs, later, fused, results
+        )
+        grad_boundary, grad_qkv, vectors_one = layer_start_backward(
+            source_one, first_norm(source_one, params[1]), grad_middle, grad_projected, params[1], vectors
+        )
+        upstream = grad_boundary.astype(LOW).reshape(2, block_rows, width)
+        grad_middle, grad_heads, *later, found, line = mlp_backward(
+            mesh, place, 0, arrived, mixed_zero, upstream, vecs, first[1:], (pack_qkv(grad_qkv),)
+        )
+        vectors = (found[2], found[0], found[1], found[3], found[4:].reshape(-1))
+        grad_projected, (*lines, piece) = attention_backward(
+            mesh, place, qkv_zero, length, grad_heads, None, None, later, fused, None, (line,)
+        )
+        grad_source, grad_qkv_zero, vectors_zero = layer_start_backward(
+            source, first_norm(source, params[0]), grad_middle, grad_projected, params[0], vectors
+        )
+        grads, done = [pack_qkv(grad_qkv_zero)], [piece] + done
+        layers = ((0, 0), (0, 1), (0, 2), (0, 3), (1, 0), (1, 1), (1, 2), (1, 3))
+    else:
+        boundary, kept_zero = first_forward(place, source, length, params[0])
+        result, cotangent, kept_one = second_forward(
+            mesh, place, boundary.astype(LOW).astype(F32), length, params[1], second, inputs[0], staged
+        )
+        results = result.astype(LOW).reshape(2, block_rows, width)
+        upstream = cotangent.reshape(-1, width).astype(F32)
+        grad_boundary, grad_qkv_one, done, vectors_one = layer_backward(
+            mesh, place, upstream, length, params[1], kept_one, pack, fused, results
+        )
+        *done, results = done
+        upstream = grad_boundary.astype(LOW).astype(F32)
+        grad_source, grad_qkv_zero, lines, vectors_zero = layer_backward(
+            mesh, place, upstream, length, params[0], kept_zero, pack, fused
+        )
+        grads = [pack_qkv(grad_qkv_zero), pack_qkv(grad_qkv_one)]
+        layers = ((0, 0), (1, 0), (0, 1), (0, 2), (0, 3), (1, 1), (1, 2), (1, 3))
     rows = grad_source.astype(LOW).reshape(2, block_rows, width)
     vectors = jnp.stack([vectors_zero, vectors_one]).reshape(2, -1, width)
-    grads = [pack_qkv(grad_qkv_zero), pack_qkv(grad_qkv_one)]
-    layers = ((0, 0), (1, 0), (0, 1), (0, 2), (0, 3), (1, 1), (1, 2), (1, 3))
     gone, sums, *matrices = finish(mesh, place, rows, vectors, grads, lines, done, layers)
     dps = mesh.shape["dp"]
     if dps > 4:

time: 483 us -> 457 us (0.946)
  matrix products: 91.1 us -> 14.5 us
  Pallas kernels: 347 us -> 404 us
  other arithmetic: 21.6 us -> 16.7 us
    dot_general x23 -> x4, matrix products: 91.1 us -> 14.5 us  [the longest x2 7.57 us: layer_start_backward(): jnp.einsum('rpse,rped->sd', grad_projected, weight, preferred_element_typ...]
    pallas_call x0 -> x2, Pallas kernels: none -> 61.6 us  [mlp_backward(): pl.pallas_call(functools.partial(mlp_backward_kernel, mesh, place, layer,...]
    pallas_call x1, Pallas kernels: 87.3 us -> 76.8 us  [joint_backward(): pl.pallas_call(functools.partial(joint_backward_kernel, mesh, place, pair...]
    pallas_call x1, Pallas kernels: 67.4 us -> 76.4 us  [joint_forward(): pl.pallas_call(functools.partial(joint_forward_kernel, mesh, place, pairs...]
    reduce_sum x4 -> x0, other arithmetic: 7.05 us -> none  [the longest x2 4.97 us: layer_backward(): jnp.sum(upstream, 0)]
where the time goes in v5:
time: 457 us; the launch traced here: 451 us
  Pallas kernels  404 us (88%)
  other arithmetic  16.7 us (4%)
  local copies, waits for them, and re-layouts  14.5 us (3%)
  matrix products  14.5 us (3%)
    pallas_call x1, Pallas kernels, start(): pl.pallas_call(functools.partial(start_kernel, mesh, place, count, fused)...  83.9 us
    pallas_call x1, Pallas kernels, joint_backward(): pl.pallas_call(functools.partial(joint_backward_kernel, mesh, place, pair...  76.8 us
    pallas_call x1, Pallas kernels, joint_forward(): pl.pallas_call(functools.partial(joint_forward_kernel, mesh, place, pairs...  76.4 us
    pallas_call x1, Pallas kernels, finish(): pl.pallas_call(functools.partial(finish_kernel, mesh, place, layers, len(...  63.3 us
    pallas_call x2, Pallas kernels, mlp_backward(): pl.pallas_call(functools.partial(mlp_backward_kernel, mesh, place, layer,...  61.6 us
    pallas_call x1, Pallas kernels, within_backward(): pl.pallas_call(functools.partial(within_backward_kernel, mesh, place, pai...  36.7 us

profile of v5, /device:TPU:0, one launch (start us, length us, event | category | flops | bytes accessed | tf_op | source)
XLA Modules:
  0.0 451.2 jit_solution(15854104637650734516)
XLA Ops:
  0.7 2.0 copy.32
  2.7 1.8 copy.31
  5.1 1.4 stack.11.vec_ref
  6.6 83.9 %shard_map.220 = (bf16[2,520,512]{2,1,0:T(8,128)(2,1)}, f32[9,8,512]{2,1,0:T(8,128)}, bf16[4,520,512]{2,1,0:T(8,128)(2,1)}, bf16[4,2,2,2,48,512]{5,4,3,2,1,0:T(8...) custom-call(bf16[4,520,512]{2,1,0:T(8,128)(2,1)} %bitcast.130, ...), custom_call_target="tpu_custom_call" | custom-call | flops 60000002048 | tf_op jit(solution)/shard_map/pallas_call | solution.py:703
  90.5 1.4 fusion.10
  92.4 1.9 fusion.13
  95.0 76.4 %shard_map.221 = (bf16[2080,256]{1,0:T(8,128)(2,1)}, f32[2080,128]{1,0:T(8,128)}, bf16[2,520,512]{2,1,0:T(8,128)(2,1)}, bf16[4,2,2,2,16,512]{5,4,3,2,1,0:T(8,128...) custom-call(s32[1]{0:T(128)} %bitcast.10.length_ref, ...), custom_call_target="tpu_custom_call" | custom-call | flops 44999999488 | tf_op jit(solution)/shard_map/pallas_call | solution.py:1458
  171.4 24.3 %shard_map.222 = (f32[1040,512]{1,0:T(8,128)}, bf16[2,1040,256]{2,1,0:T(8,128)(2,1)}, bf16[4,2,2,2,16,512]{5,4,3,2,1,0:T(8,128)(2,1)}, bf16[4,2,2,2,64,512]{5,4,...) custom-call(bf16[2,520,512]{2,1,0:T(8,128)(2,1)} %get-tuple-element.7, ...), custom_call_target="tpu_custom_call" | custom-call | flops 24999999488 | tf_op jit(solution)/shard_map/pallas_call | solution.py:1949
  195.8 76.8 %shard_map.223 = (bf16[2,2,1040,384]{3,2,1,0:T(8,128)(2,1)}, bf16[16,512]{1,0:T(8,128)(2,1)}, bf16[64,512]{1,0:T(8,128)(2,1)}, bf16[64,512]{1,0:T(8,128)(2,1)}, bf16[4,520,512]{2,1,0:T(8,128)(2,1)}) custom-call(s32[1]{0:T(128)} %bitcast.10.length_ref, bf16[2080,768]{1,0:T(8,128)(2,1)} %get-tuple-element.82.qkv_ref, ...), custom_call_target="tpu_custom_call" | custom-call | flops 65999998976 | tf_op jit(solution)/shard_map/pallas_call | solution.py:1656
  273.8 1.7 copy-done.14
  275.5 3.5 convolution_convert_fusion.1
  279.0 2.2 fusion.9
  282.0 2.8 add_convert_fusion.3
  284.9 37.3 %shard_map.224 = (f32[1040,512]{1,0:T(8,128)}, bf16[2,1040,256]{2,1,0:T(8,128)(2,1)}, bf16[4,2,2,2,16,512]{5,4,3,2,1,0:T(8,128)(2,1)}, bf16[4,2,2,2,64,512]{5,4,...) custom-call(bf16[2,520,512]{2,1,0:T(8,128)(2,1)} %get-tuple-element.64, ...), custom_call_target="tpu_custom_call" | custom-call | flops 24999999488 | tf_op jit(solution)/shard_map/pallas_call | solution.py:1949
  322.2 36.7 %shard_map.225 = (bf16[2,1040,768]{2,1,0:T(8,128)(2,1)}, bf16[4,16,512]{2,1,0:T(8,128)(2,1)}, bf16[4,64,512]{2,1,0:T(8,128)(2,1)}, bf16[4,64,512]{2,1,0:T(8,128)(2,1)}, bf16[48,512]{1,0:T(8,128)(2,1)}) custom-call(s32[1]{0:T(128)} %bitcast.10.length_ref, bf16[2080,768]{1,0:T(8,128)(2,1)} %get-tuple-element.92.x_ref, ...), custom_call_target="tpu_custom_call" | custom-call | flops 30000001024 | tf_op jit(solution)/shard_map/pallas_call | solution.py:1803
  360.8 3.5 convolution_convert_fusion
  364.7 1.0 copy-done.11
  365.7 5.4 %fusion.8 = (f32[512]{0:T(512)S(1)}, f32[1040]{0:T(1024)S(1)}, f32[512]{0:T(512)S(1)}, f32[1040,512]{1,0:T(8,128)}) fusion(f32[1040,512]{1,0:T(8,128)S(1)} %bitcast_subtract_fusion, f32[512]{0:T(512)S(1)} %bitcast.113, f32[1040]{0:T(1024)S(1)} %rsqrt.26, f32[1040]{0:T(1024)S(1)} %div.54, bf16[2,520,512]{2,1,0:T(8,128)(2,1)S(1)} %copy-done, ...), kind=kOutput, calls=%fused_computation.63 | convolution fusion | flops 1640568832 | bytes 10111168 | tf_op jit(solution)/shard_map/rpse,rped->sd/dot_general | solution.py:2094
  372.0 2.2 add_add_fusion
  374.4 2.8 add_convert_fusion.1
  377.3 63.3 %shard_map.226 = (bf16[4,520,512]{2,1,0:T(8,128)(2,1)}, f32[2,10,512]{2,1,0:T(8,128)}, bf16[2,2,2,48,512]{4,3,2,1,0:T(8,128)(2,1)}, bf16[2,2,2,16,512]{4,3,2,1,0...) custom-call(bf16[2,520,512]{2,1,0:T(8,128)(2,1)} %bitcast.99, ...), custom_call_target="tpu_custom_call" | custom-call | flops 40000000000 | tf_op jit(solution)/shard_map/pallas_call | solution.py:1183
  440.6 4.8 %shard_map.227 = f32[4,520,512]{2,1,0:T(8,128)} custom-call(bf16[4,520,512]{2,1,0:T(8,128)(2,1)} %get-tuple-element.109.zero_ref, bf16[4,520,512]{2,1,0:T(8,128)(2,1)} %get-tuple-element.110.one_ref), custom_call_target="tpu_custom_call" | custom-call | flops 3000000000 | tf_op jit(solution)/shard_map/pallas_call | solution.py:2117
  445.6 1.3 copy.36
  447.9 1.1 convert.13
  (88 shorter events, 9.8 us)
Async XLA Ops:
  195.8 76.8 %copy-start.1 = (bf16[2,520,512]{2,1,0:T(8,128)(2,1)S(1)}, bf16[2,520,512]{2,1,0:T(8,128)(2,1)}, u32[]{:S(2)}) copy-start(bf16[2,520,512]{2,1,0:T(8,128)(2,1)} %get-tuple-element.75.refs_0_) | copy-start | bytes 3194884
  273.6 1.9 copy-start.14
  275.5 3.5 copy-start.12
  322.2 36.7 %copy-start = (bf16[2,520,512]{2,1,0:T(8,128)(2,1)S(1)}, bf16[2,520,512]{2,1,0:T(8,128)(2,1)}, u32[]{:S(2)}) copy-start(bf16[2,520,512]{2,1,0:T(8,128)(2,1)} %get-tuple-element.64.refs_0_) | copy-start | bytes 3194884
  358.9 0.9 copy-start.7
  358.9 0.9 copy-start.10
  358.9 1.9 copy-start.13
  364.3 1.4 copy-start.11
  365.7 5.4 %copy-start.9 = (f32[8,512]{1,0:T(8,128)S(1)}, f32[8,512]{1,0:T(8,128)}, u32[]{:S(2)}) copy-start(f32[8,512]{1,0:T(8,128)} %get-tuple-element.100) | copy-start | bytes 49156
  365.7 5.5 %copy-start.8 = (f32[8,512]{1,0:T(8,128)S(1)}, f32[8,512]{1,0:T(8,128)}, u32[]{:S(2)}) copy-start(f32[8,512]{1,0:T(8,128)} %get-tuple-element.101) | copy-start | bytes 49156
  440.6 4.8 %copy-start.3 = (bf16[2,2,2,64,512]{4,3,2,1,0:T(8,128)(2,1)S(1)}, bf16[2,2,2,64,512]{4,3,2,1,0:T(8,128)(2,1)}, u32[]{:S(2)}) copy-start(bf16[2,2,2,64,512]{4,3,2,1,0:T(8,128)(2,1)} %get-tuple-element.114) | copy-start | bytes 1572868
  445.4 1.5 copy-start.4
  445.6 2.4 copy-start.2
  446.9 2.1 copy-start.5
  446.9 2.9 copy-start.6

commit v6 on v5

--- a/solution.py
+++ b/solution.py
@@ -1063,15 +1063,18 @@
             pl.when(jnp.logical_not(here))(lambda index=index: self.copy(index).wait_send())
 
 
-def finish_kernel(mesh, place, layers, hops, lines, *refs):
+def finish_kernel(mesh, place, layers, hops, lines, tail, *refs):
     def take(count):
         nonlocal refs
         taken, refs = refs[:count], refs[count:]
         return taken
 
     pieces = len(layers) // 2 * 2
-    rows_ref, vec_ref = take(2)
-    hop_refs, line_in_refs = take(hops), take(lines)
+    if tail:
+        tail_refs, (vec_ref,) = take(5), take(1)
+    else:
+        (rows_ref,), hop_refs, (vec_ref,) = take(1), take(hops), take(1)
+    line_in_refs = take(lines)
     whole_refs = take(pieces - hops - lines)
     gone_ref, vec_out_ref = take(2)
     out_refs = take(pieces // 2)
@@ -1083,17 +1086,26 @@
     ring = Ring(mesh)
     ranks = ring.ranks
     section, mp = ring.section, ring.mp
-    sums = each_of(Hops, ring, hop_refs, line_refs, take(Hops.COUNT * hops))
+    sum_scratch = take(Hops.COUNT * hops)
     alongs = each_of(Line, ring, line_refs + line_in_refs, piece_refs, take(Line.COUNT * (hops + lines)))
+    piece_refs = piece_refs + whole_refs
+    fan_sems = take(Fan.COUNT * len(out_refs))
+
+    vec_sent[0] = vec_ref[...]
+    if tail:
+        start_backward = StartBackward(place, tail_refs, take(StartBackward.COUNT), vec_sent)
+        rows_ref, hop_refs = start_backward.rows_ref, (start_backward.grad_ref,)
+        start_backward.matrix()
+    sums = each_of(Hops, ring, hop_refs, line_refs, sum_scratch)
     home = Home(ring, place, 0, rows_ref, gone_ref, home_sems)
-    piece_refs = piece_refs + whole_refs
     ring.greet_all()
-
     for one in sums:
         one.begin()
-    home.begin()
     for along in alongs[hops:]:
         along.begin()
+    if tail:
+        start_backward.rows()
+    home.begin()
     partners = (ring.other_core(), ring.other_side(), ring.other_section())
 
     def vec_copy(step):
@@ -1105,10 +1117,12 @@
             partners[step],
         )
 
-    vec_sent[0] = vec_ref[...]
     vec_copy(0).start()
 
-    fans = [Fan(ring, out_ref, take(Fan.COUNT)) for out_ref in out_refs]
+    fans = [
+        Fan(ring, out_ref, fan_sems[i * Fan.COUNT : (i + 1) * Fan.COUNT])
+        for i, out_ref in enumerate(out_refs)
+    ]
 
     def leave(which):
         layer, matrix = layers[which]
@@ -1171,23 +1185,92 @@
     others(lambda other: vec_line_copy(other).wait_send())
 
 
-def finish(mesh, place, rows, vecs, grads, lines, wholes, layers):
+class StartBackward:
+    COUNT = 5
+
+    @staticmethod
+    def scratch(rows, width, weight):
+        return [
+            pltpu.VMEM((rows, width), F32),
+            pltpu.VMEM((rows, width), F32),
+            pltpu.VMEM((rows, width), LOW),
+            pltpu.VMEM((2, rows // 2, width), LOW),
+            pltpu.VMEM(weight, LOW),
+        ]
+
+    def __init__(self, place, refs, scratch, vec_ref):
+        self.members, self.vec_ref = place.members, vec_ref
+        self.heads_ref, self.source_ref, self.middle_ref, self.vecs_ref, self.weight_ref = refs
+        self.wide_ref, self.total_ref, self.normed_ref, self.rows_ref, self.grad_ref = scratch
+        self.shards = self.weight_ref.shape[0] // self.members
+        self.cut = 8 * self.weight_ref.shape[4]
+        self.gain, self.bias = self.vecs_ref[0, 0:1], self.vecs_ref[0, 1:2]
+        block, count = Projection.BLOCK, self.wide_ref.shape[0] // Projection.BLOCK
+        self.blocks = [slice(i * block, (i + 1) * block) for i in range(count)]
+
+    def parts(self):
+        for rank in range(self.members):
+            for shard in range(self.shards):
+                yield rank, rank * self.shards + shard, slice(shard * self.cut, (shard + 1) * self.cut)
+
+    def matrix(self):
+        halves_into(self.wide_ref, self.source_ref)
+        for span in self.blocks:
+            self.normed_ref[span] = layer_norm(self.wide_ref[span], self.gain, self.bias).astype(LOW)
+        for rank, at, lanes in self.parts():
+            grad = dot_columns(self.heads_ref[rank, :, lanes], self.normed_ref[...]).astype(LOW)
+            self.grad_ref[at] = grad.reshape(self.grad_ref.shape[1:])
+
+    def rows(self):
+        width = self.wide_ref.shape[1]
+        gain_sum = bias_sum = jnp.zeros((1, width), F32)
+        for span in self.blocks:
+            grad = None
+            for rank, at, lanes in self.parts():
+                part = dot(self.heads_ref[rank, span, lanes], self.weight_ref[at].reshape(self.cut, width))
+                grad = part if grad is None else grad + part
+            source = self.wide_ref[span]
+            offset = source - jnp.mean(source, -1, keepdims=True)
+            scale = lax.rsqrt(jnp.mean(offset * offset, -1, keepdims=True) + 1e-05)
+            unit = offset * scale
+            inner = grad * self.gain
+            back = inner - jnp.mean(inner, -1, keepdims=True) - unit * jnp.mean(inner * unit, -1, keepdims=True)
+            self.total_ref[span] = self.middle_ref[span] + back * scale
+            gain_sum = gain_sum + jnp.sum(grad * unit, 0, keepdims=True)
+            bias_sum = bias_sum + jnp.sum(grad, 0, keepdims=True)
+        half = self.wide_ref.shape[0] // 2
+        for part in range(2):
+            self.rows_ref[part] = self.total_ref[part * half : (part + 1) * half].astype(LOW)
+        self.vec_ref[0, 0, 0:1] = gain_sum
+        self.vec_ref[0, 0, 1:2] = bias_sum
+
+
+def finish(mesh, place, rows, vecs, grads, lines, wholes, layers, tail=None):
     ranks, items = place.ranks, place.items
     held = pl.BlockSpec(memory_space=pltpu.VMEM)
     dma = pltpu.SemaphoreType.DMA
     pieces = len(layers)
+    if tail is None:
+        first, more = (rows, *grads), []
+    else:
+        heads, source, _, _, weight = tail
+        first, grads = tail, [weight]
+        rows = source
+        more = StartBackward.scratch(2 * source.shape[1], source.shape[2], weight.shape)
     sources = list(grads) + list(lines) + list(wholes)
     sizes = [None] * (pieces // 2)
     for (_, matrix), source in zip(layers, sources):
         sizes[matrix] = (2, 2, 2) + source.shape[-2:]
     return pl.pallas_call(
-        functools.partial(finish_kernel, mesh, place, layers, len(grads), len(lines)),
+        functools.partial(
+            finish_kernel, mesh, place, layers, len(grads), len(lines), tail is not None
+        ),
         out_shape=(
-            jax.ShapeDtypeStruct((items,) + rows.shape[1:], rows.dtype),
+            jax.ShapeDtypeStruct((items,) + rows.shape[1:], LOW),
             jax.ShapeDtypeStruct(vecs.shape, F32),
         )
         + tuple(jax.ShapeDtypeStruct(size, LOW) for size in sizes),
-        in_specs=[held] * (2 + pieces),
+        in_specs=[held] * (len(first) + 1 + len(lines) + len(wholes)),
         out_specs=(pl.BlockSpec(memory_space=pl.ANY),) + (held,) * (1 + pieces // 2),
         scratch_shapes=[
             pltpu.VMEM((3,) + vecs.shape, F32),
@@ -1203,12 +1286,13 @@
         + [pltpu.VMEM((ranks,) + x.shape[-2:], LOW) for x in grads]
         + scratch_of(Hops, grads)
         + scratch_of(Line, sources[: len(grads) + len(lines)])
-        + Fan.scratch() * (pieces // 2),
+        + Fan.scratch() * (pieces // 2)
+        + more,
         cost_estimate=cost(40),
         compiler_params=pltpu.CompilerParams(
             collective_id=1, has_side_effects=True, vmem_limit_bytes=VMEM_BYTES
         ),
-    )(rows, vecs, *sources)
+    )(*first, vecs, *lines, *wholes)
 
 
 def dot_rows(left, right):
@@ -1317,10 +1401,9 @@
             pre = dot_rows(second_ref[...], up) + vecs_ref[rank, 6:7]
             hidden_ref[...] = gelu_of(pre).astype(LOW)
             result_ref[...] += dot(hidden_ref[...], down)
-            if rank == 0:
+            if rank == ring.ranks - 1:
                 gather_phase(1)
-            for item in range(place.items):
-                if item * 2 // place.items == rank:
+                for item in range(place.items):
                     rows.give(item)
         for part in range(2):
             low = result_ref[part * here // 2 : (part + 1) * here // 2].astype(LOW)
@@ -1329,7 +1412,6 @@
         projection.norm()
         for member in range(members):
             projection.project(member)
-        gather_phase(2)
         mask_keys(bias_ref, used_slots(place, vecs_ref))
     else:
         gather_phase(1)
@@ -1356,9 +1438,8 @@
         return here if top is None else jnp.maximum(top, here)
 
     def phases(step):
-        if not fused:
-            pl.when(step == 3)(functools.partial(gather_phase, 2))
-        pl.when(step == 4)(functools.partial(gather_phase, 3))
+        pl.when(step == 2)(functools.partial(gather_phase, 2))
+        pl.when(step == 5)(functools.partial(gather_phase, 3))
         if fused:
             for member in range(1, members):
                 pl.when(step == member * each)(lambda member=member: to_rows.copy(member).start())
@@ -1636,7 +1717,7 @@
         back.end()
 
 
-REDUCTION_STEPS = (0, 1, 4, 6, 9)
+REDUCTION_STEPS = (0, 1, 5, 7, 9)
 
 
 def joint_backward(mesh, place, qkv, length, grad, out, log, blocks, matrices, fused):
@@ -2203,10 +2284,9 @@
         grad_projected, (*lines, piece) = attention_backward(
             mesh, place, qkv_zero, length, grad_heads, None, None, later, fused, None, (line,)
         )
-        grad_source, grad_qkv_zero, vectors_zero = layer_start_backward(
-            source, first_norm(source, params[0]), grad_middle, grad_projected, params[0], vectors
-        )
-        grads, done = [pack_qkv(grad_qkv_zero)], [piece] + done
+        grads, done, rows = [], [piece] + done, None
+        tail = (grad_projected[:, 0], arrived, grad_middle, vecs, first[0])
+        vectors_zero = jnp.concatenate((jnp.zeros((2 * width,), F32),) + vectors)
         layers = ((0, 0), (0, 1), (0, 2), (0, 3), (1, 0), (1, 1), (1, 2), (1, 3))
     else:
         boundary, kept_zero = first_forward(place, source, length, params[0])
@@ -2225,9 +2305,11 @@
         )
         grads = [pack_qkv(grad_qkv_zero), pack_qkv(grad_qkv_one)]
         layers = ((0, 0), (1, 0), (0, 1), (0, 2), (0, 3), (1, 1), (1, 2), (1, 3))
-    rows = grad_source.astype(LOW).reshape(2, block_rows, width)
+        rows, tail = grad_source.astype(LOW).reshape(2, block_rows, width), None
     vectors = jnp.stack([vectors_zero, vectors_one]).reshape(2, -1, width)
-    gone, sums, *matrices = finish(mesh, place, rows, vectors, grads, lines, done, layers)
+    gone, sums, *matrices = finish(
+        mesh, place, rows, vectors, grads, lines, done, layers, tail
+    )
     dps = mesh.shape["dp"]
     if dps > 4:
         sums, *matrices = (

time: 457 us -> 437 us (0.956)
  matrix products: 14.5 us -> 5.67 us
  other arithmetic: 16.7 us -> 9.98 us
    dot_general x2 -> x1, matrix products: 7.57 us -> 2.2 us  [layer_start_backward(): jnp.einsum('rpse,rped->sd', grad_projected, weight, preferred_element_typ...]
    pallas_call x1, Pallas kernels: 76.8 us -> 71.5 us  [joint_backward(): pl.pallas_call(functools.partial(joint_backward_kernel, mesh, place, pair...]
    pallas_call x1, Pallas kernels: 63.3 us -> 68.1 us  [finish(): pl.pallas_call(functools.partial(finish_kernel, mesh, place, layers, len(...]
where the time goes in v6:
time: 437 us; the launch traced here: 432 us
  Pallas kernels  400 us (92%)
  local copies, waits for them, and re-layouts  13.7 us (3%)
  other arithmetic  9.98 us (2%)
  matrix products  5.67 us (1%)
    pallas_call x1, Pallas kernels, start(): pl.pallas_call(functools.partial(start_kernel, mesh, place, count, fused)...  83.9 us
    pallas_call x1, Pallas kernels, joint_forward(): pl.pallas_call(functools.partial(joint_forward_kernel, mesh, place, pairs...  74.1 us
    pallas_call x1, Pallas kernels, joint_backward(): pl.pallas_call(functools.partial(joint_backward_kernel, mesh, place, pair...  71.5 us
    pallas_call x1, Pallas kernels, finish(): pl.pallas_call(functools.partial(finish_kernel, mesh, place, layers, len(...  68.1 us
    pallas_call x2, Pallas kernels, mlp_backward(): pl.pallas_call(functools.partial(mlp_backward_kernel, mesh, place, layer,...  61.3 us
    pallas_call x1, Pallas kernels, within_backward(): pl.pallas_call(functools.partial(within_backward_kernel, mesh, place, pai...  36.6 us

profile of v6, /device:TPU:0, one launch (start us, length us, event | category | flops | bytes accessed | tf_op | source)
XLA Modules:
  0.0 431.5 jit_solution(6213821901702610263)
XLA Ops:
  0.7 2.0 copy.32
  2.7 1.8 copy.31
  4.5 0.7 convert_element_type.66
  5.1 1.4 stack.11.vec_ref
  6.6 83.9 %shard_map.220 = (bf16[2,520,512]{2,1,0:T(8,128)(2,1)}, f32[9,8,512]{2,1,0:T(8,128)}, bf16[4,520,512]{2,1,0:T(8,128)(2,1)}, bf16[4,2,2,2,48,512]{5,4,3,2,1,0:T(8...) custom-call(bf16[4,520,512]{2,1,0:T(8,128)(2,1)} %bitcast.104, ...), custom_call_target="tpu_custom_call" | custom-call | flops 60000002048 | tf_op jit(solution)/shard_map/pallas_call | solution.py:703
  90.5 0.8 fusion.8
  91.9 1.9 fusion.11
  94.4 74.1 %shard_map.221 = (bf16[2080,256]{1,0:T(8,128)(2,1)}, f32[2080,128]{1,0:T(8,128)}, bf16[2,520,512]{2,1,0:T(8,128)(2,1)}, bf16[4,2,2,2,16,512]{5,4,3,2,1,0:T(8,128...) custom-call(s32[1]{0:T(128)} %bitcast.10.length_ref, ...), custom_call_target="tpu_custom_call" | custom-call | flops 44999999488 | tf_op jit(solution)/shard_map/pallas_call | solution.py:1539
  168.5 24.3 %shard_map.222 = (f32[1040,512]{1,0:T(8,128)}, bf16[2,1040,256]{2,1,0:T(8,128)(2,1)}, bf16[4,2,2,2,16,512]{5,4,3,2,1,0:T(8,128)(2,1)}, bf16[4,2,2,2,64,512]{5,4,...) custom-call(bf16[2,520,512]{2,1,0:T(8,128)(2,1)} %get-tuple-element.7, ...), custom_call_target="tpu_custom_call" | custom-call | flops 24999999488 | tf_op jit(solution)/shard_map/pallas_call | solution.py:2030
  192.8 71.5 %shard_map.223 = (bf16[2,2,1040,384]{3,2,1,0:T(8,128)(2,1)}, bf16[16,512]{1,0:T(8,128)(2,1)}, bf16[64,512]{1,0:T(8,128)(2,1)}, bf16[64,512]{1,0:T(8,128)(2,1)}, bf16[4,520,512]{2,1,0:T(8,128)(2,1)}) custom-call(s32[1]{0:T(128)} %bitcast.10.length_ref, bf16[2080,768]{1,0:T(8,128)(2,1)} %get-tuple-element.83.qkv_ref, ...), custom_call_target="tpu_custom_call" | custom-call | flops 65999998976 | tf_op jit(solution)/shard_map/pallas_call | solution.py:1737
  265.5 1.7 copy-done.8
  267.2 3.5 convolution_convert_fusion
  270.7 2.2 fusion.7
  273.8 2.8 add_convert_fusion.1
  276.6 37.1 %shard_map.224 = (f32[1040,512]{1,0:T(8,128)}, bf16[2,1040,256]{2,1,0:T(8,128)(2,1)}, bf16[4,2,2,2,16,512]{5,4,3,2,1,0:T(8,128)(2,1)}, bf16[4,2,2,2,64,512]{5,4,...) custom-call(bf16[2,520,512]{2,1,0:T(8,128)(2,1)} %get-tuple-element.66, ...), custom_call_target="tpu_custom_call" | custom-call | flops 24999999488 | tf_op jit(solution)/shard_map/pallas_call | solution.py:2030
  313.7 0.9 fusion.9
  314.6 0.7 slice_bitcast_fusion.1
  316.1 36.6 %shard_map.225 = (bf16[2,1040,768]{2,1,0:T(8,128)(2,1)}, bf16[4,16,512]{2,1,0:T(8,128)(2,1)}, bf16[4,64,512]{2,1,0:T(8,128)(2,1)}, bf16[4,64,512]{2,1,0:T(8,128)(2,1)}, bf16[48,512]{1,0:T(8,128)(2,1)}) custom-call(s32[1]{0:T(128)} %bitcast.10.length_ref, bf16[2080,768]{1,0:T(8,128)(2,1)} %get-tuple-element.65.x_ref, ...), custom_call_target="tpu_custom_call" | custom-call | flops 30000001024 | tf_op jit(solution)/shard_map/pallas_call | solution.py:1884
  352.7 68.1 %shard_map.226 = (bf16[4,520,512]{2,1,0:T(8,128)(2,1)}, f32[2,10,512]{2,1,0:T(8,128)}, bf16[2,2,2,48,512]{4,3,2,1,0:T(8,128)(2,1)}, bf16[2,2,2,16,512]{4,3,2,1,0...) custom-call(bf16[2,1040,768]{2,1,0:T(8,128)(2,1)} %get-tuple-element.97.refs_0_, ...), custom_call_target="tpu_custom_call" | custom-call | flops 40000000000 | tf_op jit(solution)/shard_map/pallas_call | solution.py:1264
  420.9 4.8 %shard_map.227 = f32[4,520,512]{2,1,0:T(8,128)} custom-call(bf16[4,520,512]{2,1,0:T(8,128)(2,1)} %get-tuple-element.109.zero_ref, bf16[4,520,512]{2,1,0:T(8,128)(2,1)} %get-tuple-element.110.one_ref), custom_call_target="tpu_custom_call" | custom-call | flops 3000000000 | tf_op jit(solution)/shard_map/pallas_call | solution.py:2198
  425.8 1.3 copy.36
  427.2 0.9 copy.35
  428.2 1.1 convert.12
  429.3 0.7 convert.10
  (58 shorter events, 4.9 us)
Async XLA Ops:
  192.8 71.5 %copy-start = (bf16[2,520,512]{2,1,0:T(8,128)(2,1)S(1)}, bf16[2,520,512]{2,1,0:T(8,128)(2,1)}, u32[]{:S(2)}) copy-start(bf16[2,520,512]{2,1,0:T(8,128)(2,1)} %get-tuple-element.76.refs_0_) | copy-start | bytes 3194884
  265.3 1.9 copy-start.8
  267.2 3.5 copy-start.7
  276.6 38.8 %copy-start.6 = (f32[8,512]{1,0:T(8,128)S(1)}, f32[8,512]{1,0:T(8,128)}, u32[]{:S(2)}) copy-start(f32[8,512]{1,0:T(8,128)} %get-tuple-element.101) | copy-start | bytes 49156
  420.9 4.8 %copy-start.2 = (bf16[2,2,2,64,512]{4,3,2,1,0:T(8,128)(2,1)S(1)}, bf16[2,2,2,64,512]{4,3,2,1,0:T(8,128)(2,1)}, u32[]{:S(2)}) copy-start(bf16[2,2,2,64,512]{4,3,2,1,0:T(8,128)(2,1)} %get-tuple-element.114) | copy-start | bytes 1572868
  425.7 1.5 copy-start.3
  425.8 2.4 copy-start.1
  427.2 2.1 copy-start.4
  427.2 2.9 copy-start.5

commit v7 on v6

--- a/solution.py
+++ b/solution.py
@@ -887,6 +887,38 @@
         (self.begin, self.one, self.two, self.line)[number]()
 
 
+class FetchedHops(Hops):
+    COUNT = Hops.COUNT + 2
+
+    @staticmethod
+    def scratch(ranks, rows, width):
+        kept = (ranks, 2, 2, rows, width)
+        return Hops.scratch(ranks, rows, width) + [pltpu.VMEM(kept, LOW), pltpu.SemaphoreType.DMA]
+
+    def __init__(self, ring, grad_ref, line_ref, scratch):
+        super().__init__(ring, grad_ref, line_ref, scratch[: Hops.COUNT])
+        self.kept_ref, self.fetch_sem = scratch[Hops.COUNT :]
+
+    def fetch(self):
+        return pltpu.make_async_copy(
+            self.grad_ref.at[:, :, :, self.ring.core], self.kept_ref, self.fetch_sem
+        )
+
+    def own(self, index, half):
+        side, section = self.FLIPS[index]
+        slots = self.halves[half]
+        side, section, _ = self.ring.cell(side, section)
+        return wide(self.kept_ref[slots, side, section]) + wide(self.core_got[index, slots])
+
+    def begin(self):
+        super().begin()
+        self.fetch().start()
+
+    def one(self):
+        self.fetch().wait()
+        super().one()
+
+
 class Line:
     COUNT = 3
 
@@ -1093,7 +1125,7 @@
 
     vec_sent[0] = vec_ref[...]
     if tail:
-        start_backward = StartBackward(place, tail_refs, take(StartBackward.COUNT), vec_sent)
+        start_backward = StartBackward(place, tail_refs, take(StartBackward.COUNT), 0)
         rows_ref, hop_refs = start_backward.rows_ref, (start_backward.grad_ref,)
         start_backward.matrix()
     sums = each_of(Hops, ring, hop_refs, line_refs, sum_scratch)
@@ -1104,7 +1136,7 @@
     for along in alongs[hops:]:
         along.begin()
     if tail:
-        start_backward.rows()
+        vec_sent[0, 0, 0:1], vec_sent[0, 0, 1:2] = start_backward.rows()
     home.begin()
     partners = (ring.other_core(), ring.other_side(), ring.other_section())
 
@@ -1198,27 +1230,31 @@
             pltpu.VMEM(weight, LOW),
         ]
 
-    def __init__(self, place, refs, scratch, vec_ref):
-        self.members, self.vec_ref = place.members, vec_ref
+    def __init__(self, place, refs, scratch, slot):
+        self.members = place.members
         self.heads_ref, self.source_ref, self.middle_ref, self.vecs_ref, self.weight_ref = refs
         self.wide_ref, self.total_ref, self.normed_ref, self.rows_ref, self.grad_ref = scratch
         self.shards = self.weight_ref.shape[0] // self.members
         self.cut = 8 * self.weight_ref.shape[4]
-        self.gain, self.bias = self.vecs_ref[0, 0:1], self.vecs_ref[0, 1:2]
+        self.gain, self.bias = self.vecs_ref[slot, 0:1], self.vecs_ref[slot, 1:2]
         block, count = Projection.BLOCK, self.wide_ref.shape[0] // Projection.BLOCK
         self.blocks = [slice(i * block, (i + 1) * block) for i in range(count)]
 
-    def parts(self):
+    def parts(self, span):
         for rank in range(self.members):
             for shard in range(self.shards):
-                yield rank, rank * self.shards + shard, slice(shard * self.cut, (shard + 1) * self.cut)
+                at = rank * self.shards + shard
+                if len(self.heads_ref.shape) == 4:
+                    yield at, self.heads_ref[rank, shard, span]
+                else:
+                    yield at, self.heads_ref[rank, span, shard * self.cut : (shard + 1) * self.cut]
 
     def matrix(self):
         halves_into(self.wide_ref, self.source_ref)
         for span in self.blocks:
             self.normed_ref[span] = layer_norm(self.wide_ref[span], self.gain, self.bias).astype(LOW)
-        for rank, at, lanes in self.parts():
-            grad = dot_columns(self.heads_ref[rank, :, lanes], self.normed_ref[...]).astype(LOW)
+        for at, heads in self.parts(slice(None)):
+            grad = dot_columns(heads, self.normed_ref[...]).astype(LOW)
             self.grad_ref[at] = grad.reshape(self.grad_ref.shape[1:])
 
     def rows(self):
@@ -1226,8 +1262,8 @@
         gain_sum = bias_sum = jnp.zeros((1, width), F32)
         for span in self.blocks:
             grad = None
-            for rank, at, lanes in self.parts():
-                part = dot(self.heads_ref[rank, span, lanes], self.weight_ref[at].reshape(self.cut, width))
+            for at, heads in self.parts(span):
+                part = dot(heads, self.weight_ref[at].reshape(self.cut, width))
                 grad = part if grad is None else grad + part
             source = self.wide_ref[span]
             offset = source - jnp.mean(source, -1, keepdims=True)
@@ -1241,8 +1277,7 @@
         half = self.wide_ref.shape[0] // 2
         for part in range(2):
             self.rows_ref[part] = self.total_ref[part * half : (part + 1) * half].astype(LOW)
-        self.vec_ref[0, 0, 0:1] = gain_sum
-        self.vec_ref[0, 0, 1:2] = bias_sum
+        return gain_sum, bias_sum
 
 
 def finish(mesh, place, rows, vecs, grads, lines, wholes, layers, tail=None):
@@ -1336,6 +1371,14 @@
     lengths = jnp.where(core == section, own[7:8], other[7:8])
     lane = lax.broadcasted_iota(jnp.int32, lengths.shape, 1)
     return jnp.sum(jnp.where(lane == mp // place.chips, lengths, 0.0), -1, keepdims=True)
+
+
+def slots_of(place, ref, fused):
+    return used_slots(place, ref) if fused else wide(ref[0])
+
+
+def length_spec(fused):
+    return pl.BlockSpec(memory_space=pltpu.VMEM if fused else pltpu.SMEM)
 
 
 def gelu_of(x):
@@ -1545,7 +1588,7 @@
         )
         + fulls
         + more,
-        in_specs=[pl.BlockSpec(memory_space=pltpu.SMEM), away, away]
+        in_specs=[length_spec(fused), away, away]
         + [held] * (len(inputs) + len(pieces)),
         out_specs=(held,) * 3 + (away,) * len(fulls) + (held,) * len(more),
         scratch_shapes=Gather.scratch(ranks) * len(pieces)
@@ -1572,7 +1615,7 @@
 def backward_head(q, k, v, grad, head, limit):
     scores = dot_rows(k, half_of(q, head))
     if limit is not None:
-        row = lax.broadcasted_iota(jnp.int32, (scores.shape[0], 1), 0)
+        row = wide(lax.broadcasted_iota(jnp.int32, (scores.shape[0], 1), 0))
         scores = jnp.where(row < limit, scores, MASKED)
     expon = jnp.exp(scores - jnp.max(scores, 0, keepdims=True))
     probs = expon / jnp.sum(expon, 0, keepdims=True)
@@ -1621,14 +1664,14 @@
         keep(own_ref.at[me], got_ref.at[span(me)], local)
     home_sems = take(3)
     line_refs = take(count)
-    sums = each_of(Hops, ring, matrix_refs, line_refs, take(Hops.COUNT * count))
+    sums = each_of(FetchedHops, ring, matrix_refs, line_refs, take(FetchedHops.COUNT * count))
     alongs = each_of(Line, ring, line_refs, piece_refs, take(Line.COUNT * count))
     home = Home(ring, place, 1, rows_ref, gone_ref, home_sems)
     home.begin()
-    mask_keys(bias_ref, wide(length_ref[0]))
+    mask_keys(bias_ref, slots_of(place, length_ref, fused))
 
     def phases(whole_step):
-        for number, when in enumerate(REDUCTION_STEPS[:4]):
+        for number, when in enumerate(REDUCTION_STEPS):
 
             @pl.when(whole_step == when)
             def _():
@@ -1637,15 +1680,6 @@
                 if number == 3:
                     for along in alongs:
                         along.begin()
-
-        @pl.when(whole_step == REDUCTION_STEPS[4])
-        def _():
-            for one in sums:
-                one.end()
-            for along in alongs:
-                along.total()
-                along.end()
-            home.end()
 
         if fused:
             pl.when(whole_step == 0)(to_heads.arrive)
@@ -1710,6 +1744,12 @@
                 back.begin()
                 keep(sent_ref.at[index, span(me)], swapped_ref.at[me, index], local)
 
+    for one in sums:
+        one.end()
+    for along in alongs:
+        along.total()
+        along.end()
+    home.end()
     if fused:
         to_heads.end()
     for back in backs:
@@ -1717,7 +1757,7 @@
         back.end()
 
 
-REDUCTION_STEPS = (0, 1, 5, 7, 9)
+REDUCTION_STEPS = (0, 1, 5, 7)
 
 
 def joint_backward(mesh, place, qkv, length, grad, out, log, blocks, matrices, fused):
@@ -1738,8 +1778,9 @@
         functools.partial(joint_backward_kernel, mesh, place, pairs, block, len(matrices), fused),
         out_shape=(jax.ShapeDtypeStruct(shape, LOW),) + piece_shapes(matrices) + (gone,),
         in_specs=[
-            pl.BlockSpec(memory_space=pltpu.SMEM),
-            *[held] * (5 + len(matrices)),
+            length_spec(fused),
+            *[held] * 4,
+            *[pl.BlockSpec(memory_space=pl.ANY)] * (1 + len(matrices)),
         ],
         out_specs=(held,) * (1 + len(matrices)) + (pl.BlockSpec(memory_space=pl.ANY),),
         scratch_shapes=[
@@ -1755,7 +1796,7 @@
         + swap_scratch
         + Home.scratch(place.items)
         + [pltpu.VMEM(line.shape, LOW) for line in line_shapes(matrices)]
-        + scratch_of(Hops, matrices)
+        + scratch_of(FetchedHops, matrices)
         + scratch_of(Line, matrices),
         cost_estimate=cost(66),
         compiler_params=pltpu.CompilerParams(
@@ -1822,8 +1863,8 @@
         to_heads.begin()
         keep(own_ref.at[me], got_ref.at[span(me)], local)
         grad_ref = got_ref
-    sums = each_of(Hops, ring, matrix_refs, line_refs, refs)
-    alongs = each_of(Line, ring, ready_refs, piece_refs, refs[Hops.COUNT * count :])
+    sums = each_of(FetchedHops, ring, matrix_refs, line_refs, refs)
+    alongs = each_of(Line, ring, ready_refs, piece_refs, refs[FetchedHops.COUNT * count :])
     for along in alongs:
         along.begin()
 
@@ -1853,7 +1894,7 @@
         for number, when in ((1, 0), (2, 3)):
             pl.when(view == when)(functools.partial(every, number))
 
-    group(pl.ds(PATCH_ROWS, TEXT), length_ref[0])
+    group(pl.ds(PATCH_ROWS, TEXT), slots_of(place, length_ref, fused))
     if fused:
         back.begin()
         keep(sent_ref.at[span(me)], swapped_ref.at[me], local)
@@ -1884,9 +1925,11 @@
     grads, *lines = pl.pallas_call(
         functools.partial(within_backward_kernel, mesh, place, pairs, len(matrices), len(ready), fused),
         out_shape=(jax.ShapeDtypeStruct(shape, LOW),) + line_shapes(matrices) + piece_shapes(ready),
-        in_specs=[pl.BlockSpec(memory_space=pltpu.SMEM)] + [held] * (2 + len(matrices) + len(ready)),
+        in_specs=[length_spec(fused), held, held]
+        + [pl.BlockSpec(memory_space=pl.ANY)] * len(matrices)
+        + [held] * len(ready),
         out_specs=(held,) * (1 + len(matrices) + len(ready)),
-        scratch_shapes=swap_scratch + scratch_of(Hops, matrices) + scratch_of(Line, ready),
+        scratch_shapes=swap_scratch + scratch_of(FetchedHops, matrices) + scratch_of(Line, ready),
         cost_estimate=cost(30),
         compiler_params=pltpu.CompilerParams(
             collective_id=7, has_side_effects=True, vmem_limit_bytes=VMEM_BYTES
@@ -1925,8 +1968,11 @@
         taken, refs = refs[:count], refs[count:]
         return taken
 
-    source_ref, mixed_ref, upstream_ref, vecs_ref, out_ref, up_ref, down_ref = take(7)
-    matrix_refs = take(count)
+    source_ref, mixed_ref, vecs_ref, out_ref, up_ref, down_ref = take(6)
+    if layer == 1:
+        (upstream_ref,) = take(1)
+    else:
+        tail_refs = take(4)
     middle_out_ref, heads_ref, grad_out_ref, grad_up_ref, grad_down_ref, sums_ref = take(6)
     (blocks_ref,) = take(1) if layer == 1 else (None,)
     line_refs = take(count)
@@ -1936,11 +1982,22 @@
     rows, width = middle_ref.shape
     if layer == 1:
         (result_ref,) = take(1)
-    sums = each_of(Hops, ring, matrix_refs, line_refs, take(Hops.COUNT * count))
-    if sums:
+    sums = []
+    if layer == 0:
+        heads_in_ref, source_in_ref, middle_in_ref, weight_ref = tail_refs
+        after = StartBackward(
+            place,
+            (heads_in_ref, source_in_ref, middle_in_ref, vecs_ref, weight_ref),
+            take(StartBackward.COUNT),
+            ranks,
+        )
+        upstream_ref = after.rows_ref
+        after.matrix()
+        sums = each_of(Hops, ring, (after.grad_ref,), line_refs, take(Hops.COUNT))
         ring.greet_lines()
-    for one in sums:
-        one.begin()
+        for one in sums:
+            one.begin()
+        sums_ref[4 + ranks : 5 + ranks], sums_ref[5 + ranks : 6 + ranks] = after.rows()
     slot = layer * ranks
     vector = [vecs_ref[slot, i : i + 1] for i in range(6)]
     _, _, bias_out, gain_two, bias_two, bias_down = vector
@@ -2017,7 +2074,7 @@
         one.end()
 
 
-def mlp_backward(mesh, place, layer, source, mixed, upstream, vecs, weights, matrices):
+def mlp_backward(mesh, place, layer, source, mixed, vecs, weights, upstream):
     ranks = place.ranks
     _, half, width = source.shape
     rows = 2 * half
@@ -2026,18 +2083,22 @@
     blocks, more = (), []
     if layer == 1:
         blocks, more = (shape((2, half, width), LOW),), [pltpu.VMEM((rows, width), F32)]
-    lines = line_shapes(matrices)
+    lines = ()
+    if layer == 0:
+        weight = upstream[-1]
+        lines = line_shapes((weight,))
+        more = [*StartBackward.scratch(rows, width, weight.shape), *scratch_of(Hops, (weight,))]
     return pl.pallas_call(
-        functools.partial(mlp_backward_kernel, mesh, place, layer, len(matrices)),
+        functools.partial(mlp_backward_kernel, mesh, place, layer, len(lines)),
         out_shape=(
             shape((rows, width), F32),
             shape(mixed.shape, LOW),
             *(shape(w.shape, LOW) for w in weights),
-            shape((4 + ranks, width), F32),
+            shape((4 + ranks + 2 * len(lines), width), F32),
         )
         + blocks
         + lines,
-        in_specs=[held] * (7 + len(matrices)),
+        in_specs=[held] * (6 + len(upstream)),
         out_specs=(held,) * (6 + len(blocks) + len(lines)),
         scratch_shapes=[
             pltpu.VMEM((rows, width), F32),
@@ -2048,15 +2109,14 @@
             pltpu.VMEM((rows, width), LOW),
             pltpu.VMEM((rows, width), LOW),
         ]
-        + more
-        + scratch_of(Hops, matrices),
+        + more,
         cost_estimate=cost(25),
         compiler_params=pltpu.CompilerParams(
-            collective_id=10 if matrices else None,
-            has_side_effects=bool(matrices),
+            collective_id=10 if lines else None,
+            has_side_effects=bool(lines),
             vmem_limit_bytes=VMEM_BYTES,
         ),
-    )(source, mixed, upstream, vecs, *weights, *matrices)
+    )(source, mixed, vecs, *weights, *upstream)
 
 
 def layer_norm(values, scale_vec, shift_vec):
@@ -2263,30 +2323,30 @@
         qkv_zero, mixed_zero = ready
         inputs_two = (arrived, mixed_zero, vecs, first_of_second[0], *first[1:])
         (qkv, heads, logs, mixed), cotangent, fulls, boundary = joint_forward(
-            mesh, place, inputs_two, length, second, inputs[0], staged, True
-        )
-        source_one = boundary.reshape(-1, width).astype(F32)
+            mesh, place, inputs_two, vecs, second, inputs[0], staged, True
+        )
         grad_middle, grad_heads, *later, found, results = mlp_backward(
-            mesh, place, 1, boundary, mixed, cotangent, vecs, fulls, ()
-        )
-        vectors = (found[2], found[0], found[1], found[3], found[4:].reshape(-1))
+            mesh, place, 1, boundary, mixed, vecs, fulls, (cotangent,)
+        )
+        def vectors_of(found, first):
+            return jnp.concatenate(
+                (*first, found[2], found[0], found[1], found[3], found[4 : 4 + ranks].reshape(-1))
+            )
+
         grad_projected, (*done, results) = attention_backward(
-            mesh, place, qkv, length, grad_heads, heads, logs, later, fused, results
-        )
-        grad_boundary, grad_qkv, vectors_one = layer_start_backward(
-            source_one, first_norm(source_one, params[1]), grad_middle, grad_projected, params[1], vectors
-        )
-        upstream = grad_boundary.astype(LOW).reshape(2, block_rows, width)
-        grad_middle, grad_heads, *later, found, line = mlp_backward(
-            mesh, place, 0, arrived, mixed_zero, upstream, vecs, first[1:], (pack_qkv(grad_qkv),)
-        )
-        vectors = (found[2], found[0], found[1], found[3], found[4:].reshape(-1))
+            mesh, place, qkv, vecs, grad_heads, heads, logs, later, fused, results
+        )
+        tail = (grad_projected, boundary, grad_middle, first_of_second[0])
+        grad_middle, grad_heads, *later, found_zero, line = mlp_backward(
+            mesh, place, 0, arrived, mixed_zero, vecs, first[1:], tail
+        )
+        vectors_one = vectors_of(found, found_zero[4 + ranks :])
         grad_projected, (*lines, piece) = attention_backward(
-            mesh, place, qkv_zero, length, grad_heads, None, None, later, fused, None, (line,)
+            mesh, place, qkv_zero, vecs, grad_heads, None, None, later, fused, None, (line,)
         )
         grads, done, rows = [], [piece] + done, None
         tail = (grad_projected[:, 0], arrived, grad_middle, vecs, first[0])
-        vectors_zero = jnp.concatenate((jnp.zeros((2 * width,), F32),) + vectors)
+        vectors_zero = vectors_of(found_zero, jnp.zeros((2, width), F32))
         layers = ((0, 0), (0, 1), (0, 2), (0, 3), (1, 0), (1, 1), (1, 2), (1, 3))
     else:
         boundary, kept_zero = first_forward(place, source, length, params[0])

time: 437 us -> 424 us (0.970)
  other arithmetic: 9.98 us -> 3.36 us
  matrix products: 5.67 us -> 0 us
    pallas_call x2, Pallas kernels: 61.3 us -> 67.6 us  [mlp_backward(): pl.pallas_call(functools.partial(mlp_backward_kernel, mesh, place, layer,...]
    dot_general x2 -> x0, matrix products: 5.67 us -> none  [the longest x1 3.47 us: layer_start_backward(): jnp.einsum('rpse,sd->rped', grad_projected, normed, preferred_element_typ...]
where the time goes in v7:
time: 424 us; the launch traced here: 418 us
  Pallas kernels  404 us (95%)
  local copies, waits for them, and re-layouts  10.5 us (2%)
    pallas_call x1, Pallas kernels, start(): pl.pallas_call(functools.partial(start_kernel, mesh, place, count, fused)...  84 us
    pallas_call x1, Pallas kernels, joint_forward(): pl.pallas_call(functools.partial(joint_forward_kernel, mesh, place, pairs...  74.3 us
    pallas_call x1, Pallas kernels, joint_backward(): pl.pallas_call(functools.partial(joint_backward_kernel, mesh, place, pair...  69.8 us
    pallas_call x1, Pallas kernels, finish(): pl.pallas_call(functools.partial(finish_kernel, mesh, place, layers, len(...  68.1 us
    pallas_call x2, Pallas kernels, mlp_backward(): pl.pallas_call(functools.partial(mlp_backward_kernel, mesh, place, layer,...  67.6 us
    pallas_call x1, Pallas kernels, within_backward(): pl.pallas_call(functools.partial(within_backward_kernel, mesh, place, pai...  35 us

profile of v7, /device:TPU:0, one launch (start us, length us, event | category | flops | bytes accessed | tf_op | source)
XLA Modules:
  0.0 418.4 jit_solution(12568579914474469648)
XLA Ops:
  0.6 2.0 copy.30
  2.7 1.8 copy.29
  4.5 0.7 convert_element_type.40
  5.1 1.4 stack.11.vec_ref
  6.5 84.0 %shard_map.220 = (bf16[2,520,512]{2,1,0:T(8,128)(2,1)}, f32[9,8,512]{2,1,0:T(8,128)}, bf16[4,520,512]{2,1,0:T(8,128)(2,1)}, bf16[4,2,2,2,48,512]{5,4,3,2,1,0:T(8...) custom-call(bf16[4,520,512]{2,1,0:T(8,128)(2,1)} %bitcast.80, ...), custom_call_target="tpu_custom_call" | custom-call | flops 60000002048 | tf_op jit(solution)/shard_map/pallas_call | solution.py:703
  90.5 74.3 %shard_map.221 = (bf16[2080,256]{1,0:T(8,128)(2,1)}, f32[2080,128]{1,0:T(8,128)}, bf16[2,520,512]{2,1,0:T(8,128)(2,1)}, bf16[4,2,2,2,16,512]{5,4,3,2,1,0:T(8,128...) custom-call(f32[9,8,512]{2,1,0:T(8,128)} %get-tuple-element.64.lengt, ...), custom_call_target="tpu_custom_call" | custom-call | flops 44999999488 | tf_op jit(solution)/shard_map/pallas_call | solution.py:1582
  164.8 24.2 %shard_map.222 = (f32[1040,512]{1,0:T(8,128)}, bf16[2,1040,256]{2,1,0:T(8,128)(2,1)}, bf16[4,2,2,2,16,512]{5,4,3,2,1,0:T(8,128)(2,1)}, bf16[4,2,2,2,64,512]{5,4,...) custom-call(bf16[2,520,512]{2,1,0:T(8,128)(2,1)} %get-tuple-element.7, ...), custom_call_target="tpu_custom_call" | custom-call | flops 24999999488 | tf_op jit(solution)/shard_map/pallas_call | solution.py:2091
  189.0 69.8 %shard_map.223 = (bf16[2,2,1040,384]{3,2,1,0:T(8,128)(2,1)}, bf16[16,512]{1,0:T(8,128)(2,1)}, bf16[64,512]{1,0:T(8,128)(2,1)}, bf16[64,512]{1,0:T(8,128)(2,1)}, bf16[4,520,512]{2,1,0:T(8,128)(2,1)}) custom-call(f32[9,8,512]{2,1,0:T(8,128)} %get-tuple-element.64.length_ref.refs_2_.refs_3_, bf16[2080,768]{1,0:T(8,128)(2,1)} %get-tuple-element.76.qkv_ref, ...), custom_call_target="tpu_custom_call" | custom-call | flops 65999998976 | tf_op jit(solution)/shard_map/pallas_call | solution.py:1777
  258.8 0.0 copy-start.5
  258.9 43.4 %shard_map.224 = (f32[1040,512]{1,0:T(8,128)}, bf16[2,1040,256]{2,1,0:T(8,128)(2,1)}, bf16[4,2,2,2,16,512]{5,4,3,2,1,0:T(8,128)(2,1)}, bf16[4,2,2,2,64,512]{5,4,...) custom-call(bf16[2,520,512]{2,1,0:T(8,128)(2,1)} %get-tuple-element.6, ...), custom_call_target="tpu_custom_call" | custom-call | flops 24999999488 | tf_op jit(solution)/shard_map/pallas_call | solution.py:2091
  302.3 0.9 fusion
  303.2 0.7 slice_bitcast_fusion.1
  304.1 0.6 pad_maximum_fusion.refs_5_
  304.8 35.0 %shard_map.225 = (bf16[2,1040,768]{2,1,0:T(8,128)(2,1)}, bf16[4,16,512]{2,1,0:T(8,128)(2,1)}, bf16[4,64,512]{2,1,0:T(8,128)(2,1)}, bf16[4,64,512]{2,1,0:T(8,128)(2,1)}, bf16[48,512]{1,0:T(8,128)(2,1)}) custom-call(f32[9,8,512]{2,1,0:T(8,128)} %get-tuple-element.64.length_ref.refs_2_.refs_3_, bf16[2080,768]{1,0:T(8,128)(2,1)} %get-tuple-element.65.x_ref, ...), custom_call_target="tpu_custom_call" | custom-call | flops 30000001024 | tf_op jit(solution)/shard_map/pallas_call | solution.py:1925
  339.8 68.1 %shard_map.226 = (bf16[4,520,512]{2,1,0:T(8,128)(2,1)}, f32[2,10,512]{2,1,0:T(8,128)}, bf16[2,2,2,48,512]{4,3,2,1,0:T(8,128)(2,1)}, bf16[2,2,2,16,512]{4,3,2,1,0...) custom-call(bf16[2,1040,768]{2,1,0:T(8,128)(2,1)} %get-tuple-element.97.refs_0_, ...), custom_call_target="tpu_custom_call" | custom-call | flops 40000000000 | tf_op jit(solution)/shard_map/pallas_call | solution.py:1299
  407.8 4.8 %shard_map.227 = f32[4,520,512]{2,1,0:T(8,128)} custom-call(bf16[4,520,512]{2,1,0:T(8,128)(2,1)} %get-tuple-element.109.zero_ref, bf16[4,520,512]{2,1,0:T(8,128)(2,1)} %get-tuple-element.110.one_ref), custom_call_target="tpu_custom_call" | custom-call | flops 3000000000 | tf_op jit(solution)/shard_map/pallas_call | solution.py:2258
  412.6 0.2 bitcast_convert_fusion
  412.8 1.3 copy.32
  414.1 0.1 convert_bitcast_fusion
  414.2 0.9 copy.31
  415.1 1.1 convert.11
  416.2 0.7 convert.9
  417.0 0.7 dynamic_slice.8
  417.7 0.6 dynamic-slice_bitcast_fusion
  (34 shorter events, 0.1 us)
Async XLA Ops:
  258.8 45.2 %copy-start.5 = (f32[8,512]{1,0:T(8,128)S(1)}, f32[8,512]{1,0:T(8,128)}, u32[]{:S(2)}) copy-start(f32[8,512]{1,0:T(8,128)} %get-tuple-element.101) | copy-start | bytes 49156
  407.8 4.8 %copy-start.1 = (bf16[2,2,2,64,512]{4,3,2,1,0:T(8,128)(2,1)S(1)}, bf16[2,2,2,64,512]{4,3,2,1,0:T(8,128)(2,1)}, u32[]{:S(2)}) copy-start(bf16[2,2,2,64,512]{4,3,2,1,0:T(8,128)(2,1)} %get-tuple-element.114) | copy-start | bytes 1572868
  412.6 1.5 copy-start.2
  412.8 2.4 copy-start
  414.1 2.1 copy-start.3
  414.1 2.9 copy-start.4

commit v8 on v7

--- a/solution.py
+++ b/solution.py
@@ -482,7 +482,8 @@
     for gather in rest:
         gather.split()
     lead.open()
-    for item in range(items):
+    order = [lax.rem(mp + 1 + item, items) for item in range(items)]
+    for item in order:
         rows.begin(item)
 
     @pl.when(section == 1)
@@ -494,14 +495,14 @@
     for gather in rest:
         gather.open()
     lead.along()
-    rows.forward(0)
+    rows.forward(order[0])
     lead.turn()
-    for item in range(1, items // 2):
+    for item in order[1 : items // 2]:
         rows.forward(item)
     for gather in rest:
         gather.along()
     lead.last()
-    for item in range(items // 2, items):
+    for item in order[items // 2 :]:
         rows.forward(item)
     own_vec.wait()
     for other in range(2 * ranks + 1):
@@ -1127,17 +1128,17 @@
     if tail:
         start_backward = StartBackward(place, tail_refs, take(StartBackward.COUNT), 0)
         rows_ref, hop_refs = start_backward.rows_ref, (start_backward.grad_ref,)
-        start_backward.matrix()
+        vec_sent[0, 0, 0:1], vec_sent[0, 0, 1:2] = start_backward.rows()
     sums = each_of(Hops, ring, hop_refs, line_refs, sum_scratch)
     home = Home(ring, place, 0, rows_ref, gone_ref, home_sems)
     ring.greet_all()
-    for one in sums:
-        one.begin()
+    home.begin()
     for along in alongs[hops:]:
         along.begin()
     if tail:
-        vec_sent[0, 0, 0:1], vec_sent[0, 0, 1:2] = start_backward.rows()
-    home.begin()
+        start_backward.matrix()
+    for one in sums:
+        one.begin()
     partners = (ring.other_core(), ring.other_side(), ring.other_section())
 
     def vec_copy(step):
@@ -1239,6 +1240,7 @@
         self.gain, self.bias = self.vecs_ref[slot, 0:1], self.vecs_ref[slot, 1:2]
         block, count = Projection.BLOCK, self.wide_ref.shape[0] // Projection.BLOCK
         self.blocks = [slice(i * block, (i + 1) * block) for i in range(count)]
+        halves_into(self.wide_ref, self.source_ref)
 
     def parts(self, span):
         for rank in range(self.members):
@@ -1250,7 +1252,6 @@
                     yield at, self.heads_ref[rank, span, shard * self.cut : (shard + 1) * self.cut]
 
     def matrix(self):
-        halves_into(self.wide_ref, self.source_ref)
         for span in self.blocks:
             self.normed_ref[span] = layer_norm(self.wide_ref[span], self.gain, self.bias).astype(LOW)
         for at, heads in self.parts(slice(None)):

time: 424 us -> 416 us (0.981)
  Pallas kernels: 404 us -> 395 us
    pallas_call x1, Pallas kernels: 74.3 us -> 62.3 us  [joint_forward(): pl.pallas_call(functools.partial(joint_forward_kernel, mesh, place, pairs...]
where the time goes in v8:
time: 416 us; the launch traced here: 410 us
  Pallas kernels  395 us (95%)
  local copies, waits for them, and re-layouts  10.5 us (3%)
    pallas_call x1, Pallas kernels, start(): pl.pallas_call(functools.partial(start_kernel, mesh, place, count, fused)...  87.8 us
    pallas_call x1, Pallas kernels, joint_backward(): pl.pallas_call(functools.partial(joint_backward_kernel, mesh, place, pair...  69.9 us
    pallas_call x1, Pallas kernels, finish(): pl.pallas_call(functools.partial(finish_kernel, mesh, place, layers, len(...  68 us
    pallas_call x2, Pallas kernels, mlp_backward(): pl.pallas_call(functools.partial(mlp_backward_kernel, mesh, place, layer,...  67.7 us
    pallas_call x1, Pallas kernels, joint_forward(): pl.pallas_call(functools.partial(joint_forward_kernel, mesh, place, pairs...  62.3 us
    pallas_call x1, Pallas kernels, within_backward(): pl.pallas_call(functools.partial(within_backward_kernel, mesh, place, pai...  35 us

profile of v8, /device:TPU:0, one launch (start us, length us, event | category | flops | bytes accessed | tf_op | source)
XLA Modules:
  0.0 410.4 jit_solution(6037777844836992384)
XLA Ops:
  0.6 2.0 copy.30
  2.7 1.8 copy.29
  4.5 0.7 convert_element_type.40
  5.1 1.4 stack.11.vec_ref
  6.5 87.8 %shard_map.220 = (bf16[2,520,512]{2,1,0:T(8,128)(2,1)}, f32[9,8,512]{2,1,0:T(8,128)}, bf16[4,520,512]{2,1,0:T(8,128)(2,1)}, bf16[4,2,2,2,48,512]{5,4,3,2,1,0:T(8...) custom-call(bf16[4,520,512]{2,1,0:T(8,128)(2,1)} %bitcast.80, ...), custom_call_target="tpu_custom_call" | custom-call | flops 60000002048 | tf_op jit(solution)/shard_map/pallas_call | solution.py:704
  94.4 62.3 %shard_map.221 = (bf16[2080,256]{1,0:T(8,128)(2,1)}, f32[2080,128]{1,0:T(8,128)}, bf16[2,520,512]{2,1,0:T(8,128)(2,1)}, bf16[4,2,2,2,16,512]{5,4,3,2,1,0:T(8,128...) custom-call(f32[9,8,512]{2,1,0:T(8,128)} %get-tuple-element.64.lengt, ...), custom_call_target="tpu_custom_call" | custom-call | flops 44999999488 | tf_op jit(solution)/shard_map/pallas_call | solution.py:1583
  156.7 24.2 %shard_map.222 = (f32[1040,512]{1,0:T(8,128)}, bf16[2,1040,256]{2,1,0:T(8,128)(2,1)}, bf16[4,2,2,2,16,512]{5,4,3,2,1,0:T(8,128)(2,1)}, bf16[4,2,2,2,64,512]{5,4,...) custom-call(bf16[2,520,512]{2,1,0:T(8,128)(2,1)} %get-tuple-element.7, ...), custom_call_target="tpu_custom_call" | custom-call | flops 24999999488 | tf_op jit(solution)/shard_map/pallas_call | solution.py:2092
  180.9 69.9 %shard_map.223 = (bf16[2,2,1040,384]{3,2,1,0:T(8,128)(2,1)}, bf16[16,512]{1,0:T(8,128)(2,1)}, bf16[64,512]{1,0:T(8,128)(2,1)}, bf16[64,512]{1,0:T(8,128)(2,1)}, bf16[4,520,512]{2,1,0:T(8,128)(2,1)}) custom-call(f32[9,8,512]{2,1,0:T(8,128)} %get-tuple-element.64.length_ref.refs_2_.refs_3_, bf16[2080,768]{1,0:T(8,128)(2,1)} %get-tuple-element.76.qkv_ref, ...), custom_call_target="tpu_custom_call" | custom-call | flops 65999998976 | tf_op jit(solution)/shard_map/pallas_call | solution.py:1778
  250.8 0.0 copy-start.5
  250.8 43.5 %shard_map.224 = (f32[1040,512]{1,0:T(8,128)}, bf16[2,1040,256]{2,1,0:T(8,128)(2,1)}, bf16[4,2,2,2,16,512]{5,4,3,2,1,0:T(8,128)(2,1)}, bf16[4,2,2,2,64,512]{5,4,...) custom-call(bf16[2,520,512]{2,1,0:T(8,128)(2,1)} %get-tuple-element.6, ...), custom_call_target="tpu_custom_call" | custom-call | flops 24999999488 | tf_op jit(solution)/shard_map/pallas_call | solution.py:2092
  294.3 0.9 fusion
  295.2 0.7 slice_bitcast_fusion.1
  296.1 0.6 pad_maximum_fusion.refs_5_
  296.8 35.0 %shard_map.225 = (bf16[2,1040,768]{2,1,0:T(8,128)(2,1)}, bf16[4,16,512]{2,1,0:T(8,128)(2,1)}, bf16[4,64,512]{2,1,0:T(8,128)(2,1)}, bf16[4,64,512]{2,1,0:T(8,128)(2,1)}, bf16[48,512]{1,0:T(8,128)(2,1)}) custom-call(f32[9,8,512]{2,1,0:T(8,128)} %get-tuple-element.64.length_ref.refs_2_.refs_3_, bf16[2080,768]{1,0:T(8,128)(2,1)} %get-tuple-element.65.x_ref, ...), custom_call_target="tpu_custom_call" | custom-call | flops 30000001024 | tf_op jit(solution)/shard_map/pallas_call | solution.py:1926
  331.8 68.0 %shard_map.226 = (bf16[4,520,512]{2,1,0:T(8,128)(2,1)}, f32[2,10,512]{2,1,0:T(8,128)}, bf16[2,2,2,48,512]{4,3,2,1,0:T(8,128)(2,1)}, bf16[2,2,2,16,512]{4,3,2,1,0...) custom-call(bf16[2,1040,768]{2,1,0:T(8,128)(2,1)} %get-tuple-element.97.refs_0_, ...), custom_call_target="tpu_custom_call" | custom-call | flops 40000000000 | tf_op jit(solution)/shard_map/pallas_call | solution.py:1300
  399.7 4.8 %shard_map.227 = f32[4,520,512]{2,1,0:T(8,128)} custom-call(bf16[4,520,512]{2,1,0:T(8,128)(2,1)} %get-tuple-element.109.zero_ref, bf16[4,520,512]{2,1,0:T(8,128)(2,1)} %get-tuple-element.110.one_ref), custom_call_target="tpu_custom_call" | custom-call | flops 3000000000 | tf_op jit(solution)/shard_map/pallas_call | solution.py:2259
  404.5 0.2 bitcast_convert_fusion
  404.7 1.3 copy.32
  406.0 0.1 convert_bitcast_fusion
  406.1 0.9 copy.31
  407.1 1.1 convert.11
  408.2 0.7 convert.9
  408.9 0.7 dynamic_slice.8
  409.6 0.6 dynamic-slice_bitcast_fusion
  (34 shorter events, 0.1 us)
Async XLA Ops:
  250.8 45.2 %copy-start.5 = (f32[8,512]{1,0:T(8,128)S(1)}, f32[8,512]{1,0:T(8,128)}, u32[]{:S(2)}) copy-start(f32[8,512]{1,0:T(8,128)} %get-tuple-element.101) | copy-start | bytes 49156
  399.7 4.8 %copy-start.1 = (bf16[2,2,2,64,512]{4,3,2,1,0:T(8,128)(2,1)S(1)}, bf16[2,2,2,64,512]{4,3,2,1,0:T(8,128)(2,1)}, u32[]{:S(2)}) copy-start(bf16[2,2,2,64,512]{4,3,2,1,0:T(8,128)(2,1)} %get-tuple-element.114) | copy-start | bytes 1572868
  404.5 1.5 copy-start.2
  404.7 2.4 copy-start
  406.0 2.1 copy-start.3
  406.0 2.9 copy-start.4

commit v9 on v8

--- a/solution.py
+++ b/solution.py
@@ -1393,7 +1393,8 @@
         return taken
 
     if fused:
-        rows_in_ref, before_ref, vecs_ref, weight_ref, out_ref, up_ref, down_ref = take(7)
+        rows_in_ref, before_ref, vecs_ref = take(3)
+        away_refs = take(4)
     else:
         (x_ref,) = take(1)
     piece_refs = take(count)
@@ -1421,10 +1422,19 @@
         me, members = place.member(), place.members
         here = o_ref.shape[0] // members
         span = functools.partial(row_span, here)
-        projection = Projection(place, weight_ref, vecs_ref, ring.ranks, qkv_ref, take(Projection.COUNT))
-        to_heads = projection.to_heads
+        projection_scratch = take(Projection.COUNT)
         to_rows = Swap(place, lambda rank: o_ref.at[span(rank)], lambda rank: mixed_ref.at[rank], take(2))
         local, result_ref, second_ref, hidden_ref = take(4)
+        fetched, fetch_sems = take(4), take(1)[0]
+        weight_ref, out_ref, up_ref, down_ref = fetched
+        fetches = [
+            pltpu.make_async_copy(away_ref, ref, fetch_sems.at[i])
+            for i, (away_ref, ref) in enumerate(zip(away_refs, fetched))
+        ]
+        projection = Projection(place, weight_ref, vecs_ref, ring.ranks, qkv_ref, projection_scratch)
+        to_heads = projection.to_heads
+        for i in (1, 2, 3, 0):
+            fetches[i].start()
         each = here // block
         first = each * (me + 1)
 
@@ -1432,6 +1442,7 @@
         _, _, bias_out, gain_two, bias_two, bias_down = [vecs_ref[0, i : i + 1] for i in range(6)]
         shards = ring.ranks // members
         halves_into(wide_ref, rows_in_ref)
+        fetches[1].wait()
         for at in range(0, here, Projection.BLOCK):
             some = slice(at, at + Projection.BLOCK)
             middle = wide_ref[some] + bias_out
@@ -1440,6 +1451,8 @@
                 middle = middle + dot(before_ref[rank, some], weight)
             second_ref[some] = layer_norm(middle, gain_two, bias_two).astype(LOW)
             result_ref[some] = middle + bias_down
+        fetches[2].wait()
+        fetches[3].wait()
         for rank in range(ring.ranks):
             up, down = up_ref[rank].reshape(-1, width), down_ref[rank].reshape(-1, width)
             pre = dot_rows(second_ref[...], up) + vecs_ref[rank, 6:7]
@@ -1454,6 +1467,7 @@
             boundary_ref[part] = low
             wide_ref[part * here // 2 : (part + 1) * here // 2] = wide(low)
         projection.norm()
+        fetches[0].wait()
         for member in range(members):
             projection.project(member)
         mask_keys(bias_ref, used_slots(place, vecs_ref))
@@ -1577,6 +1591,8 @@
             pltpu.VMEM((here, width), F32),
             pltpu.VMEM((here, width), LOW),
             pltpu.VMEM((here, width), LOW),
+            *[pltpu.VMEM(weight.shape, LOW) for weight in inputs[3:]],
+            pltpu.SemaphoreType.DMA((4,)),
         ]
     else:
         rows, pairs = inputs[0].shape[0], inputs[0].shape[1] // (3 * PAIR)
@@ -1590,7 +1606,9 @@
         + fulls
         + more,
         in_specs=[length_spec(fused), away, away]
-        + [held] * (len(inputs) + len(pieces)),
+        + [held] * len(inputs[:3])
+        + [away] * len(inputs[3:])
+        + [held] * len(pieces),
         out_specs=(held,) * 3 + (away,) * len(fulls) + (held,) * len(more),
         scratch_shapes=Gather.scratch(ranks) * len(pieces)
         + [
@@ -2244,29 +2262,6 @@
     return lax.dynamic_index_in_dim(x, index, axis, keepdims=False)
 
 
-def ends_kernel(zero_ref, one_ref, o_ref):
-    section = lax.axis_index("section")
-    for index, ref in enumerate((zero_ref, one_ref)):
-
-        @pl.when(section == index)
-        def _():
-            o_ref[...] = ref[...].astype(F32)
-
-
-def ends_of(zero, one):
-    block = (1,) + zero.shape[1:]
-    spec = pl.BlockSpec(block, lambda i: (i, 0, 0))
-    return pl.pallas_call(
-        ends_kernel,
-        grid=(zero.shape[0],),
-        out_shape=jax.ShapeDtypeStruct(zero.shape, F32),
-        in_specs=[spec] * 2,
-        out_specs=spec,
-        cost_estimate=cost(3),
-        compiler_params=pltpu.CompilerParams(vmem_limit_bytes=VMEM_BYTES),
-    )(zero, one)
-
-
 def far_groups(dps):
     return [[low + 4 * high for high in range(dps // 4)] for low in range(4)]
 
@@ -2377,7 +2372,7 @@
             lax.psum(m, "dp", axis_index_groups=far_groups(dps)) for m in (sums, *matrices)
         )
 
-    ends = ends_of(gone, results)[None]
+    ends = jnp.where(section == 0, gone, results).astype(F32)[None]
     parts = [m.reshape(-1, width).astype(F32) for m in matrices]
     sums = pick(sums, section, 0).reshape(-1)
     small = [sums[i * width : (i + 1) * width][None] for i in range(6)]

time: 416 us -> 413 us (level)
  Pallas kernels: 395 us -> 389 us
    pallas_call x1 -> x0, Pallas kernels: 4.79 us -> none  [ends_of(): pl.pallas_call(ends_kernel, grid=(zero.shape[0],), out_shape=jax.ShapeDty...]
where the time goes in v9:
time: 413 us; the launch traced here: 408 us
  Pallas kernels  389 us (94%)
  local copies, waits for them, and re-layouts  10.5 us (3%)
  other arithmetic  7.34 us (2%)
    pallas_call x1, Pallas kernels, start(): pl.pallas_call(functools.partial(start_kernel, mesh, place, count, fused)...  87.8 us
    pallas_call x1, Pallas kernels, joint_backward(): pl.pallas_call(functools.partial(joint_backward_kernel, mesh, place, pair...  70 us
    pallas_call x1, Pallas kernels, finish(): pl.pallas_call(functools.partial(finish_kernel, mesh, place, layers, len(...  68.1 us
    pallas_call x2, Pallas kernels, mlp_backward(): pl.pallas_call(functools.partial(mlp_backward_kernel, mesh, place, layer,...  67.6 us
    pallas_call x1, Pallas kernels, joint_forward(): pl.pallas_call(functools.partial(joint_forward_kernel, mesh, place, pairs...  60.3 us
    pallas_call x1, Pallas kernels, within_backward(): pl.pallas_call(functools.partial(within_backward_kernel, mesh, place, pai...  35 us

profile of v9, /device:TPU:0, one launch (start us, length us, event | category | flops | bytes accessed | tf_op | source)
XLA Modules:
  0.0 407.7 jit_solution(13000781548809184412)
XLA Ops:
  0.6 2.0 copy.30
  2.7 1.8 copy.29
  4.5 0.7 convert_element_type.41
  5.1 1.4 stack.11.vec_ref
  6.5 87.8 %shard_map.220 = (bf16[2,520,512]{2,1,0:T(8,128)(2,1)}, f32[9,8,512]{2,1,0:T(8,128)}, bf16[4,520,512]{2,1,0:T(8,128)(2,1)}, bf16[4,2,2,2,48,512]{5,4,3,2,1,0:T(8...) custom-call(bf16[4,520,512]{2,1,0:T(8,128)(2,1)} %bitcast.82, ...), custom_call_target="tpu_custom_call" | custom-call | flops 60000002048 | tf_op jit(solution)/shard_map/pallas_call | solution.py:704
  94.4 60.3 %shard_map.221 = (bf16[2080,256]{1,0:T(8,128)(2,1)}, f32[2080,128]{1,0:T(8,128)}, bf16[2,520,512]{2,1,0:T(8,128)(2,1)}, bf16[4,2,2,2,16,512]{5,4,3,2,1,0:T(8,128...) custom-call(f32[9,8,512]{2,1,0:T(8,128)} %get-tuple-element.64.lengt, ...), custom_call_target="tpu_custom_call" | custom-call | flops 44999999488 | tf_op jit(solution)/shard_map/pallas_call | solution.py:1599
  154.7 24.2 %shard_map.222 = (f32[1040,512]{1,0:T(8,128)}, bf16[2,1040,256]{2,1,0:T(8,128)(2,1)}, bf16[4,2,2,2,16,512]{5,4,3,2,1,0:T(8,128)(2,1)}, bf16[4,2,2,2,64,512]{5,4,...) custom-call(bf16[2,520,512]{2,1,0:T(8,128)(2,1)} %get-tuple-element.7, ...), custom_call_target="tpu_custom_call" | custom-call | flops 24999999488 | tf_op jit(solution)/shard_map/pallas_call | solution.py:2110
  178.9 70.0 %shard_map.223 = (bf16[2,2,1040,384]{3,2,1,0:T(8,128)(2,1)}, bf16[16,512]{1,0:T(8,128)(2,1)}, bf16[64,512]{1,0:T(8,128)(2,1)}, bf16[64,512]{1,0:T(8,128)(2,1)}, bf16[4,520,512]{2,1,0:T(8,128)(2,1)}) custom-call(f32[9,8,512]{2,1,0:T(8,128)} %get-tuple-element.64.length_ref.refs_2_.refs_3_, bf16[2080,768]{1,0:T(8,128)(2,1)} %get-tuple-element.76.qkv_ref, ...), custom_call_target="tpu_custom_call" | custom-call | flops 65999998976 | tf_op jit(solution)/shard_map/pallas_call | solution.py:1796
  248.9 0.0 copy-start.6
  248.9 43.4 %shard_map.224 = (f32[1040,512]{1,0:T(8,128)}, bf16[2,1040,256]{2,1,0:T(8,128)(2,1)}, bf16[4,2,2,2,16,512]{5,4,3,2,1,0:T(8,128)(2,1)}, bf16[4,2,2,2,64,512]{5,4,...) custom-call(bf16[2,520,512]{2,1,0:T(8,128)(2,1)} %get-tuple-element.6, ...), custom_call_target="tpu_custom_call" | custom-call | flops 24999999488 | tf_op jit(solution)/shard_map/pallas_call | solution.py:2110
  292.3 0.9 fusion
  293.2 0.7 slice_bitcast_fusion.1
  294.1 0.6 pad_maximum_fusion.refs_5_
  294.8 35.0 %shard_map.225 = (bf16[2,1040,768]{2,1,0:T(8,128)(2,1)}, bf16[4,16,512]{2,1,0:T(8,128)(2,1)}, bf16[4,64,512]{2,1,0:T(8,128)(2,1)}, bf16[4,64,512]{2,1,0:T(8,128)(2,1)}, bf16[48,512]{1,0:T(8,128)(2,1)}) custom-call(f32[9,8,512]{2,1,0:T(8,128)} %get-tuple-element.64.length_ref.refs_2_.refs_3_, bf16[2080,768]{1,0:T(8,128)(2,1)} %get-tuple-element.65.x_ref, ...), custom_call_target="tpu_custom_call" | custom-call | flops 30000001024 | tf_op jit(solution)/shard_map/pallas_call | solution.py:1944
  329.8 68.1 %shard_map.226 = (bf16[4,520,512]{2,1,0:T(8,128)(2,1)}, f32[2,10,512]{2,1,0:T(8,128)}, bf16[2,2,2,48,512]{4,3,2,1,0:T(8,128)(2,1)}, bf16[2,2,2,16,512]{4,3,2,1,0...) custom-call(bf16[2,1040,768]{2,1,0:T(8,128)(2,1)} %get-tuple-element.97.refs_0_, ...), custom_call_target="tpu_custom_call" | custom-call | flops 40000000000 | tf_op jit(solution)/shard_map/pallas_call | solution.py:1300
  397.9 4.0 bitcast_convert_fusion
  401.9 0.2 bitcast_convert_fusion.1
  402.1 1.3 copy.32
  403.4 0.1 convert_bitcast_fusion
  403.5 0.9 copy.31
  404.4 1.1 convert.13
  405.5 0.7 convert.11
  406.3 0.7 dynamic_slice.8
  406.9 0.6 dynamic-slice_bitcast_fusion
  (36 shorter events, 0.1 us)
Async XLA Ops:
  248.9 45.1 %copy-start.6 = (f32[8,512]{1,0:T(8,128)S(1)}, f32[8,512]{1,0:T(8,128)}, u32[]{:S(2)}) copy-start(f32[8,512]{1,0:T(8,128)} %get-tuple-element.101) | copy-start | bytes 49156
  329.8 68.1 %copy-start = (bf16[4,520,512]{2,1,0:T(8,128)(2,1)S(1)}, bf16[4,520,512]{2,1,0:T(8,128)(2,1)}, u32[]{:S(2)}) copy-start(bf16[4,520,512]{2,1,0:T(8,128)(2,1)} %get-tuple-element.110) | copy-start | bytes 6389764
  397.9 4.0 copy-start.2
  401.9 1.5 copy-start.3
  402.1 2.4 copy-start.1
  403.4 2.1 copy-start.4
  403.4 2.9 copy-start.5
